TPU v7x, 32 devices: a whole 2x2x4 slice. The times are simulated.
32 devices in a mesh: rep: 4 (over x, core), shard: 8 (over z, y).
Axes of the slice: x: 2, y: 2, z: 4, core: 2. Of those that a mesh axis runs over, the one named last changes fastest.
Arguments:
- tokens: bfloat16 [32, 1024, 1152], P(('rep', 'shard')), may hold values from -6 to 6
- cotangent: bfloat16 [32, 1024, 1152], P(('rep', 'shard'))
- segments: int32 [32, 1024], P(('rep', 'shard')), may hold values from 0 to 4, as said below
- positions: int32 [32, 1024], P(('rep', 'shard')), may hold values from 0 to 783, as said below
- wide_master: float32 [3, 1152, 3072], P(None, 'shard'), may hold values from -0.1875 to 0.1875
- square_master: float32 [2, 1152, 1152], P(None, 'shard')
- key_value_master: float32 [2, 1152, 384], P(None, 'shard'), may hold values from -0.1875 to 0.1875
- wide_moment: float32 [3, 1152, 3072], P(None, 'shard'), may hold values from -16 to 16
- square_moment: float32 [2, 1152, 1152], P(None, 'shard'), may hold values from -10 to 10
- key_value_momentum: float32 [2, 1152, 384], P(None, 'shard'), may hold values from -28 to 28
- wide_error: float32 [4, 3, 1152, 3072], P('rep', None, 'shard'), may hold values from -256 to 256
- square_error: float32 [4, 2, 1152, 1152], P('rep', None, 'shard'), may hold values from -160 to 160
- key_value_error: float32 [4, 2, 1152, 384], P('rep', None, 'shard'), may hold values from -448 to 448
- wide_factor: float32 [3, 8, 3072], replicated, may hold values from -6 to 6
- square_factor: float32 [2, 8, 1152], replicated, may hold values from -6 to 6
- key_value_factor: float32 [2, 8, 384], replicated, may hold values from -6 to 6
- norm_gains: float32 [2, 1152], P(None, 'shard')
- gain_moment: float32 [2, 1152], P(None, 'shard'), may hold values from -256 to 256
Outputs:
- output: bfloat16 [32, 1024, 1152], P(('rep', 'shard'))
- input_grad: bfloat16 [32, 1024, 1152], P(('rep', 'shard'))
- wide_new: float32 [3, 1152, 3072], P(None, 'shard')
- square_new: float32 [2, 1152, 1152], P(None, 'shard')
- narrow_new: float32 [2, 1152, 384], P(None, 'shard')
- wide_moment_new: float32 [3, 1152, 3072], P(None, 'shard')
- square_moment_new: float32 [2, 1152, 1152], P(None, 'shard')
- narrow_moment_new: float32 [2, 1152, 384], P(None, 'shard')
- wide_error_new: float32 [4, 3, 1152, 3072], P('rep', None, 'shard')
- square_error_new: float32 [4, 2, 1152, 1152], P('rep', None, 'shard')
- narrow_error_new: float32 [4, 2, 1152, 384], P('rep', None, 'shard')
- wide_factor_new: float32 [3, 8, 3072], replicated
- square_factor_new: float32 [2, 8, 1152], replicated
- narrow_factor_new: float32 [2, 8, 384], replicated
- gains_new: float32 [2, 1152], P(None, 'shard')
- gain_moment_new: float32 [2, 1152], P(None, 'shard')
Inputs may be any that keep to these rules, and one draw needn't show every extreme that they name: `segments`: within each row the number starts at 0 and rises by one at each new document; each row holds 5 documents of 60 or more tokens. `positions`: counts from 0 at the first token of each document; some row holds a document of 1024 - (5 - 1) * 60 tokens.
All inputs are finite; a program needn't handle non-finite values.
Results may differ from a plain program's by a relative error of at most 0.02.
The roundings to bfloat16 on the way count: a program that leaves them out, or rounds other values in their place, can miss the bound.
Values may be sent and summed in bfloat16 or wider, within the bound.
No kernel may reach another device: no remote copies, remote signals or barrier semaphores. Data moves between devices by JAX's collectives and lax.ppermute only.
A program may use at most 448 MiB of HBM per device.

v0:
```python
import jax
import jax.numpy as jnp
from jax import lax
from jax.sharding import PartitionSpec as P

QUERY_HEADS = 18
KEY_VALUE_HEADS = 6
HEAD_SIZE = 64


eps_norm = 1e-05
theta_base = 10000.0
decay_rate = 0.9
rate_wide = 0.03
rate_square = 0.1
rate_narrow = 0.02
rate_gains = 0.01
mask_fill = -1e30
highest = lax.Precision.HIGHEST


def normed(value_heads, gain):
    return (
        value_heads
        * lax.rsqrt(jnp.mean(value_heads * value_heads, axis=-1, keepdims=True) + eps_norm)
        * gain
    )


def rotary_tables(position, width):
    halfway = width // 2
    inverse = theta_base ** (-2.0 * jnp.arange(halfway, dtype=jnp.float32) / width)
    angles = position.astype(jnp.float32)[:, None] * inverse[None, :]
    return (jnp.cos(angles), jnp.sin(angles))


def apply_rotation(value_heads, cosine_table, sine_table):
    halfway = value_heads.shape[-1] // 2
    first_half = value_heads[..., :halfway]
    second_half = value_heads[..., halfway:]
    cos_wide = cosine_table[:, None, :]
    sin_wide = sine_table[:, None, :]
    return jnp.concatenate(
        [
            first_half * cos_wide - second_half * sin_wide,
            second_half * cos_wide + first_half * sin_wide,
        ],
        axis=-1,
    )


def block_scores(query_block, rotated_keys, segment, start_row):
    block_len = query_block.shape[0]
    scores = (
        jnp.einsum("qagd,kad->agqk", query_block, rotated_keys, preferred_element_type=jnp.float32)
        * 0.125
    )
    query_rows = start_row + jnp.arange(block_len)
    key_rows = jnp.arange(rotated_keys.shape[0])
    seg_query = segment[start_row : start_row + block_len]
    allowed = (seg_query[:, None] == segment[None, :]) & (query_rows[:, None] >= key_rows[None, :])
    return (scores, allowed)


def attend_forward(query_heads, rotated_keys, value_heads, segment, block_rows):
    outputs = []
    log_totals = []
    for start_row in range(0, query_heads.shape[0], block_rows):
        query_block = query_heads[start_row : start_row + block_rows]
        scores, allowed = block_scores(query_block, rotated_keys, segment, start_row)
        scores = jnp.where(allowed, scores, mask_fill)
        top_score = jnp.max(scores, axis=-1, keepdims=True)
        exponent_vals = jnp.exp(scores - top_score)
        row_total = jnp.sum(exponent_vals, axis=-1, keepdims=True)
        prob_low = (exponent_vals / row_total).astype(jnp.bfloat16)
        attended = jnp.einsum(
            "agqk,kad->qagd", prob_low, value_heads, preferred_element_type=jnp.float32
        )
        outputs.append(attended.reshape(query_block.shape[0], -1).astype(jnp.bfloat16))
        log_totals.append(top_score + jnp.log(row_total))
    return (jnp.concatenate(outputs, axis=0), log_totals)


def attend_backward(
    query_heads, rotated_keys, value_heads, d_attended, segment, block_rows, log_totals
):
    query_parts = []
    d_keys = jnp.zeros(rotated_keys.shape, jnp.float32)
    values_gradient = jnp.zeros(value_heads.shape, jnp.float32)
    for block_idx, start_row in enumerate(range(0, query_heads.shape[0], block_rows)):
        query_block = query_heads[start_row : start_row + block_rows]
        d_block = d_attended[start_row : start_row + block_rows]
        scores, allowed = block_scores(query_block, rotated_keys, segment, start_row)
        prob_full = jnp.where(allowed, jnp.exp(scores - log_totals[block_idx]), 0.0)
        d_prob = jnp.einsum(
            "qagd,kad->agqk", d_block, value_heads, preferred_element_type=jnp.float32
        )
        row_delta = jnp.sum(prob_full * d_prob, axis=-1, keepdims=True)
        d_scores = (prob_full * (d_prob - row_delta)).astype(jnp.bfloat16)
        query_parts.append(
            jnp.einsum("agqk,kad->qagd", d_scores, rotated_keys, preferred_element_type=jnp.float32)
            * 0.125
        )
        d_keys = (
            d_keys
            + jnp.einsum(
                "agqk,qagd->kad", d_scores, query_block, preferred_element_type=jnp.float32
            )
            * 0.125
        )
        values_gradient = values_gradient + jnp.einsum(
            "agqk,qagd->kad",
            prob_full.astype(jnp.bfloat16),
            d_block,
            preferred_element_type=jnp.float32,
        )
    return (jnp.concatenate(query_parts, axis=0), d_keys, values_gradient)


def project(mixed, factor):
    return jnp.einsum("kdn,krn->kdr", mixed, factor, precision=highest)


def inner_gram(left_factor):
    return jnp.einsum("kdr,kds->krs", left_factor, left_factor, precision=highest)


def orthonormal(left_factor, gram):
    chol = jnp.linalg.cholesky(gram)
    return lax.linalg.triangular_solve(
        chol, left_factor, left_side=False, lower=True, transpose_a=True
    )


def contract(basis, mixed):
    return jnp.einsum("kdr,kdn->krn", basis, mixed, precision=highest)


def renew(mixed, basis, factor_new, moment, master, rate):
    approx = jnp.einsum("kdr,krn->kdn", basis, factor_new, precision=highest)
    moment_new = decay_rate * moment + approx
    return (master - rate * moment_new, moment_new, (mixed - approx)[None])


def shards(
    tokens,
    cotangent,
    segments,
    positions,
    wide_master,
    square_master,
    key_value_master,
    wide_moment,
    square_moment,
    key_value_momentum,
    wide_error,
    square_error,
    key_value_error,
    wide_factor,
    square_factor,
    key_value_factor,
    norm_gains,
    gain_moment,
):
    wide_w, square_w, key_value_weight, gain_w = (
        lax.all_gather(wide_master.astype(jnp.bfloat16), "shard", axis=1, tiled=True),
        lax.all_gather(square_master.astype(jnp.bfloat16), "shard", axis=1, tiled=True),
        lax.all_gather(key_value_master.astype(jnp.bfloat16), "shard", axis=1, tiled=True),
        lax.all_gather(norm_gains.astype(jnp.bfloat16), "shard", axis=1, tiled=True),
    )
    packed_row_count = tokens.shape[1]
    block_rows = min(512, packed_row_count)
    query_groups = QUERY_HEADS // KEY_VALUE_HEADS
    hidden_in = tokens[0].astype(jnp.float32)
    segment = segments[0]
    position = positions[0]
    d_out = cotangent[0]
    gain_attn = gain_w[0].astype(jnp.float32)
    gain_mlp = gain_w[1].astype(jnp.float32)
    cosine_table, sine_table = rotary_tables(position, HEAD_SIZE)

    def rotary_embed(values_in):
        return apply_rotation(values_in, cosine_table, sine_table)

    normalized_input = normed(hidden_in, gain_attn).astype(jnp.bfloat16)
    unrotated_query = jnp.dot(
        normalized_input, square_w[0], preferred_element_type=jnp.float32
    ).reshape(packed_row_count, QUERY_HEADS, HEAD_SIZE)
    query_heads = (
        rotary_embed(unrotated_query)
        .astype(jnp.bfloat16)
        .reshape(packed_row_count, KEY_VALUE_HEADS, query_groups, HEAD_SIZE)
    )
    key_raw = jnp.dot(
        normalized_input, key_value_weight[0], preferred_element_type=jnp.float32
    ).reshape(packed_row_count, KEY_VALUE_HEADS, HEAD_SIZE)
    rotated_keys = rotary_embed(key_raw).astype(jnp.bfloat16)
    value_heads = (
        jnp.dot(normalized_input, key_value_weight[1], preferred_element_type=jnp.float32)
        .astype(jnp.bfloat16)
        .reshape(packed_row_count, KEY_VALUE_HEADS, HEAD_SIZE)
    )
    attended, log_totals = attend_forward(
        query_heads, rotated_keys, value_heads, segment, block_rows
    )
    residual = hidden_in + jnp.einsum(
        "tn,dn->td", attended, square_w[1], preferred_element_type=jnp.float32
    )
    normed_mid = normed(residual, gain_mlp).astype(jnp.bfloat16)
    gate = jnp.dot(normed_mid, wide_w[0], preferred_element_type=jnp.float32)
    upward = jnp.dot(normed_mid, wide_w[1], preferred_element_type=jnp.float32)
    hidden = (jax.nn.silu(gate) * upward).astype(jnp.bfloat16)
    result = residual + jnp.einsum(
        "tf,df->td", hidden, wide_w[2], preferred_element_type=jnp.float32
    )
    wide_w, square_w, key_value_weight = (
        lax.all_gather(wide_master.astype(jnp.bfloat16), "shard", axis=1, tiled=True),
        lax.all_gather(square_master.astype(jnp.bfloat16), "shard", axis=1, tiled=True),
        lax.all_gather(key_value_master.astype(jnp.bfloat16), "shard", axis=1, tiled=True),
    )
    d_hidden = jnp.einsum("td,df->tf", d_out, wide_w[2], preferred_element_type=jnp.float32)
    _, silu_back = jax.vjp(lambda gate_in, up_in: jax.nn.silu(gate_in) * up_in, gate, upward)
    d_gate, d_up = silu_back(d_hidden)
    d_gate = d_gate.astype(jnp.bfloat16)
    d_up = d_up.astype(jnp.bfloat16)
    grad_wide = jnp.stack(
        [
            jnp.einsum("td,tf->df", normed_mid, d_gate, preferred_element_type=jnp.float32),
            jnp.einsum("td,tf->df", normed_mid, d_up, preferred_element_type=jnp.float32),
            jnp.einsum("td,tf->df", d_out, hidden, preferred_element_type=jnp.float32),
        ]
    )
    d_normed_mid = jnp.einsum(
        "tf,df->td", d_gate, wide_w[0], preferred_element_type=jnp.float32
    ) + jnp.einsum("tf,df->td", d_up, wide_w[1], preferred_element_type=jnp.float32)
    _, mid_back = jax.vjp(normed, residual, gain_mlp)
    d_residual, grad_gain_mlp = mid_back(d_normed_mid)
    d_residual = d_residual + d_out.astype(jnp.float32)
    d_branch = d_residual.astype(jnp.bfloat16)
    grad_out = jnp.einsum("td,tn->dn", d_branch, attended, preferred_element_type=jnp.float32)
    d_attended = (
        jnp.einsum("td,dn->tn", d_branch, square_w[1], preferred_element_type=jnp.float32)
        .astype(jnp.bfloat16)
        .reshape(packed_row_count, KEY_VALUE_HEADS, query_groups, HEAD_SIZE)
    )
    d_query_rot, rotated_key_gradient, values_gradient = attend_backward(
        query_heads, rotated_keys, value_heads, d_attended, segment, block_rows, log_totals
    )
    _, query_back = jax.vjp(rotary_embed, unrotated_query)
    d_query = (
        query_back(d_query_rot.reshape(packed_row_count, QUERY_HEADS, HEAD_SIZE))[0]
        .reshape(packed_row_count, QUERY_HEADS * HEAD_SIZE)
        .astype(jnp.bfloat16)
    )
    _, key_pullback = jax.vjp(rotary_embed, key_raw)
    key_gradient = (
        key_pullback(rotated_key_gradient)[0]
        .reshape(packed_row_count, KEY_VALUE_HEADS * HEAD_SIZE)
        .astype(jnp.bfloat16)
    )
    value_gradient = values_gradient.reshape(packed_row_count, KEY_VALUE_HEADS * HEAD_SIZE).astype(
        jnp.bfloat16
    )
    grad_square = jnp.stack(
        [
            jnp.einsum("td,tn->dn", normalized_input, d_query, preferred_element_type=jnp.float32),
            grad_out,
        ]
    )
    grad_narrow = jnp.stack(
        [
            jnp.einsum(
                "td,tn->dn", normalized_input, key_gradient, preferred_element_type=jnp.float32
            ),
            jnp.einsum(
                "td,tn->dn", normalized_input, value_gradient, preferred_element_type=jnp.float32
            ),
        ]
    )
    d_normed_in = (
        jnp.einsum("tn,dn->td", d_query, square_w[0], preferred_element_type=jnp.float32)
        + jnp.einsum(
            "tn,dn->td", key_gradient, key_value_weight[0], preferred_element_type=jnp.float32
        )
        + jnp.einsum(
            "tn,dn->td", value_gradient, key_value_weight[1], preferred_element_type=jnp.float32
        )
    )
    _, in_back = jax.vjp(normed, hidden_in, gain_attn)
    d_input, grad_gain_attn = in_back(d_normed_in)
    d_input = d_input + d_residual
    wide_share, square_share, narrow_share, gain_share = (
        lax.psum_scatter(grad_wide, "shard", scatter_dimension=1, tiled=True),
        lax.psum_scatter(grad_square, "shard", scatter_dimension=1, tiled=True),
        lax.psum_scatter(grad_narrow, "shard", scatter_dimension=1, tiled=True),
        lax.psum_scatter(
            jnp.stack([grad_gain_attn, grad_gain_mlp]), "shard", scatter_dimension=1, tiled=True
        ),
    )
    replicas = lax.axis_size("rep")
    mixed_wide = wide_share + wide_error[0]
    mixed_square = square_share + square_error[0]
    mixed_narrow = narrow_share + key_value_error[0]
    left_wide, left_square, left_narrow, gain_total = lax.psum(
        (
            project(mixed_wide, wide_factor),
            project(mixed_square, square_factor),
            project(mixed_narrow, key_value_factor),
            gain_share,
        ),
        "rep",
    )
    gram_wide, gram_square, gram_narrow = lax.psum(
        (inner_gram(left_wide), inner_gram(left_square), inner_gram(left_narrow)), "shard"
    )
    basis_wide = orthonormal(left_wide, gram_wide)
    basis_square = orthonormal(left_square, gram_square)
    basis_narrow = orthonormal(left_narrow, gram_narrow)
    sum_wide, sum_square, sum_narrow = lax.psum(
        (
            contract(basis_wide, mixed_wide),
            contract(basis_square, mixed_square),
            contract(basis_narrow, mixed_narrow),
        ),
        ("rep", "shard"),
    )
    factor_wide = sum_wide / replicas
    factor_square = sum_square / replicas
    factor_narrow = sum_narrow / replicas
    wide_new, wide_moment_new, wide_error_new = renew(
        mixed_wide, basis_wide, factor_wide, wide_moment, wide_master, rate_wide
    )
    square_new, square_moment_new, square_error_new = renew(
        mixed_square, basis_square, factor_square, square_moment, square_master, rate_square
    )
    narrow_new, narrow_moment_new, narrow_error_new = renew(
        mixed_narrow, basis_narrow, factor_narrow, key_value_momentum, key_value_master, rate_narrow
    )
    gain_moment_new = decay_rate * gain_moment + gain_total / replicas
    gains_new = norm_gains - rate_gains * gain_moment_new
    return (
        result.astype(jnp.bfloat16)[None],
        d_input.astype(jnp.bfloat16)[None],
        wide_new,
        square_new,
        narrow_new,
        wide_moment_new,
        square_moment_new,
        narrow_moment_new,
        wide_error_new,
        square_error_new,
        narrow_error_new,
        factor_wide,
        factor_square,
        factor_narrow,
        gains_new,
        gain_moment_new,
    )


def solution(mesh):
    return jax.shard_map(
        shards,
        mesh=mesh,
        in_specs=(
            P(("rep", "shard"), None, None),
            P(("rep", "shard"), None, None),
            P(("rep", "shard"), None),
            P(("rep", "shard"), None),
            P(None, "shard", None),
            P(None, "shard", None),
            P(None, "shard", None),
            P(None, "shard", None),
            P(None, "shard", None),
            P(None, "shard", None),
            P("rep", None, "shard", None),
            P("rep", None, "shard", None),
            P("rep", None, "shard", None),
            P(),
            P(),
            P(),
            P(None, "shard"),
            P(None, "shard"),
        ),
        out_specs=(
            P(("rep", "shard"), None, None),
            P(("rep", "shard"), None, None),
            P(None, "shard", None),
            P(None, "shard", None),
            P(None, "shard", None),
            P(None, "shard", None),
            P(None, "shard", None),
            P(None, "shard", None),
            P("rep", None, "shard", None),
            P("rep", None, "shard", None),
            P("rep", None, "shard", None),
            P(),
            P(),
            P(),
            P(None, "shard"),
            P(None, "shard"),
        ),
        check_vma=False,
    )
```

profile of v0, /device:TPU:0, one launch (start us, length us, event | category | flops | bytes accessed | tf_op | source)
XLA Modules:
  0.0 2138.4 jit_solution(6419866488056036551)
XLA Ops:
  9.1 2.2 convert_element_type.156
  11.4 4.5 convert_element_type.166
  16.1 22.3 %all-gather = bf16[8,144,2]{1,2,0:T(2,128)(2,1)S(1)} all-gather(bf16[1,144,2]{1,2,0:T(2,128)(2,1)S(1)} %convert_bitcast_fusion.1), channel_id=1, replica_groups=mesh['rep'=4,'shard'=8] {'shard'}, dimensions={0}, use_global_device_ids=true | all-gather | bytes 5184 | tf_op jit(solution)/shard_map/all_gather | solution.py:169
  41.0 18.6 all-gather.5.cloned.1.call-done
  61.7 3.1 fusion.57
  66.6 81.9 %all-gather.7.cloned.1.call-done = bf16[2,1152,1152]{2,1,0:T(8,128)(2,1)} async-done(((bf16[2,144,1152]{2,1,0:T(8,128)(2,1)}), bf16[2,1152,1152]{2,1,0:T(8,128)(2,1)}) %all-gather.7.cloned.1.call-update) | async-done | bytes 5308432 | tf_op jit(solution)/shard_map/all_gather | solution.py:167
  148.4 3.5 slice_bitcast_fusion.18
  151.9 5.2 copy.112
  157.1 5.9 fusion.55
  164.2 15.0 fusion.11
  179.2 15.5 fusion.10
  194.7 18.4 fusion.13
  213.0 4.5 copy-done.1
  217.6 8.7 fusion.12
  226.3 16.0 fusion.70
  242.3 17.6 fusion.71
  259.9 6.7 multiply_reduce_fusion.2
  269.3 286.2 %all-gather.9.cloned.1.call-done = bf16[3,1152,3072]{2,1,0:T(8,128)(2,1)} async-done(((bf16[3,144,3072]{2,1,0:T(8,128)(2,1)}), bf16[3,1152,3072]{2,1,0:T(8,128)(2,1)}) %all-gather.9.cloned.1.call-update) | async-done | bytes 21233680 | tf_op jit(solution)/shard_map/all_gather | solution.py:166
  555.5 13.1 fusion.31
  568.6 14.1 fusion.29
  582.6 23.2 %multiply_convert_fusion = (bf16[1024,3072]{1,0:T(8,128)(2,1)}, bf16[1024,3072]{1,0:T(8,128)(2,1)}, bf16[1024,3072]{1,0:T(8,128)(2,1)}) fusion(f32[1024,3072]{1,0:T(8,128)} %fusion.29, f32[1024,3072]{1,0:T(8,128)} %fusion.31, bf16[3,1152,3072]{2,1,0:T(8,128)(2,1)} %all-gather.9.cloned.1.call-done, bf16[1,1024,1152]{2,1,0:T(8,128)(2,1)S(1)} %copy-done.33), kind=kOutput, calls=%fused_computation.42 | convolution fusion | flops 7298088960 | bytes 53477376 | tf_op jit(solution)/shard_map/td,df->tf/dot_general | solution.py:221
  605.8 14.1 fusion.28
  619.9 13.9 multiply_reduce_fusion
  635.3 7.2 convolution_convert_fusion
  643.7 2.4 copy.117
  646.0 17.3 fusion.16
  663.4 26.5 %fusion = (f32[6,3,512]{2,1,0:T(4,128)S(1)}, f32[6,1024,512,3]{2,1,3,0:T(8,128)}) fusion(f32[6,1024,512,3]{2,1,3,0:T(8,128)} %get-tuple-element.70, f32[6,3,512]{2,1,0:T(4,128)S(1)} %log_add_fusion, pred[512,1024]{0,1:T(8,128)(4,1)S(1)} %copy-done.5, bf16[1024,6,64,1]{0,2,3,1:T(8,128)(2,1)S(1)} %bitcast.391, bf16[512,6,3,64]{0,3,2,1:T(8,128)(2,1)} %bitcast.388), kind=kOutput, calls=%fused_computation.3 | convolution fusion | flops 1255136256 | bytes 78061568 | tf_op jit(solution)/shard_map/qagd,kad->agqk/dot_general | solution.py:95
  691.3 26.4 %fusion.3 = (f32[6,3,512]{2,1,0:T(4,128)S(1)}, f32[6,1024,512,3]{2,1,3,0:T(8,128)}) fusion(f32[6,1024,512,3]{2,1,3,0:T(8,128)} %get-tuple-element.72, f32[6,3,512]{2,1,0:T(4,128)S(1)} %copy-done.42, pred[512,1024]{0,1:T(8,128)(4,1)S(1)} %copy-done.3, bf16[1024,6,64,1]{0,2,3,1:T(8,128)(2,1)S(1)} %bitcast.392, bf16[512,6,3,64]{0,3,2,1:T(8,128)(2,1)} %bitcast.385), kind=kOutput, calls=%fused_computation.8 | convolution fusion | flops 1255136256 | bytes 78061568 | tf_op jit(solution)/shard_map/qagd,kad->agqk/dot_general | solution.py:95
  717.7 61.2 %fusion.2 = (bf16[6,3,512,1024]{2,3,1,0:T(8,128)(2,1)}, bf16[6,3,512,1024]{2,3,1,0:T(8,128)(2,1)}) fusion(f32[6,1024,512,3]{2,1,3,0:T(8,128)} %get-tuple-element.77, f32[6,1024,512,3]{2,1,3,0:T(8,128)} %get-tuple-element.70, f32[6,3,512]{2,1,0:T(4,128)S(1)} %get-tuple-element.76, f32[6,3,512]{2,1,0:T(4,128)S(1)} %log_add_fusion, ...), kind=kLoop, calls=%fused_computation.5 | loop fusion | flops 113246208 | bytes 189939712 | tf_op jit(solution)/shard_map/convert_element_type | solution.py:99
  778.9 13.4 fusion.119
  792.3 11.3 multiply_bitcast_fusion.1
  803.6 15.8 fusion.67
  819.5 3.0 convolution_bitcast_fusion.5
  822.5 11.1 multiply_bitcast_fusion
  833.6 14.0 fusion.69
  847.6 2.8 pad_maximum_fusion.2
  852.3 3.0 convolution_bitcast_fusion.6
  855.7 4.0 fusion.50
  861.2 3.9 fusion.42
  866.3 4.0 pad_maximum_fusion.3
  870.4 6.5 convolution_bitcast_fusion.3
  876.9 3.5 convolution_bitcast_fusion.4
  880.4 4.7 pad_maximum_fusion.1
  885.3 11.5 convolution_bitcast_fusion.1
  896.9 13.1 convolution_bitcast_fusion.2
  910.0 10.8 convolution_bitcast_fusion
  920.8 25.3 %pad_maximum_fusion = f32[3,1152,3072]{2,1,0:T(8,128)} fusion(f32[1,1152,3072]{2,1,0:T(8,128)} %convolution_bitcast_fusion, f32[1,1152,3072]{2,1,0:T(8,128)S(1)} %convolution_bitcast_fusion.1, f32[1,1152,3072]{2,1,0:T(8,128)} %convolution_bitcast_fusion.2), kind=kLoop, calls=%fused_computation | loop fusion | flops 21233664 | bytes 84934656 | tf_op jit(solution)/shard_map/stack | solution.py:226
  946.8 5.8 fusion.52
  952.6 14.8 fusion.49
  968.3 42.3 %reduce-scatter.11.cloned.1.call-done = f32[2,144,384]{2,1,0:T(8,128)} async-done(((f32[2,1152,384]{2,1,0:T(8,128)}), f32[2,144,384]{2,1,0:T(8,128)}) %reduce-scatter.11.cloned.1.call-update) | async-done | bytes 442384 | tf_op jit(solution)/shard_map/reduce_scatter | solution.py:295
  1012.2 181.8 %reduce-scatter.9.cloned.1.call-done = f32[2,144,1152]{2,1,0:T(8,128)} async-done(((f32[2,1152,1152]{2,1,0:T(8,128)}), f32[2,144,1152]{2,1,0:T(8,128)}) %reduce-scatter.9.cloned.1.call-update) | async-done | bytes 1327120 | tf_op jit(solution)/shard_map/reduce_scatter | solution.py:294
  1194.1 2.7 fusion.108
  1196.7 673.3 %reduce-scatter.7.cloned.1.call-done = f32[3,144,3072]{2,1,0:T(8,128)} async-done(((f32[3,1152,3072]{2,1,0:T(8,128)}), f32[3,144,3072]{2,1,0:T(8,128)}) %reduce-scatter.7.cloned.1.call-update) | async-done | bytes 5308432 | tf_op jit(solution)/shard_map/reduce_scatter | solution.py:293
  1870.0 7.2 fusion.110
  1877.3 11.9 all-reduce.6
  1889.6 35.1 %all-reduce.5 = (f32[3,8,8]{1,2,0:T(8,128)S(1)}, f32[2,8,8]{1,2,0:T(8,128)S(1)}, f32[2,8,8]{1,2,0:T(8,128)S(1)}) all-reduce(f32[3,8,8]{1,2,0:T(8,128)S(1)} %fusion.120, f32[2,8,8]{1,2,0:T(8,128)S(1)} %fusion.121, f32[2,8,8]{1,2,0:T(8,128)S(1)} %fusion.122), channel_id=1, replica_groups=mesh['rep'=4,'shard'=8] {'shard'}, use_global_device_ids=true, to_apply=%region_12.13 | all-reduce | flops 448 | bytes 3584 | tf_op jit(solution)/shard_map/psum | solution.py:313
  1931.3 2.2 custom-call.13
  1933.7 1.9 custom-call.14
  1937.2 37.3 %psum.78 = f32[2,8,384]{2,1,0:T(8,128)S(1)} all-reduce(f32[2,8,384]{2,1,0:T(8,128)S(1)} %fusion.105), channel_id=1, replica_groups=mesh['rep'=4,'shard'=8] {'rep','shard'}, use_global_device_ids=true, to_apply=%region_25.28 | all-reduce | flops 6144 | bytes 49152 | tf_op jit(solution)/shard_map/psum | solution.py:319
  1976.0 7.6 fusion.109
  1983.7 3.0 multiply_subtract_fusion.2
  1987.2 123.8 %all-reduce.9.cloned.1.call-done = (f32[3,8,3072]{2,1,0:T(8,128)}, f32[2,8,1152]{2,1,0:T(8,128)}) async-done(((f32[3,8,3072]{2,1,0:T(8,128)}, f32[2,8,1152]{2,1,0:T(8,128)}), (f32[3,8,3072]{2,1,0:T(8,128)}, f32[2,8,1152]{2,1,0:T(8,128)})) %all-reduce.9.cloned.1.call-update) | async-done | bytes 368656 | tf_op jit(solution)/shard_map/psum | solution.py:319
  2113.4 5.3 multiply_subtract_fusion.1
  2118.7 12.4 multiply_subtract_fusion
  (230 shorter events, 37.7 us)
Async XLA Ops:
  7.2 1862.8 %copy-start = (f32[3,8,3072]{2,1,0:T(8,128)S(1)}, f32[3,8,3072]{2,1,0:T(8,128)}, u32[]{:S(2)}) copy-start(f32[3,8,3072]{2,1,0:T(8,128)} %param.34) | copy-start | bytes 884740
  7.2 52.4 %all-gather.5.cloned.1.call-start = ((), (), s32[]{:S(2)}) async-start(), calls=%async_computation.4 | async-start | bytes 1990656 | tf_op jit(solution)/shard_map/all_gather | solution.py:168
  9.0 139.4 %all-gather.7.cloned.1.call-start = ((), (), s32[]{:S(2)}) async-start(), calls=%async_computation.5 | async-start | bytes 5971968 | tf_op jit(solution)/shard_map/all_gather | solution.py:167
  11.3 4.7 copy-start.58
  11.3 4.7 copy-start.56
  11.4 27.8 %copy-start.55 = (s32[1,1024]{1,0:T(1,128)S(1)}, s32[1,1024]{1,0:T(1,128)}, u32[]{:S(2)}) copy-start(s32[1,1024]{1,0:T(1,128)} %param.23) | copy-start | bytes 12292
  11.4 27.8 %copy-start.6 = (bf16[1,1024,1152]{2,1,0:T(8,128)(2,1)S(1)}, bf16[1,1024,1152]{2,1,0:T(8,128)(2,1)}, u32[]{:S(2)}) copy-start(bf16[1,1024,1152]{2,1,0:T(8,128)(2,1)} %param.21) | copy-start | bytes 7077892
  11.4 544.1 %all-gather.9.cloned.1.call-start = ((), (), s32[]{:S(2)}) async-start(), calls=%async_computation.6 | async-start | bytes 23887872 | tf_op jit(solution)/shard_map/all_gather | solution.py:166
  16.0 951.3 %reduce-scatter.13.cloned.1.call-start = ((), (), s32[]{:S(2)}) async-start(), calls=%async_computation.10 | async-start | bytes 663552
  39.2 118.0 %copy-start.47 = (f32[1152]{0:T(1024)}, f32[1152]{0:T(1024)S(1)}, u32[]{:S(2)}) copy-start(f32[1152]{0:T(1024)S(1)} %get-tuple-element.23) | copy-start | bytes 13828
  39.7 19.9 copy-start.50
  39.7 117.4 %copy-start.52 = (f32[1024]{0:T(1024)}, f32[1024]{0:T(1024)S(1)}, u32[]{:S(2)}) copy-start(f32[1024]{0:T(1024)S(1)} %fusion.91) | copy-start | bytes 12292
  40.3 122.7 %copy-start.27 = (f32[1024,32]{0,1:T(8,128)}, f32[1024,32]{0,1:T(8,128)S(1)}, u32[]{:S(2)}) copy-start(f32[1024,32]{0,1:T(8,128)S(1)} %get-tuple-element.61) | copy-start | bytes 393220
  40.3 122.7 %copy-start.29 = (f32[1024,32]{0,1:T(8,128)}, f32[1024,32]{0,1:T(8,128)S(1)}, u32[]{:S(2)}) copy-start(f32[1024,32]{0,1:T(8,128)S(1)} %get-tuple-element.62) | copy-start | bytes 393220
  41.0 185.3 %copy-start.4 = (pred[512,1024]{0,1:T(8,128)(4,1)}, pred[512,1024]{0,1:T(8,128)(4,1)S(1)}, u32[]{:S(2)}) copy-start(pred[512,1024]{0,1:T(8,128)(4,1)S(1)} %get-tuple-element.64) | copy-start | bytes 1572868
  41.0 201.3 %copy-start.2 = (pred[512,1024]{0,1:T(8,128)(4,1)}, pred[512,1024]{0,1:T(8,128)(4,1)S(1)}, u32[]{:S(2)}) copy-start(pred[512,1024]{0,1:T(8,128)(4,1)S(1)} %get-tuple-element.63) | copy-start | bytes 1572868
  65.1 114.0 %copy-start.16 = (bf16[1024,6,32]{0,2,1:T(8,128)(2,1)}, bf16[1024,6,32]{0,2,1:T(8,128)(2,1)S(1)}, u32[]{:S(2)}) copy-start(bf16[1024,6,32]{0,2,1:T(8,128)(2,1)S(1)} %get-tuple-element.57) | copy-start | bytes 1179652
  65.1 114.0 %copy-start.19 = (bf16[1024,6,32]{0,2,1:T(8,128)(2,1)}, bf16[1024,6,32]{0,2,1:T(8,128)(2,1)S(1)}, u32[]{:S(2)}) copy-start(bf16[1024,6,32]{0,2,1:T(8,128)(2,1)S(1)} %get-tuple-element.58) | copy-start | bytes 1179652
  66.6 175.8 %copy-start.31 = (bf16[1024,384]{0,1:T(8,128)(2,1)}, bf16[1024,384]{0,1:T(8,128)(2,1)S(1)}, u32[]{:S(2)}) copy-start(bf16[1024,384]{0,1:T(8,128)(2,1)S(1)} %fusion.74) | copy-start | bytes 2359300
  164.1 15.0 copy-start.13
  164.2 15.0 copy-start.14
  194.6 22.9 %copy-start.1 = (f32[6,1024,512,3]{2,1,3,0:T(8,128)S(1)}, f32[6,1024,512,3]{2,1,3,0:T(8,128)}, u32[]{:S(2)}) copy-start(f32[6,1024,512,3]{2,1,3,0:T(8,128)} %get-tuple-element.72) | copy-start | bytes 113246208
  242.3 17.6 copy-start.60
  259.9 6.7 copy-start.44
  259.9 8.9 copy-start.49
  269.3 286.2 %copy-start.37 = (bf16[1024,1152]{1,0:T(8,128)(2,1)}, bf16[1024,1152]{1,0:T(8,128)(2,1)S(1)}, u32[]{:S(2)}) copy-start(bf16[1024,1152]{1,0:T(8,128)(2,1)S(1)} %multiply_convert_fusion.2) | copy-start | bytes 7077892
  568.6 14.1 copy-start.33
  568.6 51.4 %slice-start.2 = ((s8[4718592]{0:T(1024)(128)(4,1)}), s8[4194304]{0:T(1024)(128)(4,1)S(1)}, s32[]{:S(2)}) async-start(s8[4718592]{0:T(1024)(128)(4,1)} %bitcast.378), calls=%async_computation.14 | async-start | bytes 8388608
  582.6 37.3 %slice-start.3 = ((s8[4718592]{0:T(1024)(128)(4,1)}), s8[524288]{0:T(1024)(128)(4,1)S(1)}, s32[]{:S(2)}) async-start(s8[4718592]{0:T(1024)(128)(4,1)} %bitcast.378), calls=%async_computation.15 | async-start | bytes 1048576
  635.2 7.2 copy-start.10
  646.0 17.3 copy-start.32
  663.4 27.9 %copy-start.3 = (pred[512,1024]{0,1:T(8,128)(4,1)S(1)}, pred[512,1024]{0,1:T(8,128)(4,1)}, u32[]{:S(2)}) copy-start(pred[512,1024]{0,1:T(8,128)(4,1)} %copy-done.2) | copy-start | bytes 1572868
  663.4 27.9 %copy-start.42 = (f32[6,3,512]{2,1,0:T(4,128)S(1)}, f32[6,3,512]{2,1,0:T(4,128)}, u32[]{:S(2)}) copy-start(f32[6,3,512]{2,1,0:T(4,128)} %log_add_fusion.1) | copy-start | bytes 110596
  717.7 61.2 %copy-start.15 = (bf16[512,18,64]{0,2,1:T(8,128)(2,1)S(1)}, bf16[512,18,64]{0,2,1:T(8,128)(2,1)}, u32[]{:S(2)}) copy-start(bf16[512,18,64]{0,2,1:T(8,128)(2,1)} %copy-done.14) | copy-start | bytes 3538948
  778.9 13.4 copy-start.17
  778.9 13.4 copy-start.20
  792.3 11.3 copy-start.23
  792.3 11.3 copy-start.61
  803.6 15.8 copy-start.8
  803.6 15.8 copy-start.48
  803.6 15.8 copy-start.53
  855.6 4.1 copy-start.35
  855.7 4.0 copy-start.26
  866.2 144.4 %reduce-scatter.11.cloned.1.call-start = ((), (), s32[]{:S(2)}) async-start(), calls=%async_computation.9 | async-start | bytes 3981312 | tf_op jit(solution)/shard_map/reduce_scatter | solution.py:295
  870.4 323.7 %reduce-scatter.9.cloned.1.call-start = ((), (), s32[]{:S(2)}) async-start(), calls=%async_computation.8 | async-start | bytes 11943936 | tf_op jit(solution)/shard_map/reduce_scatter | solution.py:294
  870.4 6.5 copy-start.36
  885.2 984.8 %reduce-scatter.7.cloned.1.call-start = ((), (), s32[]{:S(2)}) async-start(), calls=%async_computation.7 | async-start | bytes 47775744 | tf_op jit(solution)/shard_map/reduce_scatter | solution.py:293
  885.3 11.6 copy-start.38
  885.3 24.7 %slice-start.6 = ((s8[6291456]{0:T(1024)(128)(4,1)}), s8[4194304]{0:T(1024)(128)(4,1)S(1)}, s32[]{:S(2)}) async-start(s8[6291456]{0:T(1024)(128)(4,1)} %bitcast.414), calls=%async_computation.18 | async-start | bytes 8388608
  896.8 13.2 copy-start.34
  896.8 13.1 slice-start.7
  946.1 1164.9 %all-reduce.9.cloned.1.call-start = ((), (), s32[]{:S(2)}) async-start(), calls=%async_computation.11 | async-start | bytes 737280 | tf_op jit(solution)/shard_map/psum | solution.py:319
  952.5 58.1 %copy-start.24 = (f32[1,2,144,384]{3,2,1,0:T(8,128)S(1)}, f32[1,2,144,384]{3,2,1,0:T(8,128)}, u32[]{:S(2)}) copy-start(f32[1,2,144,384]{3,2,1,0:T(8,128)} %param.33) | copy-start | bytes 1327108
  952.5 58.1 %copy-start.54 = (f32[2,8,384]{2,1,0:T(8,128)S(1)}, f32[2,8,384]{2,1,0:T(8,128)}, u32[]{:S(2)}) copy-start(f32[2,8,384]{2,1,0:T(8,128)} %param.36) | copy-start | bytes 73732
  952.5 241.5 %copy-start.11 = (f32[1,2,144,1152]{3,2,1,0:T(8,128)S(1)}, f32[1,2,144,1152]{3,2,1,0:T(8,128)}, u32[]{:S(2)}) copy-start(f32[1,2,144,1152]{3,2,1,0:T(8,128)} %param.32) | copy-start | bytes 3981316
  952.5 241.5 %copy-start.46 = (f32[2,8,1152]{2,1,0:T(8,128)S(1)}, f32[2,8,1152]{2,1,0:T(8,128)}, u32[]{:S(2)}) copy-start(f32[2,8,1152]{2,1,0:T(8,128)} %param.35) | copy-start | bytes 221188
  1196.7 777.8 %copy-start.12 = (f32[2,144,1152]{2,1,0:T(8,128)S(1)}, f32[2,144,1152]{2,1,0:T(8,128)}, u32[]{:S(2)}) copy-start(f32[2,144,1152]{2,1,0:T(8,128)} %reduce-scatter.9.cloned.1.call-done) | copy-start | bytes 3981316
  1974.6 9.1 copy-start.45
  1976.0 10.6 copy-start.57
  1976.0 10.6 copy-start.59
  2111.0 7.7 slice-start
  2112.1 6.5 copy-start.39
  2113.4 17.8 copy-start.43
  2113.4 5.3 slice-start.1
  (14 other events, 37.6 us)
Sparse Core Ops, SparseCore 0:
  10.9 48.6 all-gather.4
  62.4 86.0 all-gather.6
  150.6 404.8 all-gather.8
  866.4 62.0 reduce-scatter.12
  932.4 78.1 reduce-scatter.10
  1014.5 179.5 reduce-scatter.8
  1197.9 672.0 reduce-scatter.6
  1983.8 127.1 all-reduce.8
where the time goes:
time: 2150 us; the launch traced here: 2140 us
  waiting for transfers between devices  1410 us (66%)
  matrix products  422 us (20%)
  other arithmetic  161 us (7%)
  blocking collectives  107 us (5%)
  local copies, waits for them, and re-layouts  25.3 us (1%)
    reduce_scatter x1, waiting for transfers between devices, shards(): lax.psum_scatter(grad_wide, 'shard', scatter_dimension=1, tiled=True)  673 us
    all_gather x1, waiting for transfers between devices, shards(): lax.all_gather(wide_master.astype(jnp.bfloat16), 'shard', axis=1, tiled=T...  286 us
    reduce_scatter x1, waiting for transfers between devices, shards(): lax.psum_scatter(grad_square, 'shard', scatter_dimension=1, tiled=True)  182 us
    psum x1, waiting for transfers between devices, shards(): lax.psum((contract(basis_wide, mixed_wide), contract(basis_square, mixed_...  124 us
    all_gather x1, waiting for transfers between devices, shards(): lax.all_gather(square_master.astype(jnp.bfloat16), 'shard', axis=1, tiled...  81.9 us
    convert_element_type x1, other arithmetic, attend_backward(): d_scores = (prob_full * (d_prob - row_delta)).astype(jnp.bfloat16)  61.2 us
    dot_general x2, matrix products, attend_backward(): jnp.einsum('qagd,kad->agqk', d_block, value_heads, preferred_element_type...  52.9 us
  transfers between devices with their start and end apart: 8, of which 7 were waited for; matrix products, arithmetic and copies ran while one was open for 11% of the time, Pallas kernels for 0%

commit v1 on v0

v1 whole, which is shorter than its diff:
```python
import functools

import jax
import jax.numpy as jnp
from jax import lax
from jax.experimental import pallas as pl
from jax.experimental.pallas import tpu as pltpu
from jax.sharding import PartitionSpec as P

QUERY_HEADS = 18
KEY_VALUE_HEADS = 6
HEAD_SIZE = 64
PAIRS = KEY_VALUE_HEADS // 2


eps_norm = 1e-05
theta_base = 10000.0
decay_rate = 0.9
rate_wide = 0.03
rate_square = 0.1
rate_narrow = 0.02
rate_gains = 0.01
mask_fill = -1e30
highest = lax.Precision.HIGHEST


def normed(value_heads, gain):
    return (
        value_heads
        * lax.rsqrt(jnp.mean(value_heads * value_heads, axis=-1, keepdims=True) + eps_norm)
        * gain
    )


def rotary_tables(position, width):
    halfway = width // 2
    inverse = theta_base ** (-2.0 * jnp.arange(halfway, dtype=jnp.float32) / width)
    angles = position.astype(jnp.float32)[:, None] * inverse[None, :]
    return (jnp.cos(angles), jnp.sin(angles))


BLOCK_ROWS = 256
VMEM_BYTES = 56 * 1024 * 1024


def partner_lanes(values):
    lane = lax.broadcasted_iota(jnp.int32, values.shape, 1)
    return jnp.where(
        lane % HEAD_SIZE < HEAD_SIZE // 2,
        pltpu.roll(values, 128 - HEAD_SIZE // 2, 1),
        pltpu.roll(values, HEAD_SIZE // 2, 1),
    )


def project_kernel(
    order_ref, x_ref, gain_ref, w_ref, cos_ref, sin_ref, out_ref, turned_ref, scratch_ref
):
    x = x_ref[...].astype(jnp.float32)
    scale = lax.rsqrt(jnp.mean(x * x, axis=-1, keepdims=True) + eps_norm)
    low = (x * scale * gain_ref[...]).astype(jnp.bfloat16)
    scratch_ref[...] = low.astype(jnp.float32).T
    share = scratch_ref.shape[0] // order_ref.shape[0]
    parts = [
        scratch_ref[pl.ds(pl.multiple_of(order_ref[p] * share, 8), share), :]
        for p in range(order_ref.shape[0])
    ]
    turned_ref[...] = jnp.concatenate(parts, axis=0).astype(jnp.bfloat16)
    cos, sin = cos_ref[...], sin_ref[...]
    for first in range(0, out_ref.shape[1], 640):
        got = jnp.dot(low, w_ref[:, first : first + 640], preferred_element_type=jnp.float32)
        for at in range(0, 640, 128):
            piece = got[:, at : at + 128]
            if at < 512:
                piece = piece * cos + partner_lanes(piece) * sin
            out_ref[:, first + at : first + at + 128] = piece.astype(jnp.bfloat16)


def project_qkv(order, x, gain, weights, cos, sin):
    rows, width = x.shape
    columns = weights.shape[1]
    block = min(BLOCK_ROWS, rows)
    return pl.pallas_call(
        project_kernel,
        grid_spec=pltpu.PrefetchScalarGridSpec(
            num_scalar_prefetch=1,
            grid=(rows // block,),
            in_specs=[
                pl.BlockSpec((block, width), lambda i, order: (i, 0)),
                pl.BlockSpec((1, width), lambda i, order: (0, 0)),
                pl.BlockSpec((width, columns), lambda i, order: (0, 0)),
                pl.BlockSpec((block, 128), lambda i, order: (i, 0)),
                pl.BlockSpec((block, 128), lambda i, order: (i, 0)),
            ],
            out_specs=[
                pl.BlockSpec((block, columns), lambda i, order: (i, 0)),
                pl.BlockSpec((width, block), lambda i, order: (0, i)),
            ],
            scratch_shapes=[pltpu.VMEM((width, block), jnp.float32)],
        ),
        out_shape=[
            jax.ShapeDtypeStruct((rows, columns), jnp.bfloat16),
            jax.ShapeDtypeStruct((width, rows), jnp.bfloat16),
        ],
        compiler_params=pltpu.CompilerParams(vmem_limit_bytes=VMEM_BYTES),
        cost_estimate=pl.CostEstimate(
            flops=2 * rows * width * columns,
            bytes_accessed=2 * (rows * width * 2 + rows * columns + width * columns),
            transcendentals=0,
        ),
    )(order, x, gain, weights, cos, sin)


def spread_heads(pair, spread_ref):
    wide = pair.astype(jnp.float32)
    turned = pltpu.roll(wide, HEAD_SIZE, 1)
    low_half = lax.broadcasted_iota(jnp.int32, wide.shape, 1) < HEAD_SIZE
    zero = jnp.zeros_like(wide)
    spread_ref[0] = jnp.where(low_half, wide, zero).astype(jnp.bfloat16)
    spread_ref[1] = jnp.where(low_half, zero, turned).astype(jnp.bfloat16)
    spread_ref[2] = jnp.where(low_half, turned, zero).astype(jnp.bfloat16)
    spread_ref[3] = jnp.where(low_half, zero, wide).astype(jnp.bfloat16)


def mask_bias(position, start, keys):
    rows = position.shape[0]
    row = lax.broadcasted_iota(jnp.int32, (rows, keys), 0) + start
    column = lax.broadcasted_iota(jnp.int32, (rows, keys), 1)
    allowed = (column <= row) & (column >= row - position)
    return jnp.where(allowed, 0.0, mask_fill)


def across(left, right):
    return lax.dot_general(
        left, right, (((1,), (1,)), ((), ())), preferred_element_type=jnp.float32
    )


def forward_kernel(qkv_ref, pos_ref, out_ref, log_ref, key_ref, value_ref):
    step = pl.program_id(1)
    block = out_ref.shape[0]

    @pl.when(step == 0)
    def _():
        spread_heads(qkv_ref[:, 384:512], key_ref)
        spread_heads(qkv_ref[:, 512:640], value_ref)

    for place in range(qkv_ref.shape[0] // block):

        @pl.when(step == place)
        def _(place=place):
            start = place * block
            keys = start + block
            bias = mask_bias(pos_ref[...], start, keys)
            lane = lax.broadcasted_iota(jnp.int32, (block, 128), 1)
            logs = jnp.zeros((block, 128), jnp.float32)
            for g in range(3):
                query = qkv_ref[start:keys, 128 * g : 128 * g + 128] * 0.125
                total = jnp.zeros((block, 128), jnp.float32)
                for e in range(2):
                    head = 2 * g + e
                    which = 2 * (head // 3) + e
                    scores = across(query, key_ref[which, :keys, :]) + bias
                    top = jnp.max(scores, axis=-1, keepdims=True)
                    raised = jnp.exp(scores - top)
                    row_total = jnp.sum(raised, axis=-1, keepdims=True)
                    low = (raised * (1.0 / row_total)).astype(jnp.bfloat16)
                    total += jnp.dot(
                        low, value_ref[which, :keys, :], preferred_element_type=jnp.float32
                    )
                    logs = jnp.where(lane == head, top + jnp.log(row_total), logs)
                out_ref[:, 128 * g : 128 * g + 128] = total.astype(jnp.bfloat16)
            log_ref[0] = logs


def attend_forward(qkv, position):
    rows = qkv.shape[0]
    pairs = qkv.shape[1] // 640
    block = min(BLOCK_ROWS, rows)
    return pl.pallas_call(
        forward_kernel,
        grid=(pairs, rows // block),
        in_specs=[
            pl.BlockSpec((rows, 640), lambda j, i: (0, j)),
            pl.BlockSpec((block, 1), lambda j, i: (i, 0)),
        ],
        out_specs=[
            pl.BlockSpec((block, 384), lambda j, i: (i, j)),
            pl.BlockSpec((1, block, 128), lambda j, i: (j, i, 0)),
        ],
        out_shape=[
            jax.ShapeDtypeStruct((rows, 384 * pairs), jnp.bfloat16),
            jax.ShapeDtypeStruct((pairs, rows, 128), jnp.float32),
        ],
        scratch_shapes=[
            pltpu.VMEM((4, rows, 128), jnp.bfloat16),
            pltpu.VMEM((4, rows, 128), jnp.bfloat16),
        ],
        compiler_params=pltpu.CompilerParams(vmem_limit_bytes=VMEM_BYTES),
        cost_estimate=pl.CostEstimate(
            flops=20 * pairs * rows * rows * 128,
            bytes_accessed=8 * rows * 640 * pairs,
            transcendentals=6 * pairs * rows * rows,
        ),
    )(qkv, position)


def backward_kernel(
    qkv_ref, d_ref, log_ref, pos_ref, cos_ref, sin_ref, out_ref, key_ref, value_ref, dk_ref, dv_ref
):
    step = pl.program_id(0)
    block = d_ref.shape[0]
    blocks = qkv_ref.shape[0] // block

    @pl.when(step == 0)
    def _():
        spread_heads(qkv_ref[:, 384:512], key_ref)
        spread_heads(qkv_ref[:, 512:640], value_ref)
        dk_ref[...] = jnp.zeros_like(dk_ref)
        dv_ref[...] = jnp.zeros_like(dv_ref)

    for place in range(blocks):

        @pl.when(step == place)
        def _(place=place):
            start = place * block
            keys = start + block
            bias = mask_bias(pos_ref[...], start, keys)
            logs = log_ref[0]
            cos, sin = cos_ref[start:keys, :], sin_ref[start:keys, :]
            for g in range(3):
                query = qkv_ref[start:keys, 128 * g : 128 * g + 128] * 0.125
                d_out = d_ref[:, 128 * g : 128 * g + 128]
                query_turned = query.astype(jnp.float32).T.astype(jnp.bfloat16)
                d_turned = d_out.astype(jnp.float32).T.astype(jnp.bfloat16)
                total = jnp.zeros((block, 128), jnp.float32)
                for e in range(2):
                    head = 2 * g + e
                    which = 2 * (head // 3) + e
                    at = HEAD_SIZE * (head // 3)
                    key = key_ref[which, :keys, :]
                    scores = across(query, key) + bias
                    prob = jnp.exp(scores - logs[:, head : head + 1])
                    d_prob = across(d_out, value_ref[which, :keys, :])
                    delta = jnp.sum(prob * d_prob, axis=-1, keepdims=True)
                    d_scores = (prob * (d_prob - delta)).astype(jnp.bfloat16)
                    half = slice(HEAD_SIZE * e, HEAD_SIZE * e + HEAD_SIZE)
                    dv_ref[at : at + HEAD_SIZE, :keys] += jnp.dot(
                        d_turned[half], prob.astype(jnp.bfloat16), preferred_element_type=jnp.float32
                    )
                    dk_ref[at : at + HEAD_SIZE, :keys] += jnp.dot(
                        query_turned[half], d_scores, preferred_element_type=jnp.float32
                    )
                    total += jnp.dot(d_scores, key, preferred_element_type=jnp.float32)
                total = total * 0.125
                total = total * cos - partner_lanes(total) * sin
                out_ref[start:keys, 128 * g : 128 * g + 128] = total.astype(jnp.bfloat16)

    @pl.when(step == blocks - 1)
    def _():
        d_key = dk_ref[...].T
        d_key = d_key * cos_ref[...] - partner_lanes(d_key) * sin_ref[...]
        out_ref[:, 384:512] = d_key.astype(jnp.bfloat16)
        out_ref[:, 512:640] = dv_ref[...].T.astype(jnp.bfloat16)


def attend_backward(qkv, d_attended, logs, position, cos, sin, pair):
    rows = qkv.shape[0]
    block = min(BLOCK_ROWS, rows)
    return pl.pallas_call(
        backward_kernel,
        grid=(rows // block,),
        in_specs=[
            pl.BlockSpec((rows, 640), lambda i: (0, pair)),
            pl.BlockSpec((block, 384), lambda i: (i, pair)),
            pl.BlockSpec((1, block, 128), lambda i: (pair, i, 0)),
            pl.BlockSpec((block, 1), lambda i: (i, 0)),
            pl.BlockSpec((rows, 128), lambda i: (0, 0)),
            pl.BlockSpec((rows, 128), lambda i: (0, 0)),
        ],
        out_specs=pl.BlockSpec((rows, 640), lambda i: (0, 0)),
        out_shape=jax.ShapeDtypeStruct((rows, 640), jnp.bfloat16),
        scratch_shapes=[
            pltpu.VMEM((4, rows, 128), jnp.bfloat16),
            pltpu.VMEM((4, rows, 128), jnp.bfloat16),
            pltpu.VMEM((128, rows), jnp.float32),
            pltpu.VMEM((128, rows), jnp.float32),
        ],
        compiler_params=pltpu.CompilerParams(vmem_limit_bytes=VMEM_BYTES),
        cost_estimate=pl.CostEstimate(
            flops=50 * rows * rows * 128,
            bytes_accessed=8 * rows * 640,
            transcendentals=6 * rows * rows,
        ),
    )(qkv, d_attended, logs, position, cos, sin)


def turn_kernel(order_ref, rows_ref, out_ref, turned_ref):
    turned_ref[...] = rows_ref[...].astype(jnp.float32).T
    owners = order_ref.shape[0]
    share = turned_ref.shape[0] // owners
    parts = [
        turned_ref[pl.ds(pl.multiple_of(order_ref[p] * share, 8), share), :] for p in range(owners)
    ]
    out_ref[...] = jnp.concatenate(parts, axis=0).astype(jnp.bfloat16)


def turn_rows(rows, order):
    count, model = rows.shape
    block = min(BLOCK_ROWS, count)
    return pl.pallas_call(
        turn_kernel,
        grid_spec=pltpu.PrefetchScalarGridSpec(
            num_scalar_prefetch=1,
            grid=(count // block,),
            in_specs=[pl.BlockSpec((block, model), lambda i, order: (i, 0))],
            out_specs=pl.BlockSpec((model, block), lambda i, order: (0, i)),
            scratch_shapes=[pltpu.VMEM((model, block), jnp.float32)],
        ),
        out_shape=jax.ShapeDtypeStruct((model, count), jnp.bfloat16),
        compiler_params=pltpu.CompilerParams(vmem_limit_bytes=VMEM_BYTES),
        cost_estimate=pl.CostEstimate(
            flops=0, bytes_accessed=4 * count * model, transcendentals=0
        ),
    )(order, rows)


def mlp_kernel(reps, first, slot_ref, place_ref, mid_ref, d_ref, *refs):
    del slot_ref
    mid_hbm, d_hbm = refs[:2]
    befores = refs[2 : 3 if first else 4]
    refs = refs[2 + len(befores) :]
    weight_hbm, refs = (refs[:1], refs[1:]) if place_ref.shape[0] == 1 else (refs[:2], refs[2:])
    away_ref, home_ref, result_ref, back_ref = refs[:4]
    weight_ref, mid_turned_ref, d_turned_ref, d_pair_ref, hidden_ref, weight_sem, sem = refs[4:]
    step = pl.program_id(0)
    count = mid_ref.shape[0]
    part = min(512, count)
    tile = hidden_ref.shape[1]
    half = away_ref.shape[1]

    wide = 3 * tile

    def load(i):
        if len(weight_hbm) == 1:
            pltpu.make_async_copy(
                weight_hbm[0].at[i], weight_ref.at[i], weight_sem.at[i]
            ).start()
            return
        ref, at = weight_hbm[2 * i // reps], i % (reps // 2)
        owners, share = ref.shape[:2]
        for a in range(owners):
            pltpu.make_async_copy(
                ref.at[place_ref[a], :, wide * at : wide * at + wide],
                weight_ref.at[i, share * a : share * a + share, :],
                weight_sem.at[i],
            ).start()

    sums = [pltpu.make_async_copy(befores[0], result_ref, sem.at[0])]
    if not first:
        sums.append(pltpu.make_async_copy(befores[1], back_ref, sem.at[1]))
    turned = [
        pltpu.make_async_copy(mid_hbm, mid_turned_ref, sem.at[2]),
        pltpu.make_async_copy(d_hbm, d_turned_ref, sem.at[3]),
    ]

    @pl.when(step == 0)
    def _():
        load(0)
        for copy in sums + turned:
            copy.start()
        for i in range(1, reps):
            load(i)
        if first:
            back_ref[...] = jnp.zeros_like(back_ref)

    for i in range(reps):

        @pl.when(step == i)
        def _(i=i):
            pltpu.make_async_copy(weight_ref.at[i], weight_ref.at[i], weight_sem.at[i]).wait()

    @pl.when(step == 0)
    def _():
        for copy in sums:
            copy.wait()

    @pl.loop(0, count // part)
    def _(t):
        rows = pl.ds(pl.multiple_of(t * part, part), part)
        pair_w = weight_ref[step, :, : 2 * tile]
        down_w = weight_ref[step, :, 2 * tile :]
        pair = jnp.dot(mid_ref[rows, :], pair_w, preferred_element_type=jnp.float32)
        d_hidden = jnp.dot(d_ref[rows, :], down_w, preferred_element_type=jnp.float32)
        gate, up = pair[:, :tile], pair[:, tile:]
        sig = jax.nn.sigmoid(gate)
        silu = gate * sig
        hidden = (silu * up).astype(jnp.bfloat16)
        hidden_ref[rows, :] = hidden
        d_gate = d_hidden * up * (sig * (1.0 + gate * (1.0 - sig)))
        d_pair_ref[rows, :tile] = d_gate.astype(jnp.bfloat16)
        d_pair_ref[rows, tile:] = (d_hidden * silu).astype(jnp.bfloat16)
        back_ref[rows, :] += across(d_pair_ref[rows, :], pair_w)
        result_ref[rows, :] += across(hidden, down_w)

    @pl.when(step == 0)
    def _():
        for copy in turned:
            copy.wait()

    for at, out_ref in ((0, away_ref), (half, home_ref)):
        pair = jnp.dot(
            mid_turned_ref[at : at + half, :], d_pair_ref[...], preferred_element_type=jnp.float32
        )
        out_ref[0] = pair[:, :tile].astype(jnp.bfloat16)
        out_ref[1] = pair[:, tile:].astype(jnp.bfloat16)
        out_ref[2] = jnp.dot(
            d_turned_ref[at : at + half, :], hidden_ref[...], preferred_element_type=jnp.float32
        ).astype(jnp.bfloat16)


def mlp_part(reps, slots, places, mid, d_out, mid_turned, d_turned, weights, result, back):
    count, model = mid.shape
    tile = weights[0].shape[2] // (3 if len(weights) == 1 else 3 * (reps // 2))
    units = tile * reps
    half = model // 2
    first = back is None
    befores = [result] if first else [result, back]

    def once(shape):
        return pl.BlockSpec(shape, lambda i, slots, places: (0, 0), pipeline_mode=pl.Buffered(1))

    anywhere = pl.BlockSpec(memory_space=pl.ANY)
    return pl.pallas_call(
        functools.partial(mlp_kernel, reps, first),
        grid_spec=pltpu.PrefetchScalarGridSpec(
            num_scalar_prefetch=2,
            grid=(reps,),
            in_specs=[once((count, model))] * 2 + [anywhere] * (2 + len(befores) + len(weights)),
            out_specs=[
                pl.BlockSpec((3, half, tile), lambda i, slots, places: (0, 0, slots[i])),
                pl.BlockSpec((3, half, tile), lambda i, slots, places: (0, 0, slots[i])),
                once((count, model)),
                once((count, model)),
            ],
            scratch_shapes=[
                pltpu.VMEM((reps, model, 3 * tile), jnp.bfloat16),
                pltpu.VMEM((model, count), jnp.bfloat16),
                pltpu.VMEM((model, count), jnp.bfloat16),
                pltpu.VMEM((count, 2 * tile), jnp.bfloat16),
                pltpu.VMEM((count, tile), jnp.bfloat16),
                pltpu.SemaphoreType.DMA((reps,)),
                pltpu.SemaphoreType.DMA((4,)),
            ],
        ),
        out_shape=[
            jax.ShapeDtypeStruct((3, half, units), jnp.bfloat16),
            jax.ShapeDtypeStruct((3, half, units), jnp.bfloat16),
            jax.ShapeDtypeStruct((count, model), jnp.float32),
            jax.ShapeDtypeStruct((count, model), jnp.float32),
        ],
        compiler_params=pltpu.CompilerParams(vmem_limit_bytes=VMEM_BYTES),
        cost_estimate=pl.CostEstimate(
            flops=18 * count * model * units,
            bytes_accessed=2 * (4 * count * model + 6 * model * units) + 16 * count * model,
            transcendentals=count * units,
        ),
    )(slots, places, mid, d_out, mid_turned, d_turned, *befores, *weights)


def assemble(rows, mine, other, places, core, low, high):
    owners = mine[0].shape[0]
    widths = [m.shape[2] for m in mine]
    count = len(mine)

    def kernel(place_ref, core_ref, *refs):
        del place_ref
        out_ref = refs[-1]
        for own in range(2):

            @pl.when(core_ref[0] == own)
            def _(own=own):
                at = 0
                for i in range(count):
                    for half in range(2):
                        ref = refs[i] if half == own else refs[count + i]
                        first, last = max(low, at), min(high, at + widths[i])
                        if first < last:
                            out_ref[0, :, first - low : last - low] = ref[
                                0, :, first - at : last - at
                            ]
                        at += widths[i]

    def spec(width):
        return pl.BlockSpec((1, rows, width), lambda a, place, core: (place[a], 0, 0))

    out = pl.pallas_call(
        kernel,
        grid_spec=pltpu.PrefetchScalarGridSpec(
            num_scalar_prefetch=2,
            grid=(owners,),
            in_specs=[spec(w) for w in widths] * 2,
            out_specs=pl.BlockSpec((1, rows, high - low), lambda a, place, core: (a, 0, 0)),
        ),
        out_shape=jax.ShapeDtypeStruct((owners, rows, high - low), jnp.bfloat16),
        compiler_params=pltpu.CompilerParams(vmem_limit_bytes=VMEM_BYTES),
        cost_estimate=pl.CostEstimate(
            flops=0, bytes_accessed=8 * owners * rows * sum(widths), transcendentals=0
        ),
    )(places, core, *mine, *other)
    return out.reshape(owners * rows, high - low)


def exact_dot(left, right, contract):
    return lax.dot_general(
        left, right, (contract, ((), ())), precision=highest, preferred_element_type=jnp.float32
    )


def mix_kernel(layout, count, flag_ref, *refs):
    sums, refs = refs[: 3 * count], refs[3 * count :]
    errors, refs = refs[: len(layout)], refs[len(layout) :]
    factors, refs = refs[: len(layout)], refs[len(layout) :]
    mixed, left_ref = refs[: len(layout)], refs[len(layout)]
    stays = flag_ref[0] == 1
    for m, pieces in enumerate(layout):
        at = 0
        for which, first, last in pieces:
            away, home, moved = (
                sums[3 * which + k][..., first:last].astype(jnp.float32) for k in range(3)
            )
            width = last - first
            where = (..., slice(at, at + width))
            total = away + jnp.where(stays, home, moved)
            total = total.reshape(total.shape[-2:])
            error = errors[m][where]
            error = error.reshape(error.shape[-2:])
            mixed[m][where] = (total + error).reshape(mixed[m].shape[:-1] + (width,))
            at += width
        rows = mixed[m][...].reshape(mixed[m].shape[-2:])
        factor = factors[m][...].reshape(factors[m].shape[-2:])
        left = exact_dot(factor, rows, ((1,), (1,)))
        left_ref[8 * m : 8 * m + 8, :] = left


def mix_wide(flag, parts, error, factor):
    count, rows, third = parts[0][0].shape
    number = len(parts)
    columns = third * number
    arrays = [a for part in parts for a in part]

    def kernel(flag_ref, *refs):
        error_ref, factor_ref, mixed_ref, left_ref = refs[3 * number :]
        step = pl.program_id(1)

        @pl.when(step == 0)
        def _():
            left_ref[...] = jnp.zeros_like(left_ref)

        for p in range(number):

            @pl.when(step == p)
            def _(p=p):
                away, home, moved = (refs[3 * p + k][0].astype(jnp.float32) for k in range(3))
                mixed = away + jnp.where(flag_ref[0] == 1, home, moved) + error_ref[0, 0]
                mixed_ref[0] = mixed
                left_ref[...] += exact_dot(factor_ref[0], mixed, ((1,), (1,)))

    return pl.pallas_call(
        kernel,
        grid_spec=pltpu.PrefetchScalarGridSpec(
            num_scalar_prefetch=1,
            grid=(count, number),
            in_specs=[pl.BlockSpec((1, rows, third), lambda i, k, flag: (i, 0, 0))] * len(arrays)
            + [
                pl.BlockSpec((1, 1, rows, third), lambda i, k, flag: (0, i, 0, k)),
                pl.BlockSpec((1, 8, third), lambda i, k, flag: (i, 0, k)),
            ],
            out_specs=[
                pl.BlockSpec((1, rows, third), lambda i, k, flag: (i, 0, k)),
                pl.BlockSpec((8, rows), lambda i, k, flag: (i, 0)),
            ],
        ),
        out_shape=[
            jax.ShapeDtypeStruct((count, rows, columns), jnp.float32),
            jax.ShapeDtypeStruct((8 * count, rows), jnp.float32),
        ],
        compiler_params=pltpu.CompilerParams(vmem_limit_bytes=VMEM_BYTES),
        cost_estimate=pl.CostEstimate(
            flops=96 * count * rows * columns,
            bytes_accessed=14 * count * rows * columns,
            transcendentals=0,
        ),
    )(flag, *arrays, error, factor)


def in_vmem(count):
    return [pl.BlockSpec(memory_space=pltpu.VMEM)] * count


def mix_rest(flag, parts, layout, errors, factors):
    rows = errors[0].shape[0]
    arrays = [a for part in parts for a in part]
    return pl.pallas_call(
        functools.partial(mix_kernel, layout, len(parts)),
        in_specs=[pl.BlockSpec(memory_space=pltpu.SMEM)]
        + in_vmem(len(arrays) + len(errors) + len(factors)),
        out_specs=in_vmem(len(errors) + 1),
        out_shape=[jax.ShapeDtypeStruct(e.shape, jnp.float32) for e in errors]
        + [jax.ShapeDtypeStruct((8 * len(errors), rows), jnp.float32)],
        compiler_params=pltpu.CompilerParams(vmem_limit_bytes=VMEM_BYTES),
        cost_estimate=pl.CostEstimate(
            flops=96 * sum(e.size for e in errors),
            bytes_accessed=14 * sum(e.size for e in errors),
            transcendentals=0,
        ),
    )(flag, *arrays, *errors, *factors)


def contract_all(left, mixed, width, extra=None):
    def kernel(*refs):
        left_ref, out_ref = refs[0], refs[-1]
        out_ref[...] = jnp.zeros_like(out_ref)
        at, m = 0, 0
        for ref in refs[1 : 1 + len(mixed)]:
            for k in range(ref.shape[0] if len(ref.shape) == 3 else 1):
                rows = ref[k] if len(ref.shape) == 3 else ref[...]
                own = left_ref[8 * m : 8 * m + 8, :]
                out_ref[:, at : at + rows.shape[1]] = exact_dot(own, rows, ((1,), (0,)))
                at += rows.shape[1]
                m += 1
        for k in range(m):
            own = left_ref[8 * k : 8 * k + 8, :]
            out_ref[:, at : at + 8] = exact_dot(own, own, ((1,), (1,)))
            at += 128
        if extra is not None:
            out_ref[: extra.shape[0], at : at + extra.shape[1]] = refs[-2][...]

    more = [] if extra is None else [extra]
    return pl.pallas_call(
        kernel,
        in_specs=in_vmem(1 + len(mixed) + len(more)),
        out_specs=pl.BlockSpec(memory_space=pltpu.VMEM),
        out_shape=jax.ShapeDtypeStruct((8, width), jnp.float32),
        compiler_params=pltpu.CompilerParams(vmem_limit_bytes=VMEM_BYTES),
        cost_estimate=pl.CostEstimate(
            flops=96 * sum(m.size for m in mixed),
            bytes_accessed=4 * sum(m.size for m in mixed),
            transcendentals=0,
        ),
    )(left, *mixed, *more)


def eliminate(gram, rights):
    row = lax.broadcasted_iota(jnp.int32, (8, 1), 0)
    for j in range(8):
        scale = 1.0 / jnp.sqrt(gram[j : j + 1, j : j + 1])
        below = jnp.where(row > j, gram[:, j : j + 1] * scale, 0.0)
        done = []
        for right in [gram] + list(rights):
            top = right[j : j + 1, :] * scale
            done.append(jnp.where(row == j, top, right - below * top))
        gram, rights = done[0], done[1:]
    return rights


def finish_matrix(reps, rate, row, gram, left, mixed, moment, master):
    factor, basis = eliminate(gram[:, :8] * (1.0 / reps), [row, left])
    factor = factor * (1.0 / reps)
    approx = exact_dot(basis, factor, ((0,), (0,)))
    moment_new = decay_rate * moment + approx
    return factor, moment_new, master - rate * moment_new, mixed - approx


def finish_wide(reps, packed, gram_at, left, mixed, moment, master):
    count, rows, columns = mixed.shape

    def kernel(row_ref, gram_ref, left_ref, mixed_ref, moment_ref, master_ref, *outs):
        new_ref, moment_new_ref, error_ref, factor_ref = outs
        factor_ref[0], moment_new_ref[0], new_ref[0], error_ref[0, 0] = finish_matrix(
            reps,
            rate_wide,
            row_ref[...],
            gram_ref[...],
            left_ref[...],
            mixed_ref[0],
            moment_ref[0],
            master_ref[0],
        )

    third = columns // 3
    whole = pl.BlockSpec((1, rows, third), lambda i, k: (i, 0, k))
    shape = jax.ShapeDtypeStruct((count, rows, columns), jnp.float32)
    return pl.pallas_call(
        kernel,
        grid=(count, 3),
        in_specs=[
            pl.BlockSpec((8, third), lambda i, k: (0, 3 * i + k)),
            pl.BlockSpec((8, 128), lambda i, k: (0, gram_at // 128 + i)),
            pl.BlockSpec((8, rows), lambda i, k: (i, 0)),
            whole,
            whole,
            whole,
        ],
        out_specs=[
            whole,
            whole,
            pl.BlockSpec((1, 1, rows, third), lambda i, k: (0, i, 0, k)),
            pl.BlockSpec((1, 8, third), lambda i, k: (i, 0, k)),
        ],
        out_shape=[
            shape,
            shape,
            jax.ShapeDtypeStruct((1, count, rows, columns), jnp.float32),
            jax.ShapeDtypeStruct((count, 8, columns), jnp.float32),
        ],
        compiler_params=pltpu.CompilerParams(vmem_limit_bytes=VMEM_BYTES),
        cost_estimate=pl.CostEstimate(
            flops=96 * count * rows * columns,
            bytes_accessed=24 * count * rows * columns,
            transcendentals=0,
        ),
    )(packed, packed, left, mixed, moment, master)


def finish_rest(reps, packs, lefts, mixed, where, states):
    groups = []
    at = 0
    for moment, _, rate in states:
        groups.append((at, moment.shape[0], rate))
        at += moment.shape[0]

    def kernel(*refs):
        pack_refs, refs = refs[: len(packs)], refs[len(packs) :]
        left_refs, refs = refs[: len(lefts)], refs[len(lefts) :]
        mixed_refs, refs = refs[: len(mixed)], refs[len(mixed) :]
        state_refs, outs = refs[: 2 * len(states)], refs[2 * len(states) :]
        for g, (first, count, rate) in enumerate(groups):
            new_ref, moment_new_ref, error_ref, factor_ref = outs[4 * g : 4 * g + 4]
            for k in range(count):
                pack, row_at, gram_at, left_at = where[first + k]
                rows = mixed_refs[first + k][...]
                (
                    factor_ref[k],
                    moment_new_ref[k],
                    new_ref[k],
                    error_ref[0, k],
                ) = finish_matrix(
                    reps,
                    rate,
                    pack_refs[pack][:, row_at : row_at + rows.shape[1]],
                    pack_refs[pack][:, gram_at : gram_at + 128],
                    left_refs[pack][left_at : left_at + 8, :],
                    rows,
                    state_refs[2 * g][k],
                    state_refs[2 * g + 1][k],
                )

    shapes = []
    for moment, _, _ in states:
        count, rows, columns = moment.shape
        shapes += [
            jax.ShapeDtypeStruct(moment.shape, jnp.float32),
            jax.ShapeDtypeStruct(moment.shape, jnp.float32),
            jax.ShapeDtypeStruct((1,) + moment.shape, jnp.float32),
            jax.ShapeDtypeStruct((count, 8, columns), jnp.float32),
        ]
    arrays = [a for state in states for a in state[:2]]
    return pl.pallas_call(
        kernel,
        in_specs=in_vmem(len(packs) + len(lefts) + len(mixed) + len(arrays)),
        out_specs=in_vmem(len(shapes)),
        out_shape=shapes,
        compiler_params=pltpu.CompilerParams(vmem_limit_bytes=VMEM_BYTES),
        cost_estimate=pl.CostEstimate(
            flops=96 * sum(m.size for m in mixed),
            bytes_accessed=24 * sum(m.size for m in mixed),
            transcendentals=0,
        ),
    )(*packs, *lefts, *mixed, *arrays)


def pack_wide(master, picks, groups, tile):
    count, rows, _ = master.shape
    number = picks.shape[0]

    def kernel(pick_ref, *refs):
        del pick_ref
        for group, out_ref in zip(groups, refs[number:]):
            at = 0
            for pick in group:
                for i in range(count):
                    out_ref[:, at : at + tile] = refs[pick][i].astype(jnp.bfloat16)
                    at += tile

    def spec(n):
        return pl.BlockSpec((count, rows, tile), lambda i, picks: (0, 0, picks[n]))

    shapes = [
        jax.ShapeDtypeStruct((rows, count * tile * len(group)), jnp.bfloat16) for group in groups
    ]
    return pl.pallas_call(
        kernel,
        grid_spec=pltpu.PrefetchScalarGridSpec(
            num_scalar_prefetch=1,
            grid=(1,),
            in_specs=[spec(n) for n in range(number)],
            out_specs=[pl.BlockSpec(s.shape, lambda i, picks: (0, 0)) for s in shapes],
        ),
        out_shape=shapes,
        compiler_params=pltpu.CompilerParams(vmem_limit_bytes=VMEM_BYTES),
        cost_estimate=pl.CostEstimate(
            flops=0, bytes_accessed=6 * number * count * rows * tile, transcendentals=0
        ),
    )(picks, *[master] * number)


def split_sum(home, got):
    shape = home.shape
    rows, columns = shape[-2:]
    lead = home.size // (rows * columns)
    half = rows // 2

    def kernel(home_ref, got_ref, away_ref, kept_ref):
        total = home_ref[0].astype(jnp.float32) + got_ref[0].astype(jnp.float32)
        away_ref[0] = total[:half].astype(jnp.bfloat16)
        kept_ref[0] = total[half:].astype(jnp.bfloat16)

    block = columns // 2 if columns % 256 == 0 else columns
    whole = pl.BlockSpec((1, rows, block), lambda i, j: (i, 0, j))
    part = pl.BlockSpec((1, half, block), lambda i, j: (i, 0, j))
    out = jax.ShapeDtypeStruct((lead, half, columns), jnp.bfloat16)
    away, kept = pl.pallas_call(
        kernel,
        grid=(lead, columns // block),
        in_specs=[whole, whole],
        out_specs=[part, part],
        out_shape=[out, out],
        compiler_params=pltpu.CompilerParams(vmem_limit_bytes=VMEM_BYTES),
        cost_estimate=pl.CostEstimate(
            flops=home.size, bytes_accessed=6 * home.size, transcendentals=0
        ),
    )(home.reshape(lead, rows, columns), got.reshape(lead, rows, columns))
    tail = (half, columns)
    return away.reshape(shape[:-2] + tail), kept.reshape(shape[:-2] + tail)


def out_kernel(owners, place_ref, core_ref, order_ref, att_ref, x_ref, gain_ref, *refs):
    halves, refs = refs[:4], refs[4:]
    residual_ref, mid_ref, mid_turned_ref, w_ref, turned_ref, sem = refs
    share = w_ref.shape[0] // owners

    @pl.when(pl.program_id(0) == 0)
    def _():
        for own in range(2):

            @pl.when(core_ref[0] == own)
            def _(own=own):
                spans = (
                    (halves[0 if own == 1 else 1], 384, 0, 128),
                    (halves[2 if own == 0 else 3], 0, 128, 512),
                    (halves[2 if own == 1 else 3], 0, 640, 512),
                )
                for ref, first, at, width in spans:
                    for a in range(owners):
                        pltpu.make_async_copy(
                            ref.at[place_ref[a], :, first : first + width],
                            w_ref.at[share * a : share * a + share, at : at + width],
                            sem.at[0],
                        ).start()

        pltpu.make_async_copy(w_ref, w_ref, sem.at[0]).wait()

    residual = x_ref[...].astype(jnp.float32) + across(att_ref[...], w_ref[...])
    residual_ref[...] = residual
    scale = lax.rsqrt(jnp.mean(residual * residual, axis=-1, keepdims=True) + eps_norm)
    mid = (residual * scale * gain_ref[...]).astype(jnp.bfloat16)
    mid_ref[...] = mid
    turned_ref[...] = mid.astype(jnp.float32).T
    parts = [
        turned_ref[pl.ds(pl.multiple_of(order_ref[p] * share, 8), share), :] for p in range(owners)
    ]
    mid_turned_ref[...] = jnp.concatenate(parts, axis=0).astype(jnp.bfloat16)


def project_out(places, core, order, attended, x, gain, halves):
    count, model = x.shape
    owners = order.shape[0]
    block = min(BLOCK_ROWS, count)
    rows = pl.BlockSpec((block, model), lambda i, *_: (i, 0))
    return pl.pallas_call(
        functools.partial(out_kernel, owners),
        grid_spec=pltpu.PrefetchScalarGridSpec(
            num_scalar_prefetch=3,
            grid=(count // block,),
            in_specs=[rows, rows, pl.BlockSpec((1, model), lambda i, *_: (0, 0))]
            + [pl.BlockSpec(memory_space=pl.ANY)] * 4,
            out_specs=[
                rows,
                rows,
                pl.BlockSpec((model, block), lambda i, *_: (0, i)),
                pl.BlockSpec((model, model), lambda i, *_: (0, 0)),
            ],
            scratch_shapes=[
                pltpu.VMEM((model, block), jnp.float32),
                pltpu.SemaphoreType.DMA((1,)),
            ],
        ),
        out_shape=[
            jax.ShapeDtypeStruct((count, model), jnp.float32),
            jax.ShapeDtypeStruct((count, model), jnp.bfloat16),
            jax.ShapeDtypeStruct((model, count), jnp.bfloat16),
            jax.ShapeDtypeStruct((model, model), jnp.bfloat16),
        ],
        compiler_params=pltpu.CompilerParams(vmem_limit_bytes=VMEM_BYTES),
        cost_estimate=pl.CostEstimate(
            flops=2 * count * model * model,
            bytes_accessed=12 * count * model + 4 * model * model,
            transcendentals=count,
        ),
    )(places, core, order, attended, x, gain, *halves)


class Grid:
    def __init__(self, mesh):
        self.reps = mesh.shape["rep"]
        self.shards = mesh.shape["shard"]
        self.core_bit = self.shards.bit_length() - 3
        stages = self.shards.bit_length() - 1
        self.order = [self.core_bit] + [b for b in range(stages) if b != self.core_bit]

    def swapped(self, rep, shard):
        bit = self.core_bit
        core = rep & 1
        turn = (shard >> bit) & 1
        return (rep - core + turn, shard - (turn << bit) + (core << bit))

    def flat(self, pair):
        return pair[0] * self.shards + pair[1]

    def every(self):
        return [(r, s) for r in range(self.reps) for s in range(self.shards)]

    def move(self, value, target):
        pairs = [(self.flat(p), self.flat(target(*p))) for p in self.every() if target(*p) != p]
        return lax.ppermute(value, ("rep", "shard"), pairs)

    def stays(self):
        return lax.axis_index("rep") % 2 == (lax.axis_index("shard") >> self.core_bit) % 2

    def swap_rows(self, value):
        return jnp.where(self.stays(), value, self.move(value, self.swapped))

    def partner(self, bit):
        def target(rep, shard):
            lr, ls = self.swapped(rep, shard)
            return self.swapped(lr, ls ^ (1 << bit))

        return target

    def last(self, bit):
        def target(rep, shard):
            lr, ls = self.swapped(rep, shard)
            return (lr, ls ^ (1 << bit))

        return target

    def flip_rep(self, bit):
        return lambda rep, shard: (rep ^ (1 << bit), shard)

    def flip_shard(self, bit):
        return lambda rep, shard: (rep, shard ^ (1 << bit))

    def doubling(self):
        return list(range(len(self.order)))[::-1]

    def places(self):
        out = [0] * self.shards
        for place in range(self.shards):
            distance = 0
            for k, bit in enumerate(self.doubling()):
                if (place >> k) & 1:
                    distance |= 1 << bit
            out[distance] = place
        return out

    def masks(self):
        count = len(self.order)
        out = []
        for place in range(self.shards):
            mask = 0
            for k, bit in enumerate(self.order):
                if not (place >> (count - 1 - k)) & 1:
                    mask |= 1 << bit
            out.append(mask)
        return out


def after(value, *others):
    return lax.optimization_barrier((value, others))[0]


def gather_pieces(grid, blocks):
    mine = []
    before = [None] * len(grid.order)
    for number, block in enumerate(blocks):
        held = block[None]
        for k, bit in enumerate(grid.doubling()):
            last = k == len(before) - 1
            if before[k] is not None:
                held = after(held, before[k])
            before[k] = grid.move(held, grid.flip_shard(bit))
            if not (last and number == len(blocks) - 1):
                held = jnp.concatenate([held, before[k]], axis=0)
        mine.append(held)
    return mine, before


class Sums:
    def __init__(self, grid, away, home):
        self.grid = grid
        self.stage = 0
        self.away, self.home = away, home
        self.send()

    def send(self):
        grid, bit = self.grid, self.grid.order[self.stage]
        if self.stage == len(grid.order) - 1:
            self.got = (grid.move(self.away, grid.last(bit)), grid.move(self.home, grid.swapped))
        else:
            self.got = grid.move(self.away, grid.partner(bit))

    def step(self, late, hold=False):
        self.got = after(self.got, late)
        self.away, self.home = split_sum(self.home, self.got)
        self.stage += 1
        if not hold:
            self.send()
        return (self.away, self.home)

    def join(self, other):
        self.away = jnp.concatenate([self.away, other.away], axis=-1)
        self.home = jnp.concatenate([self.home, other.home], axis=-1)
        self.send()

    def result(self, late):
        while self.stage < len(self.grid.order) - 1:
            self.step(late)
        return (self.got[0], self.home, self.got[1])


def butterfly(grid, value, moves):
    for move in moves:
        value = jax.tree.map(lambda v: v + grid.move(v, move), value)
    return value


def sum_all(grid, value, beside=None):
    rep = lax.axis_index("rep")
    bits = range(grid.reps.bit_length() - 1)
    pad = -value.shape[1] % (128 * grid.reps)
    columns = value.shape[1]
    value = jnp.pad(value, ((0, 0), (0, pad)))
    for bit in bits:
        half = value.shape[1] // 2
        upper = (rep >> bit) % 2 == 1
        low, high = value[:, :half], value[:, half:]
        got = grid.move(jnp.where(upper, low, high), grid.flip_rep(bit))
        value = jnp.where(upper, high, low) + got
    for bit in range(grid.shards.bit_length() - 1):
        value = value + grid.move(value, grid.flip_shard(bit))
    if beside is not None:
        value = after(value, beside)
    for bit in reversed(bits):
        got = grid.move(value, grid.flip_rep(bit))
        upper = (rep >> bit) % 2 == 1
        value = jnp.concatenate(
            [jnp.where(upper, got, value), jnp.where(upper, value, got)], axis=1
        )
    return value[:, :columns]


def shards(
    grid,
    tokens,
    cotangent,
    segments,
    positions,
    wide_master,
    square_master,
    key_value_master,
    wide_moment,
    square_moment,
    key_value_momentum,
    wide_error,
    square_error,
    key_value_error,
    wide_factor,
    square_factor,
    key_value_factor,
    norm_gains,
    gain_moment,
):
    reps, owners = grid.reps, grid.shards
    rep = lax.axis_index("rep")
    shard = lax.axis_index("shard")
    core = rep % 2
    turn = (shard >> grid.core_bit) % 2
    logical_shard = shard + (core - turn) * (1 << grid.core_bit)

    low_square = square_master.astype(jnp.bfloat16)
    low_narrow = key_value_master.astype(jnp.bfloat16)
    pieces = []
    for j in range(PAIRS):
        pieces.append(low_square[0, :, 384 * j : 384 * j + 384])
        pieces.append(low_narrow[0, :, 128 * j : 128 * j + 128])
        pieces.append(low_narrow[1, :, 128 * j : 128 * j + 128])
    low_attn = jnp.concatenate(pieces + [low_square[1]], axis=1)
    units = wide_master.shape[2] // 3

    position = grid.swap_rows(positions)[0]
    rows = low_attn.shape[0]
    tile = units // reps
    chained = 1 if rows % 16 == 0 else 0
    blocks = [low_attn[:, 1024 * i : 1024 * i + 1024] for i in range(3)]
    gain_row = norm_gains.astype(jnp.bfloat16).reshape(1, 2 * rows)
    gain_row = jnp.pad(gain_row, ((0, 15), (0, 512 - 2 * rows)))
    blocks[0] = jnp.concatenate([blocks[0], jnp.concatenate([gain_row] * 2, axis=1)], axis=0)
    blocks = [lax.dynamic_slice_in_dim(b, core * 512, 512, axis=1) for b in blocks]
    picks = [core * (reps // 2) + i for i in range(reps // 2)] if chained else []
    groups = [tuple(range(len(picks)))] if chained else []
    for k in range(chained, 3):
        groups.append((len(picks),))
        picks.append(reps * k + rep)
    cuts = list(pack_wide(wide_master, jnp.stack(picks).astype(jnp.int32), groups, tile))
    mine, gathering = gather_pieces(grid, blocks + cuts[:chained])
    other = [grid.move(held, grid.flip_rep(0)) for held in mine[:2]]
    places = jnp.array(grid.places(), jnp.int32)[jnp.arange(owners) ^ shard]
    cores = core[None]
    gain_w = mine[0][:, rows, : 2 * rows].reshape(owners, 2, rows)
    gain_w = jnp.take(gain_w, places, axis=0).transpose(1, 0, 2).reshape(2, -1).astype(jnp.float32)
    natural = jnp.arange(reps, dtype=jnp.int32)
    whole = jnp.zeros((1,), jnp.int32)
    moved_tokens = grid.move(after(tokens, gathering[1]), grid.swapped)
    tokens = jnp.where(grid.stays(), tokens, moved_tokens)[0]
    moved_out = grid.move(after(cotangent, moved_tokens), grid.swapped)
    model = gain_w.shape[1]
    columns = 640 * PAIRS
    qkv_w = assemble(rows, mine[:2], other[:2], places, cores, 0, columns)

    count = tokens.shape[0]
    hidden_in = tokens.astype(jnp.float32)
    gain_attn, gain_mlp = gain_w[0], gain_w[1]
    cos, sin = rotary_tables(position, HEAD_SIZE)
    cos = jnp.concatenate([cos] * 4, axis=1)
    sin = jnp.concatenate([-sin, sin] * 2, axis=1)
    place = position[:, None]
    order = jnp.array(grid.masks(), jnp.int32) ^ logical_shard

    tokens = after(tokens, mine[2])
    qkv, turned_in = project_qkv(order, tokens, gain_attn[None], qkv_w, cos, sin)
    if chained:
        held, got = after((mine[3], gathering[-1]), qkv)
        mine[3] = jnp.concatenate([held, got], axis=0)
        qkv = after(qkv, mine[3])
    else:
        mine[2] = jnp.concatenate([mine[2], gathering[-1]], axis=0)
    wide_parts = [None] * chained
    for k in range(chained, 3):
        part = after(cuts[k], mine[2:])
        part = lax.all_gather(part, ("rep", "shard"), axis=0, tiled=True)
        wide_parts.append((natural, whole, [part.reshape(reps, owners * rows, 3 * tile)]))
    mine[2] = after(mine[2], qkv)
    other += [grid.move(held, grid.flip_rep(0)) for held in mine[2:]]
    attended, logs = attend_forward(qkv, place)
    other[2:] = after(other[2:], attended)
    d_out = jnp.where(grid.stays(), cotangent, after(moved_out, attended))[0]
    if chained:
        slots = (natural + core * (reps // 2)) % reps
        wide_parts[0] = (slots, places, mine[3:] + other[3:])
        residual, normed_mid, turned_mid, out_w = project_out(
            places,
            cores,
            order,
            attended,
            tokens,
            gain_mlp[None],
            [mine[1], other[1], mine[2], other[2]],
        )
    else:
        out_w = assemble(rows, mine[1:3], other[1:3], places, cores, columns - 1024, 2048)
        residual = hidden_in + jnp.einsum(
            "tn,dn->td", attended, out_w, preferred_element_type=jnp.float32
        )
        normed_mid = normed(residual, gain_mlp).astype(jnp.bfloat16)
        turned_mid = turn_rows(normed_mid, order)
    turned_out = turn_rows(d_out, order)

    half = model // 2

    def weight_grad(turned, right):
        return Sums(
            grid,
            jnp.dot(turned[:half], right, preferred_element_type=jnp.float32).astype(jnp.bfloat16),
            jnp.dot(turned[half:], right, preferred_element_type=jnp.float32).astype(jnp.bfloat16),
        )

    wide_sums = []
    result, d_mid = residual, None
    for k in range(3):
        slots, where, weights = wide_parts[k]
        away, home, result, d_mid = mlp_part(
            reps, slots, where, normed_mid, d_out, turned_mid, turned_out, weights, result, d_mid
        )
        wide_sums.append(Sums(grid, away, home))
        for earlier in wide_sums[max(0, k - 2) : k]:
            d_mid, result = after((d_mid, result), earlier.step(away))
    result = grid.swap_rows(result.astype(jnp.bfloat16)[None])

    _, mid_back = jax.vjp(normed, residual, gain_mlp)
    d_residual, grad_gain_mlp = mid_back(d_mid)
    d_residual = d_residual + d_out.astype(jnp.float32)
    d_branch = d_residual.astype(jnp.bfloat16)
    d_attended = jnp.einsum(
        "td,dn->tn", d_branch, out_w, preferred_element_type=jnp.float32
    ).astype(jnp.bfloat16)
    out_sums = weight_grad(turn_rows(d_branch, order), attended)

    d_attended = after(d_attended, wide_sums[2].step(out_sums.away), wide_sums[0].got)
    d_stacks, pair_sums = [], []
    hold = len(grid.order) == 3
    for j in range(PAIRS):
        d_stack = attend_backward(qkv, d_attended, logs, place, cos, sin, j)
        d_stacks.append(d_stack)
        pair_sums.append(weight_grad(turned_in, d_stack))
        if j == 0:
            done = (wide_sums[1].step(d_stack), out_sums.step(d_stack), result)
        elif j == 1:
            done = (
                wide_sums[2].step(d_stack),
                out_sums.step(d_stack),
                pair_sums[0].step(d_stack),
                wide_sums[1].got,
            )
        else:
            done = (pair_sums[0].step(d_stack, hold), pair_sums[1].step(d_stack), out_sums.got)
        d_attended = after(d_attended, done, pair_sums[j].away)
        d_stacks = after(d_stacks, done, pair_sums[j].away)
    def back(j):
        return jnp.einsum(
            "tn,dn->td",
            d_stacks[j],
            qkv_w[:, 640 * j : 640 * j + 640],
            preferred_element_type=jnp.float32,
        )

    flag = grid.stays().astype(jnp.int32)[None]
    d_first = back(0) + back(1)
    d_stacks, wide_got = after(
        (d_stacks, wide_sums[2].got), pair_sums[2].step(d_first), pair_sums[1].step(d_first, hold)
    )
    wide_sums[2].got = wide_got
    spans = [(j, 0) for j in range(PAIRS)]
    late_sums = pair_sums
    if hold:
        pair_sums[0].join(pair_sums[1])
        spans = [(0, 0), (0, 640), (1, 0)]
        late_sums = [pair_sums[0], pair_sums[2]]
    mixed_wide, left_wide = mix_wide(
        flag, [part.result(d_first) for part in wide_sums], wide_error, wide_factor
    )
    mixed_out, left_out = mix_rest(
        flag,
        [out_sums.result(d_first)],
        [[(0, 0, model)]],
        [square_error[0, 1]],
        [square_factor[1]],
    )
    last_step = pair_sums[2].step(left_wide)
    d_stacks = after(d_stacks, last_step, left_out)
    d_normed_in = d_first + back(2)
    rep_moves = [grid.flip_rep(b) for b in range(reps.bit_length() - 1)]
    unit = 128 * reps
    left_early = butterfly(grid, jnp.concatenate([left_wide, left_out], axis=0), rep_moves)
    left_early = after(left_early, last_step)
    gram_early = 9 * units + model
    width = -(-(gram_early + 512) // unit) * unit
    early = contract_all(left_early, [mixed_wide, mixed_out], width)
    d_normed_in = after(d_normed_in, early)
    _, in_back = jax.vjp(normed, hidden_in, gain_attn)
    d_input, grad_gain_attn = in_back(d_normed_in)
    d_input = (d_input + d_residual).astype(jnp.bfloat16)
    early = sum_all(grid, early)
    late = d_input
    d_input = grid.swap_rows(d_input[None])
    narrow = 128 * PAIRS

    mixed_query, mixed_key, mixed_value, left_late = mix_rest(
        flag,
        [part.result(late) for part in late_sums],
        [
            [(which, at + first, at + last) for which, at in spans]
            for first, last in ((0, 384), (384, 512), (512, 640))
        ],
        [square_error[0, 0], key_value_error[0, 0], key_value_error[0, 1]],
        [square_factor[0], key_value_factor[0], key_value_factor[1]],
    )
    left_late = butterfly(grid, left_late, rep_moves)
    gram_late = columns
    gain_at = gram_late + 384
    width = -(-(gain_at + model) // unit) * unit
    gain_grad = jnp.stack([grad_gain_attn, grad_gain_mlp])
    mixed_late = [mixed_query, mixed_key, mixed_value]
    left_late = after(left_late, late)
    summed = contract_all(left_late, mixed_late, width, gain_grad)
    wide_new, wide_moment_new, wide_error_new, factor_wide = finish_wide(
        reps, early, gram_early, left_early, mixed_wide, wide_moment, wide_master
    )
    summed = butterfly(grid, summed, rep_moves + [grid.flip_shard(0)])
    summed = after(summed, wide_new)
    shard_moves = [grid.flip_shard(b) for b in range(1, owners.bit_length() - 1)]
    summed = butterfly(grid, summed, shard_moves)
    (
        square_new,
        square_moment_new,
        square_error_new,
        factor_square,
        narrow_new,
        narrow_moment_new,
        narrow_error_new,
        factor_narrow,
    ) = finish_rest(
        reps,
        [summed, early],
        [left_late, left_early],
        [mixed_query, mixed_out, mixed_key, mixed_value],
        [
            (0, 0, gram_late, 0),
            (1, 9 * units, gram_early + 384, 24),
            (0, model, gram_late + 128, 8),
            (0, model + narrow, gram_late + 256, 16),
        ],
        [
            (square_moment, square_master, rate_square),
            (key_value_momentum, key_value_master, rate_narrow),
        ],
    )
    gain_total = lax.dynamic_slice_in_dim(
        summed[:2, gain_at : gain_at + model], shard * (model // owners), model // owners, axis=1
    )
    gain_moment_new = decay_rate * gain_moment + gain_total / reps
    gains_new = norm_gains - rate_gains * gain_moment_new
    return (
        result,
        d_input,
        wide_new,
        square_new,
        narrow_new,
        wide_moment_new,
        square_moment_new,
        narrow_moment_new,
        wide_error_new,
        square_error_new,
        narrow_error_new,
        factor_wide,
        factor_square,
        factor_narrow,
        gains_new,
        gain_moment_new,
    )


def solution(mesh):
    return jax.shard_map(
        functools.partial(shards, Grid(mesh)),
        mesh=mesh,
        in_specs=(
            P(("rep", "shard"), None, None),
            P(("rep", "shard"), None, None),
            P(("rep", "shard"), None),
            P(("rep", "shard"), None),
            P(None, "shard", None),
            P(None, "shard", None),
            P(None, "shard", None),
            P(None, "shard", None),
            P(None, "shard", None),
            P(None, "shard", None),
            P("rep", None, "shard", None),
            P("rep", None, "shard", None),
            P("rep", None, "shard", None),
            P(),
            P(),
            P(),
            P(None, "shard"),
            P(None, "shard"),
        ),
        out_specs=(
            P(("rep", "shard"), None, None),
            P(("rep", "shard"), None, None),
            P(None, "shard", None),
            P(None, "shard", None),
            P(None, "shard", None),
            P(None, "shard", None),
            P(None, "shard", None),
            P(None, "shard", None),
            P("rep", None, "shard", None),
            P("rep", None, "shard", None),
            P("rep", None, "shard", None),
            P(),
            P(),
            P(),
            P(None, "shard"),
            P(None, "shard"),
        ),
        check_vma=False,
    )
```

time: 2150 us -> 695 us (0.32)
  waiting for transfers between devices: 1410 us -> 93.5 us
  matrix products: 422 us -> 46.4 us
  Pallas kernels: 0 us -> 362 us
  other arithmetic: 161 us -> 52.7 us
  blocking collectives: 107 us -> 0 us
  starting transfers between devices: 0.33 us -> 83.5 us
    reduce_scatter x3 -> x0, waiting for transfers between devices: 897 us -> none  [the longest x1 673 us: shards(): lax.psum_scatter(grad_wide, 'shard', scatter_dimension=1, tiled=True)]
    all_gather x3 -> x2, waiting for transfers between devices: 387 us -> 0.01 us  [shards(): part = lax.all_gather(part, ('rep', 'shard'), axis=0, tiled=True)]
    dot_general x45 -> x12, matrix products: 421 us -> 46.4 us  [the longest x3 15.4 us: back(): jnp.einsum('tn,dn->td', d_stacks[j], qkv_w[:, 640 * j:640 * j + 640], pre...]
    pallas_call x0 -> x34, Pallas kernels: none -> 362 us  [the longest x3 125 us: mlp_part(): pl.pallas_call(functools.partial(mlp_kernel, reps, first), grid_spec=pltp...]
    psum x1 -> x0, waiting for transfers between devices: 124 us -> none  [shards(): lax.psum((contract(basis_wide, mixed_wide), contract(basis_square, mixed_...]
    ppermute x0 -> x63, waiting for transfers between devices: none -> 92.8 us  [move(): return lax.ppermute(value, ('rep', 'shard'), pairs)]
    psum x3 -> x0, blocking collectives: 84.4 us -> none  [the longest x1 37.3 us: shards(): lax.psum((contract(basis_wide, mixed_wide), contract(basis_square, mixed_...]
    ppermute x0 -> x63, starting transfers between devices: none -> 83.4 us  [move(): return lax.ppermute(value, ('rep', 'shard'), pairs)]
  transfers between devices with their start and end apart: 8 -> 65, of which waited for: 7 -> 20; matrix products, arithmetic and copies ran while one was open for 11% -> 16% of each run, Pallas kernels for 0% -> 53%
where the time goes in v1:
time: 695 us; the launch traced here: 684 us
  Pallas kernels  362 us (52%)
  waiting for transfers between devices  93.5 us (13%)
  starting transfers between devices  83.5 us (12%)
  other arithmetic  52.7 us (8%)
  matrix products  46.4 us (7%)
  local copies, waits for them, and re-layouts  30.4 us (4%)
  between operations  15.4 us (2%)
    pallas_call x3, Pallas kernels, mlp_part(): pl.pallas_call(functools.partial(mlp_kernel, reps, first), grid_spec=pltp...  125 us
    ppermute x63, waiting for transfers between devices, move(): return lax.ppermute(value, ('rep', 'shard'), pairs)  92.8 us
    ppermute x63, starting transfers between devices, move(): return lax.ppermute(value, ('rep', 'shard'), pairs)  83.4 us
    pallas_call x3, Pallas kernels, attend_backward(): pl.pallas_call(backward_kernel, grid=(rows // block,), in_specs=[pl.Block...  54.7 us
    pallas_call x14, Pallas kernels, split_sum(): pl.pallas_call(kernel, grid=(lead, columns // block), in_specs=[whole, wh...  51.9 us
    pallas_call x1, Pallas kernels, attend_forward(): pl.pallas_call(forward_kernel, grid=(pairs, rows // block), in_specs=[pl....  33.3 us
    pallas_call x1, Pallas kernels, finish_wide(): pl.pallas_call(kernel, grid=(count, 3), in_specs=[pl.BlockSpec((8, third)...  18.3 us
    dot_general x3, matrix products, back(): jnp.einsum('tn,dn->td', d_stacks[j], qkv_w[:, 640 * j:640 * j + 640], pre...  15.4 us
  transfers between devices with their start and end apart: 65, of which 20 were waited for; matrix products, arithmetic and copies ran while one was open for 16% of the time, Pallas kernels for 53%

profile of v1, /device:TPU:0, one launch (start us, length us, event | category | flops | bytes accessed | tf_op | source)
XLA Modules:
  0.0 684.4 jit_solution(7844798796432775133)
XLA Ops:
  10.5 4.1 collective-permute-start
  14.9 7.4 %collective-permute-done = bf16[1,160,512]{2,1,0:T(8,128)(2,1)S(1)} collective-permute-done((bf16[1,160,512]{2,1,0:T(8,128)(2,1)S(1)}, bf16[1,160,512]{2,1,0:T(8,128)(2,1)S(1)}, u32[]{:S(2)}, u32[]{:S(2)}) %collective-permute-start) | collective-permute-done | bytes 163872 | tf_op jit(solution)/shard_map/ppermute | solution.py:945
  22.4 4.2 collective-permute-start.4
  26.5 6.2 collective-permute-done.1
  33.3 3.2 shard_map.306
  36.5 6.4 collective-permute-done.2
  43.8 13.5 %collective-permute-done.5 = bf16[2,144,512]{2,1,0:T(8,128)(2,1)S(1)} collective-permute-done((bf16[2,144,512]{2,1,0:T(8,128)(2,1)S(1)}, bf16[2,144,512]{2,1,0:T(8,128)(2,1)S(1)}, u32[]{:S(2)}, u32[]{:S(2)}) %collective-permute-start.5) | collective-permute-done | bytes 294944 | tf_op jit(solution)/shard_map/ppermute | solution.py:945
  57.2 2.5 collective-permute-start.6
  63.5 2.8 collective-permute-done.6
  67.9 5.6 collective-permute-done.9
  76.4 11.1 %collective-permute-done.7 = bf16[2,144,1536]{2,1,0:T(8,128)(2,1)} collective-permute-done((bf16[2,144,1536]{2,1,0:T(8,128)(2,1)S(1)}, bf16[2,144,1536]{2,1,0:T(8,128)(2,1)}, u32[]{:S(2)}, u32[]{:S(2)}) %collective-permute-start.7) | collective-permute-done | bytes 884768 | tf_op jit(solution)/shard_map/ppermute | solution.py:945
  98.0 8.2 %collective-permute-done.11 = bf16[4,144,512]{2,1,0:T(8,128)(2,1)S(1)} collective-permute-done((bf16[4,144,512]{2,1,0:T(8,128)(2,1)S(1)}, bf16[4,144,512]{2,1,0:T(8,128)(2,1)S(1)}, u32[]{:S(2)}, u32[]{:S(2)}) %collective-permute-start.11) | collective-permute-done | bytes 589856 | tf_op jit(solution)/shard_map/ppermute | solution.py:945
  116.0 7.5 %shard_map.307 = bf16[8,144,1920]{2,1,0:T(8,128)(2,1)} custom-call(s32[8]{0:T(128)} %copy-done.52, s32[1]{0:T(128)} %bitcast.1.core_ref, bf16[8,160,512]{2,1,0:T(8,128)(2,1)} %copy-done.7, bf16[8,144,512]{2,1,0:T(8,128)(2,1)} %constant_dynamic-update-slice_fusion.3.refs_1_.refs_0_, bf16[8,160,512]{2,1,0:T(8,128)(2,1)} %collective-permute-done.12.refs_2_, ...), custom_call_target="tpu_custom_call" | custom-call | bytes 9437184 | tf_op jit(solution)/shard_map/pallas_call | solution.py:496
  123.6 4.5 fusion.3
  128.1 12.0 %shard_map.308 = (bf16[1024,1920]{1,0:T(8,128)(2,1)}, bf16[1152,1024]{1,0:T(8,128)(2,1)}) custom-call(s32[8]{0:T(128)} %broadcast_xor_fusion.order_ref, bf16[1024,1152]{1,0:T(8,128)(2,1)} %get-tuple-element.155.x_ref, f32[1,1152]{1,0:T(1,128)} %slice.132.gain_ref, bf16[1152,1920]{1,0:T(8,128)(2,1)} %bitcast.131, f32[1024,128]{1,0:T(8,128)} %get-tuple-element.305.cos_ref, ...), custom_call_target="tpu_custom_call" | custom-call | flops 4529848320 | bytes 13074432 | tf_op jit(solution)/shard_map/pallas_call | solution.py:82
  140.1 6.2 collective-permute-done.15
  147.6 3.0 constant_dynamic-update-slice_fusion.5.refs_3_
  157.7 33.3 %shard_map.309 = (bf16[1024,1152]{1,0:T(8,128)(2,1)}, f32[3,1024,128]{2,1,0:T(8,128)}) custom-call(bf16[1024,1920]{1,0:T(8,128)(2,1)} %get-tuple-element.160.qkv_ref, s32[1024,1]{1,0:T(8,128)} %copy.40.pos_ref), custom_call_target="tpu_custom_call" | custom-call | flops 8053063680 | bytes 15728640 | tf_op jit(solution)/shard_map/pallas_call | solution.py:179
  192.7 5.2 shard_map.311.refs_1_
  198.9 12.2 %shard_map.310 = (f32[1024,1152]{1,0:T(8,128)}, bf16[1024,1152]{1,0:T(8,128)(2,1)}, bf16[1152,1024]{1,0:T(8,128)(2,1)}, bf16[1152,1152]{1,0:T(8,128)(2,1)}) custom-call(s32[8]{0:T(128)} %copy-done.52, s32[1]{0:T(128)} %bitcast.1.core_ref, s32[8]{0:T(128)} %broadcast_xor_fusion.order_ref, bf16[1024,1152]{1,0:T(8,128)(2,1)} %get-tuple-element.161.att_ref, ...), custom_call_target="tpu_custom_call" | custom-call | flops 2717908992 | bytes 19464192 | tf_op jit(solution)/shard_map/pallas_call | solution.py:890
  211.1 42.1 %shard_map.312 = (bf16[3,576,1024]{2,1,0:T(8,128)(2,1)}, bf16[3,576,1024]{2,1,0:T(8,128)(2,1)}, f32[1024,1152]{1,0:T(8,128)}, f32[1024,1152]{1,0:T(8,128)}) custom-call(s32[4]{0:T(128)} %and_select_fusion.slot_ref, s32[8]{0:T(128)} %copy-done.52, bf16[1024,1152]{1,0:T(8,128)(2,1)} %get-tuple-element.164.mid_ref, ...), custom_call_target="tpu_custom_call" | custom-call | flops 21743271936 | bytes 42467328 | tf_op jit(solution)/shard_map/pallas_call | solution.py:433
  253.1 7.0 %collective-permute-start.19 = (bf16[3,576,1024]{2,1,0:T(8,128)(2,1)}, bf16[3,576,1024]{2,1,0:T(8,128)(2,1)S(1)}, u32[]{:S(2)}, u32[]{:S(2)}) collective-permute-start(bf16[3,576,1024]{2,1,0:T(8,128)(2,1)} %get-tuple-element.177), channel_id=1, source_target_pairs={{0,8},{1,9},{2,10},{3,11},{4,12},{5,13},{6,14},{7,15},{8,0},{9,1},... | collective-permute-start | bytes 10616840 | tf_op jit(solution)/shard_map/ppermute | solution.py:945
  260.7 41.3 %shard_map.313 = (bf16[3,576,1024]{2,1,0:T(8,128)(2,1)}, bf16[3,576,1024]{2,1,0:T(8,128)(2,1)}, f32[1024,1152]{1,0:T(8,128)}, f32[1024,1152]{1,0:T(8,128)}) custom-call(s32[4]{0:T(128)} %iota.19.slot_ref, s32[1]{0:T(128)} %constant.117.clone.1.place_ref, bf16[1024,1152]{1,0:T(8,128)(2,1)} %get-tuple-element.164.mid_ref, ...), custom_call_target="tpu_custom_call" | custom-call | flops 21743271936 | bytes 42467328 | tf_op jit(solution)/shard_map/pallas_call | solution.py:433
  306.6 2.7 multiply_reduce_fusion.2
  311.1 6.2 shard_map.314
  318.9 41.3 %shard_map.315 = (bf16[3,576,1024]{2,1,0:T(8,128)(2,1)}, bf16[3,576,1024]{2,1,0:T(8,128)(2,1)}, f32[1024,1152]{1,0:T(8,128)}, f32[1024,1152]{1,0:T(8,128)}) custom-call(s32[4]{0:T(128)} %iota.16.slot_ref, s32[1]{0:T(128)} %constant.117.clone.1.place_ref, bf16[1024,1152]{1,0:T(8,128)(2,1)} %get-tuple-element.164.mid_ref, ...), custom_call_target="tpu_custom_call" | custom-call | flops 21743271936 | bytes 42467328 | tf_op jit(solution)/shard_map/pallas_call | solution.py:433
  361.7 5.5 shard_map.316
  367.1 3.5 collective-permute-start.24
  372.2 6.3 shard_map.317
  379.0 4.2 convert_bitcast_fusion
  389.7 4.7 convolution_convert_fusion.d_ref
  394.4 5.2 shard_map.318
  399.6 4.8 convolution_convert_fusion.2
  405.9 6.2 shard_map.319
  413.7 18.3 %shard_map.320 = bf16[1024,640]{1,0:T(8,128)(2,1)} custom-call(bf16[1024,1920]{1,0:T(8,128)(2,1)} %get-tuple-element.160.qkv_ref, bf16[1024,1152]{1,0:T(8,128)(2,1)} %convolution_convert_fusion.d_ref, f32[3,1024,128]{2,1,0:T(8,128)} %get-tuple-element.206.log_ref, s32[1024,1]{1,0:T(8,128)} %copy.40.pos_ref, f32[1024,128]{1,0:T(8,128)} %get-tuple-element.305.cos_ref, ...), custom_call_target="tpu_custom_call" | custom-call | flops 6710886400 | bytes 5242880 | tf_op jit(solution)/shard_map/pallas_call | solution.py:269
  431.9 3.8 convolution_convert_fusion.8
  439.0 2.8 fusion.7.home_ref
  441.7 3.0 shard_map.322
  445.2 5.0 shard_map.321
  452.6 4.1 broadcast_select_fusion.1
  456.7 18.0 %shard_map.323 = bf16[1024,640]{1,0:T(8,128)(2,1)} custom-call(bf16[1024,1920]{1,0:T(8,128)(2,1)} %get-tuple-element.160.qkv_ref, bf16[1024,1152]{1,0:T(8,128)(2,1)} %convolution_convert_fusion.d_ref, f32[3,1024,128]{2,1,0:T(8,128)} %get-tuple-element.206.log_ref, s32[1024,1]{1,0:T(8,128)} %copy.40.pos_ref, f32[1024,128]{1,0:T(8,128)} %get-tuple-element.305.cos_ref, ...), custom_call_target="tpu_custom_call" | custom-call | flops 6710886400 | bytes 5242880 | tf_op jit(solution)/shard_map/pallas_call | solution.py:269
  482.1 3.7 convolution_convert_fusion.6
  485.8 4.8 collective-permute-start.34
  490.6 5.0 shard_map.324
  495.6 3.6 fusion.13.home_ref
  501.0 18.4 %shard_map.327 = bf16[1024,640]{1,0:T(8,128)(2,1)} custom-call(bf16[1024,1920]{1,0:T(8,128)(2,1)} %get-tuple-element.160.qkv_ref, bf16[1024,1152]{1,0:T(8,128)(2,1)} %convolution_convert_fusion.d_ref, f32[3,1024,128]{2,1,0:T(8,128)} %get-tuple-element.206.log_ref, s32[1024,1]{1,0:T(8,128)} %copy.40.pos_ref, f32[1024,128]{1,0:T(8,128)} %get-tuple-element.305.cos_ref, ...), custom_call_target="tpu_custom_call" | custom-call | flops 6710886400 | bytes 5242880 | tf_op jit(solution)/shard_map/pallas_call | solution.py:269
  519.4 3.8 fusion.14.home_ref
  527.9 2.7 shard_map.334
  536.3 4.0 fusion.9
  540.4 5.8 convolution_add_fusion.1
  550.9 12.2 %shard_map.332 = (f32[3,144,3072]{2,1,0:T(8,128)}, f32[24,144]{1,0:T(8,128)}) custom-call(s32[1]{0:T(128)} %bitcast.54.flag_ref, bf16[3,144,1024]{2,1,0:T(8,128)(2,1)} %copy-done.22, bf16[3,144,1024]{2,1,0:T(8,128)(2,1)} %get-tuple-element.191.refs_1_, bf16[3,144,1024]{2,1,0:T(8,128)(2,1)} %collective-permute-done.25.refs_2_, ...), custom_call_target="tpu_custom_call" | custom-call | flops 127401984 | bytes 18579456 | tf_op jit(solution)/shard_map/pallas_call | solution.py:568
  568.0 2.9 collective-permute-start.52
  575.8 6.0 shard_map.335
  582.8 3.8 collective-permute-start.45
  586.6 5.5 convolution_add_fusion
  594.4 2.5 collective-permute-done.46
  598.1 3.5 shard_map.337
  604.8 6.7 fusion.2
  616.0 2.6 shard_map.338
  632.5 18.3 %shard_map.336 = (f32[3,144,3072]{2,1,0:T(8,128)}, f32[3,144,3072]{2,1,0:T(8,128)}, f32[1,3,144,3072]{3,2,1,0:T(8,128)}, f32[3,8,3072]{2,1,0:T(8,128)}) custom-call(f32[8,11264]{1,0:T(8,128)} %pad_maximum_fusion.10.row_ref.gram_ref.refs_1_, f32[8,11264]{1,0:T(8,128)} %pad_maximum_fusion.10.row_ref.gram_ref.refs_1_, f32[32,144]{1,0:T(8,128)} %add.181.refs_0_.left_ref.refs_3_, ...), custom_call_target="tpu_custom_call" | custom-call | flops 127401984 | bytes 31850496 | tf_op jit(solution)/shard_map/pallas_call | solution.py:693
  650.9 8.6 %collective-permute-done.61 = f32[8,3584]{1,0:T(8,128)S(1)} collective-permute-done((f32[8,3584]{1,0:T(8,128)S(1)}, f32[8,3584]{1,0:T(8,128)S(1)}, u32[]{:S(2)}, u32[]{:S(2)}) %collective-permute-start.61) | collective-permute-done | bytes 114720 | tf_op jit(solution)/shard_map/ppermute | solution.py:945
  659.5 2.5 collective-permute-start.62
  662.1 4.8 collective-permute-done.62
  667.6 7.4 %shard_map.339 = (f32[2,144,1152]{2,1,0:T(8,128)}, f32[2,144,1152]{2,1,0:T(8,128)}, f32[1,2,144,1152]{3,2,1,0:T(8,128)}, f32[2,8,1152]{2,1,0:T(8,128)}, f32[2,14...) custom-call(f32[8,3584]{1,0:T(8,128)} %copy-done.27, ...), custom_call_target="tpu_custom_call" | custom-call | flops 42467328 | bytes 10616832 | tf_op jit(solution)/shard_map/pallas_call | solution.py:768
  (343 shorter events, 135.2 us)
Async XLA Ops:
  7.2 253.0 %all-gather.3.cloned.1.call-start = ((), (), s32[]{:S(2)}) async-start(), calls=%async_computation | async-start | bytes 7299072 | tf_op jit(solution)/shard_map/all_gather | solution.py:1170
  10.5 11.8 %collective-permute-start = (bf16[1,160,512]{2,1,0:T(8,128)(2,1)S(1)}, bf16[1,160,512]{2,1,0:T(8,128)(2,1)S(1)}, u32[]{:S(2)}, u32[]{:S(2)}) collective-permute-start(bf16[1,160,512]{2,1,0:T(8,128)(2,1)S(1)} %fusion.28), channel_id=1, source_target_pairs={{0,4},{1,5},{2,6},{3,7},{4,0},{5,1},{6,2},{7,3},{8,12},{9,13},{10,... | collective-permute-start | bytes 491528 | tf_op jit(solution)/shard_map/ppermute | solution.py:945
  22.3 10.4 %collective-permute-start.1 = (bf16[1,144,512]{2,1,0:T(8,128)(2,1)S(1)}, bf16[1,144,512]{2,1,0:T(8,128)(2,1)S(1)}, u32[]{:S(2)}, u32[]{:S(2)}) collective-permute-start(bf16[1,144,512]{2,1,0:T(8,128)(2,1)S(1)} %dynamic-slice_bitcast_fusion), channel_id=1, source_target_pairs={{0,4},{1,5},{2,6},{3,7},{4,0},{5,1},{6,2},{7,3},{8,12},{9,13},{10,... | collective-permute-start | bytes 442376 | tf_op jit(solution)/shard_map/ppermute | solution.py:945
  22.4 20.5 %collective-permute-start.4 = (bf16[2,160,512]{2,1,0:T(8,128)(2,1)S(1)}, bf16[2,160,512]{2,1,0:T(8,128)(2,1)S(1)}, u32[]{:S(2)}, u32[]{:S(2)}) collective-permute-start(bf16[2,160,512]{2,1,0:T(8,128)(2,1)S(1)} %pad_maximum_fusion.11), channel_id=1, source_target_pairs={{0,2},{1,3},{2,0},{3,1},{4,6},{5,7},{6,4},{7,5},{8,10},{9,11},{10,... | collective-permute-start | bytes 983048 | tf_op jit(solution)/shard_map/ppermute | solution.py:945
  32.7 10.2 %collective-permute-start.2 = (bf16[1,144,512]{2,1,0:T(8,128)(2,1)S(1)}, bf16[1,144,512]{2,1,0:T(8,128)(2,1)S(1)}, u32[]{:S(2)}, u32[]{:S(2)}) collective-permute-start(bf16[1,144,512]{2,1,0:T(8,128)(2,1)S(1)} %dynamic-slice_bitcast_fusion.1), channel_id=1, source_target_pairs={{0,4},{1,5},{2,6},{3,7},{4,0},{5,1},{6,2},{7,3},{8,12},{9,13},{10,... | collective-permute-start | bytes 442376 | tf_op jit(solution)/shard_map/ppermute | solution.py:945
  42.9 19.6 %collective-permute-start.3 = (bf16[1,144,1536]{2,1,0:T(8,128)(2,1)}, bf16[1,144,1536]{2,1,0:T(8,128)(2,1)}, u32[]{:S(2)}, u32[]{:S(2)}) collective-permute-start(bf16[1,144,1536]{2,1,0:T(8,128)(2,1)} %bitcast.136), channel_id=1, source_target_pairs={{0,4},{1,5},{2,6},{3,7},{4,0},{5,1},{6,2},{7,3},{8,12},{9,13},{10,... | collective-permute-start | bytes 1327112 | tf_op jit(solution)/shard_map/ppermute | solution.py:945
  42.9 14.3 %collective-permute-start.5 = (bf16[2,144,512]{2,1,0:T(8,128)(2,1)S(1)}, bf16[2,144,512]{2,1,0:T(8,128)(2,1)S(1)}, u32[]{:S(2)}, u32[]{:S(2)}) collective-permute-start(bf16[2,144,512]{2,1,0:T(8,128)(2,1)S(1)} %pad_maximum_fusion.13), channel_id=1, source_target_pairs={{0,2},{1,3},{2,0},{3,1},{4,6},{5,7},{6,4},{7,5},{8,10},{9,11},{10,... | collective-permute-start | bytes 884744 | tf_op jit(solution)/shard_map/ppermute | solution.py:945
  43.0 46.6 %collective-permute-start.14 = (s32[1,1024]{1,0:T(1,128)S(1)}, s32[1,1024]{1,0:T(1,128)S(1)}, u32[]{:S(2)}, u32[]{:S(2)}) collective-permute-start(s32[1,1024]{1,0:T(1,128)S(1)} %copy-done.50), channel_id=1, source_target_pairs={{2,8},{3,9},{6,12},{7,13},{8,2},{9,3},{12,6},{13,7},{18,24},{19,25... | collective-permute-start | bytes 12296 | tf_op jit(solution)/shard_map/ppermute | solution.py:945
  57.2 9.1 %collective-permute-start.6 = (bf16[2,144,512]{2,1,0:T(8,128)(2,1)S(1)}, bf16[2,144,512]{2,1,0:T(8,128)(2,1)S(1)}, u32[]{:S(2)}, u32[]{:S(2)}) collective-permute-start(bf16[2,144,512]{2,1,0:T(8,128)(2,1)S(1)} %pad_maximum_fusion.12), channel_id=1, source_target_pairs={{0,2},{1,3},{2,0},{3,1},{4,6},{5,7},{6,4},{7,5},{8,10},{9,11},{10,... | collective-permute-start | bytes 884744 | tf_op jit(solution)/shard_map/ppermute | solution.py:945
  60.6 12.9 %collective-permute-start.9 = (bf16[4,160,512]{2,1,0:T(8,128)(2,1)}, bf16[4,160,512]{2,1,0:T(8,128)(2,1)S(1)}, u32[]{:S(2)}, u32[]{:S(2)}) collective-permute-start(bf16[4,160,512]{2,1,0:T(8,128)(2,1)} %pad_maximum_fusion.3), channel_id=1, source_target_pairs={{0,1},{1,0},{2,3},{3,2},{4,5},{5,4},{6,7},{7,6},{8,9},{9,8},{10,11... | collective-permute-start | bytes 1966088 | tf_op jit(solution)/shard_map/ppermute | solution.py:945
  67.0 20.5 %collective-permute-start.7 = (bf16[2,144,1536]{2,1,0:T(8,128)(2,1)S(1)}, bf16[2,144,1536]{2,1,0:T(8,128)(2,1)}, u32[]{:S(2)}, u32[]{:S(2)}) collective-permute-start(bf16[2,144,1536]{2,1,0:T(8,128)(2,1)S(1)} %pad_maximum_fusion.2), channel_id=1, source_target_pairs={{0,2},{1,3},{2,0},{3,1},{4,6},{5,7},{6,4},{7,5},{8,10},{9,11},{10,... | collective-permute-start | bytes 2654216 | tf_op jit(solution)/shard_map/ppermute | solution.py:945
  73.5 17.1 %collective-permute-start.10 = (bf16[4,144,512]{2,1,0:T(8,128)(2,1)S(1)}, bf16[4,144,512]{2,1,0:T(8,128)(2,1)}, u32[]{:S(2)}, u32[]{:S(2)}) collective-permute-start(bf16[4,144,512]{2,1,0:T(8,128)(2,1)S(1)} %pad_maximum_fusion.5), channel_id=1, source_target_pairs={{0,1},{1,0},{2,3},{3,2},{4,5},{5,4},{6,7},{7,6},{8,9},{9,8},{10,11... | collective-permute-start | bytes 1769480 | tf_op jit(solution)/shard_map/ppermute | solution.py:945
  87.5 36.1 %collective-permute-start.8 = (bf16[1,1024,1152]{2,1,0:T(8,128)(2,1)}, bf16[1,1024,1152]{2,1,0:T(8,128)(2,1)}, u32[]{:S(2)}, u32[]{:S(2)}) collective-permute-start(bf16[1,1024,1152]{2,1,0:T(8,128)(2,1)} %param.20), channel_id=1, source_target_pairs={{2,8},{3,9},{6,12},{7,13},{8,2},{9,3},{12,6},{13,7},{18,24},{19,25... | collective-permute-start | bytes 7077896 | tf_op jit(solution)/shard_map/ppermute | solution.py:945
  90.6 15.6 %collective-permute-start.11 = (bf16[4,144,512]{2,1,0:T(8,128)(2,1)S(1)}, bf16[4,144,512]{2,1,0:T(8,128)(2,1)S(1)}, u32[]{:S(2)}, u32[]{:S(2)}) collective-permute-start(bf16[4,144,512]{2,1,0:T(8,128)(2,1)S(1)} %pad_maximum_fusion.4), channel_id=1, source_target_pairs={{0,1},{1,0},{2,3},{3,2},{4,5},{5,4},{6,7},{7,6},{8,9},{9,8},{10,11... | collective-permute-start | bytes 1769480 | tf_op jit(solution)/shard_map/ppermute | solution.py:945
  93.3 21.7 %collective-permute-start.12 = (bf16[8,160,512]{2,1,0:T(8,128)(2,1)S(1)}, bf16[8,160,512]{2,1,0:T(8,128)(2,1)}, u32[]{:S(2)}, u32[]{:S(2)}) collective-permute-start(bf16[8,160,512]{2,1,0:T(8,128)(2,1)S(1)} %pad_maximum_fusion.1.refs_0_), channel_id=1, source_target_pairs={{0,8},{1,9},{2,10},{3,11},{4,12},{5,13},{6,14},{7,15},{8,0},{9,1},... | collective-permute-start | bytes 3932168 | tf_op jit(solution)/shard_map/ppermute | solution.py:945
  96.2 19.8 %collective-permute-start.13 = (bf16[8,144,512]{2,1,0:T(8,128)(2,1)}, bf16[8,144,512]{2,1,0:T(8,128)(2,1)}, u32[]{:S(2)}, u32[]{:S(2)}) collective-permute-start(bf16[8,144,512]{2,1,0:T(8,128)(2,1)} %constant_dynamic-update-slice_fusion.3.refs_1_.refs_0_), channel_id=1, source_target_pairs={{0,8},{1,9},{2,10},{3,11},{4,12},{5,13},{6,14},{7,15},{8,0},{9,1},... | collective-permute-start | bytes 3538952 | tf_op jit(solution)/shard_map/ppermute | solution.py:945
  106.2 40.1 %collective-permute-start.15 = (bf16[4,144,1536]{2,1,0:T(8,128)(2,1)S(1)}, bf16[4,144,1536]{2,1,0:T(8,128)(2,1)}, u32[]{:S(2)}, u32[]{:S(2)}) collective-permute-start(bf16[4,144,1536]{2,1,0:T(8,128)(2,1)S(1)} %pad_maximum_fusion), channel_id=1, source_target_pairs={{0,1},{1,0},{2,3},{3,2},{4,5},{5,4},{6,7},{7,6},{8,9},{9,8},{10,11... | collective-permute-start | bytes 5308424 | tf_op jit(solution)/shard_map/ppermute | solution.py:945
  150.6 167.8 %all-gather.5.cloned.1.call-start = ((), (), s32[]{:S(2)}) async-start(), calls=%async_computation.1 | async-start | bytes 7299072 | tf_op jit(solution)/shard_map/all_gather | solution.py:1170
  151.3 46.5 %collective-permute-start.17 = (bf16[8,144,1536]{2,1,0:T(8,128)(2,1)}, bf16[8,144,1536]{2,1,0:T(8,128)(2,1)}, u32[]{:S(2)}, u32[]{:S(2)}) collective-permute-start(bf16[8,144,1536]{2,1,0:T(8,128)(2,1)} %constant_dynamic-update-slice_fusion.5.refs_3_), channel_id=1, source_target_pairs={{0,8},{1,9},{2,10},{3,11},{4,12},{5,13},{6,14},{7,15},{8,0},{9,1},... | collective-permute-start | bytes 10616840 | tf_op jit(solution)/shard_map/ppermute | solution.py:945
  151.4 39.6 %collective-permute-start.18 = (bf16[1,1024,1152]{2,1,0:T(8,128)(2,1)S(1)}, bf16[1,1024,1152]{2,1,0:T(8,128)(2,1)}, u32[]{:S(2)}, u32[]{:S(2)}) collective-permute-start(bf16[1,1024,1152]{2,1,0:T(8,128)(2,1)S(1)} %copy-done.15), channel_id=1, source_target_pairs={{2,8},{3,9},{6,12},{7,13},{8,2},{9,3},{12,6},{13,7},{18,24},{19,25... | collective-permute-start | bytes 7077896 | tf_op jit(solution)/shard_map/ppermute | solution.py:945
  157.3 40.5 %collective-permute-start.16 = (bf16[8,144,512]{2,1,0:T(8,128)(2,1)}, bf16[8,144,512]{2,1,0:T(8,128)(2,1)S(1)}, u32[]{:S(2)}, u32[]{:S(2)}) collective-permute-start(bf16[8,144,512]{2,1,0:T(8,128)(2,1)} %copy-done.33), channel_id=1, source_target_pairs={{0,8},{1,9},{2,10},{3,11},{4,12},{5,13},{6,14},{7,15},{8,0},{9,1},... | collective-permute-start | bytes 3538952 | tf_op jit(solution)/shard_map/ppermute | solution.py:945
  253.1 56.2 %collective-permute-start.19 = (bf16[3,576,1024]{2,1,0:T(8,128)(2,1)}, bf16[3,576,1024]{2,1,0:T(8,128)(2,1)S(1)}, u32[]{:S(2)}, u32[]{:S(2)}) collective-permute-start(bf16[3,576,1024]{2,1,0:T(8,128)(2,1)} %get-tuple-element.177), channel_id=1, source_target_pairs={{0,8},{1,9},{2,10},{3,11},{4,12},{5,13},{6,14},{7,15},{8,0},{9,1},... | collective-permute-start | bytes 10616840 | tf_op jit(solution)/shard_map/ppermute | solution.py:945
  302.0 70.2 %collective-permute-start.21 = (bf16[3,576,1024]{2,1,0:T(8,128)(2,1)}, bf16[3,576,1024]{2,1,0:T(8,128)(2,1)}, u32[]{:S(2)}, u32[]{:S(2)}) collective-permute-start(bf16[3,576,1024]{2,1,0:T(8,128)(2,1)} %get-tuple-element.178), channel_id=1, source_target_pairs={{0,8},{1,9},{2,10},{3,11},{4,12},{5,13},{6,14},{7,15},{8,0},{9,1},... | collective-permute-start | bytes 10616840 | tf_op jit(solution)/shard_map/ppermute | solution.py:945
  317.3 43.1 %collective-permute-start.20 = (bf16[3,288,1024]{2,1,0:T(8,128)(2,1)}, bf16[3,288,1024]{2,1,0:T(8,128)(2,1)S(1)}, u32[]{:S(2)}, u32[]{:S(2)}) collective-permute-start(bf16[3,288,1024]{2,1,0:T(8,128)(2,1)} %get-tuple-element.180), channel_id=1, source_target_pairs={{0,1},{1,0},{2,3},{3,2},{4,5},{5,4},{6,7},{7,6},{8,9},{9,8},{10,11... | collective-permute-start | bytes 5308424 | tf_op jit(solution)/shard_map/ppermute | solution.py:945
  360.2 44.2 %collective-permute-start.23 = (bf16[3,576,1024]{2,1,0:T(8,128)(2,1)}, bf16[3,576,1024]{2,1,0:T(8,128)(2,1)}, u32[]{:S(2)}, u32[]{:S(2)}) collective-permute-start(bf16[3,576,1024]{2,1,0:T(8,128)(2,1)} %get-tuple-element.188), channel_id=1, source_target_pairs={{0,8},{1,9},{2,10},{3,11},{4,12},{5,13},{6,14},{7,15},{8,0},{9,1},... | collective-permute-start | bytes 10616840 | tf_op jit(solution)/shard_map/ppermute | solution.py:945
  367.1 44.9 %collective-permute-start.24 = (bf16[3,144,1024]{2,1,0:T(8,128)(2,1)}, bf16[3,144,1024]{2,1,0:T(8,128)(2,1)S(1)}, u32[]{:S(2)}, u32[]{:S(2)}) collective-permute-start(bf16[3,144,1024]{2,1,0:T(8,128)(2,1)} %get-tuple-element.190), channel_id=1, source_target_pairs={{0,4},{1,5},{2,12},{3,13},{4,0},{5,1},{6,8},{7,9},{8,6},{9,7},{10,... | collective-permute-start | bytes 2654216 | tf_op jit(solution)/shard_map/ppermute | solution.py:945
  370.6 43.0 %collective-permute-start.25 = (bf16[3,144,1024]{2,1,0:T(8,128)(2,1)}, bf16[3,144,1024]{2,1,0:T(8,128)(2,1)}, u32[]{:S(2)}, u32[]{:S(2)}) collective-permute-start(bf16[3,144,1024]{2,1,0:T(8,128)(2,1)} %get-tuple-element.191.refs_1_), channel_id=1, source_target_pairs={{2,8},{3,9},{6,12},{7,13},{8,2},{9,3},{12,6},{13,7},{18,24},{19,25... | collective-permute-start | bytes 2654216 | tf_op jit(solution)/shard_map/ppermute | solution.py:945
  378.5 66.7 %collective-permute-start.26 = (bf16[3,288,1024]{2,1,0:T(8,128)(2,1)}, bf16[3,288,1024]{2,1,0:T(8,128)(2,1)}, u32[]{:S(2)}, u32[]{:S(2)}) collective-permute-start(bf16[3,288,1024]{2,1,0:T(8,128)(2,1)} %get-tuple-element.196), channel_id=1, source_target_pairs={{0,1},{1,0},{2,3},{3,2},{4,5},{5,4},{6,7},{7,6},{8,9},{9,8},{10,11... | collective-permute-start | bytes 5308424 | tf_op jit(solution)/shard_map/ppermute | solution.py:945
  383.2 67.8 %collective-permute-start.22 = (bf16[1,1024,1152]{2,1,0:T(8,128)(2,1)}, bf16[1,1024,1152]{2,1,0:T(8,128)(2,1)}, u32[]{:S(2)}, u32[]{:S(2)}) collective-permute-start(bf16[1,1024,1152]{2,1,0:T(8,128)(2,1)} %convert_bitcast_fusion), channel_id=1, source_target_pairs={{2,8},{3,9},{6,12},{7,13},{8,2},{9,3},{12,6},{13,7},{18,24},{19,25... | collective-permute-start | bytes 7077896 | tf_op jit(solution)/shard_map/ppermute | solution.py:945
  404.3 37.4 %collective-permute-start.27 = (bf16[576,1152]{1,0:T(8,128)(2,1)}, bf16[576,1152]{1,0:T(8,128)(2,1)}, u32[]{:S(2)}, u32[]{:S(2)}) collective-permute-start(bf16[576,1152]{1,0:T(8,128)(2,1)} %convolution_convert_fusion.2), channel_id=1, source_target_pairs={{0,8},{1,9},{2,10},{3,11},{4,12},{5,13},{6,14},{7,15},{8,0},{9,1},... | collective-permute-start | bytes 3981320 | tf_op jit(solution)/shard_map/ppermute | solution.py:945
  412.1 73.7 %collective-permute-start.28 = (bf16[3,288,1024]{2,1,0:T(8,128)(2,1)}, bf16[3,288,1024]{2,1,0:T(8,128)(2,1)}, u32[]{:S(2)}, u32[]{:S(2)}) collective-permute-start(bf16[3,288,1024]{2,1,0:T(8,128)(2,1)} %get-tuple-element.203), channel_id=1, source_target_pairs={{0,1},{1,0},{2,3},{3,2},{4,5},{5,4},{6,7},{7,6},{8,9},{9,8},{10,11... | collective-permute-start | bytes 5308424 | tf_op jit(solution)/shard_map/ppermute | solution.py:945
  435.7 41.9 %collective-permute-start.30 = (bf16[576,640]{1,0:T(8,128)(2,1)}, bf16[576,640]{1,0:T(8,128)(2,1)}, u32[]{:S(2)}, u32[]{:S(2)}) collective-permute-start(bf16[576,640]{1,0:T(8,128)(2,1)} %convolution_convert_fusion.8), channel_id=1, source_target_pairs={{0,8},{1,9},{2,10},{3,11},{4,12},{5,13},{6,14},{7,15},{8,0},{9,1},... | collective-permute-start | bytes 2211848 | tf_op jit(solution)/shard_map/ppermute | solution.py:945
  444.7 30.0 %collective-permute-start.29 = (bf16[288,1152]{1,0:T(8,128)(2,1)}, bf16[288,1152]{1,0:T(8,128)(2,1)}, u32[]{:S(2)}, u32[]{:S(2)}) collective-permute-start(bf16[288,1152]{1,0:T(8,128)(2,1)} %bitcast.149), channel_id=1, source_target_pairs={{0,1},{1,0},{2,3},{3,2},{4,5},{5,4},{6,7},{7,6},{8,9},{9,8},{10,11... | collective-permute-start | bytes 1990664 | tf_op jit(solution)/shard_map/ppermute | solution.py:945
  450.2 49.2 %collective-permute-start.31 = (bf16[3,144,1024]{2,1,0:T(8,128)(2,1)}, bf16[3,144,1024]{2,1,0:T(8,128)(2,1)S(1)}, u32[]{:S(2)}, u32[]{:S(2)}) collective-permute-start(bf16[3,144,1024]{2,1,0:T(8,128)(2,1)} %get-tuple-element.208), channel_id=1, source_target_pairs={{0,4},{1,5},{2,12},{3,13},{4,0},{5,1},{6,8},{7,9},{8,6},{9,7},{10,... | collective-permute-start | bytes 2654216 | tf_op jit(solution)/shard_map/ppermute | solution.py:945
  451.0 50.0 %collective-permute-start.32 = (bf16[3,144,1024]{2,1,0:T(8,128)(2,1)}, bf16[3,144,1024]{2,1,0:T(8,128)(2,1)}, u32[]{:S(2)}, u32[]{:S(2)}) collective-permute-start(bf16[3,144,1024]{2,1,0:T(8,128)(2,1)} %get-tuple-element.209.refs_4_), channel_id=1, source_target_pairs={{2,8},{3,9},{6,12},{7,13},{8,2},{9,3},{12,6},{13,7},{18,24},{19,25... | collective-permute-start | bytes 2654216 | tf_op jit(solution)/shard_map/ppermute | solution.py:945
  476.9 50.2 %collective-permute-start.36 = (bf16[144,1152]{1,0:T(8,128)(2,1)}, bf16[144,1152]{1,0:T(8,128)(2,1)S(1)}, u32[]{:S(2)}, u32[]{:S(2)}) collective-permute-start(bf16[144,1152]{1,0:T(8,128)(2,1)} %bitcast.138), channel_id=1, source_target_pairs={{2,8},{3,9},{6,12},{7,13},{8,2},{9,3},{12,6},{13,7},{18,24},{19,25... | collective-permute-start | bytes 995336 | tf_op jit(solution)/shard_map/ppermute | solution.py:945
  479.9 45.7 %collective-permute-start.35 = (bf16[144,1152]{1,0:T(8,128)(2,1)}, bf16[144,1152]{1,0:T(8,128)(2,1)}, u32[]{:S(2)}, u32[]{:S(2)}) collective-permute-start(bf16[144,1152]{1,0:T(8,128)(2,1)} %bitcast.152), channel_id=1, source_target_pairs={{0,4},{1,5},{2,12},{3,13},{4,0},{5,1},{6,8},{7,9},{8,6},{9,7},{10,... | collective-permute-start | bytes 995336 | tf_op jit(solution)/shard_map/ppermute | solution.py:945
  485.8 46.8 %collective-permute-start.34 = (bf16[576,640]{1,0:T(8,128)(2,1)}, bf16[576,640]{1,0:T(8,128)(2,1)}, u32[]{:S(2)}, u32[]{:S(2)}) collective-permute-start(bf16[576,640]{1,0:T(8,128)(2,1)} %convolution_convert_fusion.6), channel_id=1, source_target_pairs={{0,8},{1,9},{2,10},{3,11},{4,12},{5,13},{6,14},{7,15},{8,0},{9,1},... | collective-permute-start | bytes 2211848 | tf_op jit(solution)/shard_map/ppermute | solution.py:945
  499.4 31.2 %collective-permute-start.33 = (bf16[288,640]{1,0:T(8,128)(2,1)}, bf16[288,640]{1,0:T(8,128)(2,1)}, u32[]{:S(2)}, u32[]{:S(2)}) collective-permute-start(bf16[288,640]{1,0:T(8,128)(2,1)} %bitcast.40), channel_id=1, source_target_pairs={{0,1},{1,0},{2,3},{3,2},{4,5},{5,4},{6,7},{7,6},{8,9},{9,8},{10,11... | collective-permute-start | bytes 1105928 | tf_op jit(solution)/shard_map/ppermute | solution.py:945
  501.0 49.9 %collective-permute-start.37 = (bf16[3,144,1024]{2,1,0:T(8,128)(2,1)}, bf16[3,144,1024]{2,1,0:T(8,128)(2,1)}, u32[]{:S(2)}, u32[]{:S(2)}) collective-permute-start(bf16[3,144,1024]{2,1,0:T(8,128)(2,1)} %get-tuple-element.217), channel_id=1, source_target_pairs={{0,4},{1,5},{2,12},{3,13},{4,0},{5,1},{6,8},{7,9},{8,6},{9,7},{10,... | collective-permute-start | bytes 2654216 | tf_op jit(solution)/shard_map/ppermute | solution.py:945
  525.6 25.3 %collective-permute-start.38 = (bf16[3,144,1024]{2,1,0:T(8,128)(2,1)S(1)}, bf16[3,144,1024]{2,1,0:T(8,128)(2,1)}, u32[]{:S(2)}, u32[]{:S(2)}) collective-permute-start(bf16[3,144,1024]{2,1,0:T(8,128)(2,1)S(1)} %copy-done.24), channel_id=1, source_target_pairs={{2,8},{3,9},{6,12},{7,13},{8,2},{9,3},{12,6},{13,7},{18,24},{19,25... | collective-permute-start | bytes 2654216 | tf_op jit(solution)/shard_map/ppermute | solution.py:945
  527.2 19.0 %collective-permute-start.39 = (bf16[576,640]{1,0:T(8,128)(2,1)}, bf16[576,640]{1,0:T(8,128)(2,1)}, u32[]{:S(2)}, u32[]{:S(2)}) collective-permute-start(bf16[576,640]{1,0:T(8,128)(2,1)} %convolution_convert_fusion.4), channel_id=1, source_target_pairs={{0,8},{1,9},{2,10},{3,11},{4,12},{5,13},{6,14},{7,15},{8,0},{9,1},... | collective-permute-start | bytes 2211848 | tf_op jit(solution)/shard_map/ppermute | solution.py:945
  534.8 14.2 %collective-permute-start.40 = (bf16[288,640]{1,0:T(8,128)(2,1)}, bf16[288,640]{1,0:T(8,128)(2,1)}, u32[]{:S(2)}, u32[]{:S(2)}) collective-permute-start(bf16[288,640]{1,0:T(8,128)(2,1)} %bitcast.151), channel_id=1, source_target_pairs={{0,1},{1,0},{2,3},{3,2},{4,5},{5,4},{6,7},{7,6},{8,9},{9,8},{10,11... | collective-permute-start | bytes 1105928 | tf_op jit(solution)/shard_map/ppermute | solution.py:945
  548.5 23.0 %collective-permute-start.41 = (bf16[288,640]{1,0:T(8,128)(2,1)}, bf16[288,640]{1,0:T(8,128)(2,1)}, u32[]{:S(2)}, u32[]{:S(2)}) collective-permute-start(bf16[288,640]{1,0:T(8,128)(2,1)} %bitcast.150), channel_id=1, source_target_pairs={{0,1},{1,0},{2,3},{3,2},{4,5},{5,4},{6,7},{7,6},{8,9},{9,8},{10,11... | collective-permute-start | bytes 1105928 | tf_op jit(solution)/shard_map/ppermute | solution.py:945
  565.0 5.8 collective-permute-start.43
  567.3 30.0 %collective-permute-start.53 = (bf16[144,1280]{1,0:T(8,128)(2,1)S(1)}, bf16[144,1280]{1,0:T(8,128)(2,1)S(1)}, u32[]{:S(2)}, u32[]{:S(2)}) collective-permute-start(bf16[144,1280]{1,0:T(8,128)(2,1)S(1)} %pad_maximum_fusion.9.refs_1_), channel_id=1, source_target_pairs={{2,8},{3,9},{6,12},{7,13},{8,2},{9,3},{12,6},{13,7},{18,24},{19,25... | collective-permute-start | bytes 1105928 | tf_op jit(solution)/shard_map/ppermute | solution.py:945
  568.0 29.3 %collective-permute-start.52 = (bf16[144,1280]{1,0:T(8,128)(2,1)}, bf16[144,1280]{1,0:T(8,128)(2,1)S(1)}, u32[]{:S(2)}, u32[]{:S(2)}) collective-permute-start(bf16[144,1280]{1,0:T(8,128)(2,1)} %pad_maximum_fusion.8), channel_id=1, source_target_pairs={{0,4},{1,5},{2,12},{3,13},{4,0},{5,1},{6,8},{7,9},{8,6},{9,7},{10,... | collective-permute-start | bytes 1105928 | tf_op jit(solution)/shard_map/ppermute | solution.py:945
  573.4 23.9 %collective-permute-start.54 = (bf16[144,640]{1,0:T(8,128)(2,1)}, bf16[144,640]{1,0:T(8,128)(2,1)}, u32[]{:S(2)}, u32[]{:S(2)}) collective-permute-start(bf16[144,640]{1,0:T(8,128)(2,1)} %bitcast.153), channel_id=1, source_target_pairs={{0,4},{1,5},{2,12},{3,13},{4,0},{5,1},{6,8},{7,9},{8,6},{9,7},{10,... | collective-permute-start | bytes 552968 | tf_op jit(solution)/shard_map/ppermute | solution.py:945
  574.2 23.1 %collective-permute-start.55 = (bf16[144,640]{1,0:T(8,128)(2,1)}, bf16[144,640]{1,0:T(8,128)(2,1)}, u32[]{:S(2)}, u32[]{:S(2)}) collective-permute-start(bf16[144,640]{1,0:T(8,128)(2,1)} %bitcast.141), channel_id=1, source_target_pairs={{2,8},{3,9},{6,12},{7,13},{8,2},{9,3},{12,6},{13,7},{18,24},{19,25... | collective-permute-start | bytes 552968 | tf_op jit(solution)/shard_map/ppermute | solution.py:945
  582.8 9.3 %collective-permute-start.45 = (f32[8,5632]{1,0:T(8,128)S(1)}, f32[8,5632]{1,0:T(8,128)S(1)}, u32[]{:S(2)}, u32[]{:S(2)}) collective-permute-start(f32[8,5632]{1,0:T(8,128)S(1)} %slice_select_fusion), channel_id=1, source_target_pairs={{0,8},{1,9},{2,10},{3,11},{4,12},{5,13},{6,14},{7,15},{8,0},{9,1},... | collective-permute-start | bytes 540680 | tf_op jit(solution)/shard_map/ppermute | solution.py:945
  592.3 4.6 collective-permute-start.46
  596.9 4.8 collective-permute-start.47
  601.7 9.8 %collective-permute-start.56 = (f32[24,144]{1,0:T(8,128)}, f32[24,144]{1,0:T(8,128)S(1)}, u32[]{:S(2)}, u32[]{:S(2)}) collective-permute-start(f32[24,144]{1,0:T(8,128)} %get-tuple-element.257), channel_id=1, source_target_pairs={{0,8},{1,9},{2,10},{3,11},{4,12},{5,13},{6,14},{7,15},{8,0},{9,1},... | collective-permute-start | bytes 41480 | tf_op jit(solution)/shard_map/ppermute | solution.py:945
  602.6 10.0 %collective-permute-start.48 = (f32[8,2816]{1,0:T(8,128)S(1)}, f32[8,2816]{1,0:T(8,128)S(1)}, u32[]{:S(2)}, u32[]{:S(2)}) collective-permute-start(f32[8,2816]{1,0:T(8,128)S(1)} %add.188), channel_id=1, source_target_pairs={{0,2},{1,3},{2,0},{3,1},{4,6},{5,7},{6,4},{7,5},{8,10},{9,11},{10,... | collective-permute-start | bytes 270344 | tf_op jit(solution)/shard_map/ppermute | solution.py:945
  611.5 3.9 collective-permute-start.57
  612.7 7.1 %collective-permute-start.49 = (f32[8,2816]{1,0:T(8,128)S(1)}, f32[8,2816]{1,0:T(8,128)S(1)}, u32[]{:S(2)}, u32[]{:S(2)}) collective-permute-start(f32[8,2816]{1,0:T(8,128)S(1)} %add.189), channel_id=1, source_target_pairs={{0,4},{1,5},{2,6},{3,7},{4,0},{5,1},{6,2},{7,3},{8,12},{9,13},{10,... | collective-permute-start | bytes 270344 | tf_op jit(solution)/shard_map/ppermute | solution.py:945
  618.6 2.2 collective-permute-start.58
  619.8 4.9 collective-permute-start.50
  621.7 5.1 collective-permute-start.59
  624.7 7.0 %collective-permute-start.51 = (f32[8,5632]{1,0:T(8,128)S(1)}, f32[8,5632]{1,0:T(8,128)S(1)}, u32[]{:S(2)}, u32[]{:S(2)}) collective-permute-start(f32[8,5632]{1,0:T(8,128)S(1)} %pad_maximum_fusion.14), channel_id=1, source_target_pairs={{0,8},{1,9},{2,10},{3,11},{4,12},{5,13},{6,14},{7,15},{8,0},{9,1},... | collective-permute-start | bytes 540680 | tf_op jit(solution)/shard_map/ppermute | solution.py:945
  626.9 4.9 collective-permute-start.60
  628.4 47.2 %collective-permute-start.44 = (bf16[1,1024,1152]{2,1,0:T(8,128)(2,1)S(1)}, bf16[1,1024,1152]{2,1,0:T(8,128)(2,1)}, u32[]{:S(2)}, u32[]{:S(2)}) collective-permute-start(bf16[1,1024,1152]{2,1,0:T(8,128)(2,1)S(1)} %bitcast.135), channel_id=1, source_target_pairs={{2,8},{3,9},{6,12},{7,13},{8,2},{9,3},{12,6},{13,7},{18,24},{19,25... | collective-permute-start | bytes 7077896 | tf_op jit(solution)/shard_map/ppermute | solution.py:945
  650.9 8.6 %collective-permute-start.61 = (f32[8,3584]{1,0:T(8,128)S(1)}, f32[8,3584]{1,0:T(8,128)S(1)}, u32[]{:S(2)}, u32[]{:S(2)}) collective-permute-start(f32[8,3584]{1,0:T(8,128)S(1)} %add.195), channel_id=1, source_target_pairs={{0,2},{1,3},{2,0},{3,1},{4,6},{5,7},{6,4},{7,5},{8,10},{9,11},{10,... | collective-permute-start | bytes 344072 | tf_op jit(solution)/shard_map/ppermute | solution.py:945
  659.5 7.4 %collective-permute-start.62 = (f32[8,3584]{1,0:T(8,128)S(1)}, f32[8,3584]{1,0:T(8,128)S(1)}, u32[]{:S(2)}, u32[]{:S(2)}) collective-permute-start(f32[8,3584]{1,0:T(8,128)S(1)} %add.196), channel_id=1, source_target_pairs={{0,4},{1,5},{2,6},{3,7},{4,0},{5,1},{6,2},{7,3},{8,12},{9,13},{10,... | collective-permute-start | bytes 344072 | tf_op jit(solution)/shard_map/ppermute | solution.py:945
  (62 other events, 680.8 us)
Sparse Core Ops, SparseCore 0:
  150.7 76.1 all-gather.2
  229.8 71.2 all-gather.4

commit v2 on v1

--- a/solution.py
+++ b/solution.py
@@ -339,6 +339,7 @@
     half = away_ref.shape[1]
 
     wide = 3 * tile
+    skip = weight_hbm[0].shape[2] - wide * (reps // 2)
 
     def load(i):
         if len(weight_hbm) == 1:
@@ -350,7 +351,7 @@
         owners, share = ref.shape[:2]
         for a in range(owners):
             pltpu.make_async_copy(
-                ref.at[place_ref[a], :, wide * at : wide * at + wide],
+                ref.at[place_ref[a], :, skip + wide * at : skip + wide * at + wide],
                 weight_ref.at[i, share * a : share * a + share, :],
                 weight_sem.at[i],
             ).start()
@@ -420,7 +421,9 @@
 
 def mlp_part(reps, slots, places, mid, d_out, mid_turned, d_turned, weights, result, back):
     count, model = mid.shape
-    tile = weights[0].shape[2] // (3 if len(weights) == 1 else 3 * (reps // 2))
+    tile = (weights[0].shape[2] - (512 if len(weights) == 2 else 0)) // 3
+    if len(weights) == 2:
+        tile //= reps // 2
     units = tile * reps
     half = model // 2
     first = back is None
@@ -510,6 +513,25 @@
     return out.reshape(owners * rows, high - low)
 
 
+def left_rows(factor, rows):
+    lane = lax.broadcasted_iota(jnp.int32, (rows.shape[0], 128), 1)
+    columns = jnp.zeros((rows.shape[0], 128), jnp.float32)
+    for r in range(8):
+        column = jnp.sum(rows * factor[r : r + 1, :], axis=1, keepdims=True)
+        columns = jnp.where(lane == r, column, columns)
+    return columns.T[:8, :]
+
+
+def weighted_rows(left, rows):
+    turned = left.T
+    sublane = lax.broadcasted_iota(jnp.int32, (8, 1), 0)
+    out = jnp.zeros((8, rows.shape[1]), jnp.float32)
+    for r in range(8):
+        row = jnp.sum(rows * turned[:, r : r + 1], axis=0, keepdims=True)
+        out = jnp.where(sublane == r, row, out)
+    return out
+
+
 def exact_dot(left, right, contract):
     return lax.dot_general(
         left, right, (contract, ((), ())), precision=highest, preferred_element_type=jnp.float32
@@ -538,46 +560,27 @@
             at += width
         rows = mixed[m][...].reshape(mixed[m].shape[-2:])
         factor = factors[m][...].reshape(factors[m].shape[-2:])
-        left = exact_dot(factor, rows, ((1,), (1,)))
-        left_ref[8 * m : 8 * m + 8, :] = left
+        left_ref[8 * m : 8 * m + 8, :] = left_rows(factor, rows)
 
 
 def mix_wide(flag, parts, error, factor):
     count, rows, third = parts[0][0].shape
-    number = len(parts)
-    columns = third * number
+    columns = third * len(parts)
     arrays = [a for part in parts for a in part]
-
-    def kernel(flag_ref, *refs):
-        error_ref, factor_ref, mixed_ref, left_ref = refs[3 * number :]
-        step = pl.program_id(1)
-
-        @pl.when(step == 0)
-        def _():
-            left_ref[...] = jnp.zeros_like(left_ref)
-
-        for p in range(number):
-
-            @pl.when(step == p)
-            def _(p=p):
-                away, home, moved = (refs[3 * p + k][0].astype(jnp.float32) for k in range(3))
-                mixed = away + jnp.where(flag_ref[0] == 1, home, moved) + error_ref[0, 0]
-                mixed_ref[0] = mixed
-                left_ref[...] += exact_dot(factor_ref[0], mixed, ((1,), (1,)))
-
+    layout = [[(i, 0, third) for i in range(len(parts))]]
     return pl.pallas_call(
-        kernel,
+        functools.partial(mix_kernel, layout, len(parts)),
         grid_spec=pltpu.PrefetchScalarGridSpec(
             num_scalar_prefetch=1,
-            grid=(count, number),
-            in_specs=[pl.BlockSpec((1, rows, third), lambda i, k, flag: (i, 0, 0))] * len(arrays)
+            grid=(count,),
+            in_specs=[pl.BlockSpec((1, rows, third), lambda i, flag: (i, 0, 0))] * len(arrays)
             + [
-                pl.BlockSpec((1, 1, rows, third), lambda i, k, flag: (0, i, 0, k)),
-                pl.BlockSpec((1, 8, third), lambda i, k, flag: (i, 0, k)),
+                pl.BlockSpec((1, 1, rows, columns), lambda i, flag: (0, i, 0, 0)),
+                pl.BlockSpec((1, 8, columns), lambda i, flag: (i, 0, 0)),
             ],
             out_specs=[
-                pl.BlockSpec((1, rows, third), lambda i, k, flag: (i, 0, k)),
-                pl.BlockSpec((8, rows), lambda i, k, flag: (i, 0)),
+                pl.BlockSpec((1, rows, columns), lambda i, flag: (i, 0, 0)),
+                pl.BlockSpec((8, rows), lambda i, flag: (i, 0)),
             ],
         ),
         out_shape=[
@@ -625,7 +628,7 @@
             for k in range(ref.shape[0] if len(ref.shape) == 3 else 1):
                 rows = ref[k] if len(ref.shape) == 3 else ref[...]
                 own = left_ref[8 * m : 8 * m + 8, :]
-                out_ref[:, at : at + rows.shape[1]] = exact_dot(own, rows, ((1,), (0,)))
+                out_ref[:, at : at + rows.shape[1]] = weighted_rows(own, rows)
                 at += rows.shape[1]
                 m += 1
         for k in range(m):
@@ -663,12 +666,22 @@
     return rights
 
 
-def finish_matrix(reps, rate, row, gram, left, mixed, moment, master):
+def finish_matrix(reps, rate, row, gram, left, mixed, moment, master, outs):
+    new_ref, moment_new_ref, error_ref, factor_ref = outs
     factor, basis = eliminate(gram[:, :8] * (1.0 / reps), [row, left])
     factor = factor * (1.0 / reps)
-    approx = exact_dot(basis, factor, ((0,), (0,)))
-    moment_new = decay_rate * moment + approx
-    return factor, moment_new, master - rate * moment_new, mixed - approx
+    factor_ref[...] = factor
+    turned = basis.T
+    columns = factor.shape[1]
+    for first in range(0, columns, 256):
+        span = slice(first, min(first + 256, columns))
+        approx = turned[:, 0:1] * factor[0:1, span]
+        for r in range(1, 8):
+            approx += turned[:, r : r + 1] * factor[r : r + 1, span]
+        moment_new = decay_rate * moment[:, span] + approx
+        moment_new_ref[:, span] = moment_new
+        new_ref[:, span] = master[:, span] - rate * moment_new
+        error_ref[:, span] = mixed[:, span] - approx
 
 
 def finish_wide(reps, packed, gram_at, left, mixed, moment, master):
@@ -676,27 +689,27 @@
 
     def kernel(row_ref, gram_ref, left_ref, mixed_ref, moment_ref, master_ref, *outs):
         new_ref, moment_new_ref, error_ref, factor_ref = outs
-        factor_ref[0], moment_new_ref[0], new_ref[0], error_ref[0, 0] = finish_matrix(
+        finish_matrix(
             reps,
             rate_wide,
             row_ref[...],
             gram_ref[...],
             left_ref[...],
-            mixed_ref[0],
-            moment_ref[0],
-            master_ref[0],
+            mixed_ref.at[0],
+            moment_ref.at[0],
+            master_ref.at[0],
+            (new_ref.at[0], moment_new_ref.at[0], error_ref.at[0, 0], factor_ref.at[0]),
         )
 
-    third = columns // 3
-    whole = pl.BlockSpec((1, rows, third), lambda i, k: (i, 0, k))
+    whole = pl.BlockSpec((1, rows, columns), lambda i: (i, 0, 0))
     shape = jax.ShapeDtypeStruct((count, rows, columns), jnp.float32)
     return pl.pallas_call(
         kernel,
-        grid=(count, 3),
+        grid=(count,),
         in_specs=[
-            pl.BlockSpec((8, third), lambda i, k: (0, 3 * i + k)),
-            pl.BlockSpec((8, 128), lambda i, k: (0, gram_at // 128 + i)),
-            pl.BlockSpec((8, rows), lambda i, k: (i, 0)),
+            pl.BlockSpec((8, columns), lambda i: (0, i)),
+            pl.BlockSpec((8, 128), lambda i: (0, gram_at // 128 + i)),
+            pl.BlockSpec((8, rows), lambda i: (i, 0)),
             whole,
             whole,
             whole,
@@ -704,8 +717,8 @@
         out_specs=[
             whole,
             whole,
-            pl.BlockSpec((1, 1, rows, third), lambda i, k: (0, i, 0, k)),
-            pl.BlockSpec((1, 8, third), lambda i, k: (i, 0, k)),
+            pl.BlockSpec((1, 1, rows, columns), lambda i: (0, i, 0, 0)),
+            pl.BlockSpec((1, 8, columns), lambda i: (i, 0, 0)),
         ],
         out_shape=[
             shape,
@@ -738,21 +751,17 @@
             new_ref, moment_new_ref, error_ref, factor_ref = outs[4 * g : 4 * g + 4]
             for k in range(count):
                 pack, row_at, gram_at, left_at = where[first + k]
-                rows = mixed_refs[first + k][...]
-                (
-                    factor_ref[k],
-                    moment_new_ref[k],
-                    new_ref[k],
-                    error_ref[0, k],
-                ) = finish_matrix(
+                rows = mixed_refs[first + k]
+                finish_matrix(
                     reps,
                     rate,
                     pack_refs[pack][:, row_at : row_at + rows.shape[1]],
                     pack_refs[pack][:, gram_at : gram_at + 128],
                     left_refs[pack][left_at : left_at + 8, :],
                     rows,
-                    state_refs[2 * g][k],
-                    state_refs[2 * g + 1][k],
+                    state_refs[2 * g].at[k],
+                    state_refs[2 * g + 1].at[k],
+                    (new_ref.at[k], moment_new_ref.at[k], error_ref.at[0, k], factor_ref.at[k]),
                 )
 
     shapes = []
@@ -825,13 +834,12 @@
         away_ref[0] = total[:half].astype(jnp.bfloat16)
         kept_ref[0] = total[half:].astype(jnp.bfloat16)
 
-    block = columns // 2 if columns % 256 == 0 else columns
-    whole = pl.BlockSpec((1, rows, block), lambda i, j: (i, 0, j))
-    part = pl.BlockSpec((1, half, block), lambda i, j: (i, 0, j))
+    whole = pl.BlockSpec((1, rows, columns), lambda i: (i, 0, 0))
+    part = pl.BlockSpec((1, half, columns), lambda i: (i, 0, 0))
     out = jax.ShapeDtypeStruct((lead, half, columns), jnp.bfloat16)
     away, kept = pl.pallas_call(
         kernel,
-        grid=(lead, columns // block),
+        grid=(lead,),
         in_specs=[whole, whole],
         out_specs=[part, part],
         out_shape=[out, out],
@@ -856,14 +864,14 @@
             @pl.when(core_ref[0] == own)
             def _(own=own):
                 spans = (
-                    (halves[0 if own == 1 else 1], 384, 0, 128),
+                    (halves[0 if own == 1 else 1], 896, 0, 128),
                     (halves[2 if own == 0 else 3], 0, 128, 512),
                     (halves[2 if own == 1 else 3], 0, 640, 512),
                 )
                 for ref, first, at, width in spans:
                     for a in range(owners):
                         pltpu.make_async_copy(
-                            ref.at[place_ref[a], :, first : first + width],
+                            ref.at[place_ref[a], :share, first : first + width],
                             w_ref.at[share * a : share * a + share, at : at + width],
                             sem.at[0],
                         ).start()
@@ -1121,19 +1129,21 @@
     rows = low_attn.shape[0]
     tile = units // reps
     chained = 1 if rows % 16 == 0 else 0
-    blocks = [low_attn[:, 1024 * i : 1024 * i + 1024] for i in range(3)]
     gain_row = norm_gains.astype(jnp.bfloat16).reshape(1, 2 * rows)
-    gain_row = jnp.pad(gain_row, ((0, 15), (0, 512 - 2 * rows)))
-    blocks[0] = jnp.concatenate([blocks[0], jnp.concatenate([gain_row] * 2, axis=1)], axis=0)
-    blocks = [lax.dynamic_slice_in_dim(b, core * 512, 512, axis=1) for b in blocks]
+    gain_row = jnp.pad(gain_row, ((0, 15), (0, 1024 - 2 * rows)))
+    first = lax.dynamic_slice_in_dim(low_attn, core * 1024, 1024, axis=1)
+    first = jnp.concatenate([first, gain_row], axis=0)
+    second = lax.dynamic_slice_in_dim(low_attn, 2048 + core * 512, 512, axis=1)
     picks = [core * (reps // 2) + i for i in range(reps // 2)] if chained else []
     groups = [tuple(range(len(picks)))] if chained else []
     for k in range(chained, 3):
         groups.append((len(picks),))
         picks.append(reps * k + rep)
     cuts = list(pack_wide(wide_master, jnp.stack(picks).astype(jnp.int32), groups, tile))
-    mine, gathering = gather_pieces(grid, blocks + cuts[:chained])
-    other = [grid.move(held, grid.flip_rep(0)) for held in mine[:2]]
+    if chained:
+        second = jnp.concatenate([second, cuts[0]], axis=1)
+    mine, gathering = gather_pieces(grid, [first, second])
+    other = [grid.move(mine[0], grid.flip_rep(0))]
     places = jnp.array(grid.places(), jnp.int32)[jnp.arange(owners) ^ shard]
     cores = core[None]
     gain_w = mine[0][:, rows, : 2 * rows].reshape(owners, 2, rows)
@@ -1145,7 +1155,7 @@
     moved_out = grid.move(after(cotangent, moved_tokens), grid.swapped)
     model = gain_w.shape[1]
     columns = 640 * PAIRS
-    qkv_w = assemble(rows, mine[:2], other[:2], places, cores, 0, columns)
+    qkv_w = assemble(rows, mine[:1], other[:1], places, cores, 0, columns)
 
     count = tokens.shape[0]
     hidden_in = tokens.astype(jnp.float32)
@@ -1156,27 +1166,22 @@
     place = position[:, None]
     order = jnp.array(grid.masks(), jnp.int32) ^ logical_shard
 
-    tokens = after(tokens, mine[2])
     qkv, turned_in = project_qkv(order, tokens, gain_attn[None], qkv_w, cos, sin)
-    if chained:
-        held, got = after((mine[3], gathering[-1]), qkv)
-        mine[3] = jnp.concatenate([held, got], axis=0)
-        qkv = after(qkv, mine[3])
-    else:
-        mine[2] = jnp.concatenate([mine[2], gathering[-1]], axis=0)
+    held, got = after((mine[1], gathering[-1]), qkv)
+    mine[1] = jnp.concatenate([held, got], axis=0)
+    qkv = after(qkv, mine[1])
     wide_parts = [None] * chained
     for k in range(chained, 3):
-        part = after(cuts[k], mine[2:])
+        part = after(cuts[k], mine[1])
         part = lax.all_gather(part, ("rep", "shard"), axis=0, tiled=True)
         wide_parts.append((natural, whole, [part.reshape(reps, owners * rows, 3 * tile)]))
-    mine[2] = after(mine[2], qkv)
-    other += [grid.move(held, grid.flip_rep(0)) for held in mine[2:]]
+    other.append(grid.move(mine[1], grid.flip_rep(0)))
     attended, logs = attend_forward(qkv, place)
-    other[2:] = after(other[2:], attended)
+    other[1] = after(other[1], attended)
     d_out = jnp.where(grid.stays(), cotangent, after(moved_out, attended))[0]
     if chained:
         slots = (natural + core * (reps // 2)) % reps
-        wide_parts[0] = (slots, places, mine[3:] + other[3:])
+        wide_parts[0] = (slots, places, [mine[1], other[1]])
         residual, normed_mid, turned_mid, out_w = project_out(
             places,
             cores,
@@ -1184,10 +1189,10 @@
             attended,
             tokens,
             gain_mlp[None],
-            [mine[1], other[1], mine[2], other[2]],
+            [mine[0], other[0], mine[1], other[1]],
         )
     else:
-        out_w = assemble(rows, mine[1:3], other[1:3], places, cores, columns - 1024, 2048)
+        out_w = assemble(rows, mine, other, places, cores, columns, 3072)
         residual = hidden_in + jnp.einsum(
             "tn,dn->td", attended, out_w, preferred_element_type=jnp.float32
         )

time: 695 us -> 691 us (level)
  waiting for transfers between devices: 93.5 us -> 113 us
  Pallas kernels: 362 us -> 353 us
    ppermute x63 -> x55, waiting for transfers between devices: 92.8 us -> 112 us  [move(): return lax.ppermute(value, ('rep', 'shard'), pairs)]
    pallas_call x16, Pallas kernels: 82.3 us -> 71.6 us  [the longest x14 47 us: split_sum(): pl.pallas_call(kernel, grid=(lead,), in_specs=[whole, whole], out_specs=[...]
    ppermute x63 -> x55, starting transfers between devices: 83.4 us -> 76.8 us  [move(): return lax.ppermute(value, ('rep', 'shard'), pairs)]
    unnamed x131 -> x123, local copies, waits for them, and re-layouts: 14.1 us -> 11.3 us
  transfers between devices with their start and end apart: 65 -> 57, of which waited for: 20 -> 15; matrix products, arithmetic and copies ran while one was open for 16% -> 15% of each run, Pallas kernels for 53% -> 52%
where the time goes in v2:
time: 691 us; the launch traced here: 682 us
  Pallas kernels  353 us (51%)
  waiting for transfers between devices  113 us (16%)
  starting transfers between devices  76.9 us (11%)
  other arithmetic  52.2 us (8%)
  matrix products  46.3 us (7%)
  local copies, waits for them, and re-layouts  25 us (4%)
  between operations  15.2 us (2%)
    pallas_call x3, Pallas kernels, mlp_part(): pl.pallas_call(functools.partial(mlp_kernel, reps, first), grid_spec=pltp...  125 us
    ppermute x55, waiting for transfers between devices, move(): return lax.ppermute(value, ('rep', 'shard'), pairs)  112 us
    ppermute x55, starting transfers between devices, move(): return lax.ppermute(value, ('rep', 'shard'), pairs)  76.8 us
    pallas_call x3, Pallas kernels, attend_backward(): pl.pallas_call(backward_kernel, grid=(rows // block,), in_specs=[pl.Block...  54.5 us
    pallas_call x14, Pallas kernels, split_sum(): pl.pallas_call(kernel, grid=(lead,), in_specs=[whole, whole], out_specs=[...  47 us
    pallas_call x1, Pallas kernels, attend_forward(): pl.pallas_call(forward_kernel, grid=(pairs, rows // block), in_specs=[pl....  33.3 us
    pallas_call x1, Pallas kernels, finish_wide(): pl.pallas_call(kernel, grid=(count,), in_specs=[pl.BlockSpec((8, columns)...  16 us
    dot_general x3, matrix products, back(): jnp.einsum('tn,dn->td', d_stacks[j], qkv_w[:, 640 * j:640 * j + 640], pre...  15.4 us
  transfers between devices with their start and end apart: 57, of which 15 were waited for; matrix products, arithmetic and copies ran while one was open for 15% of the time, Pallas kernels for 52%

profile of v2, /device:TPU:0, one launch (start us, length us, event | category | flops | bytes accessed | tf_op | source)
XLA Modules:
  0.0 681.7 jit_solution(15083560591368237814)
XLA Ops:
  10.1 4.1 collective-permute-start
  14.8 3.0 shard_map.306
  17.8 11.1 %collective-permute-done = bf16[1,160,1024]{2,1,0:T(8,128)(2,1)S(1)} collective-permute-done((bf16[1,160,1024]{2,1,0:T(8,128)(2,1)S(1)}, bf16[1,160,1024]{2,1,0:T(8,128)(2,1)S(1)}, u32[]{:S(2)}, u32[]{:S(2)}) %collective-permute-start) | collective-permute-done | bytes 327712 | tf_op jit(solution)/shard_map/ppermute | solution.py:953
  30.9 3.4 collective-permute-start.1
  34.3 23.3 %collective-permute-done.2 = bf16[2,160,1024]{2,1,0:T(8,128)(2,1)S(1)} collective-permute-done((bf16[2,160,1024]{2,1,0:T(8,128)(2,1)S(1)}, bf16[2,160,1024]{2,1,0:T(8,128)(2,1)S(1)}, u32[]{:S(2)}, u32[]{:S(2)}) %collective-permute-start.2) | collective-permute-done | bytes 655392 | tf_op jit(solution)/shard_map/ppermute | solution.py:953
  62.4 24.2 %collective-permute-done.3 = bf16[2,144,2048]{2,1,0:T(8,128)(2,1)S(1)} collective-permute-done((bf16[2,144,2048]{2,1,0:T(8,128)(2,1)S(1)}, bf16[2,144,2048]{2,1,0:T(8,128)(2,1)S(1)}, u32[]{:S(2)}, u32[]{:S(2)}) %collective-permute-start.3) | collective-permute-done | bytes 1179680 | tf_op jit(solution)/shard_map/ppermute | solution.py:953
  101.4 4.5 fusion.3
  105.9 7.5 %shard_map.307 = bf16[8,144,1920]{2,1,0:T(8,128)(2,1)} custom-call(s32[8]{0:T(128)} %copy-done.47, s32[1]{0:T(128)} %bitcast.1.core_ref, bf16[8,160,1024]{2,1,0:T(8,128)(2,1)} %copy-done.5, bf16[8,160,1024]{2,1,0:T(8,128)(2,1)} %collective-permute-done.6.refs_1_), custom_call_target="tpu_custom_call" | custom-call | bytes 9437184 | tf_op jit(solution)/shard_map/pallas_call | solution.py:499
  113.3 12.0 %shard_map.308 = (bf16[1024,1920]{1,0:T(8,128)(2,1)}, bf16[1152,1024]{1,0:T(8,128)(2,1)}) custom-call(s32[8]{0:T(128)} %broadcast_xor_fusion.order_ref, bf16[1024,1152]{1,0:T(8,128)(2,1)} %get-tuple-element.265.x_ref, f32[1,1152]{1,0:T(1,128)} %slice.121.gain_ref, bf16[1152,1920]{1,0:T(8,128)(2,1)} %bitcast.136, f32[1024,128]{1,0:T(8,128)} %get-tuple-element.283.cos_ref, ...), custom_call_target="tpu_custom_call" | custom-call | flops 4529848320 | bytes 13074432 | tf_op jit(solution)/shard_map/pallas_call | solution.py:82
  125.3 22.6 %collective-permute-done.8 = bf16[4,144,2048]{2,1,0:T(8,128)(2,1)} collective-permute-done((bf16[4,144,2048]{2,1,0:T(8,128)(2,1)}, bf16[4,144,2048]{2,1,0:T(8,128)(2,1)}, u32[]{:S(2)}, u32[]{:S(2)}) %collective-permute-start.8) | collective-permute-done | bytes 2359328 | tf_op jit(solution)/shard_map/ppermute | solution.py:953
  148.0 3.4 constant_dynamic-update-slice_fusion.1
  151.3 3.5 constant_dynamic-update-slice_fusion.refs_2_.refs_3_
  155.7 2.5 collective-permute-start.10
  161.9 33.3 %shard_map.309 = (bf16[1024,1152]{1,0:T(8,128)(2,1)}, f32[3,1024,128]{2,1,0:T(8,128)}) custom-call(bf16[1024,1920]{1,0:T(8,128)(2,1)} %get-tuple-element.144.qkv_ref, s32[1024,1]{1,0:T(8,128)} %copy.40.pos_ref), custom_call_target="tpu_custom_call" | custom-call | flops 8053063680 | bytes 15728640 | tf_op jit(solution)/shard_map/pallas_call | solution.py:179
  196.9 5.2 shard_map.311.refs_1_
  202.1 12.2 %shard_map.310 = (f32[1024,1152]{1,0:T(8,128)}, bf16[1024,1152]{1,0:T(8,128)(2,1)}, bf16[1152,1024]{1,0:T(8,128)(2,1)}, bf16[1152,1152]{1,0:T(8,128)(2,1)}) custom-call(s32[8]{0:T(128)} %copy-done.47, s32[1]{0:T(128)} %bitcast.1.core_ref, s32[8]{0:T(128)} %broadcast_xor_fusion.order_ref, bf16[1024,1152]{1,0:T(8,128)(2,1)} %get-tuple-element.145.att_ref, ...), custom_call_target="tpu_custom_call" | custom-call | flops 2717908992 | bytes 19464192 | tf_op jit(solution)/shard_map/pallas_call | solution.py:898
  214.4 41.9 %shard_map.312 = (bf16[3,576,1024]{2,1,0:T(8,128)(2,1)}, bf16[3,576,1024]{2,1,0:T(8,128)(2,1)}, f32[1024,1152]{1,0:T(8,128)}, f32[1024,1152]{1,0:T(8,128)}) custom-call(s32[4]{0:T(128)} %and_select_fusion.slot_ref, s32[8]{0:T(128)} %copy-done.47, bf16[1024,1152]{1,0:T(8,128)(2,1)} %get-tuple-element.147.mid_ref, ...), custom_call_target="tpu_custom_call" | custom-call | flops 21743271936 | bytes 42467328 | tf_op jit(solution)/shard_map/pallas_call | solution.py:436
  256.2 6.9 %collective-permute-start.11 = (bf16[3,576,1024]{2,1,0:T(8,128)(2,1)}, bf16[3,576,1024]{2,1,0:T(8,128)(2,1)S(1)}, u32[]{:S(2)}, u32[]{:S(2)}) collective-permute-start(bf16[3,576,1024]{2,1,0:T(8,128)(2,1)} %get-tuple-element.159), channel_id=1, source_target_pairs={{0,8},{1,9},{2,10},{3,11},{4,12},{5,13},{6,14},{7,15},{8,0},{9,1},... | collective-permute-start | bytes 10616840 | tf_op jit(solution)/shard_map/ppermute | solution.py:953
  263.6 41.3 %shard_map.313 = (bf16[3,576,1024]{2,1,0:T(8,128)(2,1)}, bf16[3,576,1024]{2,1,0:T(8,128)(2,1)}, f32[1024,1152]{1,0:T(8,128)}, f32[1024,1152]{1,0:T(8,128)}) custom-call(s32[4]{0:T(128)} %iota.19.slot_ref, s32[1]{0:T(128)} %constant.120.clone.1.place_ref, bf16[1024,1152]{1,0:T(8,128)(2,1)} %get-tuple-element.147.mid_ref, ...), custom_call_target="tpu_custom_call" | custom-call | flops 21743271936 | bytes 42467328 | tf_op jit(solution)/shard_map/pallas_call | solution.py:436
  309.6 2.7 multiply_reduce_fusion.2
  314.1 5.7 shard_map.314
  321.8 41.5 %shard_map.315 = (bf16[3,576,1024]{2,1,0:T(8,128)(2,1)}, bf16[3,576,1024]{2,1,0:T(8,128)(2,1)}, f32[1024,1152]{1,0:T(8,128)}, f32[1024,1152]{1,0:T(8,128)}) custom-call(s32[4]{0:T(128)} %iota.16.slot_ref, s32[1]{0:T(128)} %constant.120.clone.1.place_ref, bf16[1024,1152]{1,0:T(8,128)(2,1)} %get-tuple-element.147.mid_ref, ...), custom_call_target="tpu_custom_call" | custom-call | flops 21743271936 | bytes 42467328 | tf_op jit(solution)/shard_map/pallas_call | solution.py:436
  364.8 4.3 shard_map.316
  369.1 2.3 collective-permute-start.16
  373.0 5.7 shard_map.317
  379.2 4.1 convert_bitcast_fusion
  389.8 4.7 convolution_convert_fusion.d_ref
  394.5 5.2 shard_map.318
  399.7 4.8 convolution_convert_fusion.2
  406.2 5.7 shard_map.319
  413.2 18.1 %shard_map.320 = bf16[1024,640]{1,0:T(8,128)(2,1)} custom-call(bf16[1024,1920]{1,0:T(8,128)(2,1)} %get-tuple-element.144.qkv_ref, bf16[1024,1152]{1,0:T(8,128)(2,1)} %convolution_convert_fusion.d_ref, f32[3,1024,128]{2,1,0:T(8,128)} %get-tuple-element.188.log_ref, s32[1024,1]{1,0:T(8,128)} %copy.40.pos_ref, f32[1024,128]{1,0:T(8,128)} %get-tuple-element.283.cos_ref, ...), custom_call_target="tpu_custom_call" | custom-call | flops 6710886400 | bytes 5242880 | tf_op jit(solution)/shard_map/pallas_call | solution.py:269
  431.2 3.8 convolution_convert_fusion.8
  438.2 2.8 fusion.7.home_ref
  441.0 3.0 shard_map.322
  444.8 3.9 shard_map.321
  451.0 4.1 broadcast_select_fusion.1
  455.1 18.3 %shard_map.323 = bf16[1024,640]{1,0:T(8,128)(2,1)} custom-call(bf16[1024,1920]{1,0:T(8,128)(2,1)} %get-tuple-element.144.qkv_ref, bf16[1024,1152]{1,0:T(8,128)(2,1)} %convolution_convert_fusion.d_ref, f32[3,1024,128]{2,1,0:T(8,128)} %get-tuple-element.188.log_ref, s32[1024,1]{1,0:T(8,128)} %copy.40.pos_ref, f32[1024,128]{1,0:T(8,128)} %get-tuple-element.283.cos_ref, ...), custom_call_target="tpu_custom_call" | custom-call | flops 6710886400 | bytes 5242880 | tf_op jit(solution)/shard_map/pallas_call | solution.py:269
  476.3 2.3 shard_map.326
  478.6 2.3 collective-permute-start.27
  480.8 3.7 convolution_convert_fusion.6
  484.5 4.8 collective-permute-start.26
  489.3 3.9 shard_map.324
  493.3 3.6 fusion.13.home_ref
  499.2 18.2 %shard_map.327 = bf16[1024,640]{1,0:T(8,128)(2,1)} custom-call(bf16[1024,1920]{1,0:T(8,128)(2,1)} %get-tuple-element.144.qkv_ref, bf16[1024,1152]{1,0:T(8,128)(2,1)} %convolution_convert_fusion.d_ref, f32[3,1024,128]{2,1,0:T(8,128)} %get-tuple-element.188.log_ref, s32[1024,1]{1,0:T(8,128)} %copy.40.pos_ref, f32[1024,128]{1,0:T(8,128)} %get-tuple-element.283.cos_ref, ...), custom_call_target="tpu_custom_call" | custom-call | flops 6710886400 | bytes 5242880 | tf_op jit(solution)/shard_map/pallas_call | solution.py:269
  517.5 3.8 fusion.14.home_ref
  526.2 2.6 shard_map.334
  530.7 2.3 shard_map.329
  534.5 4.0 fusion.9
  538.5 5.8 convolution_add_fusion.1
  544.3 2.3 shard_map.330
  549.2 8.7 %shard_map.332 = (f32[3,144,3072]{2,1,0:T(8,128)}, f32[24,144]{1,0:T(8,128)}) custom-call(s32[1]{0:T(128)} %bitcast.52.flag_ref, bf16[3,144,1024]{2,1,0:T(8,128)(2,1)} %copy-done.24, bf16[3,144,1024]{2,1,0:T(8,128)(2,1)} %get-tuple-element.173.refs_1_, bf16[3,144,1024]{2,1,0:T(8,128)(2,1)} %collective-permute-done.17.refs_2_, ...), custom_call_target="tpu_custom_call" | custom-call | flops 127401984 | bytes 18579456 | tf_op jit(solution)/shard_map/pallas_call | solution.py:571
  570.1 8.1 %shard_map.335 = f32[8,11264]{1,0:T(8,128)} custom-call(f32[32,144]{1,0:T(8,128)} %add.185.refs_0_.left_ref.refs_3_, f32[3,144,3072]{2,1,0:T(8,128)} %get-tuple-element.235.refs_1_.mixed_ref, f32[144,1152]{1,0:T(8,128)} %get-tuple-element.236.refs_2_.refs_5_), custom_call_target="tpu_custom_call" | custom-call | flops 143327232 | bytes 5971968 | tf_op jit(solution)/shard_map/pallas_call | solution.py:642
  579.3 4.5 collective-permute-start.37
  583.8 5.5 convolution_add_fusion
  591.5 2.5 collective-permute-done.38
  595.5 3.4 shard_map.337
  602.0 6.8 %fusion.2 = bf16[1024,1152]{1,0:T(8,128)(2,1)} fusion(bf16[1024,1152]{1,0:T(8,128)(2,1)} %get-tuple-element.265.x_ref, f32[1024,1152]{1,0:T(8,128)} %copy-done.1, f32[1024]{0:T(1024)S(1)} %multiply_multiply_fusion, f32[1024]{0:T(1024)S(1)} %copy-done.40, f32[1152]{0:T(1024)S(1)} %copy-done.38, bf16[1024,1152]{1,0:T(8,128)(2,1)S(1)} %copy-done.3, ...), kind=kLoop, calls=%fused_computation.10 | loop fusion | flops 17694720 | bytes 21259264 | tf_op jit(solution)/shard_map/convert_element_type | solution.py:1296
  610.2 2.6 collective-permute-done.49
  613.4 2.9 shard_map.338
  621.5 2.5 collective-permute-done.51
  629.7 16.0 %shard_map.336 = (f32[3,144,3072]{2,1,0:T(8,128)}, f32[3,144,3072]{2,1,0:T(8,128)}, f32[1,3,144,3072]{3,2,1,0:T(8,128)}, f32[3,8,3072]{2,1,0:T(8,128)}) custom-call(f32[8,11264]{1,0:T(8,128)} %pad_maximum_fusion.9.row_ref.gram_ref.refs_1_, f32[8,11264]{1,0:T(8,128)} %pad_maximum_fusion.9.row_ref.gram_ref.refs_1_, f32[32,144]{1,0:T(8,128)} %add.185.refs_0_.left_ref.refs_3_, ...), custom_call_target="tpu_custom_call" | custom-call | flops 127401984 | bytes 31850496 | tf_op jit(solution)/shard_map/pallas_call | solution.py:706
  645.7 11.1 %collective-permute-done.53 = f32[8,3584]{1,0:T(8,128)S(1)} collective-permute-done((f32[8,3584]{1,0:T(8,128)S(1)}, f32[8,3584]{1,0:T(8,128)S(1)}, u32[]{:S(2)}, u32[]{:S(2)}) %collective-permute-start.53) | collective-permute-done | bytes 114720 | tf_op jit(solution)/shard_map/ppermute | solution.py:953
  658.4 5.9 collective-permute-done.54
  665.0 7.3 %shard_map.339 = (f32[2,144,1152]{2,1,0:T(8,128)}, f32[2,144,1152]{2,1,0:T(8,128)}, f32[1,2,144,1152]{3,2,1,0:T(8,128)}, f32[2,8,1152]{2,1,0:T(8,128)}, f32[2,14...) custom-call(f32[8,3584]{1,0:T(8,128)} %copy-done.27, ...), custom_call_target="tpu_custom_call" | custom-call | flops 42467328 | bytes 10616832 | tf_op jit(solution)/shard_map/pallas_call | solution.py:777
  (308 shorter events, 112.7 us)
Async XLA Ops:
  7.2 255.9 %all-gather.3.cloned.1.call-start = ((), (), s32[]{:S(2)}) async-start(), calls=%async_computation | async-start | bytes 7299072 | tf_op jit(solution)/shard_map/all_gather | solution.py:1176
  10.1 18.8 %collective-permute-start = (bf16[1,160,1024]{2,1,0:T(8,128)(2,1)S(1)}, bf16[1,160,1024]{2,1,0:T(8,128)(2,1)S(1)}, u32[]{:S(2)}, u32[]{:S(2)}) collective-permute-start(bf16[1,160,1024]{2,1,0:T(8,128)(2,1)S(1)} %fusion.26), channel_id=1, source_target_pairs={{0,4},{1,5},{2,6},{3,7},{4,0},{5,1},{6,2},{7,3},{8,12},{9,13},{10,... | collective-permute-start | bytes 983048 | tf_op jit(solution)/shard_map/ppermute | solution.py:953
  29.0 28.6 %collective-permute-start.2 = (bf16[2,160,1024]{2,1,0:T(8,128)(2,1)S(1)}, bf16[2,160,1024]{2,1,0:T(8,128)(2,1)S(1)}, u32[]{:S(2)}, u32[]{:S(2)}) collective-permute-start(bf16[2,160,1024]{2,1,0:T(8,128)(2,1)S(1)} %pad_maximum_fusion.4), channel_id=1, source_target_pairs={{0,2},{1,3},{2,0},{3,1},{4,6},{5,7},{6,4},{7,5},{8,10},{9,11},{10,... | collective-permute-start | bytes 1966088 | tf_op jit(solution)/shard_map/ppermute | solution.py:953
  30.9 30.1 %copy-start.48 = (s32[1,1024]{1,0:T(1,128)S(1)}, s32[1,1024]{1,0:T(1,128)}, u32[]{:S(2)}) copy-start(s32[1,1024]{1,0:T(1,128)} %param.22) | copy-start | bytes 12292
  30.9 30.8 %copy-start = (s32[8]{0:T(128)S(1)}, s32[8]{0:T(128)}, u32[]{:S(2)}) copy-start(s32[8]{0:T(128)} %constant.143.clone) | copy-start | bytes 100
  30.9 29.3 %collective-permute-start.1 = (bf16[1,144,2048]{2,1,0:T(8,128)(2,1)S(1)}, bf16[1,144,2048]{2,1,0:T(8,128)(2,1)S(1)}, u32[]{:S(2)}, u32[]{:S(2)}) collective-permute-start(bf16[1,144,2048]{2,1,0:T(8,128)(2,1)S(1)} %maximum_bitcast_fusion), channel_id=1, source_target_pairs={{0,4},{1,5},{2,6},{3,7},{4,0},{5,1},{6,2},{7,3},{8,12},{9,13},{10,... | collective-permute-start | bytes 1769480 | tf_op jit(solution)/shard_map/ppermute | solution.py:953
  58.9 29.8 %collective-permute-start.5 = (bf16[4,160,1024]{2,1,0:T(8,128)(2,1)}, bf16[4,160,1024]{2,1,0:T(8,128)(2,1)}, u32[]{:S(2)}, u32[]{:S(2)}) collective-permute-start(bf16[4,160,1024]{2,1,0:T(8,128)(2,1)} %pad_maximum_fusion.2), channel_id=1, source_target_pairs={{0,1},{1,0},{2,3},{3,2},{4,5},{5,4},{6,7},{7,6},{8,9},{9,8},{10,11... | collective-permute-start | bytes 3932168 | tf_op jit(solution)/shard_map/ppermute | solution.py:953
  60.3 28.4 %copy-start.8 = (bf16[2,144,2048]{2,1,0:T(8,128)(2,1)}, bf16[2,144,2048]{2,1,0:T(8,128)(2,1)S(1)}, u32[]{:S(2)}) copy-start(bf16[2,144,2048]{2,1,0:T(8,128)(2,1)S(1)} %pad_maximum_fusion.3) | copy-start | bytes 3538948
  60.3 26.3 %collective-permute-start.3 = (bf16[2,144,2048]{2,1,0:T(8,128)(2,1)S(1)}, bf16[2,144,2048]{2,1,0:T(8,128)(2,1)S(1)}, u32[]{:S(2)}, u32[]{:S(2)}) collective-permute-start(bf16[2,144,2048]{2,1,0:T(8,128)(2,1)S(1)} %pad_maximum_fusion.3), channel_id=1, source_target_pairs={{0,2},{1,3},{2,0},{3,1},{4,6},{5,7},{6,4},{7,5},{8,10},{9,11},{10,... | collective-permute-start | bytes 3538952 | tf_op jit(solution)/shard_map/ppermute | solution.py:953
  61.0 35.0 %collective-permute-start.7 = (s32[1,1024]{1,0:T(1,128)S(1)}, s32[1,1024]{1,0:T(1,128)S(1)}, u32[]{:S(2)}, u32[]{:S(2)}) collective-permute-start(s32[1,1024]{1,0:T(1,128)S(1)} %copy-done.48), channel_id=1, source_target_pairs={{2,8},{3,9},{6,12},{7,13},{8,2},{9,3},{12,6},{13,7},{18,24},{19,25... | collective-permute-start | bytes 12296 | tf_op jit(solution)/shard_map/ppermute | solution.py:953
  62.4 37.5 %copy-start.47 = (s32[8]{0:T(128)}, s32[8]{0:T(128)S(1)}, u32[]{:S(2)}) copy-start(s32[8]{0:T(128)S(1)} %gather_fusion) | copy-start | bytes 100
  86.6 14.8 %collective-permute-start.4 = (bf16[1,1024,1152]{2,1,0:T(8,128)(2,1)}, bf16[1,1024,1152]{2,1,0:T(8,128)(2,1)}, u32[]{:S(2)}, u32[]{:S(2)}) collective-permute-start(bf16[1,1024,1152]{2,1,0:T(8,128)(2,1)} %param.20), channel_id=1, source_target_pairs={{2,8},{3,9},{6,12},{7,13},{8,2},{9,3},{12,6},{13,7},{18,24},{19,25... | collective-permute-start | bytes 7077896 | tf_op jit(solution)/shard_map/ppermute | solution.py:953
  90.5 15.3 %collective-permute-start.6 = (bf16[8,160,1024]{2,1,0:T(8,128)(2,1)S(1)}, bf16[8,160,1024]{2,1,0:T(8,128)(2,1)}, u32[]{:S(2)}, u32[]{:S(2)}) collective-permute-start(bf16[8,160,1024]{2,1,0:T(8,128)(2,1)S(1)} %pad_maximum_fusion.refs_0_), channel_id=1, source_target_pairs={{0,8},{1,9},{2,10},{3,11},{4,12},{5,13},{6,14},{7,15},{8,0},{9,1},... | collective-permute-start | bytes 7864328 | tf_op jit(solution)/shard_map/ppermute | solution.py:953
  93.9 54.0 %collective-permute-start.8 = (bf16[4,144,2048]{2,1,0:T(8,128)(2,1)}, bf16[4,144,2048]{2,1,0:T(8,128)(2,1)}, u32[]{:S(2)}, u32[]{:S(2)}) collective-permute-start(bf16[4,144,2048]{2,1,0:T(8,128)(2,1)} %pad_maximum_fusion.1), channel_id=1, source_target_pairs={{0,1},{1,0},{2,3},{3,2},{4,5},{5,4},{6,7},{7,6},{8,9},{9,8},{10,11... | collective-permute-start | bytes 7077896 | tf_op jit(solution)/shard_map/ppermute | solution.py:953
  100.7 60.5 %copy-start.37 = (f32[8,144]{1,0:T(8,128)}, f32[8,144]{1,0:T(8,128)S(1)}, u32[]{:S(2)}) copy-start(f32[8,144]{1,0:T(8,128)S(1)} %get-tuple-element.260) | copy-start | bytes 13828
  154.9 166.5 %all-gather.5.cloned.1.call-start = ((), (), s32[]{:S(2)}) async-start(), calls=%async_computation.1 | async-start | bytes 7299072 | tf_op jit(solution)/shard_map/all_gather | solution.py:1176
  155.6 46.5 %collective-permute-start.9 = (bf16[8,144,2048]{2,1,0:T(8,128)(2,1)}, bf16[8,144,2048]{2,1,0:T(8,128)(2,1)}, u32[]{:S(2)}, u32[]{:S(2)}) collective-permute-start(bf16[8,144,2048]{2,1,0:T(8,128)(2,1)} %constant_dynamic-update-slice_fusion.refs_2_.refs_3_), channel_id=1, source_target_pairs={{0,8},{1,9},{2,10},{3,11},{4,12},{5,13},{6,14},{7,15},{8,0},{9,1},... | collective-permute-start | bytes 14155784 | tf_op jit(solution)/shard_map/ppermute | solution.py:953
  155.7 39.5 %collective-permute-start.10 = (bf16[1,1024,1152]{2,1,0:T(8,128)(2,1)S(1)}, bf16[1,1024,1152]{2,1,0:T(8,128)(2,1)}, u32[]{:S(2)}, u32[]{:S(2)}) collective-permute-start(bf16[1,1024,1152]{2,1,0:T(8,128)(2,1)S(1)} %copy-done.16), channel_id=1, source_target_pairs={{2,8},{3,9},{6,12},{7,13},{8,2},{9,3},{12,6},{13,7},{18,24},{19,25... | collective-permute-start | bytes 7077896 | tf_op jit(solution)/shard_map/ppermute | solution.py:953
  256.2 56.1 %collective-permute-start.11 = (bf16[3,576,1024]{2,1,0:T(8,128)(2,1)}, bf16[3,576,1024]{2,1,0:T(8,128)(2,1)S(1)}, u32[]{:S(2)}, u32[]{:S(2)}) collective-permute-start(bf16[3,576,1024]{2,1,0:T(8,128)(2,1)} %get-tuple-element.159), channel_id=1, source_target_pairs={{0,8},{1,9},{2,10},{3,11},{4,12},{5,13},{6,14},{7,15},{8,0},{9,1},... | collective-permute-start | bytes 10616840 | tf_op jit(solution)/shard_map/ppermute | solution.py:953
  263.6 41.5 %copy-start.41 = (f32[2,8,384]{2,1,0:T(8,128)S(1)}, f32[2,8,384]{2,1,0:T(8,128)}, u32[]{:S(2)}) copy-start(f32[2,8,384]{2,1,0:T(8,128)} %param.34) | copy-start | bytes 73732
  263.6 42.1 %copy-start.21 = (f32[1,2,144,1152]{3,2,1,0:T(8,128)S(1)}, f32[1,2,144,1152]{3,2,1,0:T(8,128)}, u32[]{:S(2)}) copy-start(f32[1,2,144,1152]{3,2,1,0:T(8,128)} %param.30) | copy-start | bytes 3981316
  304.9 68.1 %collective-permute-start.13 = (bf16[3,576,1024]{2,1,0:T(8,128)(2,1)}, bf16[3,576,1024]{2,1,0:T(8,128)(2,1)}, u32[]{:S(2)}, u32[]{:S(2)}) collective-permute-start(bf16[3,576,1024]{2,1,0:T(8,128)(2,1)} %get-tuple-element.160), channel_id=1, source_target_pairs={{0,8},{1,9},{2,10},{3,11},{4,12},{5,13},{6,14},{7,15},{8,0},{9,1},... | collective-permute-start | bytes 10616840 | tf_op jit(solution)/shard_map/ppermute | solution.py:953
  319.8 43.8 %collective-permute-start.12 = (bf16[3,288,1024]{2,1,0:T(8,128)(2,1)}, bf16[3,288,1024]{2,1,0:T(8,128)(2,1)S(1)}, u32[]{:S(2)}, u32[]{:S(2)}) collective-permute-start(bf16[3,288,1024]{2,1,0:T(8,128)(2,1)} %get-tuple-element.162), channel_id=1, source_target_pairs={{0,1},{1,0},{2,3},{3,2},{4,5},{5,4},{6,7},{7,6},{8,9},{9,8},{10,11... | collective-permute-start | bytes 5308424 | tf_op jit(solution)/shard_map/ppermute | solution.py:953
  363.3 41.2 %collective-permute-start.15 = (bf16[3,576,1024]{2,1,0:T(8,128)(2,1)}, bf16[3,576,1024]{2,1,0:T(8,128)(2,1)}, u32[]{:S(2)}, u32[]{:S(2)}) collective-permute-start(bf16[3,576,1024]{2,1,0:T(8,128)(2,1)} %get-tuple-element.170), channel_id=1, source_target_pairs={{0,8},{1,9},{2,10},{3,11},{4,12},{5,13},{6,14},{7,15},{8,0},{9,1},... | collective-permute-start | bytes 10616840 | tf_op jit(solution)/shard_map/ppermute | solution.py:953
  369.1 42.8 %collective-permute-start.16 = (bf16[3,144,1024]{2,1,0:T(8,128)(2,1)}, bf16[3,144,1024]{2,1,0:T(8,128)(2,1)S(1)}, u32[]{:S(2)}, u32[]{:S(2)}) collective-permute-start(bf16[3,144,1024]{2,1,0:T(8,128)(2,1)} %get-tuple-element.172), channel_id=1, source_target_pairs={{0,4},{1,5},{2,12},{3,13},{4,0},{5,1},{6,8},{7,9},{8,6},{9,7},{10,... | collective-permute-start | bytes 2654216 | tf_op jit(solution)/shard_map/ppermute | solution.py:953
  371.4 41.8 %collective-permute-start.17 = (bf16[3,144,1024]{2,1,0:T(8,128)(2,1)}, bf16[3,144,1024]{2,1,0:T(8,128)(2,1)}, u32[]{:S(2)}, u32[]{:S(2)}) collective-permute-start(bf16[3,144,1024]{2,1,0:T(8,128)(2,1)} %get-tuple-element.173.refs_1_), channel_id=1, source_target_pairs={{2,8},{3,9},{6,12},{7,13},{8,2},{9,3},{12,6},{13,7},{18,24},{19,25... | collective-permute-start | bytes 2654216 | tf_op jit(solution)/shard_map/ppermute | solution.py:953
  378.7 66.1 %collective-permute-start.18 = (bf16[3,288,1024]{2,1,0:T(8,128)(2,1)}, bf16[3,288,1024]{2,1,0:T(8,128)(2,1)}, u32[]{:S(2)}, u32[]{:S(2)}) collective-permute-start(bf16[3,288,1024]{2,1,0:T(8,128)(2,1)} %get-tuple-element.178), channel_id=1, source_target_pairs={{0,1},{1,0},{2,3},{3,2},{4,5},{5,4},{6,7},{7,6},{8,9},{9,8},{10,11... | collective-permute-start | bytes 5308424 | tf_op jit(solution)/shard_map/ppermute | solution.py:953
  383.4 66.0 %collective-permute-start.14 = (bf16[1,1024,1152]{2,1,0:T(8,128)(2,1)}, bf16[1,1024,1152]{2,1,0:T(8,128)(2,1)}, u32[]{:S(2)}, u32[]{:S(2)}) collective-permute-start(bf16[1,1024,1152]{2,1,0:T(8,128)(2,1)} %convert_bitcast_fusion), channel_id=1, source_target_pairs={{2,8},{3,9},{6,12},{7,13},{8,2},{9,3},{12,6},{13,7},{18,24},{19,25... | collective-permute-start | bytes 7077896 | tf_op jit(solution)/shard_map/ppermute | solution.py:953
  404.5 36.5 %collective-permute-start.19 = (bf16[576,1152]{1,0:T(8,128)(2,1)}, bf16[576,1152]{1,0:T(8,128)(2,1)}, u32[]{:S(2)}, u32[]{:S(2)}) collective-permute-start(bf16[576,1152]{1,0:T(8,128)(2,1)} %convolution_convert_fusion.2), channel_id=1, source_target_pairs={{0,8},{1,9},{2,10},{3,11},{4,12},{5,13},{6,14},{7,15},{8,0},{9,1},... | collective-permute-start | bytes 3981320 | tf_op jit(solution)/shard_map/ppermute | solution.py:953
  411.9 72.6 %collective-permute-start.20 = (bf16[3,288,1024]{2,1,0:T(8,128)(2,1)}, bf16[3,288,1024]{2,1,0:T(8,128)(2,1)}, u32[]{:S(2)}, u32[]{:S(2)}) collective-permute-start(bf16[3,288,1024]{2,1,0:T(8,128)(2,1)} %get-tuple-element.185), channel_id=1, source_target_pairs={{0,1},{1,0},{2,3},{3,2},{4,5},{5,4},{6,7},{7,6},{8,9},{9,8},{10,11... | collective-permute-start | bytes 5308424 | tf_op jit(solution)/shard_map/ppermute | solution.py:953
  435.0 41.3 %collective-permute-start.22 = (bf16[576,640]{1,0:T(8,128)(2,1)}, bf16[576,640]{1,0:T(8,128)(2,1)}, u32[]{:S(2)}, u32[]{:S(2)}) collective-permute-start(bf16[576,640]{1,0:T(8,128)(2,1)} %convolution_convert_fusion.8), channel_id=1, source_target_pairs={{0,8},{1,9},{2,10},{3,11},{4,12},{5,13},{6,14},{7,15},{8,0},{9,1},... | collective-permute-start | bytes 2211848 | tf_op jit(solution)/shard_map/ppermute | solution.py:953
  444.0 29.4 %collective-permute-start.21 = (bf16[288,1152]{1,0:T(8,128)(2,1)}, bf16[288,1152]{1,0:T(8,128)(2,1)}, u32[]{:S(2)}, u32[]{:S(2)}) collective-permute-start(bf16[288,1152]{1,0:T(8,128)(2,1)} %bitcast.152), channel_id=1, source_target_pairs={{0,1},{1,0},{2,3},{3,2},{4,5},{5,4},{6,7},{7,6},{8,9},{9,8},{10,11... | collective-permute-start | bytes 1990664 | tf_op jit(solution)/shard_map/ppermute | solution.py:953
  448.7 49.0 %collective-permute-start.23 = (bf16[3,144,1024]{2,1,0:T(8,128)(2,1)}, bf16[3,144,1024]{2,1,0:T(8,128)(2,1)S(1)}, u32[]{:S(2)}, u32[]{:S(2)}) collective-permute-start(bf16[3,144,1024]{2,1,0:T(8,128)(2,1)} %get-tuple-element.190), channel_id=1, source_target_pairs={{0,4},{1,5},{2,12},{3,13},{4,0},{5,1},{6,8},{7,9},{8,6},{9,7},{10,... | collective-permute-start | bytes 2654216 | tf_op jit(solution)/shard_map/ppermute | solution.py:953
  449.4 49.8 %collective-permute-start.24 = (bf16[3,144,1024]{2,1,0:T(8,128)(2,1)}, bf16[3,144,1024]{2,1,0:T(8,128)(2,1)}, u32[]{:S(2)}, u32[]{:S(2)}) collective-permute-start(bf16[3,144,1024]{2,1,0:T(8,128)(2,1)} %get-tuple-element.191.refs_4_), channel_id=1, source_target_pairs={{2,8},{3,9},{6,12},{7,13},{8,2},{9,3},{12,6},{13,7},{18,24},{19,25... | collective-permute-start | bytes 2654216 | tf_op jit(solution)/shard_map/ppermute | solution.py:953
  475.6 49.9 %collective-permute-start.28 = (bf16[144,1152]{1,0:T(8,128)(2,1)}, bf16[144,1152]{1,0:T(8,128)(2,1)S(1)}, u32[]{:S(2)}, u32[]{:S(2)}) collective-permute-start(bf16[144,1152]{1,0:T(8,128)(2,1)} %bitcast.141), channel_id=1, source_target_pairs={{2,8},{3,9},{6,12},{7,13},{8,2},{9,3},{12,6},{13,7},{18,24},{19,25... | collective-permute-start | bytes 995336 | tf_op jit(solution)/shard_map/ppermute | solution.py:953
  478.6 45.4 %collective-permute-start.27 = (bf16[144,1152]{1,0:T(8,128)(2,1)}, bf16[144,1152]{1,0:T(8,128)(2,1)}, u32[]{:S(2)}, u32[]{:S(2)}) collective-permute-start(bf16[144,1152]{1,0:T(8,128)(2,1)} %bitcast.155), channel_id=1, source_target_pairs={{0,4},{1,5},{2,12},{3,13},{4,0},{5,1},{6,8},{7,9},{8,6},{9,7},{10,... | collective-permute-start | bytes 995336 | tf_op jit(solution)/shard_map/ppermute | solution.py:953
  484.5 46.2 %collective-permute-start.26 = (bf16[576,640]{1,0:T(8,128)(2,1)}, bf16[576,640]{1,0:T(8,128)(2,1)}, u32[]{:S(2)}, u32[]{:S(2)}) collective-permute-start(bf16[576,640]{1,0:T(8,128)(2,1)} %convolution_convert_fusion.6), channel_id=1, source_target_pairs={{0,8},{1,9},{2,10},{3,11},{4,12},{5,13},{6,14},{7,15},{8,0},{9,1},... | collective-permute-start | bytes 2211848 | tf_op jit(solution)/shard_map/ppermute | solution.py:953
  497.8 31.1 %collective-permute-start.25 = (bf16[288,640]{1,0:T(8,128)(2,1)}, bf16[288,640]{1,0:T(8,128)(2,1)}, u32[]{:S(2)}, u32[]{:S(2)}) collective-permute-start(bf16[288,640]{1,0:T(8,128)(2,1)} %bitcast.38), channel_id=1, source_target_pairs={{0,1},{1,0},{2,3},{3,2},{4,5},{5,4},{6,7},{7,6},{8,9},{9,8},{10,11... | collective-permute-start | bytes 1105928 | tf_op jit(solution)/shard_map/ppermute | solution.py:953
  499.2 49.9 %collective-permute-start.29 = (bf16[3,144,1024]{2,1,0:T(8,128)(2,1)}, bf16[3,144,1024]{2,1,0:T(8,128)(2,1)}, u32[]{:S(2)}, u32[]{:S(2)}) collective-permute-start(bf16[3,144,1024]{2,1,0:T(8,128)(2,1)} %get-tuple-element.199), channel_id=1, source_target_pairs={{0,4},{1,5},{2,12},{3,13},{4,0},{5,1},{6,8},{7,9},{8,6},{9,7},{10,... | collective-permute-start | bytes 2654216 | tf_op jit(solution)/shard_map/ppermute | solution.py:953
  523.9 25.2 %collective-permute-start.30 = (bf16[3,144,1024]{2,1,0:T(8,128)(2,1)S(1)}, bf16[3,144,1024]{2,1,0:T(8,128)(2,1)}, u32[]{:S(2)}, u32[]{:S(2)}) collective-permute-start(bf16[3,144,1024]{2,1,0:T(8,128)(2,1)S(1)} %copy-done.26), channel_id=1, source_target_pairs={{2,8},{3,9},{6,12},{7,13},{8,2},{9,3},{12,6},{13,7},{18,24},{19,25... | collective-permute-start | bytes 2654216 | tf_op jit(solution)/shard_map/ppermute | solution.py:953
  525.5 18.8 %collective-permute-start.31 = (bf16[576,640]{1,0:T(8,128)(2,1)}, bf16[576,640]{1,0:T(8,128)(2,1)}, u32[]{:S(2)}, u32[]{:S(2)}) collective-permute-start(bf16[576,640]{1,0:T(8,128)(2,1)} %convolution_convert_fusion.4), channel_id=1, source_target_pairs={{0,8},{1,9},{2,10},{3,11},{4,12},{5,13},{6,14},{7,15},{8,0},{9,1},... | collective-permute-start | bytes 2211848 | tf_op jit(solution)/shard_map/ppermute | solution.py:953
  533.0 14.2 %collective-permute-start.32 = (bf16[288,640]{1,0:T(8,128)(2,1)}, bf16[288,640]{1,0:T(8,128)(2,1)}, u32[]{:S(2)}, u32[]{:S(2)}) collective-permute-start(bf16[288,640]{1,0:T(8,128)(2,1)} %bitcast.154), channel_id=1, source_target_pairs={{0,1},{1,0},{2,3},{3,2},{4,5},{5,4},{6,7},{7,6},{8,9},{9,8},{10,11... | collective-permute-start | bytes 1105928 | tf_op jit(solution)/shard_map/ppermute | solution.py:953
  546.6 18.8 %collective-permute-start.33 = (bf16[288,640]{1,0:T(8,128)(2,1)}, bf16[288,640]{1,0:T(8,128)(2,1)}, u32[]{:S(2)}, u32[]{:S(2)}) collective-permute-start(bf16[288,640]{1,0:T(8,128)(2,1)} %bitcast.153), channel_id=1, source_target_pairs={{0,1},{1,0},{2,3},{3,2},{4,5},{5,4},{6,7},{7,6},{8,9},{9,8},{10,11... | collective-permute-start | bytes 1105928 | tf_op jit(solution)/shard_map/ppermute | solution.py:953
  558.6 1.2 collective-permute-start.34
  559.8 5.0 collective-permute-start.35
  562.0 32.6 %collective-permute-start.45 = (bf16[144,1280]{1,0:T(8,128)(2,1)S(1)}, bf16[144,1280]{1,0:T(8,128)(2,1)S(1)}, u32[]{:S(2)}, u32[]{:S(2)}) collective-permute-start(bf16[144,1280]{1,0:T(8,128)(2,1)S(1)} %pad_maximum_fusion.8.refs_1_), channel_id=1, source_target_pairs={{2,8},{3,9},{6,12},{7,13},{8,2},{9,3},{12,6},{13,7},{18,24},{19,25... | collective-permute-start | bytes 1105928 | tf_op jit(solution)/shard_map/ppermute | solution.py:953
  562.7 32.0 %collective-permute-start.44 = (bf16[144,1280]{1,0:T(8,128)(2,1)}, bf16[144,1280]{1,0:T(8,128)(2,1)S(1)}, u32[]{:S(2)}, u32[]{:S(2)}) collective-permute-start(bf16[144,1280]{1,0:T(8,128)(2,1)} %pad_maximum_fusion.7), channel_id=1, source_target_pairs={{0,4},{1,5},{2,12},{3,13},{4,0},{5,1},{6,8},{7,9},{8,6},{9,7},{10,... | collective-permute-start | bytes 1105928 | tf_op jit(solution)/shard_map/ppermute | solution.py:953
  567.3 27.4 %collective-permute-start.46 = (bf16[144,640]{1,0:T(8,128)(2,1)}, bf16[144,640]{1,0:T(8,128)(2,1)}, u32[]{:S(2)}, u32[]{:S(2)}) collective-permute-start(bf16[144,640]{1,0:T(8,128)(2,1)} %bitcast.156), channel_id=1, source_target_pairs={{0,4},{1,5},{2,12},{3,13},{4,0},{5,1},{6,8},{7,9},{8,6},{9,7},{10,... | collective-permute-start | bytes 552968 | tf_op jit(solution)/shard_map/ppermute | solution.py:953
  568.3 26.4 %collective-permute-start.47 = (bf16[144,640]{1,0:T(8,128)(2,1)}, bf16[144,640]{1,0:T(8,128)(2,1)}, u32[]{:S(2)}, u32[]{:S(2)}) collective-permute-start(bf16[144,640]{1,0:T(8,128)(2,1)} %bitcast.144), channel_id=1, source_target_pairs={{2,8},{3,9},{6,12},{7,13},{8,2},{9,3},{12,6},{13,7},{18,24},{19,25... | collective-permute-start | bytes 552968 | tf_op jit(solution)/shard_map/ppermute | solution.py:953
  579.3 10.1 %collective-permute-start.37 = (f32[8,5632]{1,0:T(8,128)S(1)}, f32[8,5632]{1,0:T(8,128)S(1)}, u32[]{:S(2)}, u32[]{:S(2)}) collective-permute-start(f32[8,5632]{1,0:T(8,128)S(1)} %slice_select_fusion), channel_id=1, source_target_pairs={{0,8},{1,9},{2,10},{3,11},{4,12},{5,13},{6,14},{7,15},{8,0},{9,1},... | collective-permute-start | bytes 540680 | tf_op jit(solution)/shard_map/ppermute | solution.py:953
  589.5 4.6 collective-permute-start.38
  594.1 4.8 collective-permute-start.39
  598.9 10.0 %collective-permute-start.48 = (f32[24,144]{1,0:T(8,128)}, f32[24,144]{1,0:T(8,128)S(1)}, u32[]{:S(2)}, u32[]{:S(2)}) collective-permute-start(f32[24,144]{1,0:T(8,128)} %get-tuple-element.239), channel_id=1, source_target_pairs={{0,8},{1,9},{2,10},{3,11},{4,12},{5,13},{6,14},{7,15},{8,0},{9,1},... | collective-permute-start | bytes 41480 | tf_op jit(solution)/shard_map/ppermute | solution.py:953
  599.8 9.7 %collective-permute-start.40 = (f32[8,2816]{1,0:T(8,128)S(1)}, f32[8,2816]{1,0:T(8,128)S(1)}, u32[]{:S(2)}, u32[]{:S(2)}) collective-permute-start(f32[8,2816]{1,0:T(8,128)S(1)} %add.192), channel_id=1, source_target_pairs={{0,2},{1,3},{2,0},{3,1},{4,6},{5,7},{6,4},{7,5},{8,10},{9,11},{10,... | collective-permute-start | bytes 270344 | tf_op jit(solution)/shard_map/ppermute | solution.py:953
  608.9 3.9 collective-permute-start.49
  609.5 7.1 %collective-permute-start.41 = (f32[8,2816]{1,0:T(8,128)S(1)}, f32[8,2816]{1,0:T(8,128)S(1)}, u32[]{:S(2)}, u32[]{:S(2)}) collective-permute-start(f32[8,2816]{1,0:T(8,128)S(1)} %add.193), channel_id=1, source_target_pairs={{0,4},{1,5},{2,6},{3,7},{4,0},{5,1},{6,2},{7,3},{8,12},{9,13},{10,... | collective-permute-start | bytes 270344 | tf_op jit(solution)/shard_map/ppermute | solution.py:953
  616.2 1.9 collective-permute-start.50
  616.6 4.7 collective-permute-start.42
  619.1 4.9 collective-permute-start.51
  621.4 7.5 %collective-permute-start.43 = (f32[8,5632]{1,0:T(8,128)S(1)}, f32[8,5632]{1,0:T(8,128)S(1)}, u32[]{:S(2)}, u32[]{:S(2)}) collective-permute-start(f32[8,5632]{1,0:T(8,128)S(1)} %pad_maximum_fusion.10), channel_id=1, source_target_pairs={{0,8},{1,9},{2,10},{3,11},{4,12},{5,13},{6,14},{7,15},{8,0},{9,1},... | collective-permute-start | bytes 540680 | tf_op jit(solution)/shard_map/ppermute | solution.py:953
  624.0 4.9 collective-permute-start.52
  625.6 47.4 %collective-permute-start.36 = (bf16[1,1024,1152]{2,1,0:T(8,128)(2,1)S(1)}, bf16[1,1024,1152]{2,1,0:T(8,128)(2,1)}, u32[]{:S(2)}, u32[]{:S(2)}) collective-permute-start(bf16[1,1024,1152]{2,1,0:T(8,128)(2,1)S(1)} %bitcast.140), channel_id=1, source_target_pairs={{2,8},{3,9},{6,12},{7,13},{8,2},{9,3},{12,6},{13,7},{18,24},{19,25... | collective-permute-start | bytes 7077896 | tf_op jit(solution)/shard_map/ppermute | solution.py:953
  645.6 11.2 %collective-permute-start.53 = (f32[8,3584]{1,0:T(8,128)S(1)}, f32[8,3584]{1,0:T(8,128)S(1)}, u32[]{:S(2)}, u32[]{:S(2)}) collective-permute-start(f32[8,3584]{1,0:T(8,128)S(1)} %add.199), channel_id=1, source_target_pairs={{0,2},{1,3},{2,0},{3,1},{4,6},{5,7},{6,4},{7,5},{8,10},{9,11},{10,... | collective-permute-start | bytes 344072 | tf_op jit(solution)/shard_map/ppermute | solution.py:953
  656.8 7.5 %collective-permute-start.54 = (f32[8,3584]{1,0:T(8,128)S(1)}, f32[8,3584]{1,0:T(8,128)S(1)}, u32[]{:S(2)}, u32[]{:S(2)}) collective-permute-start(f32[8,3584]{1,0:T(8,128)S(1)} %add.200), channel_id=1, source_target_pairs={{0,4},{1,5},{2,6},{3,7},{4,0},{5,1},{6,2},{7,3},{8,12},{9,13},{10,... | collective-permute-start | bytes 344072 | tf_op jit(solution)/shard_map/ppermute | solution.py:953
  (49 other events, 335.1 us)
Sparse Core Ops, SparseCore 0:
  155.0 75.2 all-gather.2
  233.7 71.1 all-gather.4

commit v3 on v2

--- a/solution.py
+++ b/solution.py
@@ -41,6 +41,12 @@
 
 BLOCK_ROWS = 256
 VMEM_BYTES = 56 * 1024 * 1024
+
+
+def light(flops, bytes_accessed, transcendentals):
+    return pl.CostEstimate(
+        flops=flops // 8, bytes_accessed=bytes_accessed // 8, transcendentals=transcendentals // 8
+    )
 
 
 def partner_lanes(values):
@@ -102,7 +108,7 @@
             jax.ShapeDtypeStruct((width, rows), jnp.bfloat16),
         ],
         compiler_params=pltpu.CompilerParams(vmem_limit_bytes=VMEM_BYTES),
-        cost_estimate=pl.CostEstimate(
+        cost_estimate=light(
             flops=2 * rows * width * columns,
             bytes_accessed=2 * (rows * width * 2 + rows * columns + width * columns),
             transcendentals=0,
@@ -196,7 +202,7 @@
             pltpu.VMEM((4, rows, 128), jnp.bfloat16),
         ],
         compiler_params=pltpu.CompilerParams(vmem_limit_bytes=VMEM_BYTES),
-        cost_estimate=pl.CostEstimate(
+        cost_estimate=light(
             flops=20 * pairs * rows * rows * 128,
             bytes_accessed=8 * rows * 640 * pairs,
             transcendentals=6 * pairs * rows * rows,
@@ -205,7 +211,20 @@
 
 
 def backward_kernel(
-    qkv_ref, d_ref, log_ref, pos_ref, cos_ref, sin_ref, out_ref, key_ref, value_ref, dk_ref, dv_ref
+    qkv_ref,
+    d_ref,
+    log_ref,
+    pos_ref,
+    cos_ref,
+    sin_ref,
+    turned_ref,
+    out_ref,
+    away_ref,
+    home_ref,
+    key_ref,
+    value_ref,
+    dk_ref,
+    dv_ref,
 ):
     step = pl.program_id(0)
     block = d_ref.shape[0]
@@ -261,11 +280,20 @@
         d_key = d_key * cos_ref[...] - partner_lanes(d_key) * sin_ref[...]
         out_ref[:, 384:512] = d_key.astype(jnp.bfloat16)
         out_ref[:, 512:640] = dv_ref[...].T.astype(jnp.bfloat16)
-
-
-def attend_backward(qkv, d_attended, logs, position, cos, sin, pair):
+        half = away_ref.shape[0]
+        for first, grad_ref in ((0, away_ref), (half, home_ref)):
+            grad_ref[...] = jnp.dot(
+                turned_ref[first : first + half, :],
+                out_ref[...],
+                preferred_element_type=jnp.float32,
+            ).astype(jnp.bfloat16)
+
+
+def attend_backward(qkv, d_attended, logs, position, cos, sin, turned, pair):
     rows = qkv.shape[0]
+    model = turned.shape[0]
     block = min(BLOCK_ROWS, rows)
+    half = pl.BlockSpec((model // 2, 640), lambda i: (0, 0))
     return pl.pallas_call(
         backward_kernel,
         grid=(rows // block,),
@@ -276,9 +304,14 @@
             pl.BlockSpec((block, 1), lambda i: (i, 0)),
             pl.BlockSpec((rows, 128), lambda i: (0, 0)),
             pl.BlockSpec((rows, 128), lambda i: (0, 0)),
-        ],
-        out_specs=pl.BlockSpec((rows, 640), lambda i: (0, 0)),
-        out_shape=jax.ShapeDtypeStruct((rows, 640), jnp.bfloat16),
+            pl.BlockSpec((model, rows), lambda i: (0, 0), pipeline_mode=pl.Buffered(1)),
+        ],
+        out_specs=[pl.BlockSpec((rows, 640), lambda i: (0, 0)), half, half],
+        out_shape=[
+            jax.ShapeDtypeStruct((rows, 640), jnp.bfloat16),
+            jax.ShapeDtypeStruct((model // 2, 640), jnp.bfloat16),
+            jax.ShapeDtypeStruct((model // 2, 640), jnp.bfloat16),
+        ],
         scratch_shapes=[
             pltpu.VMEM((4, rows, 128), jnp.bfloat16),
             pltpu.VMEM((4, rows, 128), jnp.bfloat16),
@@ -286,12 +319,12 @@
             pltpu.VMEM((128, rows), jnp.float32),
         ],
         compiler_params=pltpu.CompilerParams(vmem_limit_bytes=VMEM_BYTES),
-        cost_estimate=pl.CostEstimate(
+        cost_estimate=light(
             flops=50 * rows * rows * 128,
             bytes_accessed=8 * rows * 640,
             transcendentals=6 * rows * rows,
         ),
-    )(qkv, d_attended, logs, position, cos, sin)
+    )(qkv, d_attended, logs, position, cos, sin, turned)
 
 
 def turn_kernel(order_ref, rows_ref, out_ref, turned_ref):
@@ -318,20 +351,23 @@
         ),
         out_shape=jax.ShapeDtypeStruct((model, count), jnp.bfloat16),
         compiler_params=pltpu.CompilerParams(vmem_limit_bytes=VMEM_BYTES),
-        cost_estimate=pl.CostEstimate(
+        cost_estimate=light(
             flops=0, bytes_accessed=4 * count * model, transcendentals=0
         ),
     )(order, rows)
 
 
-def mlp_kernel(reps, first, slot_ref, place_ref, mid_ref, d_ref, *refs):
+def mlp_kernel(reps, first, last, slot_ref, place_ref, mid_ref, d_ref, *refs):
     del slot_ref
     mid_hbm, d_hbm = refs[:2]
     befores = refs[2 : 3 if first else 4]
     refs = refs[2 + len(befores) :]
     weight_hbm, refs = (refs[:1], refs[1:]) if place_ref.shape[0] == 1 else (refs[:2], refs[2:])
     away_ref, home_ref, result_ref, back_ref = refs[:4]
-    weight_ref, mid_turned_ref, d_turned_ref, d_pair_ref, hidden_ref, weight_sem, sem = refs[4:]
+    weight_ref, mid_turned_ref, d_turned_ref, d_pair_ref, hidden_ref, weight_sem, sem = refs[4:11]
+    output_ref = result_ref
+    if last:
+        result_ref = refs[11]
     step = pl.program_id(0)
     count = mid_ref.shape[0]
     part = min(512, count)
@@ -402,6 +438,11 @@
         d_pair_ref[rows, tile:] = (d_hidden * silu).astype(jnp.bfloat16)
         back_ref[rows, :] += across(d_pair_ref[rows, :], pair_w)
         result_ref[rows, :] += across(hidden, down_w)
+        if last:
+
+            @pl.when(step == reps - 1)
+            def _():
+                output_ref[rows, :] = result_ref[rows, :].astype(jnp.bfloat16)
 
     @pl.when(step == 0)
     def _():
@@ -419,7 +460,7 @@
         ).astype(jnp.bfloat16)
 
 
-def mlp_part(reps, slots, places, mid, d_out, mid_turned, d_turned, weights, result, back):
+def mlp_part(reps, slots, places, mid, d_out, mid_turned, d_turned, weights, result, back, last):
     count, model = mid.shape
     tile = (weights[0].shape[2] - (512 if len(weights) == 2 else 0)) // 3
     if len(weights) == 2:
@@ -434,7 +475,7 @@
 
     anywhere = pl.BlockSpec(memory_space=pl.ANY)
     return pl.pallas_call(
-        functools.partial(mlp_kernel, reps, first),
+        functools.partial(mlp_kernel, reps, first, last),
         grid_spec=pltpu.PrefetchScalarGridSpec(
             num_scalar_prefetch=2,
             grid=(reps,),
@@ -453,16 +494,17 @@
                 pltpu.VMEM((count, tile), jnp.bfloat16),
                 pltpu.SemaphoreType.DMA((reps,)),
                 pltpu.SemaphoreType.DMA((4,)),
-            ],
+            ]
+            + ([pltpu.VMEM((count, model), jnp.float32)] if last else []),
         ),
         out_shape=[
             jax.ShapeDtypeStruct((3, half, units), jnp.bfloat16),
             jax.ShapeDtypeStruct((3, half, units), jnp.bfloat16),
+            jax.ShapeDtypeStruct((count, model), jnp.bfloat16 if last else jnp.float32),
             jax.ShapeDtypeStruct((count, model), jnp.float32),
-            jax.ShapeDtypeStruct((count, model), jnp.float32),
         ],
         compiler_params=pltpu.CompilerParams(vmem_limit_bytes=VMEM_BYTES),
-        cost_estimate=pl.CostEstimate(
+        cost_estimate=light(
             flops=18 * count * model * units,
             bytes_accessed=2 * (4 * count * model + 6 * model * units) + 16 * count * model,
             transcendentals=count * units,
@@ -506,7 +548,7 @@
         ),
         out_shape=jax.ShapeDtypeStruct((owners, rows, high - low), jnp.bfloat16),
         compiler_params=pltpu.CompilerParams(vmem_limit_bytes=VMEM_BYTES),
-        cost_estimate=pl.CostEstimate(
+        cost_estimate=light(
             flops=0, bytes_accessed=8 * owners * rows * sum(widths), transcendentals=0
         ),
     )(places, core, *mine, *other)
@@ -520,16 +562,6 @@
         column = jnp.sum(rows * factor[r : r + 1, :], axis=1, keepdims=True)
         columns = jnp.where(lane == r, column, columns)
     return columns.T[:8, :]
-
-
-def weighted_rows(left, rows):
-    turned = left.T
-    sublane = lax.broadcasted_iota(jnp.int32, (8, 1), 0)
-    out = jnp.zeros((8, rows.shape[1]), jnp.float32)
-    for r in range(8):
-        row = jnp.sum(rows * turned[:, r : r + 1], axis=0, keepdims=True)
-        out = jnp.where(sublane == r, row, out)
-    return out
 
 
 def exact_dot(left, right, contract):
@@ -588,7 +620,7 @@
             jax.ShapeDtypeStruct((8 * count, rows), jnp.float32),
         ],
         compiler_params=pltpu.CompilerParams(vmem_limit_bytes=VMEM_BYTES),
-        cost_estimate=pl.CostEstimate(
+        cost_estimate=light(
             flops=96 * count * rows * columns,
             bytes_accessed=14 * count * rows * columns,
             transcendentals=0,
@@ -611,7 +643,7 @@
         out_shape=[jax.ShapeDtypeStruct(e.shape, jnp.float32) for e in errors]
         + [jax.ShapeDtypeStruct((8 * len(errors), rows), jnp.float32)],
         compiler_params=pltpu.CompilerParams(vmem_limit_bytes=VMEM_BYTES),
-        cost_estimate=pl.CostEstimate(
+        cost_estimate=light(
             flops=96 * sum(e.size for e in errors),
             bytes_accessed=14 * sum(e.size for e in errors),
             transcendentals=0,
@@ -628,7 +660,7 @@
             for k in range(ref.shape[0] if len(ref.shape) == 3 else 1):
                 rows = ref[k] if len(ref.shape) == 3 else ref[...]
                 own = left_ref[8 * m : 8 * m + 8, :]
-                out_ref[:, at : at + rows.shape[1]] = weighted_rows(own, rows)
+                out_ref[:, at : at + rows.shape[1]] = exact_dot(own, rows, ((1,), (0,)))
                 at += rows.shape[1]
                 m += 1
         for k in range(m):
@@ -645,7 +677,7 @@
         out_specs=pl.BlockSpec(memory_space=pltpu.VMEM),
         out_shape=jax.ShapeDtypeStruct((8, width), jnp.float32),
         compiler_params=pltpu.CompilerParams(vmem_limit_bytes=VMEM_BYTES),
-        cost_estimate=pl.CostEstimate(
+        cost_estimate=light(
             flops=96 * sum(m.size for m in mixed),
             bytes_accessed=4 * sum(m.size for m in mixed),
             transcendentals=0,
@@ -727,7 +759,7 @@
             jax.ShapeDtypeStruct((count, 8, columns), jnp.float32),
         ],
         compiler_params=pltpu.CompilerParams(vmem_limit_bytes=VMEM_BYTES),
-        cost_estimate=pl.CostEstimate(
+        cost_estimate=light(
             flops=96 * count * rows * columns,
             bytes_accessed=24 * count * rows * columns,
             transcendentals=0,
@@ -780,7 +812,7 @@
         out_specs=in_vmem(len(shapes)),
         out_shape=shapes,
         compiler_params=pltpu.CompilerParams(vmem_limit_bytes=VMEM_BYTES),
-        cost_estimate=pl.CostEstimate(
+        cost_estimate=light(
             flops=96 * sum(m.size for m in mixed),
             bytes_accessed=24 * sum(m.size for m in mixed),
             transcendentals=0,
@@ -817,7 +849,7 @@
         ),
         out_shape=shapes,
         compiler_params=pltpu.CompilerParams(vmem_limit_bytes=VMEM_BYTES),
-        cost_estimate=pl.CostEstimate(
+        cost_estimate=light(
             flops=0, bytes_accessed=6 * number * count * rows * tile, transcendentals=0
         ),
     )(picks, *[master] * number)
@@ -844,7 +876,7 @@
         out_specs=[part, part],
         out_shape=[out, out],
         compiler_params=pltpu.CompilerParams(vmem_limit_bytes=VMEM_BYTES),
-        cost_estimate=pl.CostEstimate(
+        cost_estimate=light(
             flops=home.size, bytes_accessed=6 * home.size, transcendentals=0
         ),
     )(home.reshape(lead, rows, columns), got.reshape(lead, rows, columns))
@@ -920,7 +952,7 @@
             jax.ShapeDtypeStruct((model, model), jnp.bfloat16),
         ],
         compiler_params=pltpu.CompilerParams(vmem_limit_bytes=VMEM_BYTES),
-        cost_estimate=pl.CostEstimate(
+        cost_estimate=light(
             flops=2 * count * model * model,
             bytes_accessed=12 * count * model + 4 * model * model,
             transcendentals=count,
@@ -1167,17 +1199,15 @@
     order = jnp.array(grid.masks(), jnp.int32) ^ logical_shard
 
     qkv, turned_in = project_qkv(order, tokens, gain_attn[None], qkv_w, cos, sin)
-    held, got = after((mine[1], gathering[-1]), qkv)
-    mine[1] = jnp.concatenate([held, got], axis=0)
-    qkv = after(qkv, mine[1])
     wide_parts = [None] * chained
     for k in range(chained, 3):
-        part = after(cuts[k], mine[1])
+        part = after(cuts[k], mine[0])
         part = lax.all_gather(part, ("rep", "shard"), axis=0, tiled=True)
         wide_parts.append((natural, whole, [part.reshape(reps, owners * rows, 3 * tile)]))
+    attended, logs = attend_forward(qkv, place)
+    held, got = after((mine[1], gathering[-1]), attended)
+    mine[1] = jnp.concatenate([held, got], axis=0)
     other.append(grid.move(mine[1], grid.flip_rep(0)))
-    attended, logs = attend_forward(qkv, place)
-    other[1] = after(other[1], attended)
     d_out = jnp.where(grid.stays(), cotangent, after(moved_out, attended))[0]
     if chained:
         slots = (natural + core * (reps // 2)) % reps
@@ -1214,12 +1244,22 @@
     for k in range(3):
         slots, where, weights = wide_parts[k]
         away, home, result, d_mid = mlp_part(
-            reps, slots, where, normed_mid, d_out, turned_mid, turned_out, weights, result, d_mid
+            reps,
+            slots,
+            where,
+            normed_mid,
+            d_out,
+            turned_mid,
+            turned_out,
+            weights,
+            result,
+            d_mid,
+            k == 2,
         )
         wide_sums.append(Sums(grid, away, home))
         for earlier in wide_sums[max(0, k - 2) : k]:
             d_mid, result = after((d_mid, result), earlier.step(away))
-    result = grid.swap_rows(result.astype(jnp.bfloat16)[None])
+    result = grid.swap_rows(result[None])
 
     _, mid_back = jax.vjp(normed, residual, gain_mlp)
     d_residual, grad_gain_mlp = mid_back(d_mid)
@@ -1234,9 +1274,11 @@
     d_stacks, pair_sums = [], []
     hold = len(grid.order) == 3
     for j in range(PAIRS):
-        d_stack = attend_backward(qkv, d_attended, logs, place, cos, sin, j)
+        d_stack, away, home = attend_backward(
+            qkv, d_attended, logs, place, cos, sin, turned_in, j
+        )
         d_stacks.append(d_stack)
-        pair_sums.append(weight_grad(turned_in, d_stack))
+        pair_sums.append(Sums(grid, away, home))
         if j == 0:
             done = (wide_sums[1].step(d_stack), out_sums.step(d_stack), result)
         elif j == 1:

time: 691 us -> 776 us (1.12)
  waiting for transfers between devices: 113 us -> 168 us
  starting transfers between devices: 76.9 us -> 123 us
  matrix products: 46.3 us -> 24.7 us
    ppermute x55, waiting for transfers between devices: 112 us -> 168 us  [move(): return lax.ppermute(value, ('rep', 'shard'), pairs)]
    ppermute x55, starting transfers between devices: 76.8 us -> 123 us  [move(): return lax.ppermute(value, ('rep', 'shard'), pairs)]
    dot_general x4 -> x1, matrix products: 14.1 us -> 4.06 us  [weight_grad(): jnp.dot(turned[:half], right, preferred_element_type=jnp.float32)]
    dot_general x4 -> x1, matrix products: 12.1 us -> 2.75 us  [weight_grad(): jnp.dot(turned[half:], right, preferred_element_type=jnp.float32)]
    pallas_call x3, Pallas kernels: 54.5 us -> 63.6 us  [attend_backward(): pl.pallas_call(backward_kernel, grid=(rows // block,), in_specs=[pl.Block...]
  transfers between devices with their start and end apart: 57 -> 57, of which waited for: 15 -> 16; matrix products, arithmetic and copies ran while one was open for 15% -> 12% of each run, Pallas kernels for 52% -> 47%
where the time goes in v3:
time: 776 us; the launch traced here: 768 us
  Pallas kernels  359 us (46%)
  waiting for transfers between devices  168 us (22%)
  starting transfers between devices  123 us (16%)
  other arithmetic  53.3 us (7%)
  matrix products  24.7 us (3%)
  local copies, waits for them, and re-layouts  24.2 us (3%)
  between operations  15.3 us (2%)
    ppermute x55, waiting for transfers between devices, move(): return lax.ppermute(value, ('rep', 'shard'), pairs)  168 us
    pallas_call x3, Pallas kernels, mlp_part(): pl.pallas_call(functools.partial(mlp_kernel, reps, first, last), grid_spe...  124 us
    ppermute x55, starting transfers between devices, move(): return lax.ppermute(value, ('rep', 'shard'), pairs)  123 us
    pallas_call x3, Pallas kernels, attend_backward(): pl.pallas_call(backward_kernel, grid=(rows // block,), in_specs=[pl.Block...  63.6 us
    pallas_call x14, Pallas kernels, split_sum(): pl.pallas_call(kernel, grid=(lead,), in_specs=[whole, whole], out_specs=[...  46.8 us
    pallas_call x1, Pallas kernels, attend_forward(): pl.pallas_call(forward_kernel, grid=(pairs, rows // block), in_specs=[pl....  33.3 us
    pallas_call x1, Pallas kernels, finish_wide(): pl.pallas_call(kernel, grid=(count,), in_specs=[pl.BlockSpec((8, columns)...  16 us
  transfers between devices with their start and end apart: 57, of which 16 were waited for; matrix products, arithmetic and copies ran while one was open for 12% of the time, Pallas kernels for 47%

profile of v3, /device:TPU:0, one launch (start us, length us, event | category | flops | bytes accessed | tf_op | source)
XLA Modules:
  0.0 768.2 jit_solution(2747587308882403457)
XLA Ops:
  10.1 4.1 collective-permute-start
  14.2 14.7 %collective-permute-done = bf16[1,160,1024]{2,1,0:T(8,128)(2,1)S(1)} collective-permute-done((bf16[1,160,1024]{2,1,0:T(8,128)(2,1)S(1)}, bf16[1,160,1024]{2,1,0:T(8,128)(2,1)S(1)}, u32[]{:S(2)}, u32[]{:S(2)}) %collective-permute-start) | collective-permute-done | bytes 327712 | tf_op jit(solution)/shard_map/ppermute | solution.py:985
  29.8 15.2 %collective-permute-done.2 = bf16[2,160,1024]{2,1,0:T(8,128)(2,1)S(1)} collective-permute-done((bf16[2,160,1024]{2,1,0:T(8,128)(2,1)S(1)}, bf16[2,160,1024]{2,1,0:T(8,128)(2,1)S(1)}, u32[]{:S(2)}, u32[]{:S(2)}) %collective-permute-start.2) | collective-permute-done | bytes 655392 | tf_op jit(solution)/shard_map/ppermute | solution.py:985
  47.9 3.1 shard_map.306
  51.0 24.1 %collective-permute-done.5 = bf16[4,160,1024]{2,1,0:T(8,128)(2,1)} collective-permute-done((bf16[4,160,1024]{2,1,0:T(8,128)(2,1)S(1)}, bf16[4,160,1024]{2,1,0:T(8,128)(2,1)}, u32[]{:S(2)}, u32[]{:S(2)}) %collective-permute-start.5) | collective-permute-done | bytes 1310752 | tf_op jit(solution)/shard_map/ppermute | solution.py:985
  78.9 4.3 collective-permute-start.1
  83.2 29.6 %collective-permute-done.1 = bf16[1,144,2048]{2,1,0:T(8,128)(2,1)} collective-permute-done((bf16[1,144,2048]{2,1,0:T(8,128)(2,1)S(1)}, bf16[1,144,2048]{2,1,0:T(8,128)(2,1)}, u32[]{:S(2)}, u32[]{:S(2)}) %collective-permute-start.1) | collective-permute-done | bytes 589856 | tf_op jit(solution)/shard_map/ppermute | solution.py:985
  115.9 46.3 %collective-permute-done.3 = bf16[2,144,2048]{2,1,0:T(8,128)(2,1)} collective-permute-done((bf16[2,144,2048]{2,1,0:T(8,128)(2,1)}, bf16[2,144,2048]{2,1,0:T(8,128)(2,1)}, u32[]{:S(2)}, u32[]{:S(2)}) %collective-permute-start.3) | collective-permute-done | bytes 1179680 | tf_op jit(solution)/shard_map/ppermute | solution.py:985
  165.0 3.3 pad_maximum_fusion.1
  176.8 4.5 fusion.3
  181.3 7.8 %shard_map.307 = bf16[8,144,1920]{2,1,0:T(8,128)(2,1)} custom-call(s32[8]{0:T(128)} %copy-done.45, s32[1]{0:T(128)} %bitcast.1.core_ref, bf16[8,160,1024]{2,1,0:T(8,128)(2,1)} %copy-done.4, bf16[8,160,1024]{2,1,0:T(8,128)(2,1)} %collective-permute-done.6.refs_1_), custom_call_target="tpu_custom_call" | custom-call | bytes 1179648 | tf_op jit(solution)/shard_map/pallas_call | solution.py:541
  189.1 12.0 %shard_map.308 = (bf16[1024,1920]{1,0:T(8,128)(2,1)}, bf16[1152,1024]{1,0:T(8,128)(2,1)}) custom-call(s32[8]{0:T(128)} %broadcast_xor_fusion.order_ref, bf16[1024,1152]{1,0:T(8,128)(2,1)} %get-tuple-element.279.x_ref, f32[1,1152]{1,0:T(1,128)} %slice.111.gain_ref, bf16[1152,1920]{1,0:T(8,128)(2,1)} %bitcast.127, f32[1024,128]{1,0:T(8,128)} %get-tuple-element.297.cos_ref, ...), custom_call_target="tpu_custom_call" | custom-call | flops 566231040 | bytes 1634304 | tf_op jit(solution)/shard_map/pallas_call | solution.py:88
  201.2 33.3 %shard_map.309 = (bf16[1024,1152]{1,0:T(8,128)(2,1)}, f32[3,1024,128]{2,1,0:T(8,128)}) custom-call(bf16[1024,1920]{1,0:T(8,128)(2,1)} %get-tuple-element.147.qkv_ref, s32[1024,1]{1,0:T(8,128)} %copy.40.pos_ref), custom_call_target="tpu_custom_call" | custom-call | flops 1006632960 | bytes 1966080 | tf_op jit(solution)/shard_map/pallas_call | solution.py:185
  234.5 3.4 constant_dynamic-update-slice_fusion.1
  237.8 3.6 constant_dynamic-update-slice_fusion.refs_2_.refs_3_
  241.4 22.9 %collective-permute-start.9 = (bf16[8,144,2048]{2,1,0:T(8,128)(2,1)}, bf16[8,144,2048]{2,1,0:T(8,128)(2,1)}, u32[]{:S(2)}, u32[]{:S(2)}) collective-permute-start(bf16[8,144,2048]{2,1,0:T(8,128)(2,1)} %constant_dynamic-update-slice_fusion.refs_2_.refs_3_), channel_id=1, source_target_pairs={{0,8},{1,9},{2,10},{3,11},{4,12},{5,13},{6,14},{7,15},{8,0},{9,1},... | collective-permute-start | bytes 14155784 | tf_op jit(solution)/shard_map/ppermute | solution.py:985
  264.3 2.6 collective-permute-start.10
  269.8 5.2 shard_map.311.refs_1_
  275.0 11.8 %shard_map.310 = (f32[1024,1152]{1,0:T(8,128)}, bf16[1024,1152]{1,0:T(8,128)(2,1)}, bf16[1152,1024]{1,0:T(8,128)(2,1)}, bf16[1152,1152]{1,0:T(8,128)(2,1)}) custom-call(s32[8]{0:T(128)} %copy-done.45, s32[1]{0:T(128)} %bitcast.1.core_ref, s32[8]{0:T(128)} %broadcast_xor_fusion.order_ref, bf16[1024,1152]{1,0:T(8,128)(2,1)} %get-tuple-element.148.att_ref, ...), custom_call_target="tpu_custom_call" | custom-call | flops 339738624 | bytes 2433024 | tf_op jit(solution)/shard_map/pallas_call | solution.py:930
  286.7 41.5 %shard_map.312 = (bf16[3,576,1024]{2,1,0:T(8,128)(2,1)}, bf16[3,576,1024]{2,1,0:T(8,128)(2,1)}, f32[1024,1152]{1,0:T(8,128)}, f32[1024,1152]{1,0:T(8,128)}) custom-call(s32[4]{0:T(128)} %and_select_fusion.slot_ref, s32[8]{0:T(128)} %copy-done.45, bf16[1024,1152]{1,0:T(8,128)(2,1)} %get-tuple-element.152.mid_ref, ...), custom_call_target="tpu_custom_call" | custom-call | flops 2717908992 | bytes 5308416 | tf_op jit(solution)/shard_map/pallas_call | solution.py:477
  328.2 28.2 %collective-permute-start.11 = (bf16[3,576,1024]{2,1,0:T(8,128)(2,1)}, bf16[3,576,1024]{2,1,0:T(8,128)(2,1)}, u32[]{:S(2)}, u32[]{:S(2)}) collective-permute-start(bf16[3,576,1024]{2,1,0:T(8,128)(2,1)} %get-tuple-element.164), channel_id=1, source_target_pairs={{0,8},{1,9},{2,10},{3,11},{4,12},{5,13},{6,14},{7,15},{8,0},{9,1},... | collective-permute-start | bytes 10616840 | tf_op jit(solution)/shard_map/ppermute | solution.py:985
  356.9 41.1 %shard_map.313 = (bf16[3,576,1024]{2,1,0:T(8,128)(2,1)}, bf16[3,576,1024]{2,1,0:T(8,128)(2,1)}, f32[1024,1152]{1,0:T(8,128)}, f32[1024,1152]{1,0:T(8,128)}) custom-call(s32[4]{0:T(128)} %iota.19.slot_ref, s32[1]{0:T(128)} %constant.120.clone.1.place_ref, bf16[1024,1152]{1,0:T(8,128)(2,1)} %get-tuple-element.152.mid_ref, ...), custom_call_target="tpu_custom_call" | custom-call | flops 2717908992 | bytes 5308416 | tf_op jit(solution)/shard_map/pallas_call | solution.py:477
  398.2 5.7 shard_map.314
  406.6 41.6 %shard_map.315 = (bf16[3,576,1024]{2,1,0:T(8,128)(2,1)}, bf16[3,576,1024]{2,1,0:T(8,128)(2,1)}, bf16[1024,1152]{1,0:T(8,128)(2,1)}, f32[1024,1152]{1,0:T(8,128)}) custom-call(s32[4]{0:T(128)} %iota.16.slot_ref, s32[1]{0:T(128)} %constant.120.clone.1.place_ref, bf16[1024,1152]{1,0:T(8,128)(2,1)} %get-tuple-element.152.mid_ref, ...), custom_call_target="tpu_custom_call" | custom-call | flops 2717908992 | bytes 5308416 | tf_op jit(solution)/shard_map/pallas_call | solution.py:477
  450.4 2.9 multiply_reduce_fusion.2
  453.3 4.0 shard_map.316
  457.4 2.9 collective-permute-start.16
  463.6 5.6 shard_map.317
  471.8 3.4 multiply_reduce_fusion
  475.2 4.1 fusion.35.rows_ref
  479.3 5.3 shard_map.318
  484.6 4.1 convolution_convert_fusion.2
  488.7 3.4 collective-permute-start.19
  492.7 5.9 shard_map.319
  500.3 6.4 convolution_convert_fusion.d_ref
  506.8 21.3 %shard_map.320 = (bf16[1024,640]{1,0:T(8,128)(2,1)}, bf16[576,640]{1,0:T(8,128)(2,1)}, bf16[576,640]{1,0:T(8,128)(2,1)}) custom-call(bf16[1024,1920]{1,0:T(8,128)(2,1)} %get-tuple-element.147.qkv_ref, bf16[1024,1152]{1,0:T(8,128)(2,1)} %convolution_convert_fusion.d_ref, f32[3,1024,128]{2,1,0:T(8,128)} %get-tuple-element.193.log_ref, ...), custom_call_target="tpu_custom_call" | custom-call | flops 838860800 | bytes 655360 | tf_op jit(solution)/shard_map/pallas_call | solution.py:297
  528.1 2.8 fusion.7.home_ref
  530.9 3.0 shard_map.322
  535.3 3.9 shard_map.321
  543.7 20.9 %shard_map.323 = (bf16[1024,640]{1,0:T(8,128)(2,1)}, bf16[576,640]{1,0:T(8,128)(2,1)}, bf16[576,640]{1,0:T(8,128)(2,1)}) custom-call(bf16[1024,1920]{1,0:T(8,128)(2,1)} %get-tuple-element.147.qkv_ref, bf16[1024,1152]{1,0:T(8,128)(2,1)} %convolution_convert_fusion.d_ref, f32[3,1024,128]{2,1,0:T(8,128)} %get-tuple-element.193.log_ref, ...), custom_call_target="tpu_custom_call" | custom-call | flops 838860800 | bytes 655360 | tf_op jit(solution)/shard_map/pallas_call | solution.py:297
  564.7 3.7 collective-permute-start.26
  576.5 11.5 %collective-permute-done.23.refs_3_ = bf16[3,144,1024]{2,1,0:T(8,128)(2,1)S(1)} collective-permute-done((bf16[3,144,1024]{2,1,0:T(8,128)(2,1)}, bf16[3,144,1024]{2,1,0:T(8,128)(2,1)S(1)}, u32[]{:S(2)}, u32[]{:S(2)}) %collective-permute-start.23) | collective-permute-done | bytes 884768 | tf_op jit(solution)/shard_map/ppermute | solution.py:985
  589.8 3.9 shard_map.324
  593.8 21.3 %shard_map.327 = (bf16[1024,640]{1,0:T(8,128)(2,1)}, bf16[576,640]{1,0:T(8,128)(2,1)}, bf16[576,640]{1,0:T(8,128)(2,1)}) custom-call(bf16[1024,1920]{1,0:T(8,128)(2,1)} %get-tuple-element.147.qkv_ref, bf16[1024,1152]{1,0:T(8,128)(2,1)} %convolution_convert_fusion.d_ref, f32[3,1024,128]{2,1,0:T(8,128)} %get-tuple-element.193.log_ref, ...), custom_call_target="tpu_custom_call" | custom-call | flops 838860800 | bytes 655360 | tf_op jit(solution)/shard_map/pallas_call | solution.py:297
  616.8 2.6 shard_map.334
  625.0 3.6 fusion.9
  628.7 3.6 convolution_add_fusion.1
  632.3 2.3 shard_map.330
  638.0 8.6 %shard_map.332 = (f32[3,144,3072]{2,1,0:T(8,128)}, f32[24,144]{1,0:T(8,128)}) custom-call(s32[1]{0:T(128)} %bitcast.52.flag_ref, bf16[3,144,1024]{2,1,0:T(8,128)(2,1)} %collective-permute-done.16.refs_0_, bf16[3,144,1024]{2,1,0:T(8,128)(2,1)} %get-tuple-element.178.refs_1_, bf16[3,144,1024]{2,1,0:T(8,128)(2,1)} %collective-permute-done.17.refs_2_, ...), custom_call_target="tpu_custom_call" | custom-call | flops 15925248 | bytes 2322432 | tf_op jit(solution)/shard_map/pallas_call | solution.py:603
  648.5 4.2 collective-permute-start.35
  661.9 6.0 shard_map.335
  668.9 2.7 collective-permute-start.37
  671.6 4.1 convolution_add_fusion
  678.1 2.4 collective-permute-done.38
  682.9 3.4 shard_map.337
  689.4 6.7 fusion.2
  700.6 2.6 shard_map.338
  708.5 2.7 collective-permute-done.51
  711.9 2.3 collective-permute-start.36
  716.9 16.0 %shard_map.336 = (f32[3,144,3072]{2,1,0:T(8,128)}, f32[3,144,3072]{2,1,0:T(8,128)}, f32[1,3,144,3072]{3,2,1,0:T(8,128)}, f32[3,8,3072]{2,1,0:T(8,128)}) custom-call(f32[8,11264]{1,0:T(8,128)} %pad_maximum_fusion.9.row_ref.gram_ref.refs_1_, f32[8,11264]{1,0:T(8,128)} %pad_maximum_fusion.9.row_ref.gram_ref.refs_1_, f32[32,144]{1,0:T(8,128)} %add.185.refs_0_.left_ref.refs_3_, ...), custom_call_target="tpu_custom_call" | custom-call | flops 15925248 | bytes 3981312 | tf_op jit(solution)/shard_map/pallas_call | solution.py:738
  733.1 10.0 %collective-permute-done.53 = f32[8,3584]{1,0:T(8,128)S(1)} collective-permute-done((f32[8,3584]{1,0:T(8,128)S(1)}, f32[8,3584]{1,0:T(8,128)S(1)}, u32[]{:S(2)}, u32[]{:S(2)}) %collective-permute-start.53) | collective-permute-done | bytes 114720 | tf_op jit(solution)/shard_map/ppermute | solution.py:985
  743.1 2.9 collective-permute-start.54
  746.0 4.8 collective-permute-done.54
  751.5 7.3 shard_map.339
  (298 shorter events, 104.1 us)
Async XLA Ops:
  7.2 349.2 %all-gather.3.cloned.1.call-start = ((), (), s32[]{:S(2)}) async-start(), calls=%async_computation | async-start | bytes 7299072 | tf_op jit(solution)/shard_map/all_gather | solution.py:1205
  10.1 18.8 %collective-permute-start = (bf16[1,160,1024]{2,1,0:T(8,128)(2,1)S(1)}, bf16[1,160,1024]{2,1,0:T(8,128)(2,1)S(1)}, u32[]{:S(2)}, u32[]{:S(2)}) collective-permute-start(bf16[1,160,1024]{2,1,0:T(8,128)(2,1)S(1)} %fusion.17), channel_id=1, source_target_pairs={{0,4},{1,5},{2,6},{3,7},{4,0},{5,1},{6,2},{7,3},{8,12},{9,13},{10,... | collective-permute-start | bytes 983048 | tf_op jit(solution)/shard_map/ppermute | solution.py:985
  29.0 16.0 %collective-permute-start.2 = (bf16[2,160,1024]{2,1,0:T(8,128)(2,1)S(1)}, bf16[2,160,1024]{2,1,0:T(8,128)(2,1)S(1)}, u32[]{:S(2)}, u32[]{:S(2)}) collective-permute-start(bf16[2,160,1024]{2,1,0:T(8,128)(2,1)S(1)} %pad_maximum_fusion.4), channel_id=1, source_target_pairs={{0,2},{1,3},{2,0},{3,1},{4,6},{5,7},{6,4},{7,5},{8,10},{9,11},{10,... | collective-permute-start | bytes 1966088 | tf_op jit(solution)/shard_map/ppermute | solution.py:985
  46.0 29.2 %collective-permute-start.5 = (bf16[4,160,1024]{2,1,0:T(8,128)(2,1)S(1)}, bf16[4,160,1024]{2,1,0:T(8,128)(2,1)}, u32[]{:S(2)}, u32[]{:S(2)}) collective-permute-start(bf16[4,160,1024]{2,1,0:T(8,128)(2,1)S(1)} %pad_maximum_fusion.2), channel_id=1, source_target_pairs={{0,1},{1,0},{2,3},{3,2},{4,5},{5,4},{6,7},{7,6},{8,9},{9,8},{10,11... | collective-permute-start | bytes 3932168 | tf_op jit(solution)/shard_map/ppermute | solution.py:985
  47.9 27.3 %copy-start.11 = (bf16[2,160,1024]{2,1,0:T(8,128)(2,1)S(1)}, bf16[2,160,1024]{2,1,0:T(8,128)(2,1)}, u32[]{:S(2)}) copy-start(bf16[2,160,1024]{2,1,0:T(8,128)(2,1)} %copy-done.10) | copy-start | bytes 1966084
  76.6 98.6 %copy-start.4 = (bf16[8,160,1024]{2,1,0:T(8,128)(2,1)}, bf16[8,160,1024]{2,1,0:T(8,128)(2,1)S(1)}, u32[]{:S(2)}) copy-start(bf16[8,160,1024]{2,1,0:T(8,128)(2,1)S(1)} %pad_maximum_fusion.refs_0_) | copy-start | bytes 7864324
  76.6 38.6 %copy-start.46 = (s32[1,1024]{1,0:T(1,128)S(1)}, s32[1,1024]{1,0:T(1,128)}, u32[]{:S(2)}) copy-start(s32[1,1024]{1,0:T(1,128)} %param.22) | copy-start | bytes 12292
  76.7 87.6 %copy-start = (s32[8]{0:T(128)S(1)}, s32[8]{0:T(128)}, u32[]{:S(2)}) copy-start(s32[8]{0:T(128)} %constant.143.clone) | copy-start | bytes 100
  76.7 329.4 %all-gather.5.cloned.1.call-start = ((), (), s32[]{:S(2)}) async-start(), calls=%async_computation.1 | async-start | bytes 7299072 | tf_op jit(solution)/shard_map/all_gather | solution.py:1205
  78.9 33.9 %collective-permute-start.1 = (bf16[1,144,2048]{2,1,0:T(8,128)(2,1)S(1)}, bf16[1,144,2048]{2,1,0:T(8,128)(2,1)}, u32[]{:S(2)}, u32[]{:S(2)}) collective-permute-start(bf16[1,144,2048]{2,1,0:T(8,128)(2,1)S(1)} %maximum_bitcast_fusion), channel_id=1, source_target_pairs={{0,4},{1,5},{2,6},{3,7},{4,0},{5,1},{6,2},{7,3},{8,12},{9,13},{10,... | collective-permute-start | bytes 1769480 | tf_op jit(solution)/shard_map/ppermute | solution.py:985
  115.1 47.2 %collective-permute-start.3 = (bf16[2,144,2048]{2,1,0:T(8,128)(2,1)}, bf16[2,144,2048]{2,1,0:T(8,128)(2,1)}, u32[]{:S(2)}, u32[]{:S(2)}) collective-permute-start(bf16[2,144,2048]{2,1,0:T(8,128)(2,1)} %pad_maximum_fusion.3), channel_id=1, source_target_pairs={{0,2},{1,3},{2,0},{3,1},{4,6},{5,7},{6,4},{7,5},{8,10},{9,11},{10,... | collective-permute-start | bytes 3538952 | tf_op jit(solution)/shard_map/ppermute | solution.py:985
  115.2 55.2 %collective-permute-start.7 = (s32[1,1024]{1,0:T(1,128)S(1)}, s32[1,1024]{1,0:T(1,128)S(1)}, u32[]{:S(2)}, u32[]{:S(2)}) collective-permute-start(s32[1,1024]{1,0:T(1,128)S(1)} %copy-done.46), channel_id=1, source_target_pairs={{2,8},{3,9},{6,12},{7,13},{8,2},{9,3},{12,6},{13,7},{18,24},{19,25... | collective-permute-start | bytes 12296 | tf_op jit(solution)/shard_map/ppermute | solution.py:985
  162.2 14.6 %collective-permute-start.4 = (bf16[1,1024,1152]{2,1,0:T(8,128)(2,1)}, bf16[1,1024,1152]{2,1,0:T(8,128)(2,1)}, u32[]{:S(2)}, u32[]{:S(2)}) collective-permute-start(bf16[1,1024,1152]{2,1,0:T(8,128)(2,1)} %param.20), channel_id=1, source_target_pairs={{2,8},{3,9},{6,12},{7,13},{8,2},{9,3},{12,6},{13,7},{18,24},{19,25... | collective-permute-start | bytes 7077896 | tf_op jit(solution)/shard_map/ppermute | solution.py:985
  164.9 16.4 %collective-permute-start.6 = (bf16[8,160,1024]{2,1,0:T(8,128)(2,1)S(1)}, bf16[8,160,1024]{2,1,0:T(8,128)(2,1)}, u32[]{:S(2)}, u32[]{:S(2)}) collective-permute-start(bf16[8,160,1024]{2,1,0:T(8,128)(2,1)S(1)} %pad_maximum_fusion.refs_0_), channel_id=1, source_target_pairs={{0,8},{1,9},{2,10},{3,11},{4,12},{5,13},{6,14},{7,15},{8,0},{9,1},... | collective-permute-start | bytes 7864328 | tf_op jit(solution)/shard_map/ppermute | solution.py:985
  168.3 66.2 %collective-permute-start.8 = (bf16[4,144,2048]{2,1,0:T(8,128)(2,1)}, bf16[4,144,2048]{2,1,0:T(8,128)(2,1)}, u32[]{:S(2)}, u32[]{:S(2)}) collective-permute-start(bf16[4,144,2048]{2,1,0:T(8,128)(2,1)} %pad_maximum_fusion.1), channel_id=1, source_target_pairs={{0,1},{1,0},{2,3},{3,2},{4,5},{5,4},{6,7},{7,6},{8,9},{9,8},{10,11... | collective-permute-start | bytes 7077896 | tf_op jit(solution)/shard_map/ppermute | solution.py:985
  176.1 91.3 %copy-start.30 = (f32[8,144]{1,0:T(8,128)}, f32[8,144]{1,0:T(8,128)S(1)}, u32[]{:S(2)}) copy-start(f32[8,144]{1,0:T(8,128)S(1)} %get-tuple-element.274) | copy-start | bytes 13828
  241.4 33.6 %collective-permute-start.9 = (bf16[8,144,2048]{2,1,0:T(8,128)(2,1)}, bf16[8,144,2048]{2,1,0:T(8,128)(2,1)}, u32[]{:S(2)}, u32[]{:S(2)}) collective-permute-start(bf16[8,144,2048]{2,1,0:T(8,128)(2,1)} %constant_dynamic-update-slice_fusion.refs_2_.refs_3_), channel_id=1, source_target_pairs={{0,8},{1,9},{2,10},{3,11},{4,12},{5,13},{6,14},{7,15},{8,0},{9,1},... | collective-permute-start | bytes 14155784 | tf_op jit(solution)/shard_map/ppermute | solution.py:985
  264.3 3.8 collective-permute-start.10
  328.2 70.0 %collective-permute-start.11 = (bf16[3,576,1024]{2,1,0:T(8,128)(2,1)}, bf16[3,576,1024]{2,1,0:T(8,128)(2,1)}, u32[]{:S(2)}, u32[]{:S(2)}) collective-permute-start(bf16[3,576,1024]{2,1,0:T(8,128)(2,1)} %get-tuple-element.164), channel_id=1, source_target_pairs={{0,8},{1,9},{2,10},{3,11},{4,12},{5,13},{6,14},{7,15},{8,0},{9,1},... | collective-permute-start | bytes 10616840 | tf_op jit(solution)/shard_map/ppermute | solution.py:985
  398.1 63.8 %collective-permute-start.13 = (bf16[3,576,1024]{2,1,0:T(8,128)(2,1)}, bf16[3,576,1024]{2,1,0:T(8,128)(2,1)S(1)}, u32[]{:S(2)}, u32[]{:S(2)}) collective-permute-start(bf16[3,576,1024]{2,1,0:T(8,128)(2,1)} %get-tuple-element.165), channel_id=1, source_target_pairs={{0,8},{1,9},{2,10},{3,11},{4,12},{5,13},{6,14},{7,15},{8,0},{9,1},... | collective-permute-start | bytes 10616840 | tf_op jit(solution)/shard_map/ppermute | solution.py:985
  403.9 49.5 %collective-permute-start.12 = (bf16[3,288,1024]{2,1,0:T(8,128)(2,1)}, bf16[3,288,1024]{2,1,0:T(8,128)(2,1)}, u32[]{:S(2)}, u32[]{:S(2)}) collective-permute-start(bf16[3,288,1024]{2,1,0:T(8,128)(2,1)} %get-tuple-element.167), channel_id=1, source_target_pairs={{0,1},{1,0},{2,3},{3,2},{4,5},{5,4},{6,7},{7,6},{8,9},{9,8},{10,11... | collective-permute-start | bytes 5308424 | tf_op jit(solution)/shard_map/ppermute | solution.py:985
  406.6 41.8 %copy-start.17 = (f32[1,2,144,1152]{3,2,1,0:T(8,128)S(1)}, f32[1,2,144,1152]{3,2,1,0:T(8,128)}, u32[]{:S(2)}) copy-start(f32[1,2,144,1152]{3,2,1,0:T(8,128)} %param.30) | copy-start | bytes 3981316
  448.2 40.5 %collective-permute-start.15 = (bf16[3,576,1024]{2,1,0:T(8,128)(2,1)}, bf16[3,576,1024]{2,1,0:T(8,128)(2,1)}, u32[]{:S(2)}, u32[]{:S(2)}) collective-permute-start(bf16[3,576,1024]{2,1,0:T(8,128)(2,1)} %get-tuple-element.175), channel_id=1, source_target_pairs={{0,8},{1,9},{2,10},{3,11},{4,12},{5,13},{6,14},{7,15},{8,0},{9,1},... | collective-permute-start | bytes 10616840 | tf_op jit(solution)/shard_map/ppermute | solution.py:985
  457.4 42.3 %collective-permute-start.16 = (bf16[3,144,1024]{2,1,0:T(8,128)(2,1)}, bf16[3,144,1024]{2,1,0:T(8,128)(2,1)}, u32[]{:S(2)}, u32[]{:S(2)}) collective-permute-start(bf16[3,144,1024]{2,1,0:T(8,128)(2,1)} %get-tuple-element.177), channel_id=1, source_target_pairs={{0,4},{1,5},{2,12},{3,13},{4,0},{5,1},{6,8},{7,9},{8,6},{9,7},{10,... | collective-permute-start | bytes 2654216 | tf_op jit(solution)/shard_map/ppermute | solution.py:985
  460.2 46.6 %collective-permute-start.17 = (bf16[3,144,1024]{2,1,0:T(8,128)(2,1)}, bf16[3,144,1024]{2,1,0:T(8,128)(2,1)}, u32[]{:S(2)}, u32[]{:S(2)}) collective-permute-start(bf16[3,144,1024]{2,1,0:T(8,128)(2,1)} %get-tuple-element.178.refs_1_), channel_id=1, source_target_pairs={{2,8},{3,9},{6,12},{7,13},{8,2},{9,3},{12,6},{13,7},{18,24},{19,25... | collective-permute-start | bytes 2654216 | tf_op jit(solution)/shard_map/ppermute | solution.py:985
  469.3 66.0 %collective-permute-start.18 = (bf16[3,288,1024]{2,1,0:T(8,128)(2,1)}, bf16[3,288,1024]{2,1,0:T(8,128)(2,1)}, u32[]{:S(2)}, u32[]{:S(2)}) collective-permute-start(bf16[3,288,1024]{2,1,0:T(8,128)(2,1)} %get-tuple-element.183), channel_id=1, source_target_pairs={{0,1},{1,0},{2,3},{3,2},{4,5},{5,4},{6,7},{7,6},{8,9},{9,8},{10,11... | collective-permute-start | bytes 5308424 | tf_op jit(solution)/shard_map/ppermute | solution.py:985
  469.6 70.9 %collective-permute-start.14 = (bf16[1,1024,1152]{2,1,0:T(8,128)(2,1)}, bf16[1,1024,1152]{2,1,0:T(8,128)(2,1)}, u32[]{:S(2)}, u32[]{:S(2)}) collective-permute-start(bf16[1,1024,1152]{2,1,0:T(8,128)(2,1)} %bitcast.134), channel_id=1, source_target_pairs={{2,8},{3,9},{6,12},{7,13},{8,2},{9,3},{12,6},{13,7},{18,24},{19,25... | collective-permute-start | bytes 7077896 | tf_op jit(solution)/shard_map/ppermute | solution.py:985
  488.7 42.2 %collective-permute-start.19 = (bf16[576,1152]{1,0:T(8,128)(2,1)}, bf16[576,1152]{1,0:T(8,128)(2,1)}, u32[]{:S(2)}, u32[]{:S(2)}) collective-permute-start(bf16[576,1152]{1,0:T(8,128)(2,1)} %convolution_convert_fusion.2), channel_id=1, source_target_pairs={{0,8},{1,9},{2,10},{3,11},{4,12},{5,13},{6,14},{7,15},{8,0},{9,1},... | collective-permute-start | bytes 3981320 | tf_op jit(solution)/shard_map/ppermute | solution.py:985
  499.7 75.4 %collective-permute-start.20 = (bf16[3,288,1024]{2,1,0:T(8,128)(2,1)}, bf16[3,288,1024]{2,1,0:T(8,128)(2,1)}, u32[]{:S(2)}, u32[]{:S(2)}) collective-permute-start(bf16[3,288,1024]{2,1,0:T(8,128)(2,1)} %get-tuple-element.190), channel_id=1, source_target_pairs={{0,1},{1,0},{2,3},{3,2},{4,5},{5,4},{6,7},{7,6},{8,9},{9,8},{10,11... | collective-permute-start | bytes 5308424 | tf_op jit(solution)/shard_map/ppermute | solution.py:985
  528.1 43.3 %collective-permute-start.22 = (bf16[576,640]{1,0:T(8,128)(2,1)}, bf16[576,640]{1,0:T(8,128)(2,1)}, u32[]{:S(2)}, u32[]{:S(2)}) collective-permute-start(bf16[576,640]{1,0:T(8,128)(2,1)} %get-tuple-element.202), channel_id=1, source_target_pairs={{0,8},{1,9},{2,10},{3,11},{4,12},{5,13},{6,14},{7,15},{8,0},{9,1},... | collective-permute-start | bytes 2211848 | tf_op jit(solution)/shard_map/ppermute | solution.py:985
  533.9 30.7 %collective-permute-start.21 = (bf16[288,1152]{1,0:T(8,128)(2,1)}, bf16[288,1152]{1,0:T(8,128)(2,1)S(1)}, u32[]{:S(2)}, u32[]{:S(2)}) collective-permute-start(bf16[288,1152]{1,0:T(8,128)(2,1)} %bitcast.148), channel_id=1, source_target_pairs={{0,1},{1,0},{2,3},{3,2},{4,5},{5,4},{6,7},{7,6},{8,9},{9,8},{10,11... | collective-permute-start | bytes 1990664 | tf_op jit(solution)/shard_map/ppermute | solution.py:985
  539.2 48.8 %collective-permute-start.23 = (bf16[3,144,1024]{2,1,0:T(8,128)(2,1)}, bf16[3,144,1024]{2,1,0:T(8,128)(2,1)S(1)}, u32[]{:S(2)}, u32[]{:S(2)}) collective-permute-start(bf16[3,144,1024]{2,1,0:T(8,128)(2,1)} %get-tuple-element.197), channel_id=1, source_target_pairs={{0,4},{1,5},{2,12},{3,13},{4,0},{5,1},{6,8},{7,9},{8,6},{9,7},{10,... | collective-permute-start | bytes 2654216 | tf_op jit(solution)/shard_map/ppermute | solution.py:985
  540.4 53.3 %collective-permute-start.24 = (bf16[3,144,1024]{2,1,0:T(8,128)(2,1)}, bf16[3,144,1024]{2,1,0:T(8,128)(2,1)}, u32[]{:S(2)}, u32[]{:S(2)}) collective-permute-start(bf16[3,144,1024]{2,1,0:T(8,128)(2,1)} %get-tuple-element.198.refs_4_), channel_id=1, source_target_pairs={{2,8},{3,9},{6,12},{7,13},{8,2},{9,3},{12,6},{13,7},{18,24},{19,25... | collective-permute-start | bytes 2654216 | tf_op jit(solution)/shard_map/ppermute | solution.py:985
  564.7 56.6 %collective-permute-start.26 = (bf16[576,640]{1,0:T(8,128)(2,1)}, bf16[576,640]{1,0:T(8,128)(2,1)}, u32[]{:S(2)}, u32[]{:S(2)}) collective-permute-start(bf16[576,640]{1,0:T(8,128)(2,1)} %get-tuple-element.216), channel_id=1, source_target_pairs={{0,8},{1,9},{2,10},{3,11},{4,12},{5,13},{6,14},{7,15},{8,0},{9,1},... | collective-permute-start | bytes 2211848 | tf_op jit(solution)/shard_map/ppermute | solution.py:985
  571.4 43.8 %collective-permute-start.27 = (bf16[144,1152]{1,0:T(8,128)(2,1)}, bf16[144,1152]{1,0:T(8,128)(2,1)}, u32[]{:S(2)}, u32[]{:S(2)}) collective-permute-start(bf16[144,1152]{1,0:T(8,128)(2,1)} %bitcast.152), channel_id=1, source_target_pairs={{0,4},{1,5},{2,12},{3,13},{4,0},{5,1},{6,8},{7,9},{8,6},{9,7},{10,... | collective-permute-start | bytes 995336 | tf_op jit(solution)/shard_map/ppermute | solution.py:985
  575.1 40.9 %collective-permute-start.28 = (bf16[144,1152]{1,0:T(8,128)(2,1)}, bf16[144,1152]{1,0:T(8,128)(2,1)}, u32[]{:S(2)}, u32[]{:S(2)}) collective-permute-start(bf16[144,1152]{1,0:T(8,128)(2,1)} %bitcast.139), channel_id=1, source_target_pairs={{2,8},{3,9},{6,12},{7,13},{8,2},{9,3},{12,6},{13,7},{18,24},{19,25... | collective-permute-start | bytes 995336 | tf_op jit(solution)/shard_map/ppermute | solution.py:985
  588.0 31.4 %collective-permute-start.25 = (bf16[288,640]{1,0:T(8,128)(2,1)}, bf16[288,640]{1,0:T(8,128)(2,1)}, u32[]{:S(2)}, u32[]{:S(2)}) collective-permute-start(bf16[288,640]{1,0:T(8,128)(2,1)} %bitcast.149), channel_id=1, source_target_pairs={{0,1},{1,0},{2,3},{3,2},{4,5},{5,4},{6,7},{7,6},{8,9},{9,8},{10,11... | collective-permute-start | bytes 1105928 | tf_op jit(solution)/shard_map/ppermute | solution.py:985
  589.2 87.1 %copy-start.31 = (f32[1152]{0:T(1024)}, f32[1152]{0:T(1024)S(1)}, u32[]{:S(2)}) copy-start(f32[1152]{0:T(1024)S(1)} %mul.160) | copy-start | bytes 13828
  593.8 43.3 %collective-permute-start.29 = (bf16[3,144,1024]{2,1,0:T(8,128)(2,1)}, bf16[3,144,1024]{2,1,0:T(8,128)(2,1)}, u32[]{:S(2)}, u32[]{:S(2)}) collective-permute-start(bf16[3,144,1024]{2,1,0:T(8,128)(2,1)} %get-tuple-element.207), channel_id=1, source_target_pairs={{0,4},{1,5},{2,12},{3,13},{4,0},{5,1},{6,8},{7,9},{8,6},{9,7},{10,... | collective-permute-start | bytes 2654216 | tf_op jit(solution)/shard_map/ppermute | solution.py:985
  615.1 21.9 %collective-permute-start.30 = (bf16[3,144,1024]{2,1,0:T(8,128)(2,1)}, bf16[3,144,1024]{2,1,0:T(8,128)(2,1)S(1)}, u32[]{:S(2)}, u32[]{:S(2)}) collective-permute-start(bf16[3,144,1024]{2,1,0:T(8,128)(2,1)} %get-tuple-element.208.refs_7_), channel_id=1, source_target_pairs={{2,8},{3,9},{6,12},{7,13},{8,2},{9,3},{12,6},{13,7},{18,24},{19,25... | collective-permute-start | bytes 2654216 | tf_op jit(solution)/shard_map/ppermute | solution.py:985
  616.0 16.3 %collective-permute-start.31 = (bf16[576,640]{1,0:T(8,128)(2,1)}, bf16[576,640]{1,0:T(8,128)(2,1)}, u32[]{:S(2)}, u32[]{:S(2)}) collective-permute-start(bf16[576,640]{1,0:T(8,128)(2,1)} %get-tuple-element.227), channel_id=1, source_target_pairs={{0,8},{1,9},{2,10},{3,11},{4,12},{5,13},{6,14},{7,15},{8,0},{9,1},... | collective-permute-start | bytes 2211848 | tf_op jit(solution)/shard_map/ppermute | solution.py:985
  623.6 11.6 %collective-permute-start.32 = (bf16[288,640]{1,0:T(8,128)(2,1)}, bf16[288,640]{1,0:T(8,128)(2,1)}, u32[]{:S(2)}, u32[]{:S(2)}) collective-permute-start(bf16[288,640]{1,0:T(8,128)(2,1)} %bitcast.151), channel_id=1, source_target_pairs={{0,1},{1,0},{2,3},{3,2},{4,5},{5,4},{6,7},{7,6},{8,9},{9,8},{10,11... | collective-permute-start | bytes 1105928 | tf_op jit(solution)/shard_map/ppermute | solution.py:985
  634.6 22.3 %collective-permute-start.33 = (bf16[288,640]{1,0:T(8,128)(2,1)}, bf16[288,640]{1,0:T(8,128)(2,1)}, u32[]{:S(2)}, u32[]{:S(2)}) collective-permute-start(bf16[288,640]{1,0:T(8,128)(2,1)} %bitcast.150), channel_id=1, source_target_pairs={{0,1},{1,0},{2,3},{3,2},{4,5},{5,4},{6,7},{7,6},{8,9},{9,8},{10,11... | collective-permute-start | bytes 1105928 | tf_op jit(solution)/shard_map/ppermute | solution.py:985
  647.3 1.2 collective-permute-start.34
  648.5 7.7 %collective-permute-start.35 = (f32[32,144]{1,0:T(8,128)S(1)}, f32[32,144]{1,0:T(8,128)S(1)}, u32[]{:S(2)}, u32[]{:S(2)}) collective-permute-start(f32[32,144]{1,0:T(8,128)S(1)} %add.184), channel_id=1, source_target_pairs={{0,16},{1,17},{2,18},{3,19},{4,20},{5,21},{6,22},{7,23},{8,24},{9,... | collective-permute-start | bytes 55304 | tf_op jit(solution)/shard_map/ppermute | solution.py:985
  654.4 27.6 %collective-permute-start.45 = (bf16[144,1280]{1,0:T(8,128)(2,1)S(1)}, bf16[144,1280]{1,0:T(8,128)(2,1)S(1)}, u32[]{:S(2)}, u32[]{:S(2)}) collective-permute-start(bf16[144,1280]{1,0:T(8,128)(2,1)S(1)} %pad_maximum_fusion.8.refs_1_), channel_id=1, source_target_pairs={{2,8},{3,9},{6,12},{7,13},{8,2},{9,3},{12,6},{13,7},{18,24},{19,25... | collective-permute-start | bytes 1105928 | tf_op jit(solution)/shard_map/ppermute | solution.py:985
  655.1 27.0 %collective-permute-start.44 = (bf16[144,1280]{1,0:T(8,128)(2,1)}, bf16[144,1280]{1,0:T(8,128)(2,1)S(1)}, u32[]{:S(2)}, u32[]{:S(2)}) collective-permute-start(bf16[144,1280]{1,0:T(8,128)(2,1)} %pad_maximum_fusion.7), channel_id=1, source_target_pairs={{0,4},{1,5},{2,12},{3,13},{4,0},{5,1},{6,8},{7,9},{8,6},{9,7},{10,... | collective-permute-start | bytes 1105928 | tf_op jit(solution)/shard_map/ppermute | solution.py:985
  658.8 23.3 %collective-permute-start.46 = (bf16[144,640]{1,0:T(8,128)(2,1)}, bf16[144,640]{1,0:T(8,128)(2,1)}, u32[]{:S(2)}, u32[]{:S(2)}) collective-permute-start(bf16[144,640]{1,0:T(8,128)(2,1)} %bitcast.153), channel_id=1, source_target_pairs={{0,4},{1,5},{2,12},{3,13},{4,0},{5,1},{6,8},{7,9},{8,6},{9,7},{10,... | collective-permute-start | bytes 552968 | tf_op jit(solution)/shard_map/ppermute | solution.py:985
  660.6 21.5 %collective-permute-start.47 = (bf16[144,640]{1,0:T(8,128)(2,1)}, bf16[144,640]{1,0:T(8,128)(2,1)}, u32[]{:S(2)}, u32[]{:S(2)}) collective-permute-start(bf16[144,640]{1,0:T(8,128)(2,1)} %bitcast.142), channel_id=1, source_target_pairs={{2,8},{3,9},{6,12},{7,13},{8,2},{9,3},{12,6},{13,7},{18,24},{19,25... | collective-permute-start | bytes 552968 | tf_op jit(solution)/shard_map/ppermute | solution.py:985
  668.9 6.8 collective-permute-start.37
  675.9 4.6 collective-permute-start.38
  680.5 5.7 collective-permute-start.39
  686.2 9.8 %collective-permute-start.48 = (f32[24,144]{1,0:T(8,128)}, f32[24,144]{1,0:T(8,128)S(1)}, u32[]{:S(2)}, u32[]{:S(2)}) collective-permute-start(f32[24,144]{1,0:T(8,128)} %get-tuple-element.253), channel_id=1, source_target_pairs={{0,8},{1,9},{2,10},{3,11},{4,12},{5,13},{6,14},{7,15},{8,0},{9,1},... | collective-permute-start | bytes 41480 | tf_op jit(solution)/shard_map/ppermute | solution.py:985
  687.2 9.3 %collective-permute-start.40 = (f32[8,2816]{1,0:T(8,128)S(1)}, f32[8,2816]{1,0:T(8,128)S(1)}, u32[]{:S(2)}, u32[]{:S(2)}) collective-permute-start(f32[8,2816]{1,0:T(8,128)S(1)} %add.192), channel_id=1, source_target_pairs={{0,2},{1,3},{2,0},{3,1},{4,6},{5,7},{6,4},{7,5},{8,10},{9,11},{10,... | collective-permute-start | bytes 270344 | tf_op jit(solution)/shard_map/ppermute | solution.py:985
  696.1 3.9 collective-permute-start.49
  696.5 7.1 collective-permute-start.41
  703.2 2.3 collective-permute-start.50
  703.7 4.7 collective-permute-start.42
  706.4 4.9 collective-permute-start.51
  708.4 7.7 %collective-permute-start.43 = (f32[8,5632]{1,0:T(8,128)S(1)}, f32[8,5632]{1,0:T(8,128)S(1)}, u32[]{:S(2)}, u32[]{:S(2)}) collective-permute-start(f32[8,5632]{1,0:T(8,128)S(1)} %pad_maximum_fusion.10), channel_id=1, source_target_pairs={{0,8},{1,9},{2,10},{3,11},{4,12},{5,13},{6,14},{7,15},{8,0},{9,1},... | collective-permute-start | bytes 540680 | tf_op jit(solution)/shard_map/ppermute | solution.py:985
  711.2 4.9 collective-permute-start.52
  711.9 47.6 %collective-permute-start.36 = (bf16[1,1024,1152]{2,1,0:T(8,128)(2,1)S(1)}, bf16[1,1024,1152]{2,1,0:T(8,128)(2,1)}, u32[]{:S(2)}, u32[]{:S(2)}) collective-permute-start(bf16[1,1024,1152]{2,1,0:T(8,128)(2,1)S(1)} %bitcast.131), channel_id=1, source_target_pairs={{2,8},{3,9},{6,12},{7,13},{8,2},{9,3},{12,6},{13,7},{18,24},{19,25... | collective-permute-start | bytes 7077896 | tf_op jit(solution)/shard_map/ppermute | solution.py:985
  732.9 10.2 %collective-permute-start.53 = (f32[8,3584]{1,0:T(8,128)S(1)}, f32[8,3584]{1,0:T(8,128)S(1)}, u32[]{:S(2)}, u32[]{:S(2)}) collective-permute-start(f32[8,3584]{1,0:T(8,128)S(1)} %add.199), channel_id=1, source_target_pairs={{0,2},{1,3},{2,0},{3,1},{4,6},{5,7},{6,4},{7,5},{8,10},{9,11},{10,... | collective-permute-start | bytes 344072 | tf_op jit(solution)/shard_map/ppermute | solution.py:985
  743.1 7.7 %collective-permute-start.54 = (f32[8,3584]{1,0:T(8,128)S(1)}, f32[8,3584]{1,0:T(8,128)S(1)}, u32[]{:S(2)}, u32[]{:S(2)}) collective-permute-start(f32[8,3584]{1,0:T(8,128)S(1)} %add.200), channel_id=1, source_target_pairs={{0,4},{1,5},{2,6},{3,7},{4,0},{5,1},{6,2},{7,3},{8,12},{9,13},{10,... | collective-permute-start | bytes 344072 | tf_op jit(solution)/shard_map/ppermute | solution.py:985
  (47 other events, 514.9 us)
Sparse Core Ops, SparseCore 0:
  76.8 97.7 all-gather.2
  178.1 77.1 all-gather.4

commit v4 on v3

--- a/solution.py
+++ b/solution.py
@@ -108,7 +108,7 @@
             jax.ShapeDtypeStruct((width, rows), jnp.bfloat16),
         ],
         compiler_params=pltpu.CompilerParams(vmem_limit_bytes=VMEM_BYTES),
-        cost_estimate=light(
+        cost_estimate=pl.CostEstimate(
             flops=2 * rows * width * columns,
             bytes_accessed=2 * (rows * width * 2 + rows * columns + width * columns),
             transcendentals=0,
@@ -202,7 +202,7 @@
             pltpu.VMEM((4, rows, 128), jnp.bfloat16),
         ],
         compiler_params=pltpu.CompilerParams(vmem_limit_bytes=VMEM_BYTES),
-        cost_estimate=light(
+        cost_estimate=pl.CostEstimate(
             flops=20 * pairs * rows * rows * 128,
             bytes_accessed=8 * rows * 640 * pairs,
             transcendentals=6 * pairs * rows * rows,
@@ -319,7 +319,7 @@
             pltpu.VMEM((128, rows), jnp.float32),
         ],
         compiler_params=pltpu.CompilerParams(vmem_limit_bytes=VMEM_BYTES),
-        cost_estimate=light(
+        cost_estimate=pl.CostEstimate(
             flops=50 * rows * rows * 128,
             bytes_accessed=8 * rows * 640,
             transcendentals=6 * rows * rows,
@@ -351,7 +351,7 @@
         ),
         out_shape=jax.ShapeDtypeStruct((model, count), jnp.bfloat16),
         compiler_params=pltpu.CompilerParams(vmem_limit_bytes=VMEM_BYTES),
-        cost_estimate=light(
+        cost_estimate=pl.CostEstimate(
             flops=0, bytes_accessed=4 * count * model, transcendentals=0
         ),
     )(order, rows)
@@ -504,7 +504,7 @@
             jax.ShapeDtypeStruct((count, model), jnp.float32),
         ],
         compiler_params=pltpu.CompilerParams(vmem_limit_bytes=VMEM_BYTES),
-        cost_estimate=light(
+        cost_estimate=pl.CostEstimate(
             flops=18 * count * model * units,
             bytes_accessed=2 * (4 * count * model + 6 * model * units) + 16 * count * model,
             transcendentals=count * units,
@@ -548,7 +548,7 @@
         ),
         out_shape=jax.ShapeDtypeStruct((owners, rows, high - low), jnp.bfloat16),
         compiler_params=pltpu.CompilerParams(vmem_limit_bytes=VMEM_BYTES),
-        cost_estimate=light(
+        cost_estimate=pl.CostEstimate(
             flops=0, bytes_accessed=8 * owners * rows * sum(widths), transcendentals=0
         ),
     )(places, core, *mine, *other)
@@ -620,7 +620,7 @@
             jax.ShapeDtypeStruct((8 * count, rows), jnp.float32),
         ],
         compiler_params=pltpu.CompilerParams(vmem_limit_bytes=VMEM_BYTES),
-        cost_estimate=light(
+        cost_estimate=pl.CostEstimate(
             flops=96 * count * rows * columns,
             bytes_accessed=14 * count * rows * columns,
             transcendentals=0,
@@ -643,7 +643,7 @@
         out_shape=[jax.ShapeDtypeStruct(e.shape, jnp.float32) for e in errors]
         + [jax.ShapeDtypeStruct((8 * len(errors), rows), jnp.float32)],
         compiler_params=pltpu.CompilerParams(vmem_limit_bytes=VMEM_BYTES),
-        cost_estimate=light(
+        cost_estimate=pl.CostEstimate(
             flops=96 * sum(e.size for e in errors),
             bytes_accessed=14 * sum(e.size for e in errors),
             transcendentals=0,
@@ -677,7 +677,7 @@
         out_specs=pl.BlockSpec(memory_space=pltpu.VMEM),
         out_shape=jax.ShapeDtypeStruct((8, width), jnp.float32),
         compiler_params=pltpu.CompilerParams(vmem_limit_bytes=VMEM_BYTES),
-        cost_estimate=light(
+        cost_estimate=pl.CostEstimate(
             flops=96 * sum(m.size for m in mixed),
             bytes_accessed=4 * sum(m.size for m in mixed),
             transcendentals=0,
@@ -849,7 +849,7 @@
         ),
         out_shape=shapes,
         compiler_params=pltpu.CompilerParams(vmem_limit_bytes=VMEM_BYTES),
-        cost_estimate=light(
+        cost_estimate=pl.CostEstimate(
             flops=0, bytes_accessed=6 * number * count * rows * tile, transcendentals=0
         ),
     )(picks, *[master] * number)
@@ -876,7 +876,7 @@
         out_specs=[part, part],
         out_shape=[out, out],
         compiler_params=pltpu.CompilerParams(vmem_limit_bytes=VMEM_BYTES),
-        cost_estimate=light(
+        cost_estimate=pl.CostEstimate(
             flops=home.size, bytes_accessed=6 * home.size, transcendentals=0
         ),
     )(home.reshape(lead, rows, columns), got.reshape(lead, rows, columns))
@@ -952,7 +952,7 @@
             jax.ShapeDtypeStruct((model, model), jnp.bfloat16),
         ],
         compiler_params=pltpu.CompilerParams(vmem_limit_bytes=VMEM_BYTES),
-        cost_estimate=light(
+        cost_estimate=pl.CostEstimate(
             flops=2 * count * model * model,
             bytes_accessed=12 * count * model + 4 * model * model,
             transcendentals=count,
@@ -1201,14 +1201,13 @@
     qkv, turned_in = project_qkv(order, tokens, gain_attn[None], qkv_w, cos, sin)
     wide_parts = [None] * chained
     for k in range(chained, 3):
-        part = after(cuts[k], mine[0])
+        part = after(cuts[k], gathering[1])
         part = lax.all_gather(part, ("rep", "shard"), axis=0, tiled=True)
         wide_parts.append((natural, whole, [part.reshape(reps, owners * rows, 3 * tile)]))
     attended, logs = attend_forward(qkv, place)
     held, got = after((mine[1], gathering[-1]), attended)
     mine[1] = jnp.concatenate([held, got], axis=0)
     other.append(grid.move(mine[1], grid.flip_rep(0)))
-    d_out = jnp.where(grid.stays(), cotangent, after(moved_out, attended))[0]
     if chained:
         slots = (natural + core * (reps // 2)) % reps
         wide_parts[0] = (slots, places, [mine[1], other[1]])
@@ -1228,6 +1227,7 @@
         )
         normed_mid = normed(residual, gain_mlp).astype(jnp.bfloat16)
         turned_mid = turn_rows(normed_mid, order)
+    d_out = jnp.where(grid.stays(), cotangent, after(moved_out, normed_mid))[0]
     turned_out = turn_rows(d_out, order)
 
     half = model // 2
@@ -1362,10 +1362,10 @@
     wide_new, wide_moment_new, wide_error_new, factor_wide = finish_wide(
         reps, early, gram_early, left_early, mixed_wide, wide_moment, wide_master
     )
-    summed = butterfly(grid, summed, rep_moves + [grid.flip_shard(0)])
+    shard_moves = [grid.flip_shard(b) for b in range(owners.bit_length() - 1)]
+    summed = butterfly(grid, summed, shard_moves[1:] + rep_moves[:1])
     summed = after(summed, wide_new)
-    shard_moves = [grid.flip_shard(b) for b in range(1, owners.bit_length() - 1)]
-    summed = butterfly(grid, summed, shard_moves)
+    summed = butterfly(grid, summed, rep_moves[1:] + shard_moves[:1])
     (
         square_new,
         square_moment_new,

time: 776 us -> 727 us (0.937)
  waiting for transfers between devices: 168 us -> 133 us
  starting transfers between devices: 123 us -> 102 us
    ppermute x55, waiting for transfers between devices: 168 us -> 133 us  [move(): return lax.ppermute(value, ('rep', 'shard'), pairs)]
    ppermute x55, starting transfers between devices: 123 us -> 102 us  [move(): return lax.ppermute(value, ('rep', 'shard'), pairs)]
  transfers between devices with their start and end apart: 57 -> 57, of which waited for: 16 -> 17; matrix products, arithmetic and copies ran while one was open for 12% -> 14% of each run, Pallas kernels for 47% -> 50%
where the time goes in v4:
time: 727 us; the launch traced here: 718 us
  Pallas kernels  359 us (49%)
  waiting for transfers between devices  133 us (18%)
  starting transfers between devices  102 us (14%)
  other arithmetic  54.9 us (8%)
  matrix products  29.8 us (4%)
  local copies, waits for them, and re-layouts  24.1 us (3%)
  between operations  15.2 us (2%)
    ppermute x55, waiting for transfers between devices, move(): return lax.ppermute(value, ('rep', 'shard'), pairs)  133 us
    pallas_call x3, Pallas kernels, mlp_part(): pl.pallas_call(functools.partial(mlp_kernel, reps, first, last), grid_spe...  124 us
    ppermute x55, starting transfers between devices, move(): return lax.ppermute(value, ('rep', 'shard'), pairs)  102 us
    pallas_call x3, Pallas kernels, attend_backward(): pl.pallas_call(backward_kernel, grid=(rows // block,), in_specs=[pl.Block...  63.5 us
    pallas_call x14, Pallas kernels, split_sum(): pl.pallas_call(kernel, grid=(lead,), in_specs=[whole, whole], out_specs=[...  46.5 us
    pallas_call x1, Pallas kernels, attend_forward(): pl.pallas_call(forward_kernel, grid=(pairs, rows // block), in_specs=[pl....  33.6 us
    pallas_call x1, Pallas kernels, finish_wide(): pl.pallas_call(kernel, grid=(count,), in_specs=[pl.BlockSpec((8, columns)...  16 us
    dot_general x3, matrix products, back(): jnp.einsum('tn,dn->td', d_stacks[j], qkv_w[:, 640 * j:640 * j + 640], pre...  15.4 us
  transfers between devices with their start and end apart: 57, of which 17 were waited for; matrix products, arithmetic and copies ran while one was open for 14% of the time, Pallas kernels for 50%

profile of v4, /device:TPU:0, one launch (start us, length us, event | category | flops | bytes accessed | tf_op | source)
XLA Modules:
  0.0 718.5 jit_solution(9579087653964900210)
XLA Ops:
  10.1 4.1 collective-permute-start
  14.8 3.0 shard_map.306
  18.9 10.1 %collective-permute-done = bf16[1,160,1024]{2,1,0:T(8,128)(2,1)S(1)} collective-permute-done((bf16[1,160,1024]{2,1,0:T(8,128)(2,1)S(1)}, bf16[1,160,1024]{2,1,0:T(8,128)(2,1)S(1)}, u32[]{:S(2)}, u32[]{:S(2)}) %collective-permute-start) | collective-permute-done | bytes 327712 | tf_op jit(solution)/shard_map/ppermute | solution.py:985
  29.0 4.2 collective-permute-start.2
  33.2 23.9 %collective-permute-done.1 = bf16[1,144,2048]{2,1,0:T(8,128)(2,1)S(1)} collective-permute-done((bf16[1,144,2048]{2,1,0:T(8,128)(2,1)S(1)}, bf16[1,144,2048]{2,1,0:T(8,128)(2,1)S(1)}, u32[]{:S(2)}, u32[]{:S(2)}) %collective-permute-start.1) | collective-permute-done | bytes 589856 | tf_op jit(solution)/shard_map/ppermute | solution.py:985
  58.7 27.0 %collective-permute-done.3 = bf16[2,144,2048]{2,1,0:T(8,128)(2,1)S(1)} collective-permute-done((bf16[2,144,2048]{2,1,0:T(8,128)(2,1)S(1)}, bf16[2,144,2048]{2,1,0:T(8,128)(2,1)S(1)}, u32[]{:S(2)}, u32[]{:S(2)}) %collective-permute-start.3) | collective-permute-done | bytes 1179680 | tf_op jit(solution)/shard_map/ppermute | solution.py:985
  92.8 29.1 %collective-permute-done.5 = bf16[4,160,1024]{2,1,0:T(8,128)(2,1)} collective-permute-done((bf16[4,160,1024]{2,1,0:T(8,128)(2,1)}, bf16[4,160,1024]{2,1,0:T(8,128)(2,1)}, u32[]{:S(2)}, u32[]{:S(2)}) %collective-permute-start.5) | collective-permute-done | bytes 1310752 | tf_op jit(solution)/shard_map/ppermute | solution.py:985
  125.3 3.2 pad_maximum_fusion.1
  135.4 4.5 fusion.3
  139.9 7.5 %shard_map.307 = bf16[8,144,1920]{2,1,0:T(8,128)(2,1)} custom-call(s32[8]{0:T(128)} %copy-done.36, s32[1]{0:T(128)} %bitcast.1.core_ref, bf16[8,160,1024]{2,1,0:T(8,128)(2,1)} %copy-done.4, bf16[8,160,1024]{2,1,0:T(8,128)(2,1)} %collective-permute-done.6.refs_1_), custom_call_target="tpu_custom_call" | custom-call | bytes 9437184 | tf_op jit(solution)/shard_map/pallas_call | solution.py:541
  147.4 12.0 %shard_map.308 = (bf16[1024,1920]{1,0:T(8,128)(2,1)}, bf16[1152,1024]{1,0:T(8,128)(2,1)}) custom-call(s32[8]{0:T(128)} %broadcast_xor_fusion.order_ref, bf16[1024,1152]{1,0:T(8,128)(2,1)} %get-tuple-element.279.x_ref, f32[1,1152]{1,0:T(1,128)} %slice.111.gain_ref, bf16[1152,1920]{1,0:T(8,128)(2,1)} %bitcast.125, f32[1024,128]{1,0:T(8,128)} %get-tuple-element.297.cos_ref, ...), custom_call_target="tpu_custom_call" | custom-call | flops 4529848320 | bytes 13074432 | tf_op jit(solution)/shard_map/pallas_call | solution.py:88
  159.4 33.6 %shard_map.309 = (bf16[1024,1152]{1,0:T(8,128)(2,1)}, f32[3,1024,128]{2,1,0:T(8,128)}) custom-call(bf16[1024,1920]{1,0:T(8,128)(2,1)} %get-tuple-element.147.qkv_ref, s32[1024,1]{1,0:T(8,128)} %copy.40.pos_ref), custom_call_target="tpu_custom_call" | custom-call | flops 8053063680 | bytes 15728640 | tf_op jit(solution)/shard_map/pallas_call | solution.py:185
  193.0 3.6 collective-permute-done.8
  196.6 3.4 constant_dynamic-update-slice_fusion.1
  200.0 3.5 constant_dynamic-update-slice_fusion.refs_2_.refs_3_
  206.7 5.0 collective-permute-done.9.refs_3_.refs_4_
  211.7 12.3 %shard_map.310 = (f32[1024,1152]{1,0:T(8,128)}, bf16[1024,1152]{1,0:T(8,128)(2,1)}, bf16[1152,1024]{1,0:T(8,128)(2,1)}, bf16[1152,1152]{1,0:T(8,128)(2,1)}) custom-call(s32[8]{0:T(128)} %copy-done.36, s32[1]{0:T(128)} %bitcast.1.core_ref, s32[8]{0:T(128)} %broadcast_xor_fusion.order_ref, bf16[1024,1152]{1,0:T(8,128)(2,1)} %get-tuple-element.148.att_ref, ...), custom_call_target="tpu_custom_call" | custom-call | flops 2717908992 | bytes 19464192 | tf_op jit(solution)/shard_map/pallas_call | solution.py:930
  225.8 5.1 shard_map.311.refs_1_
  230.9 41.6 %shard_map.312 = (bf16[3,576,1024]{2,1,0:T(8,128)(2,1)}, bf16[3,576,1024]{2,1,0:T(8,128)(2,1)}, f32[1024,1152]{1,0:T(8,128)}, f32[1024,1152]{1,0:T(8,128)}) custom-call(s32[4]{0:T(128)} %and_select_fusion.slot_ref, s32[8]{0:T(128)} %copy-done.36, bf16[1024,1152]{1,0:T(8,128)(2,1)} %get-tuple-element.152.mid_ref, ...), custom_call_target="tpu_custom_call" | custom-call | flops 21743271936 | bytes 42467328 | tf_op jit(solution)/shard_map/pallas_call | solution.py:477
  272.4 39.5 %collective-permute-start.11 = (bf16[3,576,1024]{2,1,0:T(8,128)(2,1)}, bf16[3,576,1024]{2,1,0:T(8,128)(2,1)S(1)}, u32[]{:S(2)}, u32[]{:S(2)}) collective-permute-start(bf16[3,576,1024]{2,1,0:T(8,128)(2,1)} %get-tuple-element.164), channel_id=1, source_target_pairs={{0,8},{1,9},{2,10},{3,11},{4,12},{5,13},{6,14},{7,15},{8,0},{9,1},... | collective-permute-start | bytes 10616840 | tf_op jit(solution)/shard_map/ppermute | solution.py:985
  313.9 41.3 %shard_map.313 = (bf16[3,576,1024]{2,1,0:T(8,128)(2,1)}, bf16[3,576,1024]{2,1,0:T(8,128)(2,1)}, f32[1024,1152]{1,0:T(8,128)}, f32[1024,1152]{1,0:T(8,128)}) custom-call(s32[4]{0:T(128)} %iota.19.slot_ref, s32[1]{0:T(128)} %constant.120.clone.1.place_ref, bf16[1024,1152]{1,0:T(8,128)(2,1)} %get-tuple-element.152.mid_ref, ...), custom_call_target="tpu_custom_call" | custom-call | flops 21743271936 | bytes 42467328 | tf_op jit(solution)/shard_map/pallas_call | solution.py:477
  357.8 5.7 shard_map.314
  365.5 41.6 %shard_map.315 = (bf16[3,576,1024]{2,1,0:T(8,128)(2,1)}, bf16[3,576,1024]{2,1,0:T(8,128)(2,1)}, bf16[1024,1152]{1,0:T(8,128)(2,1)}, f32[1024,1152]{1,0:T(8,128)}) custom-call(s32[4]{0:T(128)} %iota.16.slot_ref, s32[1]{0:T(128)} %constant.120.clone.1.place_ref, bf16[1024,1152]{1,0:T(8,128)(2,1)} %get-tuple-element.152.mid_ref, ...), custom_call_target="tpu_custom_call" | custom-call | flops 21743271936 | bytes 42467328 | tf_op jit(solution)/shard_map/pallas_call | solution.py:477
  409.3 2.9 multiply_reduce_fusion.2
  413.4 3.9 shard_map.316
  417.4 2.4 collective-permute-start.16
  421.4 5.6 shard_map.317
  429.7 3.5 multiply_reduce_fusion
  433.2 4.1 fusion.35.rows_ref
  437.3 5.1 shard_map.318
  442.4 4.9 convolution_convert_fusion.2
  447.3 2.5 collective-permute-start.19
  449.9 4.7 convolution_convert_fusion.d_ref
  454.6 5.7 shard_map.319
  461.8 21.2 %shard_map.320 = (bf16[1024,640]{1,0:T(8,128)(2,1)}, bf16[576,640]{1,0:T(8,128)(2,1)}, bf16[576,640]{1,0:T(8,128)(2,1)}) custom-call(bf16[1024,1920]{1,0:T(8,128)(2,1)} %get-tuple-element.147.qkv_ref, bf16[1024,1152]{1,0:T(8,128)(2,1)} %convolution_convert_fusion.d_ref, f32[3,1024,128]{2,1,0:T(8,128)} %get-tuple-element.193.log_ref, ...), custom_call_target="tpu_custom_call" | custom-call | flops 6710886400 | bytes 5242880 | tf_op jit(solution)/shard_map/pallas_call | solution.py:297
  483.0 4.8 fusion.7.home_ref
  487.8 2.9 shard_map.322
  491.2 3.9 shard_map.321
  497.8 3.3 broadcast_select_fusion.1
  501.1 20.9 %shard_map.323 = (bf16[1024,640]{1,0:T(8,128)(2,1)}, bf16[576,640]{1,0:T(8,128)(2,1)}, bf16[576,640]{1,0:T(8,128)(2,1)}) custom-call(bf16[1024,1920]{1,0:T(8,128)(2,1)} %get-tuple-element.147.qkv_ref, bf16[1024,1152]{1,0:T(8,128)(2,1)} %convolution_convert_fusion.d_ref, f32[3,1024,128]{2,1,0:T(8,128)} %get-tuple-element.193.log_ref, ...), custom_call_target="tpu_custom_call" | custom-call | flops 6710886400 | bytes 5242880 | tf_op jit(solution)/shard_map/pallas_call | solution.py:297
  529.0 2.5 collective-permute-start.27
  532.9 4.0 shard_map.324
  536.9 6.8 collective-permute-done.23.refs_3_
  545.2 21.3 %shard_map.327 = (bf16[1024,640]{1,0:T(8,128)(2,1)}, bf16[576,640]{1,0:T(8,128)(2,1)}, bf16[576,640]{1,0:T(8,128)(2,1)}) custom-call(bf16[1024,1920]{1,0:T(8,128)(2,1)} %get-tuple-element.147.qkv_ref, bf16[1024,1152]{1,0:T(8,128)(2,1)} %convolution_convert_fusion.d_ref, f32[3,1024,128]{2,1,0:T(8,128)} %get-tuple-element.193.log_ref, ...), custom_call_target="tpu_custom_call" | custom-call | flops 6710886400 | bytes 5242880 | tf_op jit(solution)/shard_map/pallas_call | solution.py:297
  566.5 3.2 collective-permute-done.27.refs_0_
  570.9 2.6 shard_map.334
  575.4 2.3 shard_map.329
  579.2 4.0 fusion.9
  583.3 5.8 convolution_add_fusion.1
  594.7 8.6 %shard_map.332 = (f32[3,144,3072]{2,1,0:T(8,128)}, f32[24,144]{1,0:T(8,128)}) custom-call(s32[1]{0:T(128)} %bitcast.52.flag_ref, bf16[3,144,1024]{2,1,0:T(8,128)(2,1)} %copy-done.17, bf16[3,144,1024]{2,1,0:T(8,128)(2,1)} %get-tuple-element.178.refs_1_, bf16[3,144,1024]{2,1,0:T(8,128)(2,1)} %collective-permute-done.17.refs_2_, ...), custom_call_target="tpu_custom_call" | custom-call | flops 127401984 | bytes 18579456 | tf_op jit(solution)/shard_map/pallas_call | solution.py:603
  616.0 6.0 shard_map.335
  623.0 2.7 collective-permute-start.37
  625.7 5.5 convolution_add_fusion
  633.4 2.5 collective-permute-done.38
  638.9 3.4 shard_map.337
  645.4 6.7 fusion.2
  656.6 2.6 shard_map.338
  661.4 2.7 collective-permute-done.50
  665.7 5.9 collective-permute-done.51
  671.7 2.3 collective-permute-start.36
  674.9 16.0 %shard_map.336 = (f32[3,144,3072]{2,1,0:T(8,128)}, f32[3,144,3072]{2,1,0:T(8,128)}, f32[1,3,144,3072]{3,2,1,0:T(8,128)}, f32[3,8,3072]{2,1,0:T(8,128)}) custom-call(f32[8,11264]{1,0:T(8,128)} %pad_maximum_fusion.9.row_ref.gram_ref.refs_1_, f32[8,11264]{1,0:T(8,128)} %pad_maximum_fusion.9.row_ref.gram_ref.refs_1_, f32[32,144]{1,0:T(8,128)} %add.185.refs_0_.left_ref.refs_3_, ...), custom_call_target="tpu_custom_call" | custom-call | flops 15925248 | bytes 3981312 | tf_op jit(solution)/shard_map/pallas_call | solution.py:738
  691.7 4.5 collective-permute-done.53
  697.1 4.0 collective-permute-done.54
  701.7 7.3 %shard_map.339 = (f32[2,144,1152]{2,1,0:T(8,128)}, f32[2,144,1152]{2,1,0:T(8,128)}, f32[1,2,144,1152]{3,2,1,0:T(8,128)}, f32[2,8,1152]{2,1,0:T(8,128)}, f32[2,14...) custom-call(f32[8,3584]{1,0:T(8,128)} %copy-done.20, ...), custom_call_target="tpu_custom_call" | custom-call | flops 5308416 | bytes 1327104 | tf_op jit(solution)/shard_map/pallas_call | solution.py:809
  (275 shorter events, 103.1 us)
Async XLA Ops:
  7.2 306.1 %all-gather.3.cloned.1.call-start = ((), (), s32[]{:S(2)}) async-start(), calls=%async_computation | async-start | bytes 7299072 | tf_op jit(solution)/shard_map/all_gather | solution.py:1205
  10.1 18.8 %collective-permute-start = (bf16[1,160,1024]{2,1,0:T(8,128)(2,1)S(1)}, bf16[1,160,1024]{2,1,0:T(8,128)(2,1)S(1)}, u32[]{:S(2)}, u32[]{:S(2)}) collective-permute-start(bf16[1,160,1024]{2,1,0:T(8,128)(2,1)S(1)} %fusion.17), channel_id=1, source_target_pairs={{0,4},{1,5},{2,6},{3,7},{4,0},{5,1},{6,2},{7,3},{8,12},{9,13},{10,... | collective-permute-start | bytes 983048 | tf_op jit(solution)/shard_map/ppermute | solution.py:985
  28.9 28.2 %collective-permute-start.1 = (bf16[1,144,2048]{2,1,0:T(8,128)(2,1)S(1)}, bf16[1,144,2048]{2,1,0:T(8,128)(2,1)S(1)}, u32[]{:S(2)}, u32[]{:S(2)}) collective-permute-start(bf16[1,144,2048]{2,1,0:T(8,128)(2,1)S(1)} %maximum_bitcast_fusion), channel_id=1, source_target_pairs={{0,4},{1,5},{2,6},{3,7},{4,0},{5,1},{6,2},{7,3},{8,12},{9,13},{10,... | collective-permute-start | bytes 1769480 | tf_op jit(solution)/shard_map/ppermute | solution.py:985
  29.0 60.3 %copy-start.37 = (s32[1,1024]{1,0:T(1,128)S(1)}, s32[1,1024]{1,0:T(1,128)}, u32[]{:S(2)}) copy-start(s32[1,1024]{1,0:T(1,128)} %param.22) | copy-start | bytes 12292
  29.0 61.0 %copy-start = (s32[8]{0:T(128)S(1)}, s32[8]{0:T(128)}, u32[]{:S(2)}) copy-start(s32[8]{0:T(128)} %constant.143.clone) | copy-start | bytes 100
  29.0 29.7 %collective-permute-start.2 = (bf16[2,160,1024]{2,1,0:T(8,128)(2,1)S(1)}, bf16[2,160,1024]{2,1,0:T(8,128)(2,1)S(1)}, u32[]{:S(2)}, u32[]{:S(2)}) collective-permute-start(bf16[2,160,1024]{2,1,0:T(8,128)(2,1)S(1)} %pad_maximum_fusion.4), channel_id=1, source_target_pairs={{0,2},{1,3},{2,0},{3,1},{4,6},{5,7},{6,4},{7,5},{8,10},{9,11},{10,... | collective-permute-start | bytes 1966088 | tf_op jit(solution)/shard_map/ppermute | solution.py:985
  57.2 35.5 %copy-start.7 = (bf16[2,144,2048]{2,1,0:T(8,128)(2,1)}, bf16[2,144,2048]{2,1,0:T(8,128)(2,1)S(1)}, u32[]{:S(2)}) copy-start(bf16[2,144,2048]{2,1,0:T(8,128)(2,1)S(1)} %pad_maximum_fusion.3) | copy-start | bytes 3538948
  58.7 34.0 %copy-start.11 = (bf16[2,160,1024]{2,1,0:T(8,128)(2,1)}, bf16[2,160,1024]{2,1,0:T(8,128)(2,1)S(1)}, u32[]{:S(2)}) copy-start(bf16[2,160,1024]{2,1,0:T(8,128)(2,1)S(1)} %collective-permute-done.2) | copy-start | bytes 1966084
  58.7 27.0 %collective-permute-start.3 = (bf16[2,144,2048]{2,1,0:T(8,128)(2,1)S(1)}, bf16[2,144,2048]{2,1,0:T(8,128)(2,1)S(1)}, u32[]{:S(2)}, u32[]{:S(2)}) collective-permute-start(bf16[2,144,2048]{2,1,0:T(8,128)(2,1)S(1)} %pad_maximum_fusion.3), channel_id=1, source_target_pairs={{0,2},{1,3},{2,0},{3,1},{4,6},{5,7},{6,4},{7,5},{8,10},{9,11},{10,... | collective-permute-start | bytes 3538952 | tf_op jit(solution)/shard_map/ppermute | solution.py:985
  86.8 278.2 %all-gather.5.cloned.1.call-start = ((), (), s32[]{:S(2)}) async-start(), calls=%async_computation.1 | async-start | bytes 7299072 | tf_op jit(solution)/shard_map/all_gather | solution.py:1205
  88.1 33.8 %collective-permute-start.5 = (bf16[4,160,1024]{2,1,0:T(8,128)(2,1)}, bf16[4,160,1024]{2,1,0:T(8,128)(2,1)}, u32[]{:S(2)}, u32[]{:S(2)}) collective-permute-start(bf16[4,160,1024]{2,1,0:T(8,128)(2,1)} %pad_maximum_fusion.2), channel_id=1, source_target_pairs={{0,1},{1,0},{2,3},{3,2},{4,5},{5,4},{6,7},{7,6},{8,9},{9,8},{10,11... | collective-permute-start | bytes 3932168 | tf_op jit(solution)/shard_map/ppermute | solution.py:985
  89.3 34.9 %collective-permute-start.7 = (s32[1,1024]{1,0:T(1,128)S(1)}, s32[1,1024]{1,0:T(1,128)S(1)}, u32[]{:S(2)}, u32[]{:S(2)}) collective-permute-start(s32[1,1024]{1,0:T(1,128)S(1)} %copy-done.37), channel_id=1, source_target_pairs={{2,8},{3,9},{6,12},{7,13},{8,2},{9,3},{12,6},{13,7},{18,24},{19,25... | collective-permute-start | bytes 12296 | tf_op jit(solution)/shard_map/ppermute | solution.py:985
  90.7 44.7 %collective-permute-start.4 = (bf16[1,1024,1152]{2,1,0:T(8,128)(2,1)}, bf16[1,1024,1152]{2,1,0:T(8,128)(2,1)}, u32[]{:S(2)}, u32[]{:S(2)}) collective-permute-start(bf16[1,1024,1152]{2,1,0:T(8,128)(2,1)} %param.20), channel_id=1, source_target_pairs={{2,8},{3,9},{6,12},{7,13},{8,2},{9,3},{12,6},{13,7},{18,24},{19,25... | collective-permute-start | bytes 7077896 | tf_op jit(solution)/shard_map/ppermute | solution.py:985
  123.5 16.5 %collective-permute-start.6 = (bf16[8,160,1024]{2,1,0:T(8,128)(2,1)S(1)}, bf16[8,160,1024]{2,1,0:T(8,128)(2,1)}, u32[]{:S(2)}, u32[]{:S(2)}) collective-permute-start(bf16[8,160,1024]{2,1,0:T(8,128)(2,1)S(1)} %pad_maximum_fusion.refs_0_), channel_id=1, source_target_pairs={{0,8},{1,9},{2,10},{3,11},{4,12},{5,13},{6,14},{7,15},{8,0},{9,1},... | collective-permute-start | bytes 7864328 | tf_op jit(solution)/shard_map/ppermute | solution.py:985
  128.6 68.0 %collective-permute-start.8 = (bf16[4,144,2048]{2,1,0:T(8,128)(2,1)}, bf16[4,144,2048]{2,1,0:T(8,128)(2,1)}, u32[]{:S(2)}, u32[]{:S(2)}) collective-permute-start(bf16[4,144,2048]{2,1,0:T(8,128)(2,1)} %pad_maximum_fusion.1), channel_id=1, source_target_pairs={{0,1},{1,0},{2,3},{3,2},{4,5},{5,4},{6,7},{7,6},{8,9},{9,8},{10,11... | collective-permute-start | bytes 7077896 | tf_op jit(solution)/shard_map/ppermute | solution.py:985
  203.5 8.3 %collective-permute-start.9 = (bf16[8,144,2048]{2,1,0:T(8,128)(2,1)}, bf16[8,144,2048]{2,1,0:T(8,128)(2,1)}, u32[]{:S(2)}, u32[]{:S(2)}) collective-permute-start(bf16[8,144,2048]{2,1,0:T(8,128)(2,1)} %constant_dynamic-update-slice_fusion.refs_2_.refs_3_), channel_id=1, source_target_pairs={{0,8},{1,9},{2,10},{3,11},{4,12},{5,13},{6,14},{7,15},{8,0},{9,1},... | collective-permute-start | bytes 14155784 | tf_op jit(solution)/shard_map/ppermute | solution.py:985
  203.5 20.5 %collective-permute-start.10 = (bf16[1,1024,1152]{2,1,0:T(8,128)(2,1)S(1)}, bf16[1,1024,1152]{2,1,0:T(8,128)(2,1)}, u32[]{:S(2)}, u32[]{:S(2)}) collective-permute-start(bf16[1,1024,1152]{2,1,0:T(8,128)(2,1)S(1)} %copy-done.12), channel_id=1, source_target_pairs={{2,8},{3,9},{6,12},{7,13},{8,2},{9,3},{12,6},{13,7},{18,24},{19,25... | collective-permute-start | bytes 7077896 | tf_op jit(solution)/shard_map/ppermute | solution.py:985
  272.4 83.6 %collective-permute-start.11 = (bf16[3,576,1024]{2,1,0:T(8,128)(2,1)}, bf16[3,576,1024]{2,1,0:T(8,128)(2,1)S(1)}, u32[]{:S(2)}, u32[]{:S(2)}) collective-permute-start(bf16[3,576,1024]{2,1,0:T(8,128)(2,1)} %get-tuple-element.164), channel_id=1, source_target_pairs={{0,8},{1,9},{2,10},{3,11},{4,12},{5,13},{6,14},{7,15},{8,0},{9,1},... | collective-permute-start | bytes 10616840 | tf_op jit(solution)/shard_map/ppermute | solution.py:985
  313.9 41.4 %copy-start.21 = (f32[1,2,144,384]{3,2,1,0:T(8,128)S(1)}, f32[1,2,144,384]{3,2,1,0:T(8,128)}, u32[]{:S(2)}) copy-start(f32[1,2,144,384]{3,2,1,0:T(8,128)} %param.31) | copy-start | bytes 1327108
  355.1 66.3 %collective-permute-start.13 = (bf16[3,576,1024]{2,1,0:T(8,128)(2,1)}, bf16[3,576,1024]{2,1,0:T(8,128)(2,1)}, u32[]{:S(2)}, u32[]{:S(2)}) collective-permute-start(bf16[3,576,1024]{2,1,0:T(8,128)(2,1)} %get-tuple-element.165), channel_id=1, source_target_pairs={{0,8},{1,9},{2,10},{3,11},{4,12},{5,13},{6,14},{7,15},{8,0},{9,1},... | collective-permute-start | bytes 10616840 | tf_op jit(solution)/shard_map/ppermute | solution.py:985
  363.5 48.7 %collective-permute-start.12 = (bf16[3,288,1024]{2,1,0:T(8,128)(2,1)}, bf16[3,288,1024]{2,1,0:T(8,128)(2,1)S(1)}, u32[]{:S(2)}, u32[]{:S(2)}) collective-permute-start(bf16[3,288,1024]{2,1,0:T(8,128)(2,1)} %get-tuple-element.167), channel_id=1, source_target_pairs={{0,1},{1,0},{2,3},{3,2},{4,5},{5,4},{6,7},{7,6},{8,9},{9,8},{10,11... | collective-permute-start | bytes 5308424 | tf_op jit(solution)/shard_map/ppermute | solution.py:985
  365.5 41.8 %copy-start.29 = (f32[2,8,384]{2,1,0:T(8,128)S(1)}, f32[2,8,384]{2,1,0:T(8,128)}, u32[]{:S(2)}) copy-start(f32[2,8,384]{2,1,0:T(8,128)} %param.34) | copy-start | bytes 73732
  365.5 42.4 %copy-start.15 = (f32[1,2,144,1152]{3,2,1,0:T(8,128)S(1)}, f32[1,2,144,1152]{3,2,1,0:T(8,128)}, u32[]{:S(2)}) copy-start(f32[1,2,144,1152]{3,2,1,0:T(8,128)} %param.30) | copy-start | bytes 3981316
  407.1 40.3 %collective-permute-start.15 = (bf16[3,576,1024]{2,1,0:T(8,128)(2,1)}, bf16[3,576,1024]{2,1,0:T(8,128)(2,1)}, u32[]{:S(2)}, u32[]{:S(2)}) collective-permute-start(bf16[3,576,1024]{2,1,0:T(8,128)(2,1)} %get-tuple-element.175), channel_id=1, source_target_pairs={{0,8},{1,9},{2,10},{3,11},{4,12},{5,13},{6,14},{7,15},{8,0},{9,1},... | collective-permute-start | bytes 10616840 | tf_op jit(solution)/shard_map/ppermute | solution.py:985
  417.4 42.8 %collective-permute-start.16 = (bf16[3,144,1024]{2,1,0:T(8,128)(2,1)}, bf16[3,144,1024]{2,1,0:T(8,128)(2,1)S(1)}, u32[]{:S(2)}, u32[]{:S(2)}) collective-permute-start(bf16[3,144,1024]{2,1,0:T(8,128)(2,1)} %get-tuple-element.177), channel_id=1, source_target_pairs={{0,4},{1,5},{2,12},{3,13},{4,0},{5,1},{6,8},{7,9},{8,6},{9,7},{10,... | collective-permute-start | bytes 2654216 | tf_op jit(solution)/shard_map/ppermute | solution.py:985
  419.8 42.0 %collective-permute-start.17 = (bf16[3,144,1024]{2,1,0:T(8,128)(2,1)}, bf16[3,144,1024]{2,1,0:T(8,128)(2,1)}, u32[]{:S(2)}, u32[]{:S(2)}) collective-permute-start(bf16[3,144,1024]{2,1,0:T(8,128)(2,1)} %get-tuple-element.178.refs_1_), channel_id=1, source_target_pairs={{2,8},{3,9},{6,12},{7,13},{8,2},{9,3},{12,6},{13,7},{18,24},{19,25... | collective-permute-start | bytes 2654216 | tf_op jit(solution)/shard_map/ppermute | solution.py:985
  427.1 64.1 %collective-permute-start.18 = (bf16[3,288,1024]{2,1,0:T(8,128)(2,1)}, bf16[3,288,1024]{2,1,0:T(8,128)(2,1)}, u32[]{:S(2)}, u32[]{:S(2)}) collective-permute-start(bf16[3,288,1024]{2,1,0:T(8,128)(2,1)} %get-tuple-element.183), channel_id=1, source_target_pairs={{0,1},{1,0},{2,3},{3,2},{4,5},{5,4},{6,7},{7,6},{8,9},{9,8},{10,11... | collective-permute-start | bytes 5308424 | tf_op jit(solution)/shard_map/ppermute | solution.py:985
  427.6 68.6 %collective-permute-start.14 = (bf16[1,1024,1152]{2,1,0:T(8,128)(2,1)}, bf16[1,1024,1152]{2,1,0:T(8,128)(2,1)}, u32[]{:S(2)}, u32[]{:S(2)}) collective-permute-start(bf16[1,1024,1152]{2,1,0:T(8,128)(2,1)} %bitcast.130), channel_id=1, source_target_pairs={{2,8},{3,9},{6,12},{7,13},{8,2},{9,3},{12,6},{13,7},{18,24},{19,25... | collective-permute-start | bytes 7077896 | tf_op jit(solution)/shard_map/ppermute | solution.py:985
  447.3 40.5 %collective-permute-start.19 = (bf16[576,1152]{1,0:T(8,128)(2,1)}, bf16[576,1152]{1,0:T(8,128)(2,1)}, u32[]{:S(2)}, u32[]{:S(2)}) collective-permute-start(bf16[576,1152]{1,0:T(8,128)(2,1)} %convolution_convert_fusion.2), channel_id=1, source_target_pairs={{0,8},{1,9},{2,10},{3,11},{4,12},{5,13},{6,14},{7,15},{8,0},{9,1},... | collective-permute-start | bytes 3981320 | tf_op jit(solution)/shard_map/ppermute | solution.py:985
  460.2 71.3 %collective-permute-start.20 = (bf16[3,288,1024]{2,1,0:T(8,128)(2,1)}, bf16[3,288,1024]{2,1,0:T(8,128)(2,1)}, u32[]{:S(2)}, u32[]{:S(2)}) collective-permute-start(bf16[3,288,1024]{2,1,0:T(8,128)(2,1)} %get-tuple-element.190), channel_id=1, source_target_pairs={{0,1},{1,0},{2,3},{3,2},{4,5},{5,4},{6,7},{7,6},{8,9},{9,8},{10,11... | collective-permute-start | bytes 5308424 | tf_op jit(solution)/shard_map/ppermute | solution.py:985
  487.8 38.9 %collective-permute-start.22 = (bf16[576,640]{1,0:T(8,128)(2,1)}, bf16[576,640]{1,0:T(8,128)(2,1)}, u32[]{:S(2)}, u32[]{:S(2)}) collective-permute-start(bf16[576,640]{1,0:T(8,128)(2,1)} %get-tuple-element.202), channel_id=1, source_target_pairs={{0,8},{1,9},{2,10},{3,11},{4,12},{5,13},{6,14},{7,15},{8,0},{9,1},... | collective-permute-start | bytes 2211848 | tf_op jit(solution)/shard_map/ppermute | solution.py:985
  490.7 31.3 %collective-permute-start.21 = (bf16[288,1152]{1,0:T(8,128)(2,1)}, bf16[288,1152]{1,0:T(8,128)(2,1)}, u32[]{:S(2)}, u32[]{:S(2)}) collective-permute-start(bf16[288,1152]{1,0:T(8,128)(2,1)} %bitcast.145), channel_id=1, source_target_pairs={{0,1},{1,0},{2,3},{3,2},{4,5},{5,4},{6,7},{7,6},{8,9},{9,8},{10,11... | collective-permute-start | bytes 1990664 | tf_op jit(solution)/shard_map/ppermute | solution.py:985
  495.1 48.5 %collective-permute-start.23 = (bf16[3,144,1024]{2,1,0:T(8,128)(2,1)}, bf16[3,144,1024]{2,1,0:T(8,128)(2,1)S(1)}, u32[]{:S(2)}, u32[]{:S(2)}) collective-permute-start(bf16[3,144,1024]{2,1,0:T(8,128)(2,1)} %get-tuple-element.197), channel_id=1, source_target_pairs={{0,4},{1,5},{2,12},{3,13},{4,0},{5,1},{6,8},{7,9},{8,6},{9,7},{10,... | collective-permute-start | bytes 2654216 | tf_op jit(solution)/shard_map/ppermute | solution.py:985
  496.2 49.0 %collective-permute-start.24 = (bf16[3,144,1024]{2,1,0:T(8,128)(2,1)}, bf16[3,144,1024]{2,1,0:T(8,128)(2,1)}, u32[]{:S(2)}, u32[]{:S(2)}) collective-permute-start(bf16[3,144,1024]{2,1,0:T(8,128)(2,1)} %get-tuple-element.198.refs_4_), channel_id=1, source_target_pairs={{2,8},{3,9},{6,12},{7,13},{8,2},{9,3},{12,6},{13,7},{18,24},{19,25... | collective-permute-start | bytes 2654216 | tf_op jit(solution)/shard_map/ppermute | solution.py:985
  522.0 53.4 %collective-permute-start.26 = (bf16[576,640]{1,0:T(8,128)(2,1)}, bf16[576,640]{1,0:T(8,128)(2,1)}, u32[]{:S(2)}, u32[]{:S(2)}) collective-permute-start(bf16[576,640]{1,0:T(8,128)(2,1)} %get-tuple-element.216), channel_id=1, source_target_pairs={{0,8},{1,9},{2,10},{3,11},{4,12},{5,13},{6,14},{7,15},{8,0},{9,1},... | collective-permute-start | bytes 2211848 | tf_op jit(solution)/shard_map/ppermute | solution.py:985
  529.0 40.8 %collective-permute-start.27 = (bf16[144,1152]{1,0:T(8,128)(2,1)}, bf16[144,1152]{1,0:T(8,128)(2,1)S(1)}, u32[]{:S(2)}, u32[]{:S(2)}) collective-permute-start(bf16[144,1152]{1,0:T(8,128)(2,1)} %bitcast.149), channel_id=1, source_target_pairs={{0,4},{1,5},{2,12},{3,13},{4,0},{5,1},{6,8},{7,9},{8,6},{9,7},{10,... | collective-permute-start | bytes 995336 | tf_op jit(solution)/shard_map/ppermute | solution.py:985
  531.5 39.0 %collective-permute-start.28 = (bf16[144,1152]{1,0:T(8,128)(2,1)}, bf16[144,1152]{1,0:T(8,128)(2,1)}, u32[]{:S(2)}, u32[]{:S(2)}) collective-permute-start(bf16[144,1152]{1,0:T(8,128)(2,1)} %bitcast.134), channel_id=1, source_target_pairs={{2,8},{3,9},{6,12},{7,13},{8,2},{9,3},{12,6},{13,7},{18,24},{19,25... | collective-permute-start | bytes 995336 | tf_op jit(solution)/shard_map/ppermute | solution.py:985
  543.7 29.9 %collective-permute-start.25 = (bf16[288,640]{1,0:T(8,128)(2,1)}, bf16[288,640]{1,0:T(8,128)(2,1)}, u32[]{:S(2)}, u32[]{:S(2)}) collective-permute-start(bf16[288,640]{1,0:T(8,128)(2,1)} %bitcast.147), channel_id=1, source_target_pairs={{0,1},{1,0},{2,3},{3,2},{4,5},{5,4},{6,7},{7,6},{8,9},{9,8},{10,11... | collective-permute-start | bytes 1105928 | tf_op jit(solution)/shard_map/ppermute | solution.py:985
  545.2 48.6 %collective-permute-start.29 = (bf16[3,144,1024]{2,1,0:T(8,128)(2,1)}, bf16[3,144,1024]{2,1,0:T(8,128)(2,1)}, u32[]{:S(2)}, u32[]{:S(2)}) collective-permute-start(bf16[3,144,1024]{2,1,0:T(8,128)(2,1)} %get-tuple-element.207), channel_id=1, source_target_pairs={{0,4},{1,5},{2,12},{3,13},{4,0},{5,1},{6,8},{7,9},{8,6},{9,7},{10,... | collective-permute-start | bytes 2654216 | tf_op jit(solution)/shard_map/ppermute | solution.py:985
  569.7 24.0 %collective-permute-start.30 = (bf16[3,144,1024]{2,1,0:T(8,128)(2,1)}, bf16[3,144,1024]{2,1,0:T(8,128)(2,1)S(1)}, u32[]{:S(2)}, u32[]{:S(2)}) collective-permute-start(bf16[3,144,1024]{2,1,0:T(8,128)(2,1)} %get-tuple-element.208.refs_7_), channel_id=1, source_target_pairs={{2,8},{3,9},{6,12},{7,13},{8,2},{9,3},{12,6},{13,7},{18,24},{19,25... | collective-permute-start | bytes 2654216 | tf_op jit(solution)/shard_map/ppermute | solution.py:985
  570.5 18.6 %collective-permute-start.31 = (bf16[576,640]{1,0:T(8,128)(2,1)}, bf16[576,640]{1,0:T(8,128)(2,1)}, u32[]{:S(2)}, u32[]{:S(2)}) collective-permute-start(bf16[576,640]{1,0:T(8,128)(2,1)} %get-tuple-element.227), channel_id=1, source_target_pairs={{0,8},{1,9},{2,10},{3,11},{4,12},{5,13},{6,14},{7,15},{8,0},{9,1},... | collective-permute-start | bytes 2211848 | tf_op jit(solution)/shard_map/ppermute | solution.py:985
  577.7 14.2 %collective-permute-start.32 = (bf16[288,640]{1,0:T(8,128)(2,1)}, bf16[288,640]{1,0:T(8,128)(2,1)}, u32[]{:S(2)}, u32[]{:S(2)}) collective-permute-start(bf16[288,640]{1,0:T(8,128)(2,1)} %bitcast.148), channel_id=1, source_target_pairs={{0,1},{1,0},{2,3},{3,2},{4,5},{5,4},{6,7},{7,6},{8,9},{9,8},{10,11... | collective-permute-start | bytes 1105928 | tf_op jit(solution)/shard_map/ppermute | solution.py:985
  591.4 19.7 %collective-permute-start.33 = (bf16[288,640]{1,0:T(8,128)(2,1)}, bf16[288,640]{1,0:T(8,128)(2,1)}, u32[]{:S(2)}, u32[]{:S(2)}) collective-permute-start(bf16[288,640]{1,0:T(8,128)(2,1)} %bitcast.146), channel_id=1, source_target_pairs={{0,1},{1,0},{2,3},{3,2},{4,5},{5,4},{6,7},{7,6},{8,9},{9,8},{10,11... | collective-permute-start | bytes 1105928 | tf_op jit(solution)/shard_map/ppermute | solution.py:985
  604.0 1.2 collective-permute-start.34
  605.3 5.1 collective-permute-start.35
  608.4 29.6 %collective-permute-start.45 = (bf16[144,1280]{1,0:T(8,128)(2,1)S(1)}, bf16[144,1280]{1,0:T(8,128)(2,1)S(1)}, u32[]{:S(2)}, u32[]{:S(2)}) collective-permute-start(bf16[144,1280]{1,0:T(8,128)(2,1)S(1)} %pad_maximum_fusion.8.refs_1_), channel_id=1, source_target_pairs={{2,8},{3,9},{6,12},{7,13},{8,2},{9,3},{12,6},{13,7},{18,24},{19,25... | collective-permute-start | bytes 1105928 | tf_op jit(solution)/shard_map/ppermute | solution.py:985
  609.1 29.0 %collective-permute-start.44 = (bf16[144,1280]{1,0:T(8,128)(2,1)}, bf16[144,1280]{1,0:T(8,128)(2,1)S(1)}, u32[]{:S(2)}, u32[]{:S(2)}) collective-permute-start(bf16[144,1280]{1,0:T(8,128)(2,1)} %pad_maximum_fusion.7), channel_id=1, source_target_pairs={{0,4},{1,5},{2,12},{3,13},{4,0},{5,1},{6,8},{7,9},{8,6},{9,7},{10,... | collective-permute-start | bytes 1105928 | tf_op jit(solution)/shard_map/ppermute | solution.py:985
  612.9 25.2 %collective-permute-start.46 = (bf16[144,640]{1,0:T(8,128)(2,1)}, bf16[144,640]{1,0:T(8,128)(2,1)}, u32[]{:S(2)}, u32[]{:S(2)}) collective-permute-start(bf16[144,640]{1,0:T(8,128)(2,1)} %bitcast.150), channel_id=1, source_target_pairs={{0,4},{1,5},{2,12},{3,13},{4,0},{5,1},{6,8},{7,9},{8,6},{9,7},{10,... | collective-permute-start | bytes 552968 | tf_op jit(solution)/shard_map/ppermute | solution.py:985
  614.6 23.5 %collective-permute-start.47 = (bf16[144,640]{1,0:T(8,128)(2,1)}, bf16[144,640]{1,0:T(8,128)(2,1)}, u32[]{:S(2)}, u32[]{:S(2)}) collective-permute-start(bf16[144,640]{1,0:T(8,128)(2,1)} %bitcast.137), channel_id=1, source_target_pairs={{2,8},{3,9},{6,12},{7,13},{8,2},{9,3},{12,6},{13,7},{18,24},{19,25... | collective-permute-start | bytes 552968 | tf_op jit(solution)/shard_map/ppermute | solution.py:985
  623.0 8.2 %collective-permute-start.37 = (f32[8,5632]{1,0:T(8,128)S(1)}, f32[8,5632]{1,0:T(8,128)S(1)}, u32[]{:S(2)}, u32[]{:S(2)}) collective-permute-start(f32[8,5632]{1,0:T(8,128)S(1)} %slice_select_fusion), channel_id=1, source_target_pairs={{0,8},{1,9},{2,10},{3,11},{4,12},{5,13},{6,14},{7,15},{8,0},{9,1},... | collective-permute-start | bytes 540680 | tf_op jit(solution)/shard_map/ppermute | solution.py:985
  631.3 4.6 collective-permute-start.38
  635.9 6.4 collective-permute-start.39
  642.3 9.8 %collective-permute-start.48 = (f32[24,144]{1,0:T(8,128)}, f32[24,144]{1,0:T(8,128)S(1)}, u32[]{:S(2)}, u32[]{:S(2)}) collective-permute-start(f32[24,144]{1,0:T(8,128)} %get-tuple-element.253), channel_id=1, source_target_pairs={{0,8},{1,9},{2,10},{3,11},{4,12},{5,13},{6,14},{7,15},{8,0},{9,1},... | collective-permute-start | bytes 41480 | tf_op jit(solution)/shard_map/ppermute | solution.py:985
  643.2 9.5 %collective-permute-start.40 = (f32[8,2816]{1,0:T(8,128)S(1)}, f32[8,2816]{1,0:T(8,128)S(1)}, u32[]{:S(2)}, u32[]{:S(2)}) collective-permute-start(f32[8,2816]{1,0:T(8,128)S(1)} %add.192), channel_id=1, source_target_pairs={{0,2},{1,3},{2,0},{3,1},{4,6},{5,7},{6,4},{7,5},{8,10},{9,11},{10,... | collective-permute-start | bytes 270344 | tf_op jit(solution)/shard_map/ppermute | solution.py:985
  652.1 3.9 collective-permute-start.49
  652.8 7.1 collective-permute-start.41
  659.2 5.0 collective-permute-start.50
  659.9 5.6 collective-permute-start.42
  665.1 6.5 collective-permute-start.51
  665.6 8.5 %collective-permute-start.43 = (f32[8,5632]{1,0:T(8,128)S(1)}, f32[8,5632]{1,0:T(8,128)S(1)}, u32[]{:S(2)}, u32[]{:S(2)}) collective-permute-start(f32[8,5632]{1,0:T(8,128)S(1)} %pad_maximum_fusion.10), channel_id=1, source_target_pairs={{0,8},{1,9},{2,10},{3,11},{4,12},{5,13},{6,14},{7,15},{8,0},{9,1},... | collective-permute-start | bytes 540680 | tf_op jit(solution)/shard_map/ppermute | solution.py:985
  671.6 2.4 collective-permute-start.52
  671.7 38.1 %collective-permute-start.36 = (bf16[1,1024,1152]{2,1,0:T(8,128)(2,1)S(1)}, bf16[1,1024,1152]{2,1,0:T(8,128)(2,1)}, u32[]{:S(2)}, u32[]{:S(2)}) collective-permute-start(bf16[1,1024,1152]{2,1,0:T(8,128)(2,1)S(1)} %bitcast.129), channel_id=1, source_target_pairs={{2,8},{3,9},{6,12},{7,13},{8,2},{9,3},{12,6},{13,7},{18,24},{19,25... | collective-permute-start | bytes 7077896 | tf_op jit(solution)/shard_map/ppermute | solution.py:985
  690.8 5.4 collective-permute-start.53
  696.2 4.9 collective-permute-start.54
  (36 other events, 353.2 us)
Sparse Core Ops, SparseCore 0:
  86.9 89.6 all-gather.2
  180.1 76.3 all-gather.4

commit v5 on v4

--- a/solution.py
+++ b/solution.py
@@ -1199,15 +1199,18 @@
     order = jnp.array(grid.masks(), jnp.int32) ^ logical_shard
 
     qkv, turned_in = project_qkv(order, tokens, gain_attn[None], qkv_w, cos, sin)
+    held, got = after((mine[1], gathering[-1]), qkv)
+    mine[1] = jnp.concatenate([held, got], axis=0)
+    qkv = after(qkv, mine[1])
     wide_parts = [None] * chained
     for k in range(chained, 3):
-        part = after(cuts[k], gathering[1])
+        part = after(cuts[k], mine[1])
         part = lax.all_gather(part, ("rep", "shard"), axis=0, tiled=True)
         wide_parts.append((natural, whole, [part.reshape(reps, owners * rows, 3 * tile)]))
+    other.append(grid.move(mine[1], grid.flip_rep(0)))
     attended, logs = attend_forward(qkv, place)
-    held, got = after((mine[1], gathering[-1]), attended)
-    mine[1] = jnp.concatenate([held, got], axis=0)
-    other.append(grid.move(mine[1], grid.flip_rep(0)))
+    other[1] = after(other[1], attended)
+    d_out = jnp.where(grid.stays(), cotangent, after(moved_out, attended))[0]
     if chained:
         slots = (natural + core * (reps // 2)) % reps
         wide_parts[0] = (slots, places, [mine[1], other[1]])
@@ -1227,7 +1230,6 @@
         )
         normed_mid = normed(residual, gain_mlp).astype(jnp.bfloat16)
         turned_mid = turn_rows(normed_mid, order)
-    d_out = jnp.where(grid.stays(), cotangent, after(moved_out, normed_mid))[0]
     turned_out = turn_rows(d_out, order)
 
     half = model // 2
@@ -1301,11 +1303,12 @@
         )
 
     flag = grid.stays().astype(jnp.int32)[None]
-    d_first = back(0) + back(1)
+    d_first = back(0)
     d_stacks, wide_got = after(
         (d_stacks, wide_sums[2].got), pair_sums[2].step(d_first), pair_sums[1].step(d_first, hold)
     )
     wide_sums[2].got = wide_got
+    d_second = d_first + back(1)
     spans = [(j, 0) for j in range(PAIRS)]
     late_sums = pair_sums
     if hold:
@@ -1323,8 +1326,6 @@
         [square_factor[1]],
     )
     last_step = pair_sums[2].step(left_wide)
-    d_stacks = after(d_stacks, last_step, left_out)
-    d_normed_in = d_first + back(2)
     rep_moves = [grid.flip_rep(b) for b in range(reps.bit_length() - 1)]
     unit = 128 * reps
     left_early = butterfly(grid, jnp.concatenate([left_wide, left_out], axis=0), rep_moves)
@@ -1332,32 +1333,32 @@
     gram_early = 9 * units + model
     width = -(-(gram_early + 512) // unit) * unit
     early = contract_all(left_early, [mixed_wide, mixed_out], width)
-    d_normed_in = after(d_normed_in, early)
+    narrow = 128 * PAIRS
+    early = sum_all(grid, early)
+
+    mixed_query, mixed_key, mixed_value, left_late = mix_rest(
+        flag,
+        [part.result(left_wide) for part in late_sums],
+        [
+            [(which, at + first, at + last) for which, at in spans]
+            for first, last in ((0, 384), (384, 512), (512, 640))
+        ],
+        [square_error[0, 0], key_value_error[0, 0], key_value_error[0, 1]],
+        [square_factor[0], key_value_factor[0], key_value_factor[1]],
+    )
+    d_stacks = after(d_stacks, left_late)
+    d_normed_in = d_second + back(2)
     _, in_back = jax.vjp(normed, hidden_in, gain_attn)
     d_input, grad_gain_attn = in_back(d_normed_in)
     d_input = (d_input + d_residual).astype(jnp.bfloat16)
-    early = sum_all(grid, early)
-    late = d_input
     d_input = grid.swap_rows(d_input[None])
-    narrow = 128 * PAIRS
-
-    mixed_query, mixed_key, mixed_value, left_late = mix_rest(
-        flag,
-        [part.result(late) for part in late_sums],
-        [
-            [(which, at + first, at + last) for which, at in spans]
-            for first, last in ((0, 384), (384, 512), (512, 640))
-        ],
-        [square_error[0, 0], key_value_error[0, 0], key_value_error[0, 1]],
-        [square_factor[0], key_value_factor[0], key_value_factor[1]],
-    )
+
     left_late = butterfly(grid, left_late, rep_moves)
     gram_late = columns
     gain_at = gram_late + 384
     width = -(-(gain_at + model) // unit) * unit
     gain_grad = jnp.stack([grad_gain_attn, grad_gain_mlp])
     mixed_late = [mixed_query, mixed_key, mixed_value]
-    left_late = after(left_late, late)
     summed = contract_all(left_late, mixed_late, width, gain_grad)
     wide_new, wide_moment_new, wide_error_new, factor_wide = finish_wide(
         reps, early, gram_early, left_early, mixed_wide, wide_moment, wide_master

time: 727 us -> 699 us (0.961)
  starting transfers between devices: 102 us -> 63.6 us
  Pallas kernels: 359 us -> 373 us
    ppermute x55, starting transfers between devices: 102 us -> 63.6 us  [move(): return lax.ppermute(value, ('rep', 'shard'), pairs)]
    pallas_call x3, Pallas kernels: 124 us -> 138 us  [mlp_part(): pl.pallas_call(functools.partial(mlp_kernel, reps, first, last), grid_spe...]
  transfers between devices with their start and end apart: 57 -> 57, of which waited for: 17 -> 17; matrix products, arithmetic and copies ran while one was open for 14% -> 12% of each run, Pallas kernels for 50% -> 54%
where the time goes in v5:
time: 699 us; the launch traced here: 697 us
  Pallas kernels  373 us (53%)
  waiting for transfers between devices  138 us (20%)
  starting transfers between devices  63.6 us (9%)
  other arithmetic  48.7 us (7%)
  matrix products  32.5 us (5%)
  local copies, waits for them, and re-layouts  25.7 us (4%)
  between operations  15.3 us (2%)
    pallas_call x3, Pallas kernels, mlp_part(): pl.pallas_call(functools.partial(mlp_kernel, reps, first, last), grid_spe...  138 us
    ppermute x55, waiting for transfers between devices, move(): return lax.ppermute(value, ('rep', 'shard'), pairs)  137 us
    pallas_call x3, Pallas kernels, attend_backward(): pl.pallas_call(backward_kernel, grid=(rows // block,), in_specs=[pl.Block...  63.6 us
    ppermute x55, starting transfers between devices, move(): return lax.ppermute(value, ('rep', 'shard'), pairs)  63.6 us
    pallas_call x14, Pallas kernels, split_sum(): pl.pallas_call(kernel, grid=(lead,), in_specs=[whole, whole], out_specs=[...  46.8 us
    pallas_call x1, Pallas kernels, attend_forward(): pl.pallas_call(forward_kernel, grid=(pairs, rows // block), in_specs=[pl....  33.3 us
    dot_general x3, matrix products, back(): jnp.einsum('tn,dn->td', d_stacks[j], qkv_w[:, 640 * j:640 * j + 640], pre...  20.9 us
    pallas_call x1, Pallas kernels, finish_wide(): pl.pallas_call(kernel, grid=(count,), in_specs=[pl.BlockSpec((8, columns)...  15.9 us
  transfers between devices with their start and end apart: 57, of which 17 were waited for; matrix products, arithmetic and copies ran while one was open for 12% of the time, Pallas kernels for 54%

profile of v5, /device:TPU:0, one launch (start us, length us, event | category | flops | bytes accessed | tf_op | source)
XLA Modules:
  0.0 697.2 jit_solution(13452638860983000821)
XLA Ops:
  10.1 4.1 collective-permute-start
  14.8 3.0 shard_map.306
  17.8 11.1 %collective-permute-done = bf16[1,160,1024]{2,1,0:T(8,128)(2,1)S(1)} collective-permute-done((bf16[1,160,1024]{2,1,0:T(8,128)(2,1)S(1)}, bf16[1,160,1024]{2,1,0:T(8,128)(2,1)S(1)}, u32[]{:S(2)}, u32[]{:S(2)}) %collective-permute-start) | collective-permute-done | bytes 327712 | tf_op jit(solution)/shard_map/ppermute | solution.py:985
  30.9 3.4 collective-permute-start.1
  34.3 23.3 %collective-permute-done.2 = bf16[2,160,1024]{2,1,0:T(8,128)(2,1)S(1)} collective-permute-done((bf16[2,160,1024]{2,1,0:T(8,128)(2,1)S(1)}, bf16[2,160,1024]{2,1,0:T(8,128)(2,1)S(1)}, u32[]{:S(2)}, u32[]{:S(2)}) %collective-permute-start.2) | collective-permute-done | bytes 655392 | tf_op jit(solution)/shard_map/ppermute | solution.py:985
  62.4 24.2 %collective-permute-done.3 = bf16[2,144,2048]{2,1,0:T(8,128)(2,1)S(1)} collective-permute-done((bf16[2,144,2048]{2,1,0:T(8,128)(2,1)S(1)}, bf16[2,144,2048]{2,1,0:T(8,128)(2,1)S(1)}, u32[]{:S(2)}, u32[]{:S(2)}) %collective-permute-start.3) | collective-permute-done | bytes 1179680 | tf_op jit(solution)/shard_map/ppermute | solution.py:985
  101.4 4.5 fusion.3
  105.9 7.5 %shard_map.307 = bf16[8,144,1920]{2,1,0:T(8,128)(2,1)} custom-call(s32[8]{0:T(128)} %copy-done.47, s32[1]{0:T(128)} %bitcast.1.core_ref, bf16[8,160,1024]{2,1,0:T(8,128)(2,1)} %copy-done.3, bf16[8,160,1024]{2,1,0:T(8,128)(2,1)} %collective-permute-done.6.refs_1_), custom_call_target="tpu_custom_call" | custom-call | bytes 9437184 | tf_op jit(solution)/shard_map/pallas_call | solution.py:541
  113.4 12.0 %shard_map.308 = (bf16[1024,1920]{1,0:T(8,128)(2,1)}, bf16[1152,1024]{1,0:T(8,128)(2,1)}) custom-call(s32[8]{0:T(128)} %broadcast_xor_fusion.order_ref, bf16[1024,1152]{1,0:T(8,128)(2,1)} %get-tuple-element.281.x_ref, f32[1,1152]{1,0:T(1,128)} %slice.111.gain_ref, bf16[1152,1920]{1,0:T(8,128)(2,1)} %bitcast.127, f32[1024,128]{1,0:T(8,128)} %get-tuple-element.300.cos_ref, ...), custom_call_target="tpu_custom_call" | custom-call | flops 4529848320 | bytes 13074432 | tf_op jit(solution)/shard_map/pallas_call | solution.py:88
  125.4 22.6 %collective-permute-done.8 = bf16[4,144,2048]{2,1,0:T(8,128)(2,1)} collective-permute-done((bf16[4,144,2048]{2,1,0:T(8,128)(2,1)}, bf16[4,144,2048]{2,1,0:T(8,128)(2,1)}, u32[]{:S(2)}, u32[]{:S(2)}) %collective-permute-start.8) | collective-permute-done | bytes 2359328 | tf_op jit(solution)/shard_map/ppermute | solution.py:985
  148.0 3.4 constant_dynamic-update-slice_fusion.1
  151.3 3.5 constant_dynamic-update-slice_fusion.refs_2_.refs_3_
  155.7 2.3 collective-permute-start.10
  160.2 33.3 %shard_map.309 = (bf16[1024,1152]{1,0:T(8,128)(2,1)}, f32[3,1024,128]{2,1,0:T(8,128)}) custom-call(bf16[1024,1920]{1,0:T(8,128)(2,1)} %get-tuple-element.152.qkv_ref, s32[1024,1]{1,0:T(8,128)} %copy.40.pos_ref), custom_call_target="tpu_custom_call" | custom-call | flops 8053063680 | bytes 15728640 | tf_op jit(solution)/shard_map/pallas_call | solution.py:185
  195.2 5.2 shard_map.311.refs_1_
  200.4 11.9 %shard_map.310 = (f32[1024,1152]{1,0:T(8,128)}, bf16[1024,1152]{1,0:T(8,128)(2,1)}, bf16[1152,1024]{1,0:T(8,128)(2,1)}, bf16[1152,1152]{1,0:T(8,128)(2,1)}) custom-call(s32[8]{0:T(128)} %copy-done.47, s32[1]{0:T(128)} %bitcast.1.core_ref, s32[8]{0:T(128)} %broadcast_xor_fusion.order_ref, bf16[1024,1152]{1,0:T(8,128)(2,1)} %get-tuple-element.153.att_ref, ...), custom_call_target="tpu_custom_call" | custom-call | flops 2717908992 | bytes 19464192 | tf_op jit(solution)/shard_map/pallas_call | solution.py:930
  212.3 54.9 %shard_map.312 = (bf16[3,576,1024]{2,1,0:T(8,128)(2,1)}, bf16[3,576,1024]{2,1,0:T(8,128)(2,1)}, f32[1024,1152]{1,0:T(8,128)}, f32[1024,1152]{1,0:T(8,128)}) custom-call(s32[4]{0:T(128)} %and_select_fusion.slot_ref, s32[8]{0:T(128)} %copy-done.47, bf16[1024,1152]{1,0:T(8,128)(2,1)} %get-tuple-element.155.mid_ref, ...), custom_call_target="tpu_custom_call" | custom-call | flops 21743271936 | bytes 42467328 | tf_op jit(solution)/shard_map/pallas_call | solution.py:477
  267.2 8.6 %collective-permute-start.11 = (bf16[3,576,1024]{2,1,0:T(8,128)(2,1)}, bf16[3,576,1024]{2,1,0:T(8,128)(2,1)}, u32[]{:S(2)}, u32[]{:S(2)}) collective-permute-start(bf16[3,576,1024]{2,1,0:T(8,128)(2,1)} %get-tuple-element.167), channel_id=1, source_target_pairs={{0,8},{1,9},{2,10},{3,11},{4,12},{5,13},{6,14},{7,15},{8,0},{9,1},... | collective-permute-start | bytes 10616840 | tf_op jit(solution)/shard_map/ppermute | solution.py:985
  276.3 41.9 %shard_map.313 = (bf16[3,576,1024]{2,1,0:T(8,128)(2,1)}, bf16[3,576,1024]{2,1,0:T(8,128)(2,1)}, f32[1024,1152]{1,0:T(8,128)}, f32[1024,1152]{1,0:T(8,128)}) custom-call(s32[4]{0:T(128)} %iota.19.slot_ref, s32[1]{0:T(128)} %constant.120.clone.1.place_ref, bf16[1024,1152]{1,0:T(8,128)(2,1)} %get-tuple-element.155.mid_ref, ...), custom_call_target="tpu_custom_call" | custom-call | flops 21743271936 | bytes 42467328 | tf_op jit(solution)/shard_map/pallas_call | solution.py:477
  318.3 5.7 shard_map.314
  325.7 41.4 %shard_map.315 = (bf16[3,576,1024]{2,1,0:T(8,128)(2,1)}, bf16[3,576,1024]{2,1,0:T(8,128)(2,1)}, bf16[1024,1152]{1,0:T(8,128)(2,1)}, f32[1024,1152]{1,0:T(8,128)}) custom-call(s32[4]{0:T(128)} %iota.16.slot_ref, s32[1]{0:T(128)} %constant.120.clone.1.place_ref, bf16[1024,1152]{1,0:T(8,128)(2,1)} %get-tuple-element.155.mid_ref, ...), custom_call_target="tpu_custom_call" | custom-call | flops 21743271936 | bytes 42467328 | tf_op jit(solution)/shard_map/pallas_call | solution.py:477
  369.3 2.9 multiply_reduce_fusion.2
  372.2 4.0 shard_map.316
  381.7 5.6 shard_map.317
  389.0 3.4 multiply_reduce_fusion
  392.4 4.1 fusion.40.rows_ref
  396.6 5.3 shard_map.318
  401.9 4.2 convolution_convert_fusion.2
  406.1 3.5 collective-permute-start.19
  409.6 4.7 convolution_convert_fusion.d_ref
  414.3 5.7 shard_map.319
  421.3 21.3 %shard_map.320 = (bf16[1024,640]{1,0:T(8,128)(2,1)}, bf16[576,640]{1,0:T(8,128)(2,1)}, bf16[576,640]{1,0:T(8,128)(2,1)}) custom-call(bf16[1024,1920]{1,0:T(8,128)(2,1)} %get-tuple-element.152.qkv_ref, bf16[1024,1152]{1,0:T(8,128)(2,1)} %convolution_convert_fusion.d_ref, f32[3,1024,128]{2,1,0:T(8,128)} %get-tuple-element.196.log_ref, ...), custom_call_target="tpu_custom_call" | custom-call | flops 6710886400 | bytes 5242880 | tf_op jit(solution)/shard_map/pallas_call | solution.py:297
  442.6 2.8 fusion.7.home_ref
  445.3 3.0 shard_map.322
  449.0 4.0 shard_map.321
  455.8 20.9 %shard_map.323 = (bf16[1024,640]{1,0:T(8,128)(2,1)}, bf16[576,640]{1,0:T(8,128)(2,1)}, bf16[576,640]{1,0:T(8,128)(2,1)}) custom-call(bf16[1024,1920]{1,0:T(8,128)(2,1)} %get-tuple-element.152.qkv_ref, bf16[1024,1152]{1,0:T(8,128)(2,1)} %convolution_convert_fusion.d_ref, f32[3,1024,128]{2,1,0:T(8,128)} %get-tuple-element.196.log_ref, ...), custom_call_target="tpu_custom_call" | custom-call | flops 6710886400 | bytes 5242880 | tf_op jit(solution)/shard_map/pallas_call | solution.py:297
  476.7 4.4 collective-permute-done.21
  484.4 2.3 shard_map.326
  488.6 4.0 shard_map.324
  492.6 9.1 %collective-permute-done.23.refs_3_ = bf16[3,144,1024]{2,1,0:T(8,128)(2,1)S(1)} collective-permute-done((bf16[3,144,1024]{2,1,0:T(8,128)(2,1)}, bf16[3,144,1024]{2,1,0:T(8,128)(2,1)S(1)}, u32[]{:S(2)}, u32[]{:S(2)}) %collective-permute-start.23) | collective-permute-done | bytes 884768 | tf_op jit(solution)/shard_map/ppermute | solution.py:985
  502.5 21.4 %shard_map.327 = (bf16[1024,640]{1,0:T(8,128)(2,1)}, bf16[576,640]{1,0:T(8,128)(2,1)}, bf16[576,640]{1,0:T(8,128)(2,1)}) custom-call(bf16[1024,1920]{1,0:T(8,128)(2,1)} %get-tuple-element.152.qkv_ref, bf16[1024,1152]{1,0:T(8,128)(2,1)} %convolution_convert_fusion.d_ref, f32[3,1024,128]{2,1,0:T(8,128)} %get-tuple-element.196.log_ref, ...), custom_call_target="tpu_custom_call" | custom-call | flops 6710886400 | bytes 5242880 | tf_op jit(solution)/shard_map/pallas_call | solution.py:297
  523.9 3.9 collective-permute-done.27.refs_0_
  531.8 2.7 shard_map.335
  536.4 2.3 shard_map.329
  539.8 5.7 fusion.15
  546.4 2.3 shard_map.330
  553.8 8.6 %shard_map.332 = (f32[3,144,3072]{2,1,0:T(8,128)}, f32[24,144]{1,0:T(8,128)}) custom-call(s32[1]{0:T(128)} %bitcast.52.flag_ref, bf16[3,144,1024]{2,1,0:T(8,128)(2,1)} %collective-permute-done.16.refs_0_, bf16[3,144,1024]{2,1,0:T(8,128)(2,1)} %get-tuple-element.181.refs_1_, bf16[3,144,1024]{2,1,0:T(8,128)(2,1)} %collective-permute-done.17.refs_2_, ...), custom_call_target="tpu_custom_call" | custom-call | flops 127401984 | bytes 18579456 | tf_op jit(solution)/shard_map/pallas_call | solution.py:603
  571.6 6.1 shard_map.336
  580.1 2.4 collective-permute-start.36
  585.3 5.7 fusion.13
  591.1 12.5 %collective-permute-done.33.refs_0_ = bf16[144,1280]{1,0:T(8,128)(2,1)S(1)} collective-permute-done((bf16[144,1280]{1,0:T(8,128)(2,1)S(1)}, bf16[144,1280]{1,0:T(8,128)(2,1)S(1)}, u32[]{:S(2)}, u32[]{:S(2)}) %collective-permute-start.33) | collective-permute-done | bytes 368672 | tf_op jit(solution)/shard_map/ppermute | solution.py:985
  603.5 2.8 collective-permute-done.36.refs_3_
  607.1 3.4 shard_map.334
  611.6 9.5 %fusion.6 = (f32[1152]{0:T(1024)S(1)}, f32[1024]{0:T(1024)S(1)}, f32[1024,1152]{1,0:T(8,128)}) fusion(bf16[1024,1152]{1,0:T(8,128)(2,1)S(1)} %copy-done.1, f32[1024]{0:T(1024)S(1)} %fusion.34, f32[1152]{0:T(1024)S(1)} %mul.160, bf16[1024,640]{1,0:T(8,128)(2,1)} %get-tuple-element.251, bf16[1152,1920]{1,0:T(8,128)(2,1)} %bitcast.130, ...), kind=kOutput, calls=%fused_computation.14 | convolution fusion | flops 1520564096 | bytes 19317760 | tf_op jit(solution)/shard_map/tn,dn->td/dot_general | solution.py:1298
  625.6 2.6 shard_map.338
  628.4 2.4 collective-permute-start.45
  630.8 3.8 collective-permute-done.50
  636.9 4.9 collective-permute-done.51
  642.4 6.7 fusion.8
  651.0 15.9 %shard_map.337 = (f32[3,144,3072]{2,1,0:T(8,128)}, f32[3,144,3072]{2,1,0:T(8,128)}, f32[1,3,144,3072]{3,2,1,0:T(8,128)}, f32[3,8,3072]{2,1,0:T(8,128)}) custom-call(f32[8,11264]{1,0:T(8,128)} %pad_maximum_fusion.9.row_ref.gram_ref.refs_1_, f32[8,11264]{1,0:T(8,128)} %pad_maximum_fusion.9.row_ref.gram_ref.refs_1_, f32[32,144]{1,0:T(8,128)} %add.189.refs_0_.left_ref.refs_3_, ...), custom_call_target="tpu_custom_call" | custom-call | flops 15925248 | bytes 3981312 | tf_op jit(solution)/shard_map/pallas_call | solution.py:738
  667.8 5.0 collective-permute-done.53
  673.6 4.5 collective-permute-done.54
  678.8 7.3 %shard_map.339 = (f32[2,144,1152]{2,1,0:T(8,128)}, f32[2,144,1152]{2,1,0:T(8,128)}, f32[1,2,144,1152]{3,2,1,0:T(8,128)}, f32[2,8,1152]{2,1,0:T(8,128)}, f32[2,14...) custom-call(f32[8,3584]{1,0:T(8,128)} %copy-done.24, ...), custom_call_target="tpu_custom_call" | custom-call | flops 5308416 | bytes 1327104 | tf_op jit(solution)/shard_map/pallas_call | solution.py:809
  686.8 3.3 broadcast_select_fusion
  (307 shorter events, 93.2 us)
Async XLA Ops:
  7.2 268.6 %all-gather.3.cloned.1.call-start = ((), (), s32[]{:S(2)}) async-start(), calls=%async_computation | async-start | bytes 7299072 | tf_op jit(solution)/shard_map/all_gather | solution.py:1208
  10.1 18.8 %collective-permute-start = (bf16[1,160,1024]{2,1,0:T(8,128)(2,1)S(1)}, bf16[1,160,1024]{2,1,0:T(8,128)(2,1)S(1)}, u32[]{:S(2)}, u32[]{:S(2)}) collective-permute-start(bf16[1,160,1024]{2,1,0:T(8,128)(2,1)S(1)} %fusion.22), channel_id=1, source_target_pairs={{0,4},{1,5},{2,6},{3,7},{4,0},{5,1},{6,2},{7,3},{8,12},{9,13},{10,... | collective-permute-start | bytes 983048 | tf_op jit(solution)/shard_map/ppermute | solution.py:985
  29.0 28.6 %collective-permute-start.2 = (bf16[2,160,1024]{2,1,0:T(8,128)(2,1)S(1)}, bf16[2,160,1024]{2,1,0:T(8,128)(2,1)S(1)}, u32[]{:S(2)}, u32[]{:S(2)}) collective-permute-start(bf16[2,160,1024]{2,1,0:T(8,128)(2,1)S(1)} %pad_maximum_fusion.4), channel_id=1, source_target_pairs={{0,2},{1,3},{2,0},{3,1},{4,6},{5,7},{6,4},{7,5},{8,10},{9,11},{10,... | collective-permute-start | bytes 1966088 | tf_op jit(solution)/shard_map/ppermute | solution.py:985
  30.9 30.1 %copy-start.48 = (s32[1,1024]{1,0:T(1,128)S(1)}, s32[1,1024]{1,0:T(1,128)}, u32[]{:S(2)}) copy-start(s32[1,1024]{1,0:T(1,128)} %param.22) | copy-start | bytes 12292
  30.9 30.8 %copy-start = (s32[8]{0:T(128)S(1)}, s32[8]{0:T(128)}, u32[]{:S(2)}) copy-start(s32[8]{0:T(128)} %constant.143.clone) | copy-start | bytes 100
  30.9 29.3 %collective-permute-start.1 = (bf16[1,144,2048]{2,1,0:T(8,128)(2,1)S(1)}, bf16[1,144,2048]{2,1,0:T(8,128)(2,1)S(1)}, u32[]{:S(2)}, u32[]{:S(2)}) collective-permute-start(bf16[1,144,2048]{2,1,0:T(8,128)(2,1)S(1)} %maximum_bitcast_fusion), channel_id=1, source_target_pairs={{0,4},{1,5},{2,6},{3,7},{4,0},{5,1},{6,2},{7,3},{8,12},{9,13},{10,... | collective-permute-start | bytes 1769480 | tf_op jit(solution)/shard_map/ppermute | solution.py:985
  58.9 29.8 %collective-permute-start.5 = (bf16[4,160,1024]{2,1,0:T(8,128)(2,1)}, bf16[4,160,1024]{2,1,0:T(8,128)(2,1)}, u32[]{:S(2)}, u32[]{:S(2)}) collective-permute-start(bf16[4,160,1024]{2,1,0:T(8,128)(2,1)} %pad_maximum_fusion.2), channel_id=1, source_target_pairs={{0,1},{1,0},{2,3},{3,2},{4,5},{5,4},{6,7},{7,6},{8,9},{9,8},{10,11... | collective-permute-start | bytes 3932168 | tf_op jit(solution)/shard_map/ppermute | solution.py:985
  60.3 26.3 %collective-permute-start.3 = (bf16[2,144,2048]{2,1,0:T(8,128)(2,1)S(1)}, bf16[2,144,2048]{2,1,0:T(8,128)(2,1)S(1)}, u32[]{:S(2)}, u32[]{:S(2)}) collective-permute-start(bf16[2,144,2048]{2,1,0:T(8,128)(2,1)S(1)} %pad_maximum_fusion.3), channel_id=1, source_target_pairs={{0,2},{1,3},{2,0},{3,1},{4,6},{5,7},{6,4},{7,5},{8,10},{9,11},{10,... | collective-permute-start | bytes 3538952 | tf_op jit(solution)/shard_map/ppermute | solution.py:985
  61.0 35.0 %collective-permute-start.7 = (s32[1,1024]{1,0:T(1,128)S(1)}, s32[1,1024]{1,0:T(1,128)S(1)}, u32[]{:S(2)}, u32[]{:S(2)}) collective-permute-start(s32[1,1024]{1,0:T(1,128)S(1)} %copy-done.48), channel_id=1, source_target_pairs={{2,8},{3,9},{6,12},{7,13},{8,2},{9,3},{12,6},{13,7},{18,24},{19,25... | collective-permute-start | bytes 12296 | tf_op jit(solution)/shard_map/ppermute | solution.py:985
  62.4 37.5 %copy-start.47 = (s32[8]{0:T(128)}, s32[8]{0:T(128)S(1)}, u32[]{:S(2)}) copy-start(s32[8]{0:T(128)S(1)} %gather_fusion) | copy-start | bytes 100
  86.6 14.8 %collective-permute-start.4 = (bf16[1,1024,1152]{2,1,0:T(8,128)(2,1)}, bf16[1,1024,1152]{2,1,0:T(8,128)(2,1)}, u32[]{:S(2)}, u32[]{:S(2)}) collective-permute-start(bf16[1,1024,1152]{2,1,0:T(8,128)(2,1)} %param.20), channel_id=1, source_target_pairs={{2,8},{3,9},{6,12},{7,13},{8,2},{9,3},{12,6},{13,7},{18,24},{19,25... | collective-permute-start | bytes 7077896 | tf_op jit(solution)/shard_map/ppermute | solution.py:985
  90.5 15.4 %collective-permute-start.6 = (bf16[8,160,1024]{2,1,0:T(8,128)(2,1)S(1)}, bf16[8,160,1024]{2,1,0:T(8,128)(2,1)}, u32[]{:S(2)}, u32[]{:S(2)}) collective-permute-start(bf16[8,160,1024]{2,1,0:T(8,128)(2,1)S(1)} %pad_maximum_fusion.refs_0_), channel_id=1, source_target_pairs={{0,8},{1,9},{2,10},{3,11},{4,12},{5,13},{6,14},{7,15},{8,0},{9,1},... | collective-permute-start | bytes 7864328 | tf_op jit(solution)/shard_map/ppermute | solution.py:985
  93.9 54.0 %collective-permute-start.8 = (bf16[4,144,2048]{2,1,0:T(8,128)(2,1)}, bf16[4,144,2048]{2,1,0:T(8,128)(2,1)}, u32[]{:S(2)}, u32[]{:S(2)}) collective-permute-start(bf16[4,144,2048]{2,1,0:T(8,128)(2,1)} %pad_maximum_fusion.1), channel_id=1, source_target_pairs={{0,1},{1,0},{2,3},{3,2},{4,5},{5,4},{6,7},{7,6},{8,9},{9,8},{10,11... | collective-permute-start | bytes 7077896 | tf_op jit(solution)/shard_map/ppermute | solution.py:985
  154.9 170.3 %all-gather.5.cloned.1.call-start = ((), (), s32[]{:S(2)}) async-start(), calls=%async_computation.1 | async-start | bytes 7299072 | tf_op jit(solution)/shard_map/all_gather | solution.py:1208
  155.6 44.8 %collective-permute-start.9 = (bf16[8,144,2048]{2,1,0:T(8,128)(2,1)}, bf16[8,144,2048]{2,1,0:T(8,128)(2,1)}, u32[]{:S(2)}, u32[]{:S(2)}) collective-permute-start(bf16[8,144,2048]{2,1,0:T(8,128)(2,1)} %constant_dynamic-update-slice_fusion.refs_2_.refs_3_), channel_id=1, source_target_pairs={{0,8},{1,9},{2,10},{3,11},{4,12},{5,13},{6,14},{7,15},{8,0},{9,1},... | collective-permute-start | bytes 14155784 | tf_op jit(solution)/shard_map/ppermute | solution.py:985
  155.7 37.9 %collective-permute-start.10 = (bf16[1,1024,1152]{2,1,0:T(8,128)(2,1)S(1)}, bf16[1,1024,1152]{2,1,0:T(8,128)(2,1)}, u32[]{:S(2)}, u32[]{:S(2)}) collective-permute-start(bf16[1,1024,1152]{2,1,0:T(8,128)(2,1)S(1)} %copy-done.9), channel_id=1, source_target_pairs={{2,8},{3,9},{6,12},{7,13},{8,2},{9,3},{12,6},{13,7},{18,24},{19,25... | collective-permute-start | bytes 7077896 | tf_op jit(solution)/shard_map/ppermute | solution.py:985
  267.2 51.1 %collective-permute-start.11 = (bf16[3,576,1024]{2,1,0:T(8,128)(2,1)}, bf16[3,576,1024]{2,1,0:T(8,128)(2,1)}, u32[]{:S(2)}, u32[]{:S(2)}) collective-permute-start(bf16[3,576,1024]{2,1,0:T(8,128)(2,1)} %get-tuple-element.167), channel_id=1, source_target_pairs={{0,8},{1,9},{2,10},{3,11},{4,12},{5,13},{6,14},{7,15},{8,0},{9,1},... | collective-permute-start | bytes 10616840 | tf_op jit(solution)/shard_map/ppermute | solution.py:985
  318.2 61.7 %collective-permute-start.13 = (bf16[3,576,1024]{2,1,0:T(8,128)(2,1)}, bf16[3,576,1024]{2,1,0:T(8,128)(2,1)S(1)}, u32[]{:S(2)}, u32[]{:S(2)}) collective-permute-start(bf16[3,576,1024]{2,1,0:T(8,128)(2,1)} %get-tuple-element.168), channel_id=1, source_target_pairs={{0,8},{1,9},{2,10},{3,11},{4,12},{5,13},{6,14},{7,15},{8,0},{9,1},... | collective-permute-start | bytes 10616840 | tf_op jit(solution)/shard_map/ppermute | solution.py:985
  324.0 48.2 %collective-permute-start.12 = (bf16[3,288,1024]{2,1,0:T(8,128)(2,1)}, bf16[3,288,1024]{2,1,0:T(8,128)(2,1)}, u32[]{:S(2)}, u32[]{:S(2)}) collective-permute-start(bf16[3,288,1024]{2,1,0:T(8,128)(2,1)} %get-tuple-element.170), channel_id=1, source_target_pairs={{0,1},{1,0},{2,3},{3,2},{4,5},{5,4},{6,7},{7,6},{8,9},{9,8},{10,11... | collective-permute-start | bytes 5308424 | tf_op jit(solution)/shard_map/ppermute | solution.py:985
  325.6 41.7 %copy-start.38 = (f32[2,8,1152]{2,1,0:T(8,128)S(1)}, f32[2,8,1152]{2,1,0:T(8,128)}, u32[]{:S(2)}) copy-start(f32[2,8,1152]{2,1,0:T(8,128)} %param.33) | copy-start | bytes 221188
  325.7 42.3 %copy-start.14 = (f32[1,2,144,1152]{3,2,1,0:T(8,128)S(1)}, f32[1,2,144,1152]{3,2,1,0:T(8,128)}, u32[]{:S(2)}) copy-start(f32[1,2,144,1152]{3,2,1,0:T(8,128)} %param.30) | copy-start | bytes 3981316
  367.1 39.0 %collective-permute-start.15 = (bf16[3,576,1024]{2,1,0:T(8,128)(2,1)}, bf16[3,576,1024]{2,1,0:T(8,128)(2,1)}, u32[]{:S(2)}, u32[]{:S(2)}) collective-permute-start(bf16[3,576,1024]{2,1,0:T(8,128)(2,1)} %get-tuple-element.178), channel_id=1, source_target_pairs={{0,8},{1,9},{2,10},{3,11},{4,12},{5,13},{6,14},{7,15},{8,0},{9,1},... | collective-permute-start | bytes 10616840 | tf_op jit(solution)/shard_map/ppermute | solution.py:985
  376.2 43.7 %collective-permute-start.16 = (bf16[3,144,1024]{2,1,0:T(8,128)(2,1)}, bf16[3,144,1024]{2,1,0:T(8,128)(2,1)}, u32[]{:S(2)}, u32[]{:S(2)}) collective-permute-start(bf16[3,144,1024]{2,1,0:T(8,128)(2,1)} %get-tuple-element.180), channel_id=1, source_target_pairs={{0,4},{1,5},{2,12},{3,13},{4,0},{5,1},{6,8},{7,9},{8,6},{9,7},{10,... | collective-permute-start | bytes 2654216 | tf_op jit(solution)/shard_map/ppermute | solution.py:985
  378.4 42.9 %collective-permute-start.17 = (bf16[3,144,1024]{2,1,0:T(8,128)(2,1)}, bf16[3,144,1024]{2,1,0:T(8,128)(2,1)}, u32[]{:S(2)}, u32[]{:S(2)}) collective-permute-start(bf16[3,144,1024]{2,1,0:T(8,128)(2,1)} %get-tuple-element.181.refs_1_), channel_id=1, source_target_pairs={{2,8},{3,9},{6,12},{7,13},{8,2},{9,3},{12,6},{13,7},{18,24},{19,25... | collective-permute-start | bytes 2654216 | tf_op jit(solution)/shard_map/ppermute | solution.py:985
  387.3 61.6 %collective-permute-start.18 = (bf16[3,288,1024]{2,1,0:T(8,128)(2,1)}, bf16[3,288,1024]{2,1,0:T(8,128)(2,1)}, u32[]{:S(2)}, u32[]{:S(2)}) collective-permute-start(bf16[3,288,1024]{2,1,0:T(8,128)(2,1)} %get-tuple-element.186), channel_id=1, source_target_pairs={{0,1},{1,0},{2,3},{3,2},{4,5},{5,4},{6,7},{7,6},{8,9},{9,8},{10,11... | collective-permute-start | bytes 5308424 | tf_op jit(solution)/shard_map/ppermute | solution.py:985
  388.0 65.4 %collective-permute-start.14 = (bf16[1,1024,1152]{2,1,0:T(8,128)(2,1)}, bf16[1,1024,1152]{2,1,0:T(8,128)(2,1)S(1)}, u32[]{:S(2)}, u32[]{:S(2)}) collective-permute-start(bf16[1,1024,1152]{2,1,0:T(8,128)(2,1)} %bitcast.131), channel_id=1, source_target_pairs={{2,8},{3,9},{6,12},{7,13},{8,2},{9,3},{12,6},{13,7},{18,24},{19,25... | collective-permute-start | bytes 7077896 | tf_op jit(solution)/shard_map/ppermute | solution.py:985
  406.1 39.3 %collective-permute-start.19 = (bf16[576,1152]{1,0:T(8,128)(2,1)}, bf16[576,1152]{1,0:T(8,128)(2,1)}, u32[]{:S(2)}, u32[]{:S(2)}) collective-permute-start(bf16[576,1152]{1,0:T(8,128)(2,1)} %convolution_convert_fusion.2), channel_id=1, source_target_pairs={{0,8},{1,9},{2,10},{3,11},{4,12},{5,13},{6,14},{7,15},{8,0},{9,1},... | collective-permute-start | bytes 3981320 | tf_op jit(solution)/shard_map/ppermute | solution.py:985
  419.9 64.3 %collective-permute-start.20 = (bf16[3,288,1024]{2,1,0:T(8,128)(2,1)}, bf16[3,288,1024]{2,1,0:T(8,128)(2,1)}, u32[]{:S(2)}, u32[]{:S(2)}) collective-permute-start(bf16[3,288,1024]{2,1,0:T(8,128)(2,1)} %get-tuple-element.193), channel_id=1, source_target_pairs={{0,1},{1,0},{2,3},{3,2},{4,5},{5,4},{6,7},{7,6},{8,9},{9,8},{10,11... | collective-permute-start | bytes 5308424 | tf_op jit(solution)/shard_map/ppermute | solution.py:985
  442.6 41.7 %collective-permute-start.22 = (bf16[576,640]{1,0:T(8,128)(2,1)}, bf16[576,640]{1,0:T(8,128)(2,1)}, u32[]{:S(2)}, u32[]{:S(2)}) collective-permute-start(bf16[576,640]{1,0:T(8,128)(2,1)} %get-tuple-element.205), channel_id=1, source_target_pairs={{0,8},{1,9},{2,10},{3,11},{4,12},{5,13},{6,14},{7,15},{8,0},{9,1},... | collective-permute-start | bytes 2211848 | tf_op jit(solution)/shard_map/ppermute | solution.py:985
  448.3 32.9 %collective-permute-start.21 = (bf16[288,1152]{1,0:T(8,128)(2,1)}, bf16[288,1152]{1,0:T(8,128)(2,1)S(1)}, u32[]{:S(2)}, u32[]{:S(2)}) collective-permute-start(bf16[288,1152]{1,0:T(8,128)(2,1)} %bitcast.150), channel_id=1, source_target_pairs={{0,1},{1,0},{2,3},{3,2},{4,5},{5,4},{6,7},{7,6},{8,9},{9,8},{10,11... | collective-permute-start | bytes 1990664 | tf_op jit(solution)/shard_map/ppermute | solution.py:985
  453.0 48.7 %collective-permute-start.23 = (bf16[3,144,1024]{2,1,0:T(8,128)(2,1)}, bf16[3,144,1024]{2,1,0:T(8,128)(2,1)S(1)}, u32[]{:S(2)}, u32[]{:S(2)}) collective-permute-start(bf16[3,144,1024]{2,1,0:T(8,128)(2,1)} %get-tuple-element.200), channel_id=1, source_target_pairs={{0,4},{1,5},{2,12},{3,13},{4,0},{5,1},{6,8},{7,9},{8,6},{9,7},{10,... | collective-permute-start | bytes 2654216 | tf_op jit(solution)/shard_map/ppermute | solution.py:985
  453.4 48.9 %collective-permute-start.24 = (bf16[3,144,1024]{2,1,0:T(8,128)(2,1)}, bf16[3,144,1024]{2,1,0:T(8,128)(2,1)S(1)}, u32[]{:S(2)}, u32[]{:S(2)}) collective-permute-start(bf16[3,144,1024]{2,1,0:T(8,128)(2,1)} %get-tuple-element.201.refs_4_), channel_id=1, source_target_pairs={{2,8},{3,9},{6,12},{7,13},{8,2},{9,3},{12,6},{13,7},{18,24},{19,25... | collective-permute-start | bytes 2654216 | tf_op jit(solution)/shard_map/ppermute | solution.py:985
  484.3 52.2 %collective-permute-start.26 = (bf16[576,640]{1,0:T(8,128)(2,1)}, bf16[576,640]{1,0:T(8,128)(2,1)}, u32[]{:S(2)}, u32[]{:S(2)}) collective-permute-start(bf16[576,640]{1,0:T(8,128)(2,1)} %get-tuple-element.219), channel_id=1, source_target_pairs={{0,8},{1,9},{2,10},{3,11},{4,12},{5,13},{6,14},{7,15},{8,0},{9,1},... | collective-permute-start | bytes 2211848 | tf_op jit(solution)/shard_map/ppermute | solution.py:985
  486.8 47.8 %collective-permute-start.25 = (bf16[288,640]{1,0:T(8,128)(2,1)}, bf16[288,640]{1,0:T(8,128)(2,1)}, u32[]{:S(2)}, u32[]{:S(2)}) collective-permute-start(bf16[288,640]{1,0:T(8,128)(2,1)} %bitcast.151), channel_id=1, source_target_pairs={{0,1},{1,0},{2,3},{3,2},{4,5},{5,4},{6,7},{7,6},{8,9},{9,8},{10,11... | collective-permute-start | bytes 1105928 | tf_op jit(solution)/shard_map/ppermute | solution.py:985
  487.4 40.4 %collective-permute-start.27 = (bf16[144,1152]{1,0:T(8,128)(2,1)}, bf16[144,1152]{1,0:T(8,128)(2,1)}, u32[]{:S(2)}, u32[]{:S(2)}) collective-permute-start(bf16[144,1152]{1,0:T(8,128)(2,1)} %bitcast.154), channel_id=1, source_target_pairs={{0,4},{1,5},{2,12},{3,13},{4,0},{5,1},{6,8},{7,9},{8,6},{9,7},{10,... | collective-permute-start | bytes 995336 | tf_op jit(solution)/shard_map/ppermute | solution.py:985
  501.7 26.9 %collective-permute-start.28 = (bf16[144,1152]{1,0:T(8,128)(2,1)S(1)}, bf16[144,1152]{1,0:T(8,128)(2,1)S(1)}, u32[]{:S(2)}, u32[]{:S(2)}) collective-permute-start(bf16[144,1152]{1,0:T(8,128)(2,1)S(1)} %bitcast.140), channel_id=1, source_target_pairs={{2,8},{3,9},{6,12},{7,13},{8,2},{9,3},{12,6},{13,7},{18,24},{19,25... | collective-permute-start | bytes 995336 | tf_op jit(solution)/shard_map/ppermute | solution.py:985
  502.4 50.2 %collective-permute-start.29 = (bf16[3,144,1024]{2,1,0:T(8,128)(2,1)}, bf16[3,144,1024]{2,1,0:T(8,128)(2,1)S(1)}, u32[]{:S(2)}, u32[]{:S(2)}) collective-permute-start(bf16[3,144,1024]{2,1,0:T(8,128)(2,1)} %get-tuple-element.210), channel_id=1, source_target_pairs={{0,4},{1,5},{2,12},{3,13},{4,0},{5,1},{6,8},{7,9},{8,6},{9,7},{10,... | collective-permute-start | bytes 2654216 | tf_op jit(solution)/shard_map/ppermute | solution.py:985
  527.8 24.7 %collective-permute-start.30 = (bf16[3,144,1024]{2,1,0:T(8,128)(2,1)S(1)}, bf16[3,144,1024]{2,1,0:T(8,128)(2,1)S(1)}, u32[]{:S(2)}, u32[]{:S(2)}) collective-permute-start(bf16[3,144,1024]{2,1,0:T(8,128)(2,1)S(1)} %copy-done.19), channel_id=1, source_target_pairs={{2,8},{3,9},{6,12},{7,13},{8,2},{9,3},{12,6},{13,7},{18,24},{19,25... | collective-permute-start | bytes 2654216 | tf_op jit(solution)/shard_map/ppermute | solution.py:985
  529.3 16.3 %collective-permute-start.31 = (bf16[576,640]{1,0:T(8,128)(2,1)}, bf16[576,640]{1,0:T(8,128)(2,1)S(1)}, u32[]{:S(2)}, u32[]{:S(2)}) collective-permute-start(bf16[576,640]{1,0:T(8,128)(2,1)} %get-tuple-element.230), channel_id=1, source_target_pairs={{0,8},{1,9},{2,10},{3,11},{4,12},{5,13},{6,14},{7,15},{8,0},{9,1},... | collective-permute-start | bytes 2211848 | tf_op jit(solution)/shard_map/ppermute | solution.py:985
  538.7 11.2 %collective-permute-start.32 = (bf16[288,640]{1,0:T(8,128)(2,1)}, bf16[288,640]{1,0:T(8,128)(2,1)S(1)}, u32[]{:S(2)}, u32[]{:S(2)}) collective-permute-start(bf16[288,640]{1,0:T(8,128)(2,1)} %bitcast.153), channel_id=1, source_target_pairs={{0,1},{1,0},{2,3},{3,2},{4,5},{5,4},{6,7},{7,6},{8,9},{9,8},{10,11... | collective-permute-start | bytes 1105928 | tf_op jit(solution)/shard_map/ppermute | solution.py:985
  548.8 20.2 %collective-permute-start.35 = (bf16[288,640]{1,0:T(8,128)(2,1)}, bf16[288,640]{1,0:T(8,128)(2,1)S(1)}, u32[]{:S(2)}, u32[]{:S(2)}) collective-permute-start(bf16[288,640]{1,0:T(8,128)(2,1)} %bitcast.152), channel_id=1, source_target_pairs={{0,1},{1,0},{2,3},{3,2},{4,5},{5,4},{6,7},{7,6},{8,9},{9,8},{10,11... | collective-permute-start | bytes 1105928 | tf_op jit(solution)/shard_map/ppermute | solution.py:985
  563.2 1.2 collective-permute-start.39
  564.4 3.9 collective-permute-start.40
  565.9 25.2 %collective-permute-start.34 = (bf16[144,1280]{1,0:T(8,128)(2,1)S(1)}, bf16[144,1280]{1,0:T(8,128)(2,1)S(1)}, u32[]{:S(2)}, u32[]{:S(2)}) collective-permute-start(bf16[144,1280]{1,0:T(8,128)(2,1)S(1)} %pad_maximum_fusion.8.refs_1_), channel_id=1, source_target_pairs={{2,8},{3,9},{6,12},{7,13},{8,2},{9,3},{12,6},{13,7},{18,24},{19,25... | collective-permute-start | bytes 1105928 | tf_op jit(solution)/shard_map/ppermute | solution.py:985
  578.7 4.6 collective-permute-start.41
  579.5 24.0 %collective-permute-start.33 = (bf16[144,1280]{1,0:T(8,128)(2,1)S(1)}, bf16[144,1280]{1,0:T(8,128)(2,1)S(1)}, u32[]{:S(2)}, u32[]{:S(2)}) collective-permute-start(bf16[144,1280]{1,0:T(8,128)(2,1)S(1)} %pad_maximum_fusion.7), channel_id=1, source_target_pairs={{0,4},{1,5},{2,12},{3,13},{4,0},{5,1},{6,8},{7,9},{8,6},{9,7},{10,... | collective-permute-start | bytes 1105928 | tf_op jit(solution)/shard_map/ppermute | solution.py:985
  580.1 26.3 %collective-permute-start.36 = (bf16[144,640]{1,0:T(8,128)(2,1)S(1)}, bf16[144,640]{1,0:T(8,128)(2,1)S(1)}, u32[]{:S(2)}, u32[]{:S(2)}) collective-permute-start(bf16[144,640]{1,0:T(8,128)(2,1)S(1)} %bitcast.155), channel_id=1, source_target_pairs={{0,4},{1,5},{2,12},{3,13},{4,0},{5,1},{6,8},{7,9},{8,6},{9,7},{10,... | collective-permute-start | bytes 552968 | tf_op jit(solution)/shard_map/ppermute | solution.py:985
  582.5 23.9 %collective-permute-start.37 = (bf16[144,640]{1,0:T(8,128)(2,1)S(1)}, bf16[144,640]{1,0:T(8,128)(2,1)S(1)}, u32[]{:S(2)}, u32[]{:S(2)}) collective-permute-start(bf16[144,640]{1,0:T(8,128)(2,1)S(1)} %bitcast.145), channel_id=1, source_target_pairs={{2,8},{3,9},{6,12},{7,13},{8,2},{9,3},{12,6},{13,7},{18,24},{19,25... | collective-permute-start | bytes 552968 | tf_op jit(solution)/shard_map/ppermute | solution.py:985
  584.4 26.0 %collective-permute-start.42 = (f32[8,2816]{1,0:T(8,128)S(1)}, f32[8,2816]{1,0:T(8,128)S(1)}, u32[]{:S(2)}, u32[]{:S(2)}) collective-permute-start(f32[8,2816]{1,0:T(8,128)S(1)} %slice_select_fusion.1), channel_id=1, source_target_pairs={{0,16},{1,17},{2,18},{3,19},{4,20},{5,21},{6,22},{7,23},{8,24},{9,... | collective-permute-start | bytes 270344 | tf_op jit(solution)/shard_map/ppermute | solution.py:985
  610.4 10.7 %collective-permute-start.48 = (f32[24,144]{1,0:T(8,128)}, f32[24,144]{1,0:T(8,128)S(1)}, u32[]{:S(2)}, u32[]{:S(2)}) collective-permute-start(f32[24,144]{1,0:T(8,128)} %get-tuple-element.250), channel_id=1, source_target_pairs={{0,8},{1,9},{2,10},{3,11},{4,12},{5,13},{6,14},{7,15},{8,0},{9,1},... | collective-permute-start | bytes 41480 | tf_op jit(solution)/shard_map/ppermute | solution.py:985
  610.4 32.0 %slice-start.2 = ((s8[4718592]{0:T(1024)(128)(4,1)}), s8[4194304]{0:T(1024)(128)(4,1)S(1)}, s32[]{:S(2)}) async-start(s8[4718592]{0:T(1024)(128)(4,1)} %bitcast.125), calls=%async_computation.4 | async-start | bytes 8388608
  610.5 32.0 %slice-start.3 = ((s8[4718592]{0:T(1024)(128)(4,1)}), s8[524288]{0:T(1024)(128)(4,1)S(1)}, s32[]{:S(2)}) async-start(s8[4718592]{0:T(1024)(128)(4,1)} %bitcast.125), calls=%async_computation.5 | async-start | bytes 1048576
  610.5 12.0 %collective-permute-start.43 = (f32[8,2816]{1,0:T(8,128)S(1)}, f32[8,2816]{1,0:T(8,128)S(1)}, u32[]{:S(2)}, u32[]{:S(2)}) collective-permute-start(f32[8,2816]{1,0:T(8,128)S(1)} %select_add_fusion.1), channel_id=1, source_target_pairs={{0,1},{1,0},{2,3},{3,2},{4,5},{5,4},{6,7},{7,6},{8,9},{9,8},{10,11... | collective-permute-start | bytes 270344 | tf_op jit(solution)/shard_map/ppermute | solution.py:985
  621.1 3.9 collective-permute-start.49
  622.5 5.9 collective-permute-start.44
  628.2 6.4 collective-permute-start.50
  628.4 7.5 %collective-permute-start.45 = (f32[8,2816]{1,0:T(8,128)S(1)}, f32[8,2816]{1,0:T(8,128)S(1)}, u32[]{:S(2)}, u32[]{:S(2)}) collective-permute-start(f32[8,2816]{1,0:T(8,128)S(1)} %add.193), channel_id=1, source_target_pairs={{0,4},{1,5},{2,6},{3,7},{4,0},{5,1},{6,2},{7,3},{8,12},{9,13},{10,... | collective-permute-start | bytes 270344 | tf_op jit(solution)/shard_map/ppermute | solution.py:985
  635.5 6.2 collective-permute-start.51
  635.9 5.9 collective-permute-start.46
  641.7 8.4 %collective-permute-start.52 = (f32[8,3584]{1,0:T(8,128)S(1)}, f32[8,3584]{1,0:T(8,128)S(1)}, u32[]{:S(2)}, u32[]{:S(2)}) collective-permute-start(f32[8,3584]{1,0:T(8,128)S(1)} %add.198), channel_id=1, source_target_pairs={{0,8},{1,9},{2,10},{3,11},{4,12},{5,13},{6,14},{7,15},{8,0},{9,1},... | collective-permute-start | bytes 344072 | tf_op jit(solution)/shard_map/ppermute | solution.py:985
  641.9 8.3 %collective-permute-start.47 = (f32[8,5632]{1,0:T(8,128)S(1)}, f32[8,5632]{1,0:T(8,128)S(1)}, u32[]{:S(2)}, u32[]{:S(2)}) collective-permute-start(f32[8,5632]{1,0:T(8,128)S(1)} %pad_maximum_fusion.10), channel_id=1, source_target_pairs={{0,8},{1,9},{2,10},{3,11},{4,12},{5,13},{6,14},{7,15},{8,0},{9,1},... | collective-permute-start | bytes 540680 | tf_op jit(solution)/shard_map/ppermute | solution.py:985
  649.1 37.6 %collective-permute-start.38 = (bf16[1,1024,1152]{2,1,0:T(8,128)(2,1)}, bf16[1,1024,1152]{2,1,0:T(8,128)(2,1)S(1)}, u32[]{:S(2)}, u32[]{:S(2)}) collective-permute-start(bf16[1,1024,1152]{2,1,0:T(8,128)(2,1)} %fusion.8), channel_id=1, source_target_pairs={{2,8},{3,9},{6,12},{7,13},{8,2},{9,3},{12,6},{13,7},{18,24},{19,25... | collective-permute-start | bytes 7077896 | tf_op jit(solution)/shard_map/ppermute | solution.py:985
  667.0 5.9 collective-permute-start.53
  672.9 5.2 collective-permute-start.54
  (52 other events, 481.9 us)
Sparse Core Ops, SparseCore 0:
  155.0 75.2 all-gather.2
  233.7 71.1 all-gather.4

commit v6 on v4

--- a/solution.py
+++ b/solution.py
@@ -1199,15 +1199,18 @@
     order = jnp.array(grid.masks(), jnp.int32) ^ logical_shard
 
     qkv, turned_in = project_qkv(order, tokens, gain_attn[None], qkv_w, cos, sin)
+    held, got = after((mine[1], gathering[-1]), qkv)
+    mine[1] = jnp.concatenate([held, got], axis=0)
+    qkv = after(qkv, mine[1])
     wide_parts = [None] * chained
     for k in range(chained, 3):
-        part = after(cuts[k], gathering[1])
+        part = after(cuts[k], mine[1])
         part = lax.all_gather(part, ("rep", "shard"), axis=0, tiled=True)
         wide_parts.append((natural, whole, [part.reshape(reps, owners * rows, 3 * tile)]))
+    other.append(grid.move(mine[1], grid.flip_rep(0)))
     attended, logs = attend_forward(qkv, place)
-    held, got = after((mine[1], gathering[-1]), attended)
-    mine[1] = jnp.concatenate([held, got], axis=0)
-    other.append(grid.move(mine[1], grid.flip_rep(0)))
+    other[1] = after(other[1], attended)
+    d_out = jnp.where(grid.stays(), cotangent, after(moved_out, attended))[0]
     if chained:
         slots = (natural + core * (reps // 2)) % reps
         wide_parts[0] = (slots, places, [mine[1], other[1]])
@@ -1227,7 +1230,6 @@
         )
         normed_mid = normed(residual, gain_mlp).astype(jnp.bfloat16)
         turned_mid = turn_rows(normed_mid, order)
-    d_out = jnp.where(grid.stays(), cotangent, after(moved_out, normed_mid))[0]
     turned_out = turn_rows(d_out, order)
 
     half = model // 2

time: 727 us -> 685 us (0.942)
  starting transfers between devices: 102 us -> 73.6 us
  waiting for transfers between devices: 133 us -> 116 us
  Pallas kernels: 359 us -> 372 us
    ppermute x55, starting transfers between devices: 102 us -> 73.5 us  [move(): return lax.ppermute(value, ('rep', 'shard'), pairs)]
    ppermute x55, waiting for transfers between devices: 133 us -> 115 us  [move(): return lax.ppermute(value, ('rep', 'shard'), pairs)]
    pallas_call x3, Pallas kernels: 124 us -> 138 us  [mlp_part(): pl.pallas_call(functools.partial(mlp_kernel, reps, first, last), grid_spe...]
  transfers between devices with their start and end apart: 57 -> 57, of which waited for: 17 -> 15; matrix products, arithmetic and copies ran while one was open for 14% -> 13% of each run, Pallas kernels for 50% -> 54%
where the time goes in v6:
time: 685 us; the launch traced here: 683 us
  Pallas kernels  372 us (54%)
  waiting for transfers between devices  116 us (17%)
  starting transfers between devices  73.6 us (11%)
  other arithmetic  53.4 us (8%)
  matrix products  29.8 us (4%)
  local copies, waits for them, and re-layouts  23.1 us (3%)
  between operations  15.2 us (2%)
    pallas_call x3, Pallas kernels, mlp_part(): pl.pallas_call(functools.partial(mlp_kernel, reps, first, last), grid_spe...  138 us
    ppermute x55, waiting for transfers between devices, move(): return lax.ppermute(value, ('rep', 'shard'), pairs)  115 us
    ppermute x55, starting transfers between devices, move(): return lax.ppermute(value, ('rep', 'shard'), pairs)  73.5 us
    pallas_call x3, Pallas kernels, attend_backward(): pl.pallas_call(backward_kernel, grid=(rows // block,), in_specs=[pl.Block...  63.4 us
    pallas_call x14, Pallas kernels, split_sum(): pl.pallas_call(kernel, grid=(lead,), in_specs=[whole, whole], out_specs=[...  46.4 us
    pallas_call x1, Pallas kernels, attend_forward(): pl.pallas_call(forward_kernel, grid=(pairs, rows // block), in_specs=[pl....  33.3 us
    pallas_call x1, Pallas kernels, finish_wide(): pl.pallas_call(kernel, grid=(count,), in_specs=[pl.BlockSpec((8, columns)...  16 us
    dot_general x3, matrix products, back(): jnp.einsum('tn,dn->td', d_stacks[j], qkv_w[:, 640 * j:640 * j + 640], pre...  15.4 us
  transfers between devices with their start and end apart: 57, of which 15 were waited for; matrix products, arithmetic and copies ran while one was open for 13% of the time, Pallas kernels for 54%

profile of v6, /device:TPU:0, one launch (start us, length us, event | category | flops | bytes accessed | tf_op | source)
XLA Modules:
  0.0 682.8 jit_solution(17778648684421979729)
XLA Ops:
  10.1 4.1 collective-permute-start
  14.8 3.0 shard_map.306
  17.8 11.1 %collective-permute-done = bf16[1,160,1024]{2,1,0:T(8,128)(2,1)S(1)} collective-permute-done((bf16[1,160,1024]{2,1,0:T(8,128)(2,1)S(1)}, bf16[1,160,1024]{2,1,0:T(8,128)(2,1)S(1)}, u32[]{:S(2)}, u32[]{:S(2)}) %collective-permute-start) | collective-permute-done | bytes 327712 | tf_op jit(solution)/shard_map/ppermute | solution.py:985
  30.9 3.4 collective-permute-start.1
  34.3 23.3 %collective-permute-done.2 = bf16[2,160,1024]{2,1,0:T(8,128)(2,1)S(1)} collective-permute-done((bf16[2,160,1024]{2,1,0:T(8,128)(2,1)S(1)}, bf16[2,160,1024]{2,1,0:T(8,128)(2,1)S(1)}, u32[]{:S(2)}, u32[]{:S(2)}) %collective-permute-start.2) | collective-permute-done | bytes 655392 | tf_op jit(solution)/shard_map/ppermute | solution.py:985
  62.4 24.2 %collective-permute-done.3 = bf16[2,144,2048]{2,1,0:T(8,128)(2,1)S(1)} collective-permute-done((bf16[2,144,2048]{2,1,0:T(8,128)(2,1)S(1)}, bf16[2,144,2048]{2,1,0:T(8,128)(2,1)S(1)}, u32[]{:S(2)}, u32[]{:S(2)}) %collective-permute-start.3) | collective-permute-done | bytes 1179680 | tf_op jit(solution)/shard_map/ppermute | solution.py:985
  101.4 4.5 fusion.3
  105.9 7.4 %shard_map.307 = bf16[8,144,1920]{2,1,0:T(8,128)(2,1)} custom-call(s32[8]{0:T(128)} %copy-done.38, s32[1]{0:T(128)} %bitcast.1.core_ref, bf16[8,160,1024]{2,1,0:T(8,128)(2,1)} %copy-done.4, bf16[8,160,1024]{2,1,0:T(8,128)(2,1)} %collective-permute-done.6.refs_1_), custom_call_target="tpu_custom_call" | custom-call | bytes 9437184 | tf_op jit(solution)/shard_map/pallas_call | solution.py:541
  113.3 12.0 %shard_map.308 = (bf16[1024,1920]{1,0:T(8,128)(2,1)}, bf16[1152,1024]{1,0:T(8,128)(2,1)}) custom-call(s32[8]{0:T(128)} %broadcast_xor_fusion.order_ref, bf16[1024,1152]{1,0:T(8,128)(2,1)} %get-tuple-element.283.x_ref, f32[1,1152]{1,0:T(1,128)} %slice.111.gain_ref, bf16[1152,1920]{1,0:T(8,128)(2,1)} %bitcast.125, f32[1024,128]{1,0:T(8,128)} %get-tuple-element.301.cos_ref, ...), custom_call_target="tpu_custom_call" | custom-call | flops 4529848320 | bytes 13074432 | tf_op jit(solution)/shard_map/pallas_call | solution.py:88
  125.3 22.6 %collective-permute-done.8 = bf16[4,144,2048]{2,1,0:T(8,128)(2,1)} collective-permute-done((bf16[4,144,2048]{2,1,0:T(8,128)(2,1)}, bf16[4,144,2048]{2,1,0:T(8,128)(2,1)}, u32[]{:S(2)}, u32[]{:S(2)}) %collective-permute-start.8) | collective-permute-done | bytes 2359328 | tf_op jit(solution)/shard_map/ppermute | solution.py:985
  148.0 3.4 constant_dynamic-update-slice_fusion.1
  151.3 3.5 constant_dynamic-update-slice_fusion.refs_2_.refs_3_
  155.7 2.4 collective-permute-start.10
  160.4 33.3 %shard_map.309 = (bf16[1024,1152]{1,0:T(8,128)(2,1)}, f32[3,1024,128]{2,1,0:T(8,128)}) custom-call(bf16[1024,1920]{1,0:T(8,128)(2,1)} %get-tuple-element.153.qkv_ref, s32[1024,1]{1,0:T(8,128)} %copy.40.pos_ref), custom_call_target="tpu_custom_call" | custom-call | flops 8053063680 | bytes 15728640 | tf_op jit(solution)/shard_map/pallas_call | solution.py:185
  195.4 5.1 shard_map.311.refs_1_
  200.5 12.1 %shard_map.310 = (f32[1024,1152]{1,0:T(8,128)}, bf16[1024,1152]{1,0:T(8,128)(2,1)}, bf16[1152,1024]{1,0:T(8,128)(2,1)}, bf16[1152,1152]{1,0:T(8,128)(2,1)}) custom-call(s32[8]{0:T(128)} %copy-done.38, s32[1]{0:T(128)} %bitcast.1.core_ref, s32[8]{0:T(128)} %broadcast_xor_fusion.order_ref, bf16[1024,1152]{1,0:T(8,128)(2,1)} %get-tuple-element.154.att_ref, ...), custom_call_target="tpu_custom_call" | custom-call | flops 2717908992 | bytes 19464192 | tf_op jit(solution)/shard_map/pallas_call | solution.py:930
  212.6 55.0 %shard_map.312 = (bf16[3,576,1024]{2,1,0:T(8,128)(2,1)}, bf16[3,576,1024]{2,1,0:T(8,128)(2,1)}, f32[1024,1152]{1,0:T(8,128)}, f32[1024,1152]{1,0:T(8,128)}) custom-call(s32[4]{0:T(128)} %and_select_fusion.slot_ref, s32[8]{0:T(128)} %copy-done.38, bf16[1024,1152]{1,0:T(8,128)(2,1)} %get-tuple-element.156.mid_ref, ...), custom_call_target="tpu_custom_call" | custom-call | flops 21743271936 | bytes 42467328 | tf_op jit(solution)/shard_map/pallas_call | solution.py:477
  267.5 8.4 %collective-permute-start.11 = (bf16[3,576,1024]{2,1,0:T(8,128)(2,1)}, bf16[3,576,1024]{2,1,0:T(8,128)(2,1)S(1)}, u32[]{:S(2)}, u32[]{:S(2)}) collective-permute-start(bf16[3,576,1024]{2,1,0:T(8,128)(2,1)} %get-tuple-element.168), channel_id=1, source_target_pairs={{0,8},{1,9},{2,10},{3,11},{4,12},{5,13},{6,14},{7,15},{8,0},{9,1},... | collective-permute-start | bytes 10616840 | tf_op jit(solution)/shard_map/ppermute | solution.py:985
  277.8 41.4 %shard_map.313 = (bf16[3,576,1024]{2,1,0:T(8,128)(2,1)}, bf16[3,576,1024]{2,1,0:T(8,128)(2,1)}, f32[1024,1152]{1,0:T(8,128)}, f32[1024,1152]{1,0:T(8,128)}) custom-call(s32[4]{0:T(128)} %iota.19.slot_ref, s32[1]{0:T(128)} %constant.120.clone.1.place_ref, bf16[1024,1152]{1,0:T(8,128)(2,1)} %get-tuple-element.156.mid_ref, ...), custom_call_target="tpu_custom_call" | custom-call | flops 21743271936 | bytes 42467328 | tf_op jit(solution)/shard_map/pallas_call | solution.py:477
  322.1 5.6 shard_map.314
  330.0 41.4 %shard_map.315 = (bf16[3,576,1024]{2,1,0:T(8,128)(2,1)}, bf16[3,576,1024]{2,1,0:T(8,128)(2,1)}, bf16[1024,1152]{1,0:T(8,128)(2,1)}, f32[1024,1152]{1,0:T(8,128)}) custom-call(s32[4]{0:T(128)} %iota.16.slot_ref, s32[1]{0:T(128)} %constant.120.clone.1.place_ref, bf16[1024,1152]{1,0:T(8,128)(2,1)} %get-tuple-element.156.mid_ref, ...), custom_call_target="tpu_custom_call" | custom-call | flops 21743271936 | bytes 42467328 | tf_op jit(solution)/shard_map/pallas_call | solution.py:477
  373.5 2.9 multiply_reduce_fusion.2
  377.6 3.9 shard_map.316
  381.6 2.4 collective-permute-start.16
  385.6 5.6 shard_map.317
  393.9 3.5 multiply_reduce_fusion
  397.4 4.1 fusion.35.rows_ref
  401.5 5.1 shard_map.318
  406.6 4.9 convolution_convert_fusion.2
  413.1 4.7 convolution_convert_fusion.d_ref
  417.8 5.7 shard_map.319
  424.7 21.2 %shard_map.320 = (bf16[1024,640]{1,0:T(8,128)(2,1)}, bf16[576,640]{1,0:T(8,128)(2,1)}, bf16[576,640]{1,0:T(8,128)(2,1)}) custom-call(bf16[1024,1920]{1,0:T(8,128)(2,1)} %get-tuple-element.153.qkv_ref, bf16[1024,1152]{1,0:T(8,128)(2,1)} %convolution_convert_fusion.d_ref, f32[3,1024,128]{2,1,0:T(8,128)} %get-tuple-element.197.log_ref, ...), custom_call_target="tpu_custom_call" | custom-call | flops 6710886400 | bytes 5242880 | tf_op jit(solution)/shard_map/pallas_call | solution.py:297
  445.9 4.8 fusion.7.home_ref
  450.7 2.9 shard_map.322
  454.5 3.9 shard_map.321
  460.8 3.3 broadcast_select_fusion.1
  464.2 20.9 %shard_map.323 = (bf16[1024,640]{1,0:T(8,128)(2,1)}, bf16[576,640]{1,0:T(8,128)(2,1)}, bf16[576,640]{1,0:T(8,128)(2,1)}) custom-call(bf16[1024,1920]{1,0:T(8,128)(2,1)} %get-tuple-element.153.qkv_ref, bf16[1024,1152]{1,0:T(8,128)(2,1)} %convolution_convert_fusion.d_ref, f32[3,1024,128]{2,1,0:T(8,128)} %get-tuple-element.197.log_ref, ...), custom_call_target="tpu_custom_call" | custom-call | flops 6710886400 | bytes 5242880 | tf_op jit(solution)/shard_map/pallas_call | solution.py:297
  489.8 2.3 shard_map.326
  492.1 2.6 collective-permute-start.27
  496.2 3.9 shard_map.324
  500.1 7.6 %collective-permute-done.23.refs_3_ = bf16[3,144,1024]{2,1,0:T(8,128)(2,1)S(1)} collective-permute-done((bf16[3,144,1024]{2,1,0:T(8,128)(2,1)}, bf16[3,144,1024]{2,1,0:T(8,128)(2,1)S(1)}, u32[]{:S(2)}, u32[]{:S(2)}) %collective-permute-start.23) | collective-permute-done | bytes 884768 | tf_op jit(solution)/shard_map/ppermute | solution.py:985
  509.2 21.3 %shard_map.327 = (bf16[1024,640]{1,0:T(8,128)(2,1)}, bf16[576,640]{1,0:T(8,128)(2,1)}, bf16[576,640]{1,0:T(8,128)(2,1)}) custom-call(bf16[1024,1920]{1,0:T(8,128)(2,1)} %get-tuple-element.153.qkv_ref, bf16[1024,1152]{1,0:T(8,128)(2,1)} %convolution_convert_fusion.d_ref, f32[3,1024,128]{2,1,0:T(8,128)} %get-tuple-element.197.log_ref, ...), custom_call_target="tpu_custom_call" | custom-call | flops 6710886400 | bytes 5242880 | tf_op jit(solution)/shard_map/pallas_call | solution.py:297
  530.5 3.3 collective-permute-done.27.refs_0_
  535.2 2.6 shard_map.334
  539.7 2.3 shard_map.329
  543.5 4.0 fusion.9
  547.6 5.8 convolution_add_fusion.1
  553.4 2.3 shard_map.330
  559.0 8.6 %shard_map.332 = (f32[3,144,3072]{2,1,0:T(8,128)}, f32[24,144]{1,0:T(8,128)}) custom-call(s32[1]{0:T(128)} %bitcast.52.flag_ref, bf16[3,144,1024]{2,1,0:T(8,128)(2,1)} %copy-done.19, bf16[3,144,1024]{2,1,0:T(8,128)(2,1)} %get-tuple-element.182.refs_1_, bf16[3,144,1024]{2,1,0:T(8,128)(2,1)} %collective-permute-done.17.refs_2_, ...), custom_call_target="tpu_custom_call" | custom-call | flops 127401984 | bytes 18579456 | tf_op jit(solution)/shard_map/pallas_call | solution.py:603
  576.3 2.5 collective-permute-start.46
  580.2 6.0 shard_map.335
  587.3 2.6 collective-permute-start.37
  589.9 5.5 convolution_add_fusion
  597.7 2.5 collective-permute-done.38
  603.2 3.4 shard_map.337
  609.7 6.7 fusion.2
  620.9 2.6 shard_map.338
  625.7 2.8 collective-permute-done.50
  630.0 5.9 collective-permute-done.51
  636.0 2.3 collective-permute-start.36
  639.1 16.0 %shard_map.336 = (f32[3,144,3072]{2,1,0:T(8,128)}, f32[3,144,3072]{2,1,0:T(8,128)}, f32[1,3,144,3072]{3,2,1,0:T(8,128)}, f32[3,8,3072]{2,1,0:T(8,128)}) custom-call(f32[8,11264]{1,0:T(8,128)} %pad_maximum_fusion.9.row_ref.gram_ref.refs_1_, f32[8,11264]{1,0:T(8,128)} %pad_maximum_fusion.9.row_ref.gram_ref.refs_1_, f32[32,144]{1,0:T(8,128)} %add.185.refs_0_.left_ref.refs_3_, ...), custom_call_target="tpu_custom_call" | custom-call | flops 15925248 | bytes 3981312 | tf_op jit(solution)/shard_map/pallas_call | solution.py:738
  656.1 4.4 collective-permute-done.53
  661.1 4.3 collective-permute-done.54
  666.0 7.3 %shard_map.339 = (f32[2,144,1152]{2,1,0:T(8,128)}, f32[2,144,1152]{2,1,0:T(8,128)}, f32[1,2,144,1152]{3,2,1,0:T(8,128)}, f32[2,8,1152]{2,1,0:T(8,128)}, f32[2,14...) custom-call(f32[8,3584]{1,0:T(8,128)} %copy-done.22, ...), custom_call_target="tpu_custom_call" | custom-call | flops 5308416 | bytes 1327104 | tf_op jit(solution)/shard_map/pallas_call | solution.py:809
  (279 shorter events, 99.1 us)
Async XLA Ops:
  7.2 270.1 %all-gather.3.cloned.1.call-start = ((), (), s32[]{:S(2)}) async-start(), calls=%async_computation | async-start | bytes 7299072 | tf_op jit(solution)/shard_map/all_gather | solution.py:1208
  10.1 18.8 %collective-permute-start = (bf16[1,160,1024]{2,1,0:T(8,128)(2,1)S(1)}, bf16[1,160,1024]{2,1,0:T(8,128)(2,1)S(1)}, u32[]{:S(2)}, u32[]{:S(2)}) collective-permute-start(bf16[1,160,1024]{2,1,0:T(8,128)(2,1)S(1)} %fusion.17), channel_id=1, source_target_pairs={{0,4},{1,5},{2,6},{3,7},{4,0},{5,1},{6,2},{7,3},{8,12},{9,13},{10,... | collective-permute-start | bytes 983048 | tf_op jit(solution)/shard_map/ppermute | solution.py:985
  29.0 28.6 %collective-permute-start.2 = (bf16[2,160,1024]{2,1,0:T(8,128)(2,1)S(1)}, bf16[2,160,1024]{2,1,0:T(8,128)(2,1)S(1)}, u32[]{:S(2)}, u32[]{:S(2)}) collective-permute-start(bf16[2,160,1024]{2,1,0:T(8,128)(2,1)S(1)} %pad_maximum_fusion.4), channel_id=1, source_target_pairs={{0,2},{1,3},{2,0},{3,1},{4,6},{5,7},{6,4},{7,5},{8,10},{9,11},{10,... | collective-permute-start | bytes 1966088 | tf_op jit(solution)/shard_map/ppermute | solution.py:985
  30.9 30.1 %copy-start.39 = (s32[1,1024]{1,0:T(1,128)S(1)}, s32[1,1024]{1,0:T(1,128)}, u32[]{:S(2)}) copy-start(s32[1,1024]{1,0:T(1,128)} %param.22) | copy-start | bytes 12292
  30.9 30.8 %copy-start = (s32[8]{0:T(128)S(1)}, s32[8]{0:T(128)}, u32[]{:S(2)}) copy-start(s32[8]{0:T(128)} %constant.143.clone) | copy-start | bytes 100
  30.9 29.3 %collective-permute-start.1 = (bf16[1,144,2048]{2,1,0:T(8,128)(2,1)S(1)}, bf16[1,144,2048]{2,1,0:T(8,128)(2,1)S(1)}, u32[]{:S(2)}, u32[]{:S(2)}) collective-permute-start(bf16[1,144,2048]{2,1,0:T(8,128)(2,1)S(1)} %maximum_bitcast_fusion), channel_id=1, source_target_pairs={{0,4},{1,5},{2,6},{3,7},{4,0},{5,1},{6,2},{7,3},{8,12},{9,13},{10,... | collective-permute-start | bytes 1769480 | tf_op jit(solution)/shard_map/ppermute | solution.py:985
  58.9 29.8 %collective-permute-start.5 = (bf16[4,160,1024]{2,1,0:T(8,128)(2,1)}, bf16[4,160,1024]{2,1,0:T(8,128)(2,1)}, u32[]{:S(2)}, u32[]{:S(2)}) collective-permute-start(bf16[4,160,1024]{2,1,0:T(8,128)(2,1)} %pad_maximum_fusion.2), channel_id=1, source_target_pairs={{0,1},{1,0},{2,3},{3,2},{4,5},{5,4},{6,7},{7,6},{8,9},{9,8},{10,11... | collective-permute-start | bytes 3932168 | tf_op jit(solution)/shard_map/ppermute | solution.py:985
  60.3 28.4 %copy-start.7 = (bf16[2,144,2048]{2,1,0:T(8,128)(2,1)}, bf16[2,144,2048]{2,1,0:T(8,128)(2,1)S(1)}, u32[]{:S(2)}) copy-start(bf16[2,144,2048]{2,1,0:T(8,128)(2,1)S(1)} %pad_maximum_fusion.3) | copy-start | bytes 3538948
  60.3 26.3 %collective-permute-start.3 = (bf16[2,144,2048]{2,1,0:T(8,128)(2,1)S(1)}, bf16[2,144,2048]{2,1,0:T(8,128)(2,1)S(1)}, u32[]{:S(2)}, u32[]{:S(2)}) collective-permute-start(bf16[2,144,2048]{2,1,0:T(8,128)(2,1)S(1)} %pad_maximum_fusion.3), channel_id=1, source_target_pairs={{0,2},{1,3},{2,0},{3,1},{4,6},{5,7},{6,4},{7,5},{8,10},{9,11},{10,... | collective-permute-start | bytes 3538952 | tf_op jit(solution)/shard_map/ppermute | solution.py:985
  61.0 35.0 %collective-permute-start.7 = (s32[1,1024]{1,0:T(1,128)S(1)}, s32[1,1024]{1,0:T(1,128)S(1)}, u32[]{:S(2)}, u32[]{:S(2)}) collective-permute-start(s32[1,1024]{1,0:T(1,128)S(1)} %copy-done.39), channel_id=1, source_target_pairs={{2,8},{3,9},{6,12},{7,13},{8,2},{9,3},{12,6},{13,7},{18,24},{19,25... | collective-permute-start | bytes 12296 | tf_op jit(solution)/shard_map/ppermute | solution.py:985
  62.4 37.5 %copy-start.38 = (s32[8]{0:T(128)}, s32[8]{0:T(128)S(1)}, u32[]{:S(2)}) copy-start(s32[8]{0:T(128)S(1)} %gather_fusion) | copy-start | bytes 100
  86.6 14.8 %collective-permute-start.4 = (bf16[1,1024,1152]{2,1,0:T(8,128)(2,1)}, bf16[1,1024,1152]{2,1,0:T(8,128)(2,1)}, u32[]{:S(2)}, u32[]{:S(2)}) collective-permute-start(bf16[1,1024,1152]{2,1,0:T(8,128)(2,1)} %param.20), channel_id=1, source_target_pairs={{2,8},{3,9},{6,12},{7,13},{8,2},{9,3},{12,6},{13,7},{18,24},{19,25... | collective-permute-start | bytes 7077896 | tf_op jit(solution)/shard_map/ppermute | solution.py:985
  90.5 15.3 %collective-permute-start.6 = (bf16[8,160,1024]{2,1,0:T(8,128)(2,1)S(1)}, bf16[8,160,1024]{2,1,0:T(8,128)(2,1)}, u32[]{:S(2)}, u32[]{:S(2)}) collective-permute-start(bf16[8,160,1024]{2,1,0:T(8,128)(2,1)S(1)} %pad_maximum_fusion.refs_0_), channel_id=1, source_target_pairs={{0,8},{1,9},{2,10},{3,11},{4,12},{5,13},{6,14},{7,15},{8,0},{9,1},... | collective-permute-start | bytes 7864328 | tf_op jit(solution)/shard_map/ppermute | solution.py:985
  93.9 54.0 %collective-permute-start.8 = (bf16[4,144,2048]{2,1,0:T(8,128)(2,1)}, bf16[4,144,2048]{2,1,0:T(8,128)(2,1)}, u32[]{:S(2)}, u32[]{:S(2)}) collective-permute-start(bf16[4,144,2048]{2,1,0:T(8,128)(2,1)} %pad_maximum_fusion.1), channel_id=1, source_target_pairs={{0,1},{1,0},{2,3},{3,2},{4,5},{5,4},{6,7},{7,6},{8,9},{9,8},{10,11... | collective-permute-start | bytes 7077896 | tf_op jit(solution)/shard_map/ppermute | solution.py:985
  154.9 174.6 %all-gather.5.cloned.1.call-start = ((), (), s32[]{:S(2)}) async-start(), calls=%async_computation.1 | async-start | bytes 7299072 | tf_op jit(solution)/shard_map/all_gather | solution.py:1208
  155.6 44.9 %collective-permute-start.9 = (bf16[8,144,2048]{2,1,0:T(8,128)(2,1)}, bf16[8,144,2048]{2,1,0:T(8,128)(2,1)}, u32[]{:S(2)}, u32[]{:S(2)}) collective-permute-start(bf16[8,144,2048]{2,1,0:T(8,128)(2,1)} %constant_dynamic-update-slice_fusion.refs_2_.refs_3_), channel_id=1, source_target_pairs={{0,8},{1,9},{2,10},{3,11},{4,12},{5,13},{6,14},{7,15},{8,0},{9,1},... | collective-permute-start | bytes 14155784 | tf_op jit(solution)/shard_map/ppermute | solution.py:985
  155.7 38.0 %collective-permute-start.10 = (bf16[1,1024,1152]{2,1,0:T(8,128)(2,1)S(1)}, bf16[1,1024,1152]{2,1,0:T(8,128)(2,1)}, u32[]{:S(2)}, u32[]{:S(2)}) collective-permute-start(bf16[1,1024,1152]{2,1,0:T(8,128)(2,1)S(1)} %copy-done.13), channel_id=1, source_target_pairs={{2,8},{3,9},{6,12},{7,13},{8,2},{9,3},{12,6},{13,7},{18,24},{19,25... | collective-permute-start | bytes 7077896 | tf_op jit(solution)/shard_map/ppermute | solution.py:985
  267.5 52.8 %collective-permute-start.11 = (bf16[3,576,1024]{2,1,0:T(8,128)(2,1)}, bf16[3,576,1024]{2,1,0:T(8,128)(2,1)S(1)}, u32[]{:S(2)}, u32[]{:S(2)}) collective-permute-start(bf16[3,576,1024]{2,1,0:T(8,128)(2,1)} %get-tuple-element.168), channel_id=1, source_target_pairs={{0,8},{1,9},{2,10},{3,11},{4,12},{5,13},{6,14},{7,15},{8,0},{9,1},... | collective-permute-start | bytes 10616840 | tf_op jit(solution)/shard_map/ppermute | solution.py:985
  277.8 41.7 %copy-start.23 = (f32[1,2,144,384]{3,2,1,0:T(8,128)S(1)}, f32[1,2,144,384]{3,2,1,0:T(8,128)}, u32[]{:S(2)}) copy-start(f32[1,2,144,384]{3,2,1,0:T(8,128)} %param.31) | copy-start | bytes 1327108
  319.3 66.4 %collective-permute-start.13 = (bf16[3,576,1024]{2,1,0:T(8,128)(2,1)}, bf16[3,576,1024]{2,1,0:T(8,128)(2,1)}, u32[]{:S(2)}, u32[]{:S(2)}) collective-permute-start(bf16[3,576,1024]{2,1,0:T(8,128)(2,1)} %get-tuple-element.169), channel_id=1, source_target_pairs={{0,8},{1,9},{2,10},{3,11},{4,12},{5,13},{6,14},{7,15},{8,0},{9,1},... | collective-permute-start | bytes 10616840 | tf_op jit(solution)/shard_map/ppermute | solution.py:985
  327.8 48.6 %collective-permute-start.12 = (bf16[3,288,1024]{2,1,0:T(8,128)(2,1)}, bf16[3,288,1024]{2,1,0:T(8,128)(2,1)S(1)}, u32[]{:S(2)}, u32[]{:S(2)}) collective-permute-start(bf16[3,288,1024]{2,1,0:T(8,128)(2,1)} %get-tuple-element.171), channel_id=1, source_target_pairs={{0,1},{1,0},{2,3},{3,2},{4,5},{5,4},{6,7},{7,6},{8,9},{9,8},{10,11... | collective-permute-start | bytes 5308424 | tf_op jit(solution)/shard_map/ppermute | solution.py:985
  330.0 41.5 %copy-start.31 = (f32[2,8,384]{2,1,0:T(8,128)S(1)}, f32[2,8,384]{2,1,0:T(8,128)}, u32[]{:S(2)}) copy-start(f32[2,8,384]{2,1,0:T(8,128)} %param.34) | copy-start | bytes 73732
  330.0 42.1 %copy-start.16 = (f32[1,2,144,1152]{3,2,1,0:T(8,128)S(1)}, f32[1,2,144,1152]{3,2,1,0:T(8,128)}, u32[]{:S(2)}) copy-start(f32[1,2,144,1152]{3,2,1,0:T(8,128)} %param.30) | copy-start | bytes 3981316
  371.4 40.1 %collective-permute-start.15 = (bf16[3,576,1024]{2,1,0:T(8,128)(2,1)}, bf16[3,576,1024]{2,1,0:T(8,128)(2,1)}, u32[]{:S(2)}, u32[]{:S(2)}) collective-permute-start(bf16[3,576,1024]{2,1,0:T(8,128)(2,1)} %get-tuple-element.179), channel_id=1, source_target_pairs={{0,8},{1,9},{2,10},{3,11},{4,12},{5,13},{6,14},{7,15},{8,0},{9,1},... | collective-permute-start | bytes 10616840 | tf_op jit(solution)/shard_map/ppermute | solution.py:985
  381.6 42.0 %collective-permute-start.16 = (bf16[3,144,1024]{2,1,0:T(8,128)(2,1)}, bf16[3,144,1024]{2,1,0:T(8,128)(2,1)S(1)}, u32[]{:S(2)}, u32[]{:S(2)}) collective-permute-start(bf16[3,144,1024]{2,1,0:T(8,128)(2,1)} %get-tuple-element.181), channel_id=1, source_target_pairs={{0,4},{1,5},{2,12},{3,13},{4,0},{5,1},{6,8},{7,9},{8,6},{9,7},{10,... | collective-permute-start | bytes 2654216 | tf_op jit(solution)/shard_map/ppermute | solution.py:985
  384.0 40.7 %collective-permute-start.17 = (bf16[3,144,1024]{2,1,0:T(8,128)(2,1)}, bf16[3,144,1024]{2,1,0:T(8,128)(2,1)}, u32[]{:S(2)}, u32[]{:S(2)}) collective-permute-start(bf16[3,144,1024]{2,1,0:T(8,128)(2,1)} %get-tuple-element.182.refs_1_), channel_id=1, source_target_pairs={{2,8},{3,9},{6,12},{7,13},{8,2},{9,3},{12,6},{13,7},{18,24},{19,25... | collective-permute-start | bytes 2654216 | tf_op jit(solution)/shard_map/ppermute | solution.py:985
  391.3 63.2 %collective-permute-start.18 = (bf16[3,288,1024]{2,1,0:T(8,128)(2,1)}, bf16[3,288,1024]{2,1,0:T(8,128)(2,1)}, u32[]{:S(2)}, u32[]{:S(2)}) collective-permute-start(bf16[3,288,1024]{2,1,0:T(8,128)(2,1)} %get-tuple-element.187), channel_id=1, source_target_pairs={{0,1},{1,0},{2,3},{3,2},{4,5},{5,4},{6,7},{7,6},{8,9},{9,8},{10,11... | collective-permute-start | bytes 5308424 | tf_op jit(solution)/shard_map/ppermute | solution.py:985
  391.8 67.5 %collective-permute-start.14 = (bf16[1,1024,1152]{2,1,0:T(8,128)(2,1)}, bf16[1,1024,1152]{2,1,0:T(8,128)(2,1)}, u32[]{:S(2)}, u32[]{:S(2)}) collective-permute-start(bf16[1,1024,1152]{2,1,0:T(8,128)(2,1)} %bitcast.130), channel_id=1, source_target_pairs={{2,8},{3,9},{6,12},{7,13},{8,2},{9,3},{12,6},{13,7},{18,24},{19,25... | collective-permute-start | bytes 7077896 | tf_op jit(solution)/shard_map/ppermute | solution.py:985
  411.5 39.2 %collective-permute-start.19 = (bf16[576,1152]{1,0:T(8,128)(2,1)}, bf16[576,1152]{1,0:T(8,128)(2,1)}, u32[]{:S(2)}, u32[]{:S(2)}) collective-permute-start(bf16[576,1152]{1,0:T(8,128)(2,1)} %convolution_convert_fusion.2), channel_id=1, source_target_pairs={{0,8},{1,9},{2,10},{3,11},{4,12},{5,13},{6,14},{7,15},{8,0},{9,1},... | collective-permute-start | bytes 3981320 | tf_op jit(solution)/shard_map/ppermute | solution.py:985
  423.5 71.2 %collective-permute-start.20 = (bf16[3,288,1024]{2,1,0:T(8,128)(2,1)}, bf16[3,288,1024]{2,1,0:T(8,128)(2,1)}, u32[]{:S(2)}, u32[]{:S(2)}) collective-permute-start(bf16[3,288,1024]{2,1,0:T(8,128)(2,1)} %get-tuple-element.194), channel_id=1, source_target_pairs={{0,1},{1,0},{2,3},{3,2},{4,5},{5,4},{6,7},{7,6},{8,9},{9,8},{10,11... | collective-permute-start | bytes 5308424 | tf_op jit(solution)/shard_map/ppermute | solution.py:985
  450.7 39.1 %collective-permute-start.22 = (bf16[576,640]{1,0:T(8,128)(2,1)}, bf16[576,640]{1,0:T(8,128)(2,1)}, u32[]{:S(2)}, u32[]{:S(2)}) collective-permute-start(bf16[576,640]{1,0:T(8,128)(2,1)} %get-tuple-element.206), channel_id=1, source_target_pairs={{0,8},{1,9},{2,10},{3,11},{4,12},{5,13},{6,14},{7,15},{8,0},{9,1},... | collective-permute-start | bytes 2211848 | tf_op jit(solution)/shard_map/ppermute | solution.py:985
  453.6 31.5 %collective-permute-start.21 = (bf16[288,1152]{1,0:T(8,128)(2,1)}, bf16[288,1152]{1,0:T(8,128)(2,1)}, u32[]{:S(2)}, u32[]{:S(2)}) collective-permute-start(bf16[288,1152]{1,0:T(8,128)(2,1)} %bitcast.145), channel_id=1, source_target_pairs={{0,1},{1,0},{2,3},{3,2},{4,5},{5,4},{6,7},{7,6},{8,9},{9,8},{10,11... | collective-permute-start | bytes 1990664 | tf_op jit(solution)/shard_map/ppermute | solution.py:985
  458.4 49.3 %collective-permute-start.23 = (bf16[3,144,1024]{2,1,0:T(8,128)(2,1)}, bf16[3,144,1024]{2,1,0:T(8,128)(2,1)S(1)}, u32[]{:S(2)}, u32[]{:S(2)}) collective-permute-start(bf16[3,144,1024]{2,1,0:T(8,128)(2,1)} %get-tuple-element.201), channel_id=1, source_target_pairs={{0,4},{1,5},{2,12},{3,13},{4,0},{5,1},{6,8},{7,9},{8,6},{9,7},{10,... | collective-permute-start | bytes 2654216 | tf_op jit(solution)/shard_map/ppermute | solution.py:985
  459.2 49.9 %collective-permute-start.24 = (bf16[3,144,1024]{2,1,0:T(8,128)(2,1)}, bf16[3,144,1024]{2,1,0:T(8,128)(2,1)}, u32[]{:S(2)}, u32[]{:S(2)}) collective-permute-start(bf16[3,144,1024]{2,1,0:T(8,128)(2,1)} %get-tuple-element.202.refs_4_), channel_id=1, source_target_pairs={{2,8},{3,9},{6,12},{7,13},{8,2},{9,3},{12,6},{13,7},{18,24},{19,25... | collective-permute-start | bytes 2654216 | tf_op jit(solution)/shard_map/ppermute | solution.py:985
  485.1 54.6 %collective-permute-start.26 = (bf16[576,640]{1,0:T(8,128)(2,1)}, bf16[576,640]{1,0:T(8,128)(2,1)}, u32[]{:S(2)}, u32[]{:S(2)}) collective-permute-start(bf16[576,640]{1,0:T(8,128)(2,1)} %get-tuple-element.220), channel_id=1, source_target_pairs={{0,8},{1,9},{2,10},{3,11},{4,12},{5,13},{6,14},{7,15},{8,0},{9,1},... | collective-permute-start | bytes 2211848 | tf_op jit(solution)/shard_map/ppermute | solution.py:985
  492.1 41.7 %collective-permute-start.27 = (bf16[144,1152]{1,0:T(8,128)(2,1)}, bf16[144,1152]{1,0:T(8,128)(2,1)S(1)}, u32[]{:S(2)}, u32[]{:S(2)}) collective-permute-start(bf16[144,1152]{1,0:T(8,128)(2,1)} %bitcast.149), channel_id=1, source_target_pairs={{0,4},{1,5},{2,12},{3,13},{4,0},{5,1},{6,8},{7,9},{8,6},{9,7},{10,... | collective-permute-start | bytes 995336 | tf_op jit(solution)/shard_map/ppermute | solution.py:985
  494.8 39.7 %collective-permute-start.28 = (bf16[144,1152]{1,0:T(8,128)(2,1)}, bf16[144,1152]{1,0:T(8,128)(2,1)}, u32[]{:S(2)}, u32[]{:S(2)}) collective-permute-start(bf16[144,1152]{1,0:T(8,128)(2,1)} %bitcast.134), channel_id=1, source_target_pairs={{2,8},{3,9},{6,12},{7,13},{8,2},{9,3},{12,6},{13,7},{18,24},{19,25... | collective-permute-start | bytes 995336 | tf_op jit(solution)/shard_map/ppermute | solution.py:985
  507.7 30.0 %collective-permute-start.25 = (bf16[288,640]{1,0:T(8,128)(2,1)}, bf16[288,640]{1,0:T(8,128)(2,1)}, u32[]{:S(2)}, u32[]{:S(2)}) collective-permute-start(bf16[288,640]{1,0:T(8,128)(2,1)} %bitcast.147), channel_id=1, source_target_pairs={{0,1},{1,0},{2,3},{3,2},{4,5},{5,4},{6,7},{7,6},{8,9},{9,8},{10,11... | collective-permute-start | bytes 1105928 | tf_op jit(solution)/shard_map/ppermute | solution.py:985
  509.2 48.9 %collective-permute-start.29 = (bf16[3,144,1024]{2,1,0:T(8,128)(2,1)}, bf16[3,144,1024]{2,1,0:T(8,128)(2,1)}, u32[]{:S(2)}, u32[]{:S(2)}) collective-permute-start(bf16[3,144,1024]{2,1,0:T(8,128)(2,1)} %get-tuple-element.211), channel_id=1, source_target_pairs={{0,4},{1,5},{2,12},{3,13},{4,0},{5,1},{6,8},{7,9},{8,6},{9,7},{10,... | collective-permute-start | bytes 2654216 | tf_op jit(solution)/shard_map/ppermute | solution.py:985
  533.8 24.3 %collective-permute-start.30 = (bf16[3,144,1024]{2,1,0:T(8,128)(2,1)}, bf16[3,144,1024]{2,1,0:T(8,128)(2,1)S(1)}, u32[]{:S(2)}, u32[]{:S(2)}) collective-permute-start(bf16[3,144,1024]{2,1,0:T(8,128)(2,1)} %get-tuple-element.212.refs_7_), channel_id=1, source_target_pairs={{2,8},{3,9},{6,12},{7,13},{8,2},{9,3},{12,6},{13,7},{18,24},{19,25... | collective-permute-start | bytes 2654216 | tf_op jit(solution)/shard_map/ppermute | solution.py:985
  534.5 18.9 %collective-permute-start.31 = (bf16[576,640]{1,0:T(8,128)(2,1)}, bf16[576,640]{1,0:T(8,128)(2,1)}, u32[]{:S(2)}, u32[]{:S(2)}) collective-permute-start(bf16[576,640]{1,0:T(8,128)(2,1)} %get-tuple-element.231), channel_id=1, source_target_pairs={{0,8},{1,9},{2,10},{3,11},{4,12},{5,13},{6,14},{7,15},{8,0},{9,1},... | collective-permute-start | bytes 2211848 | tf_op jit(solution)/shard_map/ppermute | solution.py:985
  542.0 14.2 %collective-permute-start.32 = (bf16[288,640]{1,0:T(8,128)(2,1)}, bf16[288,640]{1,0:T(8,128)(2,1)}, u32[]{:S(2)}, u32[]{:S(2)}) collective-permute-start(bf16[288,640]{1,0:T(8,128)(2,1)} %bitcast.148), channel_id=1, source_target_pairs={{0,1},{1,0},{2,3},{3,2},{4,5},{5,4},{6,7},{7,6},{8,9},{9,8},{10,11... | collective-permute-start | bytes 1105928 | tf_op jit(solution)/shard_map/ppermute | solution.py:985
  555.7 18.8 %collective-permute-start.33 = (bf16[288,640]{1,0:T(8,128)(2,1)}, bf16[288,640]{1,0:T(8,128)(2,1)}, u32[]{:S(2)}, u32[]{:S(2)}) collective-permute-start(bf16[288,640]{1,0:T(8,128)(2,1)} %bitcast.146), channel_id=1, source_target_pairs={{0,1},{1,0},{2,3},{3,2},{4,5},{5,4},{6,7},{7,6},{8,9},{9,8},{10,11... | collective-permute-start | bytes 1105928 | tf_op jit(solution)/shard_map/ppermute | solution.py:985
  568.3 1.2 collective-permute-start.34
  569.5 4.3 collective-permute-start.35
  572.7 29.7 %collective-permute-start.45 = (bf16[144,1280]{1,0:T(8,128)(2,1)S(1)}, bf16[144,1280]{1,0:T(8,128)(2,1)S(1)}, u32[]{:S(2)}, u32[]{:S(2)}) collective-permute-start(bf16[144,1280]{1,0:T(8,128)(2,1)S(1)} %pad_maximum_fusion.8.refs_1_), channel_id=1, source_target_pairs={{2,8},{3,9},{6,12},{7,13},{8,2},{9,3},{12,6},{13,7},{18,24},{19,25... | collective-permute-start | bytes 1105928 | tf_op jit(solution)/shard_map/ppermute | solution.py:985
  573.4 29.0 %collective-permute-start.44 = (bf16[144,1280]{1,0:T(8,128)(2,1)}, bf16[144,1280]{1,0:T(8,128)(2,1)S(1)}, u32[]{:S(2)}, u32[]{:S(2)}) collective-permute-start(bf16[144,1280]{1,0:T(8,128)(2,1)} %pad_maximum_fusion.7), channel_id=1, source_target_pairs={{0,4},{1,5},{2,12},{3,13},{4,0},{5,1},{6,8},{7,9},{8,6},{9,7},{10,... | collective-permute-start | bytes 1105928 | tf_op jit(solution)/shard_map/ppermute | solution.py:985
  576.3 26.0 %collective-permute-start.46 = (bf16[144,640]{1,0:T(8,128)(2,1)}, bf16[144,640]{1,0:T(8,128)(2,1)}, u32[]{:S(2)}, u32[]{:S(2)}) collective-permute-start(bf16[144,640]{1,0:T(8,128)(2,1)} %bitcast.150), channel_id=1, source_target_pairs={{0,4},{1,5},{2,12},{3,13},{4,0},{5,1},{6,8},{7,9},{8,6},{9,7},{10,... | collective-permute-start | bytes 552968 | tf_op jit(solution)/shard_map/ppermute | solution.py:985
  578.9 23.5 %collective-permute-start.47 = (bf16[144,640]{1,0:T(8,128)(2,1)}, bf16[144,640]{1,0:T(8,128)(2,1)}, u32[]{:S(2)}, u32[]{:S(2)}) collective-permute-start(bf16[144,640]{1,0:T(8,128)(2,1)} %bitcast.137), channel_id=1, source_target_pairs={{2,8},{3,9},{6,12},{7,13},{8,2},{9,3},{12,6},{13,7},{18,24},{19,25... | collective-permute-start | bytes 552968 | tf_op jit(solution)/shard_map/ppermute | solution.py:985
  587.3 8.2 %collective-permute-start.37 = (f32[8,5632]{1,0:T(8,128)S(1)}, f32[8,5632]{1,0:T(8,128)S(1)}, u32[]{:S(2)}, u32[]{:S(2)}) collective-permute-start(f32[8,5632]{1,0:T(8,128)S(1)} %slice_select_fusion), channel_id=1, source_target_pairs={{0,8},{1,9},{2,10},{3,11},{4,12},{5,13},{6,14},{7,15},{8,0},{9,1},... | collective-permute-start | bytes 540680 | tf_op jit(solution)/shard_map/ppermute | solution.py:985
  595.5 4.6 collective-permute-start.38
  600.2 6.4 collective-permute-start.39
  606.6 9.8 %collective-permute-start.48 = (f32[24,144]{1,0:T(8,128)}, f32[24,144]{1,0:T(8,128)S(1)}, u32[]{:S(2)}, u32[]{:S(2)}) collective-permute-start(f32[24,144]{1,0:T(8,128)} %get-tuple-element.257), channel_id=1, source_target_pairs={{0,8},{1,9},{2,10},{3,11},{4,12},{5,13},{6,14},{7,15},{8,0},{9,1},... | collective-permute-start | bytes 41480 | tf_op jit(solution)/shard_map/ppermute | solution.py:985
  607.5 9.6 %collective-permute-start.40 = (f32[8,2816]{1,0:T(8,128)S(1)}, f32[8,2816]{1,0:T(8,128)S(1)}, u32[]{:S(2)}, u32[]{:S(2)}) collective-permute-start(f32[8,2816]{1,0:T(8,128)S(1)} %add.192), channel_id=1, source_target_pairs={{0,2},{1,3},{2,0},{3,1},{4,6},{5,7},{6,4},{7,5},{8,10},{9,11},{10,... | collective-permute-start | bytes 270344 | tf_op jit(solution)/shard_map/ppermute | solution.py:985
  616.4 3.9 collective-permute-start.49
  617.1 7.1 %collective-permute-start.41 = (f32[8,2816]{1,0:T(8,128)S(1)}, f32[8,2816]{1,0:T(8,128)S(1)}, u32[]{:S(2)}, u32[]{:S(2)}) collective-permute-start(f32[8,2816]{1,0:T(8,128)S(1)} %add.193), channel_id=1, source_target_pairs={{0,4},{1,5},{2,6},{3,7},{4,0},{5,1},{6,2},{7,3},{8,12},{9,13},{10,... | collective-permute-start | bytes 270344 | tf_op jit(solution)/shard_map/ppermute | solution.py:985
  623.5 5.0 collective-permute-start.50
  624.2 5.7 collective-permute-start.42
  629.4 6.5 collective-permute-start.51
  629.9 8.4 %collective-permute-start.43 = (f32[8,5632]{1,0:T(8,128)S(1)}, f32[8,5632]{1,0:T(8,128)S(1)}, u32[]{:S(2)}, u32[]{:S(2)}) collective-permute-start(f32[8,5632]{1,0:T(8,128)S(1)} %pad_maximum_fusion.10), channel_id=1, source_target_pairs={{0,8},{1,9},{2,10},{3,11},{4,12},{5,13},{6,14},{7,15},{8,0},{9,1},... | collective-permute-start | bytes 540680 | tf_op jit(solution)/shard_map/ppermute | solution.py:985
  635.9 2.4 collective-permute-start.52
  636.0 38.1 %collective-permute-start.36 = (bf16[1,1024,1152]{2,1,0:T(8,128)(2,1)S(1)}, bf16[1,1024,1152]{2,1,0:T(8,128)(2,1)}, u32[]{:S(2)}, u32[]{:S(2)}) collective-permute-start(bf16[1,1024,1152]{2,1,0:T(8,128)(2,1)S(1)} %bitcast.129), channel_id=1, source_target_pairs={{2,8},{3,9},{6,12},{7,13},{8,2},{9,3},{12,6},{13,7},{18,24},{19,25... | collective-permute-start | bytes 7077896 | tf_op jit(solution)/shard_map/ppermute | solution.py:985
  655.1 5.4 collective-permute-start.53
  660.5 4.9 collective-permute-start.54
  (38 other events, 299.3 us)
Sparse Core Ops, SparseCore 0:
  155.0 75.0 all-gather.2
  233.6 71.1 all-gather.4
